TPU v7x, 32 devices: a whole 2x2x4 slice. The times are simulated.
32 devices in a mesh: fsdp: 8 (over z, core), replica: 4 (over y, x).
Axes of the slice: x: 2, y: 2, z: 4, core: 2. Of those that a mesh axis runs over, the one named last changes fastest.
Arguments:
- grads: bfloat16 [4, 2304, 18432], P('replica', 'fsdp'), may hold values from -5 to 5
- slots: int32 [4, 32], replicated, may hold values from 0 to 31, each once within a row
- stats_left: float32 [4, 32, 2, 4, 72, 576], P(None, 'fsdp', None, 'replica'), may hold values from -6 to 6
- stats_right: float32 [4, 32, 2, 4, 72, 576], P(None, 'fsdp', None, 'replica'), may hold values from -6 to 6
- root_left: bfloat16 [4, 32, 2, 4, 72, 576], P(None, 'fsdp', None, 'replica'), may hold values from -0.25 to 0.25
- root_right: bfloat16 [4, 32, 2, 4, 72, 576], P(None, 'fsdp', None, 'replica'), may hold values from -0.25 to 0.25
- second_moment: float32 [4, 32, 2, 4, 72, 576], P(None, 'fsdp', None, 'replica'), may hold values from 0.25 to 60, as said below
Outputs:
- update: bfloat16 [2304, 18432], P('fsdp')
- left_new: float32 [4, 32, 2, 4, 72, 576], P(None, 'fsdp', None, 'replica')
- right_new: float32 [4, 32, 2, 4, 72, 576], P(None, 'fsdp', None, 'replica')
- moment_new: float32 [4, 32, 2, 4, 72, 576], P(None, 'fsdp', None, 'replica')
Inputs may be any that keep to these rules, and one draw needn't show every extreme that they name: Each row of slots names every slot 0 to 31 once; slot s of a block row is held by fsdp index s // 4. `second_moment`: positive entries.
All inputs are finite; a program needn't handle non-finite values.
Results may differ from a plain program's by a relative error of at most 0.014.
Values may be sent and summed in bfloat16 or wider, within the bound.
No kernel may reach another device: no remote copies, remote signals or barrier semaphores. Data moves between devices by JAX's collectives and lax.ppermute only.
A program may use at most 256 MiB of HBM per device.

v0:
```python
import jax
import jax.numpy as jnp
from jax import lax
from jax.sharding import PartitionSpec as P

B = 576


def slot_columns(row_slots, row_count):
    column_ids = jnp.arange(row_count, dtype=jnp.int32)
    matches = row_slots[None, :] == column_ids[:, None]
    return jnp.sum(jnp.where(matches, column_ids[None, :], 0), axis=1)


def local(grads, slots, stats_left, stats_right, root_left, root_right, second_moment):
    fsdp_count = lax.axis_size("fsdp")
    replica_count = lax.axis_size("replica")
    local_grad = grads[0]
    shard_rows, full_width = local_grad.shape
    columns = full_width // B
    row_blocks = slots.shape[0]
    per_owner = columns // fsdp_count
    sub_count = B // shard_rows
    part_rows = shard_rows // replica_count
    mine_rows = sub_count * part_rows
    fsdp_index = lax.axis_index("fsdp")
    replica_index = lax.axis_index("replica")
    row_slots = lax.dynamic_index_in_dim(slots, fsdp_index // sub_count, 0, keepdims=False)
    slot_cols = slot_columns(row_slots, columns)
    summed = lax.psum_scatter(
        local_grad.astype(jnp.float32).astype(jnp.bfloat16),
        "replica",
        scatter_dimension=0,
        tiled=True,
    )
    row_count = summed.shape[0]
    ordered = jnp.take(summed.reshape(row_count, columns, B), slot_cols, axis=1)
    arrived = lax.all_to_all(
        ordered.reshape(row_count, fsdp_count, per_owner * B).transpose(1, 0, 2),
        "fsdp",
        split_axis=0,
        concat_axis=0,
        tiled=True,
    )
    own_split = arrived.reshape(row_blocks, sub_count, part_rows, per_owner, B).transpose(
        0, 3, 1, 2, 4
    )
    gathered = lax.all_gather(own_split[:, :, :, None], "replica", axis=3, tiled=True)
    full_grad = gathered.reshape(row_blocks, per_owner, B, B)
    own_rows = own_split.reshape(row_blocks, per_owner, mine_rows, B)

    def as_rows(array_in):
        return array_in.reshape(row_blocks, per_owner, mine_rows, B)

    column_split = full_grad.reshape(row_blocks, per_owner, B, sub_count, replica_count, part_rows)
    column_part = lax.dynamic_index_in_dim(column_split, replica_index, 4, keepdims=False).reshape(
        row_blocks, per_owner, B, mine_rows
    )
    left_gram = jnp.einsum(
        "abmk,abnk->abmn", own_rows, full_grad, preferred_element_type=jnp.float32
    )
    right_gram = jnp.einsum(
        "abkm,abkn->abmn", column_part, full_grad, preferred_element_type=jnp.float32
    )
    left_new = 0.95 * as_rows(stats_left) + 0.05 * left_gram
    right_new = 0.95 * as_rows(stats_right) + 0.05 * right_gram
    right_full = lax.all_gather(root_right, "replica", axis=3, tiled=True).reshape(
        row_blocks, per_owner, B, B
    )
    inner_left = jnp.einsum(
        "abmk,abkn->abmn", as_rows(root_left), full_grad, preferred_element_type=jnp.float32
    ).astype(jnp.bfloat16)
    direction = jnp.einsum(
        "abmk,abkn->abmn", inner_left, right_full, preferred_element_type=jnp.float32
    )
    grad_float = own_rows.astype(jnp.float32)
    moment = 0.95 * as_rows(second_moment) + 0.05 * grad_float * grad_float
    adam_step = grad_float / (jnp.sqrt(moment) + 1e-08)
    adam_square, shampoo_square = lax.psum(
        (jnp.sum(adam_step * adam_step, axis=(2, 3)), jnp.sum(direction * direction, axis=(2, 3))),
        "replica",
    )
    graft_scale = jnp.sqrt(adam_square) / jnp.sqrt(shampoo_square + 1e-06)
    update_part = (direction * graft_scale[:, :, None, None]).astype(jnp.bfloat16)
    outgoing = (
        update_part.reshape(row_blocks, per_owner, sub_count, part_rows, B)
        .transpose(0, 2, 3, 1, 4)
        .reshape(fsdp_count, part_rows, per_owner * B)
    )
    returned = lax.all_to_all(outgoing, "fsdp", split_axis=0, concat_axis=0, tiled=True)
    ordered = returned.transpose(1, 0, 2).reshape(part_rows, columns, B)
    update = lax.all_gather(
        jnp.take(ordered, row_slots, axis=1).reshape(part_rows, full_width),
        "replica",
        axis=0,
        tiled=True,
    )
    return (
        update,
        left_new.reshape(stats_left.shape),
        right_new.reshape(stats_right.shape),
        moment.reshape(second_moment.shape),
    )


def solution(mesh):
    placed = (
        P("replica", "fsdp", None),
        P(),
        P(None, "fsdp", None, "replica", None, None),
        P(None, "fsdp", None, "replica", None, None),
        P(None, "fsdp", None, "replica", None, None),
        P(None, "fsdp", None, "replica", None, None),
        P(None, "fsdp", None, "replica", None, None),
    )
    return jax.shard_map(
        local,
        mesh=mesh,
        in_specs=placed,
        out_specs=(
            P("fsdp", None),
            P(None, "fsdp", None, "replica", None, None),
            P(None, "fsdp", None, "replica", None, None),
            P(None, "fsdp", None, "replica", None, None),
        ),
        check_vma=False,
    )
```

profile of v0, /device:TPU:0, one launch (start us, length us, event | category | flops | bytes accessed | tf_op | source)
XLA Modules:
  0.0 709.5 jit_solution(6675729218726200671)
XLA Ops:
  8.9 109.5 %reduce-scatter.4.cloned.1.call-done = bf16[72,18432]{1,0:T(8,128)(2,1)} async-done(((bf16[288,18432]{1,0:T(8,128)(2,1)}), bf16[72,18432]{1,0:T(8,128)(2,1)}) %reduce-scatter.4.cloned.1.call-update) | async-done | bytes 2654224
  118.4 6.3 reshape.72
  124.8 4.4 copy.68
  129.2 4.4 gather_fusion
  137.8 6.1 reshape.73
  146.0 65.5 %all_to_all.10 = bf16[8,72,2304]{2,1,0:T(8,128)(2,1)} all-to-all(bf16[8,72,2304]{2,1,0:T(8,128)(2,1)S(1)} %copy.70), channel_id=1, replica_groups=mesh['fsdp'=8,'replica'=4] {'fsdp'}, dimensions={0} | all-to-all | bytes 5308416 | tf_op jit(solution)/shard_map/all_to_all | solution.py:38
  211.6 7.1 %reshape.74 = bf16[4,2,72,4,576]{4,3,2,1,0:T(4,128)(2,1)} reshape(bf16[8,72,2304]{2,1,0:T(8,128)(2,1)} %all_to_all.10) | data formatting | bytes 5308416 | tf_op jit(solution)/shard_map/reshape | solution.py:45
  219.4 9.5 %fusion.6 = f32[4,4]{1,0:T(4,128)S(1)} fusion(f32[4,4,2,1,72,576]{5,4,3,2,1,0:T(8,128)} %param.15, bf16[4,2,72,4,576]{4,3,2,1,0:T(4,128)(2,1)} %reshape.74), kind=kLoop, calls=%fused_computation.15 | loop fusion | flops 11943920 | bytes 7962688 | tf_op jit(solution)/shard_map/reduce_sum | solution.py:80
  228.9 103.9 %all-gather.9.cloned.1.call-done = bf16[4,4,2,288,576]{4,1,3,2,0:T(4,128)(2,1)} async-done(((bf16[4,4,2,72,576]{4,1,3,2,0:T(4,128)(2,1)}), bf16[4,4,2,288,576]{4,1,3,2,0:T(4,128)(2,1)}) %all-gather.9.cloned.1.call-update) | async-done | bytes 10616848 | tf_op jit(solution)/shard_map/all_gather | solution.py:48
  332.8 11.6 %copy.71 = bf16[4,4,2,288,576]{4,3,2,1,0:T(8,128)(2,1)} copy(bf16[4,4,2,288,576]{4,1,3,2,0:T(4,128)(2,1)} %all-gather.9.cloned.1.call-done) | data formatting | bytes 21233664 | tf_op jit(solution)/shard_map/all_gather | solution.py:48
  344.4 106.2 %all-gather.5.cloned.1.call-done = bf16[4,4,2,4,72,576]{5,4,3,2,1,0:T(8,128)(2,1)} async-done(((bf16[4,4,2,1,72,576]{5,4,3,2,1,0:T(8,128)(2,1)}), bf16[4,4,2,4,72,576]{5,4,3,2,1,0:T(8,128)(2,1)}) %all-gather.5.cloned.1.call-update) | async-done | bytes 10616848 | tf_op jit(solution)/shard_map/all_gather | solution.py:67
  450.6 12.4 %multiply_reduce_fusion = (f32[4,4]{1,0:T(4,128)S(1)}, f32[4,4,144,576]{3,2,1,0:T(8,128)}) fusion(bf16[4,4,576,576]{3,2,1,0:T(8,128)(2,1)} %bitcast.65, bf16[4,4,144,576]{3,2,1,0:T(8,128)(2,1)S(1)} %bitcast.52, bf16[4,4,576,576]{3,2,1,0:T(8,128)(2,1)} %bitcast.53), kind=kOutput, calls=%fused_computation.14 | convolution fusion | flops 3061628928 | bytes 29196352 | tf_op jit(solution)/shard_map/abmk,abkn->abmn/dot_general | solution.py:73
  463.0 8.9 %all-reduce.1 = (f32[4,4]{1,0:T(4,128)S(1)}, f32[4,4]{1,0:T(4,128)S(1)}) all-reduce(f32[4,4]{1,0:T(4,128)S(1)} %get-tuple-element.29, f32[4,4]{1,0:T(4,128)S(1)} %fusion.6), channel_id=1, replica_groups=mesh['fsdp'=8,'replica'=4] {'replica'}, use_global_device_ids=true, to_apply=%region_5.7 | all-reduce | flops 32 | bytes 256 | tf_op jit(solution)/shard_map/psum | solution.py:79
  471.9 3.2 multiply_convert_fusion
  475.1 2.7 copy.96
  477.9 6.1 reshape.79
  484.0 4.6 all-to-all-start.1
  488.9 60.7 %all-to-all-done.1 = bf16[8,72,2304]{2,1,0:T(8,128)(2,1)S(1)} async-done(((bf16[8,72,2304]{2,1,0:T(8,128)(2,1)}), bf16[8,72,2304]{2,1,0:T(8,128)(2,1)S(1)}, u32[]{:S(2)}, u32[]{:S(2)}) %all-to-all-start.1) | async-done | bytes 2654240 | tf_op jit(solution)/shard_map/all_to_all | solution.py:90
  551.5 5.4 reshape.80
  556.9 2.6 copy.75
  559.5 2.9 gather_fusion.1
  563.3 4.3 reshape.81
  567.6 6.7 broadcast_multiply_fusion
  574.3 6.7 broadcast_multiply_fusion.1
  582.9 6.6 fusion.5
  589.5 5.7 copy.85
  595.1 40.8 %copy.82 = bf16[4,4,2,288,576]{3,2,4,1,0:T(2,128)(2,1)} copy(bf16[4,4,2,288,576]{4,1,3,2,0:T(4,128)(2,1)} %all-gather.9.cloned.1.call-done) | data formatting | bytes 21233664 | tf_op jit(solution)/shard_map/all_gather | solution.py:48
  636.0 27.8 %reshape_reshape.3 = bf16[4,4,576,2,4,72]{2,5,4,3,1,0:T(8,128)(2,1)} reshape(bf16[4,4,2,288,576]{3,2,4,1,0:T(2,128)(2,1)} %copy.82) | data formatting | bytes 21233664 | tf_op jit(solution)/shard_map/reshape;reshape | solution.py:55
  663.8 3.9 constant_dynamic-slice_fusion
  667.6 12.8 %multiply_add_fusion.1 = f32[4,4,144,576]{3,2,1,0:T(8,128)} fusion(f32[4,4,144,576]{3,2,1,0:T(8,128)} %bitcast.61, bf16[4,4,144,576]{3,2,1,0:T(8,128)(2,1)S(1)} %bitcast.62, bf16[4,4,576,576]{3,2,1,0:T(8,128)(2,1)} %bitcast.54), kind=kOutput, calls=%fused_computation.12 | convolution fusion | flops 1531478016 | bytes 23887872 | tf_op jit(solution)/shard_map/abmk,abnk->abmn/dot_general | solution.py:59
  680.5 12.4 %multiply_add_fusion = f32[4,4,144,576]{3,2,1,0:T(8,128)} fusion(f32[4,4,144,576]{3,2,1,0:T(8,128)} %bitcast.60, bf16[4,4,576,144]{2,3,1,0:T(8,128)(2,1)} %bitcast.63, bf16[4,4,576,576]{3,2,1,0:T(8,128)(2,1)} %bitcast.55), kind=kOutput, calls=%fused_computation.11 | convolution fusion | flops 1531478016 | bytes 23887872 | tf_op jit(solution)/shard_map/abkm,abkn->abmn/dot_general | solution.py:62
  692.8 10.1 %copy.98 = bf16[288,18432]{1,0:T(8,128)(2,1)} copy(bf16[288,18432]{1,0:T(8,128)(2,1)} %all-gather.7.cloned.1.call-done) | data formatting | bytes 21233664
  (37 shorter events, 13.7 us)
Async XLA Ops:
  7.2 443.5 %copy-start = (bf16[4,4,2,1,72,576]{5,4,3,2,1,0:T(8,128)(2,1)S(1)}, bf16[4,4,2,1,72,576]{5,4,3,2,1,0:T(8,128)(2,1)}, u32[]{:S(2)}) copy-start(bf16[4,4,2,1,72,576]{5,4,3,2,1,0:T(8,128)(2,1)} %param.13) | copy-start | bytes 7962628
  7.2 111.3 %reduce-scatter.4.cloned.1.call-start = ((), (), s32[]{:S(2)}) async-start(), calls=%async_computation.6 | async-start | bytes 13271040
  7.9 324.8 %all-gather.9.cloned.1.call-start = ((), (), s32[]{:S(2)}) async-start(), calls=%async_computation.5 | async-start | bytes 14745600 | tf_op jit(solution)/shard_map/all_gather | solution.py:48
  218.7 231.9 %all-gather.5.cloned.1.call-start = ((), (), s32[]{:S(2)}) async-start(), calls=%async_computation.3 | async-start | bytes 14745600 | tf_op jit(solution)/shard_map/all_gather | solution.py:67
  484.0 65.6 %all-to-all-start.1 = ((bf16[8,72,2304]{2,1,0:T(8,128)(2,1)}), bf16[8,72,2304]{2,1,0:T(8,128)(2,1)S(1)}, u32[]{:S(2)}, u32[]{:S(2)}) async-start(bf16[8,72,2304]{2,1,0:T(8,128)(2,1)} %reshape.79), calls=%async_computation.1 | async-start | bytes 5308416 | tf_op jit(solution)/shard_map/all_to_all | solution.py:90
  488.6 204.3 %all-gather.7.cloned.1.call-start = ((), (), s32[]{:S(2)}) async-start(), calls=%async_computation.4 | async-start | bytes 13271040 | tf_op jit(solution)/shard_map/all_gather | solution.py:92
  567.6 15.3 %slice-start = ((s8[5898240]{0:T(1024)(128)(4,1)}), s8[4194304]{0:T(1024)(128)(4,1)S(1)}, s32[]{:S(2)}) async-start(s8[5898240]{0:T(1024)(128)(4,1)} %bitcast.58), calls=%async_computation.7 | async-start | bytes 8388608
  574.3 6.7 copy-start.2
  574.3 8.6 %slice-start.1 = ((s8[5898240]{0:T(1024)(128)(4,1)}), s8[1703936]{0:T(1024)(128)(4,1)S(1)}, s32[]{:S(2)}) async-start(s8[5898240]{0:T(1024)(128)(4,1)} %bitcast.58), calls=%async_computation.8 | async-start | bytes 3407872
  663.8 3.9 copy-start.3
  692.8 10.1 %copy-start.1 = (bf16[4,4,2,1,72,576]{5,4,3,2,1,0:T(8,128)(2,1)S(1)}, bf16[4,4,2,1,72,576]{5,4,3,2,1,0:T(8,128)(2,1)}, u32[]{:S(2)}) copy-start(bf16[4,4,2,1,72,576]{5,4,3,2,1,0:T(8,128)(2,1)} %param.13) | copy-start | bytes 7962628
Sparse Core Ops, SparseCore 0:
  11.1 107.2 reduce-scatter.3
  218.8 113.8 all-gather.8
  334.6 115.9 all-gather.4
  567.7 104.0 all-gather.6
where the time goes:
time: 713 us; the launch traced here: 709 us
  waiting for transfers between devices  382 us (54%)
  local copies, waits for them, and re-layouts  161 us (23%)
  blocking collectives  74.4 us (10%)
  matrix products  37.6 us (5%)
  other arithmetic  36.1 us (5%)
  between operations  13.9 us (2%)
    unnamed x5, waiting for transfers between devices  111 us
    all_gather x1, waiting for transfers between devices, local(): lax.all_gather(root_right, 'replica', axis=3, tiled=True)  106 us
    all_gather x1, waiting for transfers between devices, local(): lax.all_gather(own_split[:, :, :, None], 'replica', axis=3, tiled=True)  104 us
    all_to_all x1, blocking collectives, local(): lax.all_to_all(ordered.reshape(row_count, fsdp_count, per_owner * B).tran...  65.5 us
    all_to_all x1, waiting for transfers between devices, local(): lax.all_to_all(outgoing, 'fsdp', split_axis=0, concat_axis=0, tiled=True)  60.7 us
    all_gather x2, local copies, waits for them, and re-layouts, local(): lax.all_gather(own_split[:, :, :, None], 'replica', axis=3, tiled=True)  52.5 us
    another operation x1, local copies, waits for them, and re-layouts, local(): full_grad.reshape(row_blocks, per_owner, B, sub_count, replica_count, par...  27.8 us
    unnamed x14, local copies, waits for them, and re-layouts  15.8 us
  transfers between devices with their start and end apart: 5, of which 4 were waited for; matrix products, arithmetic and copies ran while one was open for 21% of the time, Pallas kernels for 0%

commit v1 on v0

--- a/solution.py
+++ b/solution.py
@@ -1,9 +1,368 @@
+import functools
+
 import jax
 import jax.numpy as jnp
 from jax import lax
+from jax.experimental import pallas as pl
+from jax.experimental.pallas import tpu as pltpu
 from jax.sharding import PartitionSpec as P
 
 B = 576
+VMEM = 56 * 1024 * 1024
+
+
+def params():
+    return pltpu.CompilerParams(vmem_limit_bytes=VMEM)
+
+
+def cost(flops, moved):
+    return pl.CostEstimate(flops=flops, bytes_accessed=moved, transcendentals=0)
+
+
+def arrange_body(n_add, halves, half, cols, grad, *refs):
+    adds, outs = refs[: n_add * 2], refs[n_add * 2 :]
+    i = pl.program_id(0)
+    hr = outs[0].shape[1]
+    parity = lax.rem(cols[i], 2)
+
+    def emit(out, terms):
+        for side in range(2):
+
+            @pl.when(parity == side)
+            def _():
+                part = grad[:, side * B : side * B + B]
+                out[0, :, :B] = part[:hr]
+                out[0, :, B:] = part[hr:]
+
+        if terms:
+            total = out[0].astype(jnp.float32)
+            for term in terms:
+                total = total + term[0].astype(jnp.float32)
+            out[0] = total.astype(out.dtype)
+
+    if halves or n_add:
+
+        @pl.when(i < half)
+        def _():
+            emit(outs[0], adds[0::2])
+
+        @pl.when(i >= half)
+        def _():
+            emit(outs[-1], adds[1::2])
+    else:
+        emit(outs[0], ())
+
+
+def arrange(cols, grad, adds, halves):
+    n = cols.shape[0]
+    half = n // 2
+    rows = grad.shape[0]
+    hr, w = rows // 2, 2 * B
+    low = pl.BlockSpec((1, hr, w), lambda i, c: (jnp.minimum(i, half - 1), 0, 0))
+    high = pl.BlockSpec((1, hr, w), lambda i, c: (jnp.maximum(i - half, 0), 0, 0))
+    whole = pl.BlockSpec((1, hr, w), lambda i, c: (i, 0, 0))
+    out_specs = [low, high] if halves else [whole]
+    out_rows = half if halves else n
+    return pl.pallas_call(
+        functools.partial(arrange_body, len(adds), halves, half),
+        grid_spec=pltpu.PrefetchScalarGridSpec(
+            num_scalar_prefetch=1,
+            grid=(n,),
+            in_specs=[pl.BlockSpec((rows, w), lambda i, c: (0, c[i] // 2))]
+            + [low, high] * len(adds),
+            out_specs=out_specs,
+        ),
+        out_shape=[jax.ShapeDtypeStruct((out_rows, hr, w), grad.dtype) for _ in out_specs],
+        compiler_params=params(),
+        cost_estimate=cost(0, n * rows * w * 2 * (2 + len(adds))),
+    )(cols, grad, *[term for pair in adds for term in pair])
+
+
+def pack_roots_body(js, left, right, *outs):
+    m = pl.program_id(0)
+    for k, out in enumerate(outs):
+
+        @pl.when(m == k)
+        def _():
+            for kind, ref in enumerate((left, right)):
+                for q in range(2):
+                    out[kind, 0, :, q * B : q * B + B] = ref[q, 0]
+
+
+def visit(k, m, p, last):
+    return jnp.where(m == k, p, jnp.where(m < k, 0, last))
+
+
+def pack_roots(js, left, right):
+    blocks, _, rows, _ = left.shape
+    pairs, n, w = blocks // 2, js.shape[0], 2 * B
+    source = pl.BlockSpec((2, 1, rows, B), lambda m, p, j: (p, j[m], 0, 0))
+    return pl.pallas_call(
+        pack_roots_body,
+        grid_spec=pltpu.PrefetchScalarGridSpec(
+            num_scalar_prefetch=1,
+            grid=(n, pairs),
+            in_specs=[source, source],
+            out_specs=[
+                pl.BlockSpec(
+                    (2, 1, rows, w),
+                    lambda m, p, j, k=k: (0, visit(k, m, p, pairs - 1), 0, 0),
+                )
+                for k in range(n)
+            ],
+        ),
+        out_shape=[jax.ShapeDtypeStruct((2, pairs, rows, w), left.dtype)] * n,
+        compiler_params=params(),
+        cost_estimate=cost(0, 4 * left.size * 2),
+    )(js, left, right)
+
+
+def dot(x, y, dims):
+    return lax.dot_general(x, y, (dims, ((), ())), preferred_element_type=jnp.float32)
+
+
+def precondition_body(n, rd, js, grad, *refs):
+    roots, outs = refs[:n], refs[n : 2 * n]
+    direction_out, square_out, g16, g32, l32, r32 = refs[2 * n :]
+    hr = grad.shape[1]
+    for q in range(2):
+        for h in range(2):
+            for side in range(2):
+                g16[h * 2 * hr + side * hr : h * 2 * hr + side * hr + hr, :] = grad[
+                    2 * q + h, :, side * B : side * B + B
+                ]
+        for k in range(n):
+            for kind, full in enumerate((l32, r32)):
+                part = roots[k][kind, 0, :, q * B : q * B + B].astype(jnp.float32)
+                for h in range(2):
+                    start = pl.multiple_of(h * 2 * hr + js[k] * rd, 8)
+                    full[pl.ds(start, rd), :] = part[h * rd : h * rd + rd]
+        g = g16[...]
+        inner = dot(l32[...].astype(jnp.bfloat16), g, ((1,), (0,))).astype(jnp.bfloat16)
+        direction = dot(inner, r32[...].astype(jnp.bfloat16), ((1,), (0,)))
+        square_out[0, q : q + 1, :] = jnp.full((1, 128), jnp.sum(direction * direction))
+        direction = direction.astype(jnp.bfloat16)
+        for h in range(2):
+            for side in range(2):
+                start = h * 2 * hr + side * hr
+                direction_out[2 * q + h, :, side * B : side * B + B] = direction[start : start + hr]
+        g32[...] = g.astype(jnp.float32)
+        l32[...] = dot(g, g, ((1,), (1,)))
+        r32[...] = dot(g, g, ((0,), (0,)))
+        for k in range(n):
+            for kind, full in enumerate((g32, l32, r32)):
+                parts = [
+                    full[pl.ds(pl.multiple_of(h * 2 * hr + js[k] * rd, 8), rd), :] for h in range(2)
+                ]
+                outs[k][kind, 0, :, q * B : q * B + B] = jnp.concatenate(parts, axis=0).astype(
+                    jnp.bfloat16
+                )
+
+
+def precondition(js, grad, roots, rd):
+    n = js.shape[0]
+    count, hr, w = grad.shape
+    pairs, rows = roots[0].shape[1], roots[0].shape[2]
+    return pl.pallas_call(
+        functools.partial(precondition_body, n, rd),
+        grid_spec=pltpu.PrefetchScalarGridSpec(
+            num_scalar_prefetch=1,
+            grid=(pairs,),
+            in_specs=[pl.BlockSpec((4, hr, w), lambda p, j: (p, 0, 0))]
+            + [pl.BlockSpec((2, 1, rows, w), lambda p, j: (0, p, 0, 0))] * n,
+            out_specs=[pl.BlockSpec((3, 1, rows, w), lambda p, j: (0, p, 0, 0))] * n
+            + [
+                pl.BlockSpec((4, hr, w), lambda p, j: (p, 0, 0)),
+                pl.BlockSpec((1, 8, 128), lambda p, j: (p, 0, 0)),
+            ],
+            scratch_shapes=[pltpu.VMEM((B, B), jnp.bfloat16)] + [pltpu.VMEM((B, B), jnp.float32)] * 3,
+        ),
+        out_shape=[jax.ShapeDtypeStruct((3, pairs, rows, w), jnp.bfloat16)] * n
+        + [
+            jax.ShapeDtypeStruct((count, hr, w), jnp.bfloat16),
+            jax.ShapeDtypeStruct((pairs, 8, 128), jnp.float32),
+        ],
+        compiler_params=params(),
+        cost_estimate=cost(pairs * 16 * B**3, pairs * B * B * 2 * 14),
+    )(js, grad, *roots)
+
+
+def statistics_body(n, js, *refs):
+    received = refs[:n]
+    left, right, moment, left_out, right_out, moment_out, square_out = refs[n:]
+    m = pl.program_id(0)
+    for k in range(n):
+
+        @pl.when(m == k)
+        def _():
+            for q in range(2):
+                lanes = slice(q * B, q * B + B)
+                g, left_gram, right_gram = (
+                    received[k][kind, 0, :, lanes].astype(jnp.float32) for kind in range(3)
+                )
+                left_out[q, 0] = 0.95 * left[q, 0] + 0.05 * left_gram
+                right_out[q, 0] = 0.95 * right[q, 0] + 0.05 * right_gram
+                second = 0.95 * moment[q, 0] + 0.05 * g * g
+                moment_out[q, 0] = second
+                adam = g / (jnp.sqrt(second) + 1e-08)
+                square_out[0, 0, q : q + 1, :] = jnp.full((1, 128), jnp.sum(adam * adam))
+
+
+def statistics(js, received, left, right, moment):
+    n = js.shape[0]
+    blocks, _, rows, _ = left.shape
+    pairs, w = blocks // 2, 2 * B
+    own = pl.BlockSpec((2, 1, rows, B), lambda m, p, j: (p, j[m], 0, 0))
+    like = jax.ShapeDtypeStruct(left.shape, jnp.float32)
+    return pl.pallas_call(
+        functools.partial(statistics_body, n),
+        grid_spec=pltpu.PrefetchScalarGridSpec(
+            num_scalar_prefetch=1,
+            grid=(n, pairs),
+            in_specs=[
+                pl.BlockSpec(
+                    (3, 1, rows, w),
+                    lambda m, p, j, k=k: (0, visit(k, m, p, pairs - 1), 0, 0),
+                )
+                for k in range(n)
+            ]
+            + [own] * 3,
+            out_specs=[own] * 3 + [pl.BlockSpec((1, 1, 8, 128), lambda m, p, j: (m, p, 0, 0))],
+        ),
+        out_shape=[like] * 3 + [jax.ShapeDtypeStruct((n, pairs, 8, 128), jnp.float32)],
+        compiler_params=params(),
+        cost_estimate=cost(0, left.size * 4 * 7),
+    )(js, *received, left, right, moment)
+
+
+def restore_body(n_src, half, src, item, scale, *refs):
+    sources, out, buffer, sems = refs[:n_src], refs[n_src], refs[n_src + 1], refs[n_src + 2]
+    p = pl.program_id(0)
+    hr = buffer.shape[2]
+
+    def fetch(pair, slot):
+        for e in range(2):
+            for k in range(n_src):
+
+                @pl.when(src[2 * pair + e] == k)
+                def _():
+                    pltpu.make_async_copy(
+                        sources[k].at[item[2 * pair + e]], buffer.at[slot, e], sems.at[slot, e]
+                    ).start()
+
+    @pl.when(p == 0)
+    def _():
+        fetch(0, 0)
+
+    @pl.when(p + 1 < pl.num_programs(0))
+    def _():
+        fetch(p + 1, lax.rem(p + 1, 2))
+
+    slot = lax.rem(p, 2)
+    for e in range(2):
+        pltpu.make_async_copy(sources[0].at[0], buffer.at[slot, e], sems.at[slot, e]).wait()
+        scaled = (buffer[slot, e].astype(jnp.float32) * scale[2 * p + e]).astype(out.dtype)
+        out[:hr, e * B : e * B + B] = scaled[:, :B]
+        out[hr:, e * B : e * B + B] = scaled[:, B:]
+
+
+def restore(src, item, scale, sources):
+    half, hr, w = sources[0].shape
+    columns = src.shape[0]
+    return pl.pallas_call(
+        functools.partial(restore_body, len(sources), half),
+        grid_spec=pltpu.PrefetchScalarGridSpec(
+            num_scalar_prefetch=3,
+            grid=(columns // 2,),
+            in_specs=[pl.BlockSpec(memory_space=pl.ANY)] * len(sources),
+            out_specs=pl.BlockSpec((2 * hr, w), lambda p, a, b, c: (0, p)),
+            scratch_shapes=[
+                pltpu.VMEM((2, 2, hr, w), jnp.bfloat16),
+                pltpu.SemaphoreType.DMA((2, 2)),
+            ],
+        ),
+        out_shape=jax.ShapeDtypeStruct((2 * hr, columns * B), jnp.bfloat16),
+        compiler_params=params(),
+        cost_estimate=cost(0, columns * hr * w * 4),
+    )(src, item, scale, *sources)
+
+
+def owner_local(grads, slots, stats_left, stats_right, root_left, root_right, second_moment):
+    owners = lax.axis_size("fsdp")
+    replicas = lax.axis_size("replica")
+    grad = grads[0]
+    rows, full_width = grad.shape
+    columns = full_width // B
+    row_blocks = slots.shape[0]
+    sub_count = B // rows
+    rd = rows // replicas
+    half = owners // 2
+    f = lax.axis_index("fsdp")
+    r = lax.axis_index("replica")
+    js = r ^ jnp.arange(replicas, dtype=jnp.int32)
+    row_slots = lax.dynamic_index_in_dim(slots, f // sub_count, 0, keepdims=False)
+    column_ids = jnp.arange(columns, dtype=jnp.int32)
+    wanted = (
+        replicas * jnp.arange(owners, dtype=jnp.int32)[None, :, None] + js[:, None, None]
+    )
+    cols = jnp.sum(jnp.where(row_slots == wanted, column_ids, 0), axis=2)
+
+    def swap(x, k):
+        return lax.ppermute(x, "replica", [(i, i ^ k) for i in range(replicas)])
+
+    def as_rows(x):
+        return x.reshape(row_blocks, -1, sub_count * rd, B)
+
+    far_a, far_b = arrange(cols[3], grad, (), True)
+    from_x_far, from_y_far = swap(far_a, 1), swap(far_b, 2)
+    x_a, y_b = arrange(jnp.concatenate([cols[1, :half], cols[2, half:]]), grad, (), True)
+    from_x_a, from_y_b = swap(x_a, 1), swap(y_b, 2)
+    y_a, x_b = arrange(
+        jnp.concatenate([cols[2, :half], cols[1, half:]]), grad, [(from_x_far, from_y_far)], True
+    )
+    from_y_a, from_x_b = swap(y_a, 2), swap(x_b, 1)
+    (owned,) = arrange(cols[0], grad, [(from_x_a, from_x_b), (from_y_a, from_y_b)], False)
+    roots = pack_roots(js, as_rows(root_left), as_rows(root_right))
+    roots = [roots[0]] + [swap(roots[k], k) for k in (1, 2, 3)]
+    blocks = lax.all_to_all(owned, "fsdp", split_axis=0, concat_axis=0, tiled=True)
+
+    *products, direction, direction_square = precondition(js, blocks, roots, rd)
+    received = [products[0]] + [swap(products[k], k) for k in (1, 2, 3)]
+    returned = lax.all_to_all(direction, "fsdp", split_axis=0, concat_axis=0, tiled=True)
+
+    mine_a, mine_b = returned[:half], returned[half:]
+    x_a, y_b = swap(mine_a, 1), swap(mine_b, 2)
+    x_b, y_a = swap(mine_b, 1), swap(mine_a, 2)
+    far_a, far_b = swap(x_a, 2), swap(y_b, 1)
+
+    left_new, right_new, moment, adam_square = statistics(
+        js, received, as_rows(stats_left), as_rows(stats_right), as_rows(second_moment)
+    )
+    adam_square = adam_square[:, :, :2, 0].reshape(replicas, row_blocks)
+    direction_square = direction_square[:, :2, 0].reshape(row_blocks)
+    place = (replicas * f + js)[:, None] == column_ids
+    squares = jnp.stack(
+        [
+            jnp.sum(jnp.where(place[:, None, :], adam_square[:, :, None], 0.0), axis=0),
+            jnp.where(place[0], direction_square[:, None], 0.0),
+        ]
+    )
+    squares = lax.psum(squares, ("fsdp", "replica"))
+    ratio = jnp.sqrt(squares[0]) / jnp.sqrt(squares[1] + 1e-06)
+    row_ratio = lax.dynamic_index_in_dim(ratio, f // sub_count, 0, keepdims=False)
+    scale = jnp.sum(jnp.where(row_slots[:, None] == column_ids, row_ratio, 0.0), axis=1)
+
+    owner = row_slots // replicas
+    src = 2 * (lax.rem(row_slots, replicas) ^ r) + owner // half
+    update = restore(
+        src, lax.rem(owner, half), scale, (mine_a, mine_b, x_a, x_b, y_a, y_b, far_a, far_b)
+    )
+    return (
+        update,
+        left_new.reshape(stats_left.shape),
+        right_new.reshape(stats_right.shape),
+        moment.reshape(second_moment.shape),
+    )
 
 
 def slot_columns(row_slots, row_count):
@@ -12,7 +371,7 @@
     return jnp.sum(jnp.where(matches, column_ids[None, :], 0), axis=1)
 
 
-def local(grads, slots, stats_left, stats_right, root_left, root_right, second_moment):
+def row_local(grads, slots, stats_left, stats_right, root_left, root_right, second_moment):
     fsdp_count = lax.axis_size("fsdp")
     replica_count = lax.axis_size("replica")
     local_grad = grads[0]
@@ -103,6 +462,15 @@
     )
 
 
+def local(*arrays):
+    replicas = lax.axis_size("replica")
+    rows, full_width = arrays[0].shape[1:]
+    per_owner = full_width // B // lax.axis_size("fsdp")
+    if replicas == 4 and per_owner == replicas and 2 * rows == B:
+        return owner_local(*arrays)
+    return row_local(*arrays)
+
+
 def solution(mesh):
     placed = (
         P("replica", "fsdp", None),

time: 713 us -> 455 us (0.64)
  waiting for transfers between devices: 382 us -> 206 us
  local copies, waits for them, and re-layouts: 161 us -> 10.2 us
  Pallas kernels: 0 us -> 94.4 us
  starting transfers between devices: 5.16 us -> 73.7 us
  matrix products: 37.6 us -> 0 us
  other arithmetic: 36.1 us -> 4.35 us
  between operations: 13.9 us -> 0.91 us
  blocking collectives: 74.4 us -> 64.2 us
    all_gather x3 -> x0, waiting for transfers between devices: 210 us -> none  [the longest x1 106 us: local(): lax.all_gather(root_right, 'replica', axis=3, tiled=True)]
    ppermute x0 -> x18, waiting for transfers between devices: none -> 148 us  [swap(): return lax.ppermute(x, 'replica', [(i, i ^ k) for i in range(replicas)])]
    unnamed x5 -> x0, waiting for transfers between devices: 111 us -> none
    pallas_call x0 -> x8, Pallas kernels: none -> 94.4 us  [the longest x4 32.8 us: arrange(): pl.pallas_call(functools.partial(arrange_body, len(adds), halves, half),...]
    all_to_all x1 -> x0, blocking collectives: 65.5 us -> none  [local(): lax.all_to_all(ordered.reshape(row_count, fsdp_count, per_owner * B).tran...]
    ppermute x0 -> x18, starting transfers between devices: none -> 64.1 us  [swap(): return lax.ppermute(x, 'replica', [(i, i ^ k) for i in range(replicas)])]
    psum x1, blocking collectives: 8.91 us -> 64.2 us  [owner_local(): squares = lax.psum(squares, ('fsdp', 'replica'))]
    all_gather x2 -> x0, local copies, waits for them, and re-layouts: 52.5 us -> none  [local(): lax.all_gather(own_split[:, :, :, None], 'replica', axis=3, tiled=True)]
  transfers between devices with their start and end apart: 5 -> 20, of which waited for: 4 -> 11; matrix products, arithmetic and copies ran while one was open for 21% -> 1% of each run, Pallas kernels for 0% -> 10%
where the time goes in v1:
time: 455 us; the launch traced here: 454 us
  waiting for transfers between devices  206 us (45%)
  Pallas kernels  94.4 us (21%)
  starting transfers between devices  73.7 us (16%)
  blocking collectives  64.2 us (14%)
  local copies, waits for them, and re-layouts  10.2 us (2%)
    ppermute x18, waiting for transfers between devices, swap(): return lax.ppermute(x, 'replica', [(i, i ^ k) for i in range(replicas)])  148 us
    psum x1, blocking collectives, owner_local(): squares = lax.psum(squares, ('fsdp', 'replica'))  64.2 us
    ppermute x18, starting transfers between devices, swap(): return lax.ppermute(x, 'replica', [(i, i ^ k) for i in range(replicas)])  64.1 us
    all_to_all x1, waiting for transfers between devices, owner_local(): lax.all_to_all(direction, 'fsdp', split_axis=0, concat_axis=0, tiled=True)  57.7 us
    pallas_call x4, Pallas kernels, arrange(): pl.pallas_call(functools.partial(arrange_body, len(adds), halves, half),...  32.8 us
    pallas_call x1, Pallas kernels, statistics(): pl.pallas_call(functools.partial(statistics_body, n), grid_spec=pltpu.Pre...  19.8 us
    pallas_call x1, Pallas kernels, precondition(): pl.pallas_call(functools.partial(precondition_body, n, rd), grid_spec=plt...  18.5 us
    pallas_call x1, Pallas kernels, restore(): pl.pallas_call(functools.partial(restore_body, len(sources), half), grid_...  14.4 us
  transfers between devices with their start and end apart: 20, of which 11 were waited for; matrix products, arithmetic and copies ran while one was open for 1% of the time, Pallas kernels for 10%

profile of v1, /device:TPU:0, one launch (start us, length us, event | category | flops | bytes accessed | tf_op | source)
XLA Modules:
  0.0 453.6 jit_solution(8091167548449160872)
XLA Ops:
  2.7 7.6 %shard_map.103 = (bf16[4,144,1152]{2,1,0:T(8,128)(2,1)}, bf16[4,144,1152]{2,1,0:T(8,128)(2,1)}) custom-call(s32[8]{0:T(128)} %get-tuple-element.61.cols, bf16[288,18432]{1,0:T(8,128)(2,1)} %bitcast.36), custom_call_target="tpu_custom_call" | custom-call | bytes 10616832 | tf_op jit(solution)/shard_map/pallas_call | solution.py:66
  10.4 2.9 collective-permute-start.1
  13.3 1.5 collective-permute-start.2
  15.6 7.6 %shard_map.102 = (bf16[4,144,1152]{2,1,0:T(8,128)(2,1)}, bf16[4,144,1152]{2,1,0:T(8,128)(2,1)}) custom-call(s32[8]{0:T(128)} %pad_add_fusion.cols, bf16[288,18432]{1,0:T(8,128)(2,1)} %bitcast.37), custom_call_target="tpu_custom_call" | custom-call | bytes 10616832 | tf_op jit(solution)/shard_map/pallas_call | solution.py:66
  24.3 19.1 %collective-permute-done.1.refs_0_ = bf16[4,144,1152]{2,1,0:T(8,128)(2,1)S(1)} collective-permute-done((bf16[4,144,1152]{2,1,0:T(8,128)(2,1)}, bf16[4,144,1152]{2,1,0:T(8,128)(2,1)S(1)}, u32[]{:S(2)}, u32[]{:S(2)}) %collective-permute-start.1) | collective-permute-done | bytes 1327136 | tf_op jit(solution)/shard_map/ppermute | solution.py:311
  43.5 2.1 collective-permute-done.2.refs_1_
  46.7 8.5 %shard_map.104 = (bf16[4,144,1152]{2,1,0:T(8,128)(2,1)}, bf16[4,144,1152]{2,1,0:T(8,128)(2,1)}) custom-call(s32[8]{0:T(128)} %pad_add_fusion.1.cols, bf16[288,18432]{1,0:T(8,128)(2,1)} %bitcast.38, bf16[4,144,1152]{2,1,0:T(8,128)(2,1)} %copy-done.2, bf16[4,144,1152]{2,1,0:T(8,128)(2,1)} %copy-done.3), custom_call_target="tpu_custom_call" | custom-call | bytes 15925248 | tf_op jit(solution)/shard_map/pallas_call | solution.py:66
  56.2 1.5 collective-permute-start.4
  57.7 14.3 %collective-permute-done.refs_0_ = bf16[4,144,1152]{2,1,0:T(8,128)(2,1)S(1)} collective-permute-done((bf16[4,144,1152]{2,1,0:T(8,128)(2,1)}, bf16[4,144,1152]{2,1,0:T(8,128)(2,1)S(1)}, u32[]{:S(2)}, u32[]{:S(2)}) %collective-permute-start) | collective-permute-done | bytes 1327136 | tf_op jit(solution)/shard_map/ppermute | solution.py:311
  71.9 2.1 collective-permute-done.5.refs_3_
  74.0 25.5 %collective-permute-done.3.refs_1_ = bf16[4,144,1152]{2,1,0:T(8,128)(2,1)S(1)} collective-permute-done((bf16[4,144,1152]{2,1,0:T(8,128)(2,1)}, bf16[4,144,1152]{2,1,0:T(8,128)(2,1)S(1)}, u32[]{:S(2)}, u32[]{:S(2)}) %collective-permute-start.3) | collective-permute-done | bytes 1327136 | tf_op jit(solution)/shard_map/ppermute | solution.py:311
  99.5 1.5 collective-permute-done.4.refs_2_
  102.1 9.0 %shard_map.105 = bf16[8,144,1152]{2,1,0:T(8,128)(2,1)} custom-call(s32[8]{0:T(128)} %get-tuple-element.62.cols, bf16[288,18432]{1,0:T(8,128)(2,1)} %bitcast.39, bf16[4,144,1152]{2,1,0:T(8,128)(2,1)} %copy-done.5, bf16[4,144,1152]{2,1,0:T(8,128)(2,1)} %copy-done.7, bf16[4,144,1152]{2,1,0:T(8,128)(2,1)} %copy-done.8, bf16[4,144,1152]{2,1,0:T(8,128)(2,1)} %copy-done.6), custom_call_target="tpu_custom_call" | custom-call | bytes 21233664 | tf_op jit(solution)/shard_map/pallas_call | solution.py:66
  111.1 4.9 %all-to-all-start = ((bf16[8,144,1152]{2,1,0:T(8,128)(2,1)}), bf16[8,144,1152]{2,1,0:T(8,128)(2,1)S(1)}, u32[]{:S(2)}, u32[]{:S(2)}) async-start(bf16[8,144,1152]{2,1,0:T(8,128)(2,1)} %shard_map.105), calls=%async_computation | async-start | bytes 5308416 | tf_op jit(solution)/shard_map/all_to_all | solution.py:327
  116.0 8.9 %shard_map.106 = (bf16[2,2,144,1152]{3,2,1,0:T(8,128)(2,1)}, bf16[2,2,144,1152]{3,2,1,0:T(8,128)(2,1)}, bf16[2,2,144,1152]{3,2,1,0:T(8,128)(2,1)}, bf16[2,2,144,1152]{3,2,1,0:T(8,128)(2,1)}) custom-call(s32[4]{0:T(128)} %copy-done.9, bf16[4,4,144,576]{3,2,1,0:T(8,128)(2,1)} %bitcast.43, bf16[4,4,144,576]{3,2,1,0:T(8,128)(2,1)} %bitcast.44), custom_call_target="tpu_custom_call" | custom-call | bytes 10616832 | tf_op jit(solution)/shard_map/pallas_call | solution.py:100
  125.6 1.5 collective-permute-start.7
  128.3 28.6 %collective-permute-done.6.refs_1_ = bf16[2,2,144,1152]{3,2,1,0:T(8,128)(2,1)S(1)} collective-permute-done((bf16[2,2,144,1152]{3,2,1,0:T(8,128)(2,1)}, bf16[2,2,144,1152]{3,2,1,0:T(8,128)(2,1)S(1)}, u32[]{:S(2)}, u32[]{:S(2)}) %collective-permute-start.6) | collective-permute-done | bytes 1327136 | tf_op jit(solution)/shard_map/ppermute | solution.py:311
  157.0 27.7 %collective-permute-done.7.refs_2_ = bf16[2,2,144,1152]{3,2,1,0:T(8,128)(2,1)S(1)} collective-permute-done((bf16[2,2,144,1152]{3,2,1,0:T(8,128)(2,1)}, bf16[2,2,144,1152]{3,2,1,0:T(8,128)(2,1)S(1)}, u32[]{:S(2)}, u32[]{:S(2)}) %collective-permute-start.7) | collective-permute-done | bytes 1327136 | tf_op jit(solution)/shard_map/ppermute | solution.py:311
  186.1 1.5 copy-done
  187.6 18.5 %shard_map.107 = (bf16[3,2,144,1152]{3,2,1,0:T(8,128)(2,1)}, bf16[3,2,144,1152]{3,2,1,0:T(8,128)(2,1)}, bf16[3,2,144,1152]{3,2,1,0:T(8,128)(2,1)}, bf16[3,2,144,...) custom-call(s32[4]{0:T(128)} %copy-done.9, bf16[8,144,1152]{2,1,0:T(8,128)(2,1)} %copy-done, ...), custom_call_target="tpu_custom_call" | custom-call | flops 6115295232 | bytes 18579456 | tf_op jit(solution)/shard_map/pallas_call | solution.py:166
  206.1 4.7 %all-to-all-start.1 = ((bf16[8,144,1152]{2,1,0:T(8,128)(2,1)}), bf16[8,144,1152]{2,1,0:T(8,128)(2,1)S(1)}, u32[]{:S(2)}, u32[]{:S(2)}) async-start(bf16[8,144,1152]{2,1,0:T(8,128)(2,1)} %get-tuple-element.40), calls=%async_computation.1 | async-start | bytes 5308416 | tf_op jit(solution)/shard_map/all_to_all | solution.py:331
  211.8 2.4 collective-permute-start.10
  214.1 57.7 %all-to-all-done.1 = bf16[8,144,1152]{2,1,0:T(8,128)(2,1)S(1)} async-done(((bf16[8,144,1152]{2,1,0:T(8,128)(2,1)}), bf16[8,144,1152]{2,1,0:T(8,128)(2,1)S(1)}, u32[]{:S(2)}, u32[]{:S(2)}) %all-to-all-start.1) | async-done | bytes 2654240 | tf_op jit(solution)/shard_map/all_to_all | solution.py:331
  271.9 1.7 fusion.2
  273.6 1.9 collective-permute-start.15
  278.4 2.0 collective-permute-start.14
  280.4 26.8 %collective-permute-done.15.refs_5_ = bf16[4,144,1152]{2,1,0:T(8,128)(2,1)S(1)} collective-permute-done((bf16[4,144,1152]{2,1,0:T(8,128)(2,1)}, bf16[4,144,1152]{2,1,0:T(8,128)(2,1)S(1)}, u32[]{:S(2)}, u32[]{:S(2)}) %collective-permute-start.15) | collective-permute-done | bytes 1327136 | tf_op jit(solution)/shard_map/ppermute | solution.py:311
  308.3 41.9 %collective-permute-start.16 = (bf16[4,144,1152]{2,1,0:T(8,128)(2,1)}, bf16[4,144,1152]{2,1,0:T(8,128)(2,1)}, u32[]{:S(2)}, u32[]{:S(2)}) collective-permute-start(bf16[4,144,1152]{2,1,0:T(8,128)(2,1)} %collective-permute-done.12.refs_2_), channel_id=1, source_target_pairs={{0,2},{1,3},{2,0},{3,1},{4,6},{5,7},{6,4},{7,5},{8,10},{9,11},{10,... | collective-permute-start | bytes 3981320 | tf_op jit(solution)/shard_map/ppermute | solution.py:311
  351.8 1.3 copy-done.1
  353.1 19.8 %shard_map.108 = (f32[4,4,144,576]{3,2,1,0:T(8,128)}, f32[4,4,144,576]{3,2,1,0:T(8,128)}, f32[4,4,144,576]{3,2,1,0:T(8,128)}, f32[4,2,8,128]{3,2,1,0:T(8,128)}) custom-call(s32[4]{0:T(128)} %copy-done.9, bf16[3,2,144,1152]{3,2,1,0:T(8,128)(2,1)} %get-tuple-element.34.refs_0_, bf16[3,2,144,1152]{3,2,1,0:T(8,128)(2,1)} %collective-permute-done.9.refs_1_, ...), custom_call_target="tpu_custom_call" | custom-call | bytes 37158912 | tf_op jit(solution)/shard_map/pallas_call | solution.py:217
  373.9 64.2 %psum.7 = f32[2,4,32]{2,1,0:T(4,128)S(1)} all-reduce(f32[2,4,32]{2,1,0:T(4,128)S(1)} %pad_maximum_fusion), channel_id=1, replica_groups=mesh['fsdp'=8,'replica'=4] {'fsdp','replica'}, use_global_device_ids=true, to_apply=%region_2.3 | all-reduce | flops 256 | bytes 2048 | tf_op jit(solution)/shard_map/psum | solution.py:350
  439.0 14.4 %shard_map.109 = bf16[288,18432]{1,0:T(8,128)(2,1)} custom-call(s32[32]{0:T(128)} %multiply_add_fusion.src, s32[32]{0:T(128)} %get-tuple-element.56.item, f32[32]{0:T(128)} %select_reduce_fusion.scale, bf16[4,144,1152]{2,1,0:T(8,128)(2,1)} %get-tuple-element.60.refs_0_, bf16[4,144,1152]{2,1,0:T(8,128)(2,1)} %get-tuple-element.59.refs_1_, ...), custom_call_target="tpu_custom_call" | custom-call | bytes 21233664 | tf_op jit(solution)/shard_map/pallas_call | solution.py:272
  (65 shorter events, 18.7 us)
Async XLA Ops:
  0.7 9.7 %copy-start.9 = (s32[4]{0:T(128)}, s32[4]{0:T(128)S(1)}, u32[]{:S(2)}) copy-start(s32[4]{0:T(128)S(1)} %get-tuple-element.67.js) | copy-start | bytes 52
  10.4 33.1 %collective-permute-start.1 = (bf16[4,144,1152]{2,1,0:T(8,128)(2,1)}, bf16[4,144,1152]{2,1,0:T(8,128)(2,1)S(1)}, u32[]{:S(2)}, u32[]{:S(2)}) collective-permute-start(bf16[4,144,1152]{2,1,0:T(8,128)(2,1)} %get-tuple-element.25), channel_id=1, source_target_pairs={{0,1},{1,0},{2,3},{3,2},{4,5},{5,4},{6,7},{7,6},{8,9},{9,8},{10,11... | collective-permute-start | bytes 3981320 | tf_op jit(solution)/shard_map/ppermute | solution.py:311
  13.3 32.3 %collective-permute-start.2 = (bf16[4,144,1152]{2,1,0:T(8,128)(2,1)}, bf16[4,144,1152]{2,1,0:T(8,128)(2,1)S(1)}, u32[]{:S(2)}, u32[]{:S(2)}) collective-permute-start(bf16[4,144,1152]{2,1,0:T(8,128)(2,1)} %get-tuple-element.26), channel_id=1, source_target_pairs={{0,2},{1,3},{2,0},{3,1},{4,6},{5,7},{6,4},{7,5},{8,10},{9,11},{10,... | collective-permute-start | bytes 3981320 | tf_op jit(solution)/shard_map/ppermute | solution.py:311
  23.2 48.7 %collective-permute-start = (bf16[4,144,1152]{2,1,0:T(8,128)(2,1)}, bf16[4,144,1152]{2,1,0:T(8,128)(2,1)S(1)}, u32[]{:S(2)}, u32[]{:S(2)}) collective-permute-start(bf16[4,144,1152]{2,1,0:T(8,128)(2,1)} %get-tuple-element.24), channel_id=1, source_target_pairs={{0,1},{1,0},{2,3},{3,2},{4,5},{5,4},{6,7},{7,6},{8,9},{9,8},{10,11... | collective-permute-start | bytes 3981320 | tf_op jit(solution)/shard_map/ppermute | solution.py:311
  23.7 50.3 %collective-permute-start.5 = (bf16[4,144,1152]{2,1,0:T(8,128)(2,1)}, bf16[4,144,1152]{2,1,0:T(8,128)(2,1)S(1)}, u32[]{:S(2)}, u32[]{:S(2)}) collective-permute-start(bf16[4,144,1152]{2,1,0:T(8,128)(2,1)} %get-tuple-element.29), channel_id=1, source_target_pairs={{0,2},{1,3},{2,0},{3,1},{4,6},{5,7},{6,4},{7,5},{8,10},{9,11},{10,... | collective-permute-start | bytes 3981320 | tf_op jit(solution)/shard_map/ppermute | solution.py:311
  43.5 2.1 copy-start.2
  45.6 1.1 copy-start.3
  55.1 44.4 %collective-permute-start.3 = (bf16[4,144,1152]{2,1,0:T(8,128)(2,1)}, bf16[4,144,1152]{2,1,0:T(8,128)(2,1)S(1)}, u32[]{:S(2)}, u32[]{:S(2)}) collective-permute-start(bf16[4,144,1152]{2,1,0:T(8,128)(2,1)} %get-tuple-element.27), channel_id=1, source_target_pairs={{0,1},{1,0},{2,3},{3,2},{4,5},{5,4},{6,7},{7,6},{8,9},{9,8},{10,11... | collective-permute-start | bytes 3981320 | tf_op jit(solution)/shard_map/ppermute | solution.py:311
  56.2 44.8 %collective-permute-start.4 = (bf16[4,144,1152]{2,1,0:T(8,128)(2,1)}, bf16[4,144,1152]{2,1,0:T(8,128)(2,1)S(1)}, u32[]{:S(2)}, u32[]{:S(2)}) collective-permute-start(bf16[4,144,1152]{2,1,0:T(8,128)(2,1)} %get-tuple-element.28), channel_id=1, source_target_pairs={{0,2},{1,3},{2,0},{3,1},{4,6},{5,7},{6,4},{7,5},{8,10},{9,11},{10,... | collective-permute-start | bytes 3981320 | tf_op jit(solution)/shard_map/ppermute | solution.py:311
  71.9 29.1 %copy-start.5 = (bf16[4,144,1152]{2,1,0:T(8,128)(2,1)}, bf16[4,144,1152]{2,1,0:T(8,128)(2,1)S(1)}, u32[]{:S(2)}) copy-start(bf16[4,144,1152]{2,1,0:T(8,128)(2,1)S(1)} %collective-permute-done.refs_0_) | copy-start | bytes 3981316
  74.0 27.0 %copy-start.6 = (bf16[4,144,1152]{2,1,0:T(8,128)(2,1)}, bf16[4,144,1152]{2,1,0:T(8,128)(2,1)S(1)}, u32[]{:S(2)}) copy-start(bf16[4,144,1152]{2,1,0:T(8,128)(2,1)S(1)} %collective-permute-done.5.refs_3_) | copy-start | bytes 3981316
  99.5 1.5 copy-start.7
  101.0 1.1 copy-start.8
  111.1 75.0 %all-to-all-start = ((bf16[8,144,1152]{2,1,0:T(8,128)(2,1)}), bf16[8,144,1152]{2,1,0:T(8,128)(2,1)S(1)}, u32[]{:S(2)}, u32[]{:S(2)}) async-start(bf16[8,144,1152]{2,1,0:T(8,128)(2,1)} %shard_map.105), calls=%async_computation | async-start | bytes 5308416 | tf_op jit(solution)/shard_map/all_to_all | solution.py:327
  124.9 32.1 %collective-permute-start.6 = (bf16[2,2,144,1152]{3,2,1,0:T(8,128)(2,1)}, bf16[2,2,144,1152]{3,2,1,0:T(8,128)(2,1)S(1)}, u32[]{:S(2)}, u32[]{:S(2)}) collective-permute-start(bf16[2,2,144,1152]{3,2,1,0:T(8,128)(2,1)} %get-tuple-element.31), channel_id=1, source_target_pairs={{0,1},{1,0},{2,3},{3,2},{4,5},{5,4},{6,7},{7,6},{8,9},{9,8},{10,11... | collective-permute-start | bytes 3981320 | tf_op jit(solution)/shard_map/ppermute | solution.py:311
  125.6 59.1 %collective-permute-start.7 = (bf16[2,2,144,1152]{3,2,1,0:T(8,128)(2,1)}, bf16[2,2,144,1152]{3,2,1,0:T(8,128)(2,1)S(1)}, u32[]{:S(2)}, u32[]{:S(2)}) collective-permute-start(bf16[2,2,144,1152]{3,2,1,0:T(8,128)(2,1)} %get-tuple-element.32), channel_id=1, source_target_pairs={{0,2},{1,3},{2,0},{3,1},{4,6},{5,7},{6,4},{7,5},{8,10},{9,11},{10,... | collective-permute-start | bytes 3981320 | tf_op jit(solution)/shard_map/ppermute | solution.py:311
  127.1 59.0 %collective-permute-start.8 = (bf16[2,2,144,1152]{3,2,1,0:T(8,128)(2,1)}, bf16[2,2,144,1152]{3,2,1,0:T(8,128)(2,1)}, u32[]{:S(2)}, u32[]{:S(2)}) collective-permute-start(bf16[2,2,144,1152]{3,2,1,0:T(8,128)(2,1)} %get-tuple-element.33), channel_id=1, source_target_pairs={{0,3},{1,2},{2,1},{3,0},{4,7},{5,6},{6,5},{7,4},{8,11},{9,10},{10,... | collective-permute-start | bytes 3981320 | tf_op jit(solution)/shard_map/ppermute | solution.py:311
  157.0 27.7 %copy-start.10 = (bf16[2,2,144,1152]{3,2,1,0:T(8,128)(2,1)}, bf16[2,2,144,1152]{3,2,1,0:T(8,128)(2,1)S(1)}, u32[]{:S(2)}) copy-start(bf16[2,2,144,1152]{3,2,1,0:T(8,128)(2,1)S(1)} %collective-permute-done.6.refs_1_) | copy-start | bytes 3981316
  184.7 1.1 copy-start.11
  186.1 1.5 copy-start
  206.1 65.8 %all-to-all-start.1 = ((bf16[8,144,1152]{2,1,0:T(8,128)(2,1)}), bf16[8,144,1152]{2,1,0:T(8,128)(2,1)S(1)}, u32[]{:S(2)}, u32[]{:S(2)}) async-start(bf16[8,144,1152]{2,1,0:T(8,128)(2,1)} %get-tuple-element.40), calls=%async_computation.1 | async-start | bytes 5308416 | tf_op jit(solution)/shard_map/all_to_all | solution.py:331
  210.9 66.3 %collective-permute-start.9 = (bf16[3,2,144,1152]{3,2,1,0:T(8,128)(2,1)}, bf16[3,2,144,1152]{3,2,1,0:T(8,128)(2,1)}, u32[]{:S(2)}, u32[]{:S(2)}) collective-permute-start(bf16[3,2,144,1152]{3,2,1,0:T(8,128)(2,1)} %get-tuple-element.35), channel_id=1, source_target_pairs={{0,1},{1,0},{2,3},{3,2},{4,5},{5,4},{6,7},{7,6},{8,9},{9,8},{10,11... | collective-permute-start | bytes 5971976 | tf_op jit(solution)/shard_map/ppermute | solution.py:311
  211.8 66.6 %collective-permute-start.10 = (bf16[3,2,144,1152]{3,2,1,0:T(8,128)(2,1)}, bf16[3,2,144,1152]{3,2,1,0:T(8,128)(2,1)}, u32[]{:S(2)}, u32[]{:S(2)}) collective-permute-start(bf16[3,2,144,1152]{3,2,1,0:T(8,128)(2,1)} %get-tuple-element.36), channel_id=1, source_target_pairs={{0,2},{1,3},{2,0},{3,1},{4,6},{5,7},{6,4},{7,5},{8,10},{9,11},{10,... | collective-permute-start | bytes 5971976 | tf_op jit(solution)/shard_map/ppermute | solution.py:311
  273.6 33.6 %collective-permute-start.15 = (bf16[4,144,1152]{2,1,0:T(8,128)(2,1)}, bf16[4,144,1152]{2,1,0:T(8,128)(2,1)S(1)}, u32[]{:S(2)}, u32[]{:S(2)}) collective-permute-start(bf16[4,144,1152]{2,1,0:T(8,128)(2,1)} %get-tuple-element.59.refs_1_), channel_id=1, source_target_pairs={{0,2},{1,3},{2,0},{3,1},{4,6},{5,7},{6,4},{7,5},{8,10},{9,11},{10,... | collective-permute-start | bytes 3981320 | tf_op jit(solution)/shard_map/ppermute | solution.py:311
  275.5 32.7 %collective-permute-start.12 = (bf16[4,144,1152]{2,1,0:T(8,128)(2,1)}, bf16[4,144,1152]{2,1,0:T(8,128)(2,1)}, u32[]{:S(2)}, u32[]{:S(2)}) collective-permute-start(bf16[4,144,1152]{2,1,0:T(8,128)(2,1)} %get-tuple-element.60.refs_0_), channel_id=1, source_target_pairs={{0,1},{1,0},{2,3},{3,2},{4,5},{5,4},{6,7},{7,6},{8,9},{9,8},{10,11... | collective-permute-start | bytes 3981320 | tf_op jit(solution)/shard_map/ppermute | solution.py:311
  276.8 74.9 %collective-permute-start.11 = (bf16[3,2,144,1152]{3,2,1,0:T(8,128)(2,1)}, bf16[3,2,144,1152]{3,2,1,0:T(8,128)(2,1)S(1)}, u32[]{:S(2)}, u32[]{:S(2)}) collective-permute-start(bf16[3,2,144,1152]{3,2,1,0:T(8,128)(2,1)} %get-tuple-element.37), channel_id=1, source_target_pairs={{0,3},{1,2},{2,1},{3,0},{4,7},{5,6},{6,5},{7,4},{8,11},{9,10},{10,... | collective-permute-start | bytes 5971976 | tf_op jit(solution)/shard_map/ppermute | solution.py:311
  277.1 161.8 %collective-permute-start.13 = (bf16[4,144,1152]{2,1,0:T(8,128)(2,1)}, bf16[4,144,1152]{2,1,0:T(8,128)(2,1)}, u32[]{:S(2)}, u32[]{:S(2)}) collective-permute-start(bf16[4,144,1152]{2,1,0:T(8,128)(2,1)} %get-tuple-element.59.refs_1_), channel_id=1, source_target_pairs={{0,1},{1,0},{2,3},{3,2},{4,5},{5,4},{6,7},{7,6},{8,9},{9,8},{10,11... | collective-permute-start | bytes 3981320 | tf_op jit(solution)/shard_map/ppermute | solution.py:311
  278.4 160.6 %collective-permute-start.14 = (bf16[4,144,1152]{2,1,0:T(8,128)(2,1)}, bf16[4,144,1152]{2,1,0:T(8,128)(2,1)}, u32[]{:S(2)}, u32[]{:S(2)}) collective-permute-start(bf16[4,144,1152]{2,1,0:T(8,128)(2,1)} %get-tuple-element.60.refs_0_), channel_id=1, source_target_pairs={{0,2},{1,3},{2,0},{3,1},{4,6},{5,7},{6,4},{7,5},{8,10},{9,11},{10,... | collective-permute-start | bytes 3981320 | tf_op jit(solution)/shard_map/ppermute | solution.py:311
  307.2 65.6 %copy-start.4 = (bf16[4,144,1152]{2,1,0:T(8,128)(2,1)}, bf16[4,144,1152]{2,1,0:T(8,128)(2,1)S(1)}, u32[]{:S(2)}) copy-start(bf16[4,144,1152]{2,1,0:T(8,128)(2,1)S(1)} %collective-permute-done.15.refs_5_) | copy-start | bytes 3981316
  307.2 131.8 %collective-permute-start.17 = (bf16[4,144,1152]{2,1,0:T(8,128)(2,1)S(1)}, bf16[4,144,1152]{2,1,0:T(8,128)(2,1)}, u32[]{:S(2)}, u32[]{:S(2)}) collective-permute-start(bf16[4,144,1152]{2,1,0:T(8,128)(2,1)S(1)} %collective-permute-done.15.refs_5_), channel_id=1, source_target_pairs={{0,1},{1,0},{2,3},{3,2},{4,5},{5,4},{6,7},{7,6},{8,9},{9,8},{10,11... | collective-permute-start | bytes 3981320 | tf_op jit(solution)/shard_map/ppermute | solution.py:311
  308.3 130.7 %collective-permute-start.16 = (bf16[4,144,1152]{2,1,0:T(8,128)(2,1)}, bf16[4,144,1152]{2,1,0:T(8,128)(2,1)}, u32[]{:S(2)}, u32[]{:S(2)}) collective-permute-start(bf16[4,144,1152]{2,1,0:T(8,128)(2,1)} %collective-permute-done.12.refs_2_), channel_id=1, source_target_pairs={{0,2},{1,3},{2,0},{3,1},{4,6},{5,7},{6,4},{7,5},{8,10},{9,11},{10,... | collective-permute-start | bytes 3981320 | tf_op jit(solution)/shard_map/ppermute | solution.py:311
  351.8 1.3 copy-start.1

commit v2 on v0

--- a/solution.py
+++ b/solution.py
@@ -1,9 +1,472 @@
+import functools
+
 import jax
 import jax.numpy as jnp
 from jax import lax
+from jax.experimental import pallas as pl
+from jax.experimental.pallas import tpu as pltpu
 from jax.sharding import PartitionSpec as P
 
 B = 576
+LANES = 128
+WINDOW = -(-B // LANES) * LANES
+VMEM = 56 * 1024 * 1024
+ANY = pl.BlockSpec(memory_space=pl.ANY)
+WHOLE = pl.BlockSpec(memory_space=pltpu.VMEM)
+SCALARS = pl.BlockSpec(memory_space=pltpu.SMEM)
+
+
+def params():
+    return pltpu.CompilerParams(vmem_limit_bytes=VMEM)
+
+
+def cost(flops, moved):
+    return pl.CostEstimate(flops=flops, bytes_accessed=moved, transcendentals=0)
+
+
+def arrange_body(n_add, n_after, n_pass, base, halves, cols, grad, *refs):
+    adds = refs[: 2 * n_add]
+    n_out = 2 if halves else 1
+    first = 2 * n_add + n_after + n_pass
+    outs = refs[first : first + n_out]
+    buffer, sems = refs[-2:]
+    n = outs[0].shape[1]
+    count = buffer.shape[0]
+    half = count // 2
+
+    def copy(i):
+        start = pl.multiple_of(cols[i] * B // LANES * LANES, LANES)
+        return pltpu.make_async_copy(
+            grad.at[pl.ds(base, 2 * n), pl.ds(start, WINDOW)], buffer.at[i], sems.at[i]
+        )
+
+    for i in range(count):
+        copy(i).start()
+    for i in range(count):
+        copy(i).wait()
+        out, at = (outs[i // half], i % half) if halves else (outs[0], i)
+        for shift in (0, B % LANES):
+
+            @pl.when(lax.rem(cols[i] * B, LANES) == shift)
+            def _():
+                part = buffer[i, :, shift : shift + B]
+                out[at, :, :B] = part[:n]
+                out[at, :, B:] = part[n:]
+
+        if n_add:
+            total = out[at].astype(jnp.float32)
+            for k in range(n_add):
+                total = total + adds[2 * k + i // half][i % half].astype(jnp.float32)
+            out[at] = total.astype(out.dtype)
+
+
+def arrange(cols, grad, base, n, adds=(), halves=True, after=(), through=()):
+    count = cols.shape[0]
+    w = 2 * B
+    shapes = [(count // 2, n, w)] * 2 if halves else [(count, n, w)]
+    before = 2 + 2 * len(adds) + len(after)
+    return pl.pallas_call(
+        functools.partial(arrange_body, len(adds), len(after), len(through), base, halves),
+        in_specs=[SCALARS, ANY]
+        + [WHOLE] * (2 * len(adds))
+        + [ANY] * (len(after) + len(through)),
+        out_specs=[WHOLE] * len(shapes) + [ANY] * len(through),
+        out_shape=[jax.ShapeDtypeStruct(s, grad.dtype) for s in shapes]
+        + [jax.ShapeDtypeStruct(x.shape, x.dtype) for x in through],
+        scratch_shapes=[
+            pltpu.VMEM((count, 2 * n, WINDOW), grad.dtype),
+            pltpu.SemaphoreType.DMA((count,)),
+        ],
+        input_output_aliases={before + k: len(shapes) + k for k in range(len(through))},
+        compiler_params=params(),
+        cost_estimate=cost(0, count * n * w * 2 * (2 + len(adds))),
+    )(cols, grad, *[term for pair in adds for term in pair], *after, *through)
+
+
+def visit(k, m, p, last):
+    return jnp.where(m == k, p, jnp.where(m < k, 0, last))
+
+
+def pack_roots_body(n, js, left, right, *refs):
+    m = pl.program_id(0)
+    for k, out in enumerate(refs[-n:]):
+
+        @pl.when(m == k)
+        def _():
+            for kind, ref in enumerate((left, right)):
+                for q in range(2):
+                    out[kind, 0, :, q * B : q * B + B] = ref[q, 0]
+
+
+def pack_roots(js, left, right, after):
+    blocks, _, rows, _ = left.shape
+    pairs, n, w = blocks // 2, js.shape[0], 2 * B
+    source = pl.BlockSpec((2, 1, rows, B), lambda m, p, j: (p, j[m], 0, 0))
+    return pl.pallas_call(
+        functools.partial(pack_roots_body, n),
+        grid_spec=pltpu.PrefetchScalarGridSpec(
+            num_scalar_prefetch=1,
+            grid=(n, pairs),
+            in_specs=[source, source] + [ANY] * len(after),
+            out_specs=[
+                pl.BlockSpec(
+                    (2, 1, rows, w),
+                    lambda m, p, j, k=k: (0, visit(k, m, p, pairs - 1), 0, 0),
+                )
+                for k in range(n)
+            ],
+        ),
+        out_shape=[jax.ShapeDtypeStruct((2, pairs, rows, w), left.dtype)] * n,
+        compiler_params=params(),
+        cost_estimate=cost(0, 4 * left.size * 2),
+    )(js, left, right, *after)
+
+
+def dot(x, y, dims):
+    return lax.dot_general(x, y, (dims, ((), ())), preferred_element_type=jnp.float32)
+
+
+def assemble(chunks, q, full):
+    base = 0
+    for chunk in chunks:
+        n = chunk.shape[1]
+        for h in range(2):
+            for side in range(2):
+                start = h * (B // 2) + base + side * n
+                full[start : start + n, :] = chunk[2 * q + h, :, side * B : side * B + B]
+        base += 2 * n
+
+
+def own_rows(j, h, rd):
+    return pl.ds(pl.multiple_of(h * (B // 2) + j * rd, 8), rd)
+
+
+def gram_body(n, rd, n_chunks, js, *refs):
+    chunks, refs = refs[:n_chunks], refs[n_chunks:]
+    rows_out, grams_out = refs[:n], refs[n : 2 * n]
+    g16, g32, l32, r32 = refs[2 * n :]
+    for q in range(2):
+        assemble(chunks, q, g16)
+        g = g16[...]
+        g32[...] = g.astype(jnp.float32)
+        l32[...] = dot(g, g, ((1,), (1,)))
+        r32[...] = dot(g, g, ((0,), (0,)))
+        lanes = slice(q * B, q * B + B)
+        for k in range(n):
+            for full, out, kind in ((g32, rows_out, 0), (l32, grams_out, 0), (r32, grams_out, 1)):
+                parts = [full[own_rows(js[k], h, rd), :] for h in range(2)]
+                out[k][kind, 0, :, lanes] = jnp.concatenate(parts, axis=0).astype(jnp.bfloat16)
+
+
+def gram(js, chunks, rd):
+    n = js.shape[0]
+    count, _, w = chunks[0].shape
+    pairs, rows = count // 4, 2 * rd
+
+    def outs(kinds):
+        return (
+            [pl.BlockSpec((kinds, 1, rows, w), lambda p, j: (0, p, 0, 0))] * n,
+            [jax.ShapeDtypeStruct((kinds, pairs, rows, w), jnp.bfloat16)] * n,
+        )
+
+    (rows_specs, rows_shapes), (gram_specs, gram_shapes) = outs(1), outs(2)
+    out = pl.pallas_call(
+        functools.partial(gram_body, n, rd, len(chunks)),
+        grid_spec=pltpu.PrefetchScalarGridSpec(
+            num_scalar_prefetch=1,
+            grid=(pairs,),
+            in_specs=[
+                pl.BlockSpec((4,) + chunk.shape[1:], lambda p, j: (p, 0, 0)) for chunk in chunks
+            ],
+            out_specs=rows_specs + gram_specs,
+            scratch_shapes=[pltpu.VMEM((B, B), jnp.bfloat16)] + [pltpu.VMEM((B, B), jnp.float32)] * 3,
+        ),
+        out_shape=rows_shapes + gram_shapes,
+        compiler_params=params(),
+        cost_estimate=cost(pairs * 8 * B**3, pairs * B * B * 2 * 8),
+    )(js, *chunks)
+    return out[:n], out[n:]
+
+
+def direct_body(n, rd, n_chunks, js, *refs):
+    chunks, roots, refs = refs[:n_chunks], refs[n_chunks : n_chunks + n], refs[n_chunks + n :]
+    outs, square_out = refs[:n_chunks], refs[n_chunks]
+    g16, l32, r32 = refs[n_chunks + 1 :]
+    for q in range(2):
+        assemble(chunks, q, g16)
+        for k in range(n):
+            for kind, full in enumerate((l32, r32)):
+                part = roots[k][kind, 0, :, q * B : q * B + B].astype(jnp.float32)
+                for h in range(2):
+                    full[own_rows(js[k], h, rd), :] = part[h * rd : h * rd + rd]
+        inner = dot(l32[...].astype(jnp.bfloat16), g16[...], ((1,), (0,))).astype(jnp.bfloat16)
+        direction = dot(inner, r32[...].astype(jnp.bfloat16), ((1,), (0,)))
+        square_out[0, q : q + 1, :] = jnp.full((1, LANES), jnp.sum(direction * direction))
+        direction = direction.astype(jnp.bfloat16)
+        base = 0
+        for out in outs:
+            size = out.shape[1]
+            for h in range(2):
+                for side in range(2):
+                    start = h * (B // 2) + base + side * size
+                    out[2 * q + h, :, side * B : side * B + B] = direction[start : start + size]
+            base += 2 * size
+
+
+def direct(js, chunks, roots, rd):
+    n = js.shape[0]
+    count, _, w = chunks[0].shape
+    pairs, rows = roots[0].shape[1], roots[0].shape[2]
+    chunk_specs = [pl.BlockSpec((4,) + chunk.shape[1:], lambda p, j: (p, 0, 0)) for chunk in chunks]
+    return pl.pallas_call(
+        functools.partial(direct_body, n, rd, len(chunks)),
+        grid_spec=pltpu.PrefetchScalarGridSpec(
+            num_scalar_prefetch=1,
+            grid=(pairs,),
+            in_specs=chunk_specs
+            + [pl.BlockSpec((2, 1, rows, w), lambda p, j: (0, p, 0, 0))] * n,
+            out_specs=chunk_specs + [pl.BlockSpec((1, 8, LANES), lambda p, j: (p, 0, 0))],
+            scratch_shapes=[pltpu.VMEM((B, B), jnp.bfloat16)] + [pltpu.VMEM((B, B), jnp.float32)] * 2,
+        ),
+        out_shape=[jax.ShapeDtypeStruct(chunk.shape, jnp.bfloat16) for chunk in chunks]
+        + [jax.ShapeDtypeStruct((pairs, 8, LANES), jnp.float32)],
+        compiler_params=params(),
+        cost_estimate=cost(pairs * 8 * B**3, pairs * B * B * 2 * 8),
+    )(js, *chunks, *roots)
+
+
+def moment_body(n, js, *refs):
+    received, (moment, moment_out, square_out) = refs[:n], refs[n:]
+    m = pl.program_id(0)
+    for k in range(n):
+
+        @pl.when(m == k)
+        def _():
+            for q in range(2):
+                g = received[k][0, 0, :, q * B : q * B + B].astype(jnp.float32)
+                second = 0.95 * moment[q, 0] + 0.05 * g * g
+                moment_out[q, 0] = second
+                adam = g / (jnp.sqrt(second) + 1e-08)
+                square_out[0, 0, q : q + 1, :] = jnp.full((1, LANES), jnp.sum(adam * adam))
+
+
+def statistics_body(n, js, *refs):
+    received, (left, right, left_out, right_out) = refs[:n], refs[n:]
+    m = pl.program_id(0)
+    for k in range(n):
+
+        @pl.when(m == k)
+        def _():
+            for q in range(2):
+                for kind, old, new in ((0, left, left_out), (1, right, right_out)):
+                    product = received[k][kind, 0, :, q * B : q * B + B].astype(jnp.float32)
+                    new[q, 0] = 0.95 * old[q, 0] + 0.05 * product
+
+
+def by_rows(body, js, received, olds, squares):
+    n = js.shape[0]
+    blocks, _, rows, _ = olds[0].shape
+    kinds, pairs, _, w = received[0].shape
+    own = pl.BlockSpec((2, 1, rows, B), lambda m, p, j: (p, j[m], 0, 0))
+    out_specs = [own] * len(olds)
+    out_shape = [jax.ShapeDtypeStruct(old.shape, jnp.float32) for old in olds]
+    if squares:
+        out_specs.append(pl.BlockSpec((1, 1, 8, LANES), lambda m, p, j: (m, p, 0, 0)))
+        out_shape.append(jax.ShapeDtypeStruct((n, pairs, 8, LANES), jnp.float32))
+    return pl.pallas_call(
+        functools.partial(body, n),
+        grid_spec=pltpu.PrefetchScalarGridSpec(
+            num_scalar_prefetch=1,
+            grid=(n, pairs),
+            in_specs=[
+                pl.BlockSpec(
+                    (kinds, 1, rows, w),
+                    lambda m, p, j, k=k: (0, visit(k, m, p, pairs - 1), 0, 0),
+                )
+                for k in range(n)
+            ]
+            + [own] * len(olds),
+            out_specs=out_specs,
+        ),
+        out_shape=out_shape,
+        compiler_params=params(),
+        cost_estimate=cost(0, olds[0].size * 10 * len(olds)),
+    )(js, *received, *olds)
+
+
+def restore_body(n_src, n_old, base, src, item, scale, *refs):
+    sources = refs[:n_src]
+    out, buffer, result, in_sems, out_sems = refs[n_src + n_old :]
+    columns, n, w = buffer.shape
+    slots = result.shape[0]
+
+    def fetch(c, _):
+        for k in range(n_src):
+
+            @pl.when(src[c] == k)
+            def _():
+                pltpu.make_async_copy(sources[k].at[item[c]], buffer.at[c], in_sems.at[c]).start()
+
+        return 0
+
+    def store(p, slot):
+        start = pl.multiple_of(p * w, LANES)
+        return pltpu.make_async_copy(
+            result.at[slot], out.at[pl.ds(base, 2 * n), pl.ds(start, w)], out_sems.at[slot]
+        )
+
+    def step(p, _):
+        slot = lax.rem(p, slots)
+
+        @pl.when(p >= slots)
+        def _():
+            store(p - slots, slot).wait()
+
+        for e in range(2):
+            c = 2 * p + e
+            pltpu.make_async_copy(sources[0].at[0], buffer.at[c], in_sems.at[c]).wait()
+            scaled = (buffer[c].astype(jnp.float32) * scale[c]).astype(result.dtype)
+            result[slot, :n, e * B : e * B + B] = scaled[:, :B]
+            result[slot, n:, e * B : e * B + B] = scaled[:, B:]
+        store(p, slot).start()
+        return 0
+
+    pairs = columns // 2
+    lax.fori_loop(0, columns, fetch, 0)
+    lax.fori_loop(0, pairs, step, 0)
+    for p in range(pairs - slots, pairs):
+        store(p, p % slots).wait()
+
+
+def restore(src, item, scale, sources, base, rows, old):
+    _, n, w = sources[0].shape
+    columns = src.shape[0]
+    slots = 4
+    return pl.pallas_call(
+        functools.partial(restore_body, len(sources), len(old), base),
+        in_specs=[SCALARS] * 3 + [ANY] * (len(sources) + len(old)),
+        out_specs=ANY,
+        out_shape=jax.ShapeDtypeStruct((rows, columns * B), jnp.bfloat16),
+        scratch_shapes=[
+            pltpu.VMEM((columns, n, w), jnp.bfloat16),
+            pltpu.VMEM((slots, 2 * n, w), jnp.bfloat16),
+            pltpu.SemaphoreType.DMA((columns,)),
+            pltpu.SemaphoreType.DMA((slots,)),
+        ],
+        input_output_aliases={3 + len(sources): 0} if old else {},
+        compiler_params=params(),
+        cost_estimate=cost(0, columns * n * w * 4),
+    )(src, item, scale, *sources, *old)
+
+
+def owner_local(grads, slots, stats_left, stats_right, root_left, root_right, second_moment):
+    owners = lax.axis_size("fsdp")
+    replicas = lax.axis_size("replica")
+    grad = grads[0]
+    rows, full_width = grad.shape
+    columns = full_width // B
+    row_blocks = slots.shape[0]
+    sub_count = B // rows
+    rd = rows // replicas
+    half = owners // 2
+    f = lax.axis_index("fsdp")
+    r = lax.axis_index("replica")
+    js = r ^ jnp.arange(replicas, dtype=jnp.int32)
+    row_slots = lax.dynamic_index_in_dim(slots, f // sub_count, 0, keepdims=False)
+    column_ids = jnp.arange(columns, dtype=jnp.int32)
+    owner_ids = replicas * jnp.arange(owners, dtype=jnp.int32)
+
+    def columns_of(low, high):
+        ids = jnp.arange(owners, dtype=jnp.int32)
+        wanted = owner_ids + (r ^ jnp.where(ids < half, low, high))
+        return jnp.sum(jnp.where(row_slots == wanted[:, None], column_ids, 0), axis=1)
+
+    far, near, cross, own = (columns_of(*k) for k in ((3, 3), (1, 2), (2, 1), (0, 0)))
+
+    def swap(x, k):
+        return lax.ppermute(x, "replica", [(i, i ^ k) for i in range(replicas)])
+
+    def as_rows(x):
+        return x.reshape(row_blocks, -1, sub_count * rd, B)
+
+    def exchange(x):
+        return lax.all_to_all(x, "fsdp", split_axis=0, concat_axis=0, tiled=True)
+
+    first = -(-rows // 64) * 16
+    chunks = ((0, first), (2 * first, rows // 2 - first))
+
+    def start_sum(base, n, after):
+        far_a, far_b = arrange(far, grad, base, n, after=after)
+        by_far = (swap(far_a, 1), swap(far_b, 2))
+        x_a, y_b = arrange(near, grad, base, n, after=(far_a,))
+        return by_far, (swap(x_a, 1), swap(y_b, 2)), x_a
+
+    def end_sum(base, n, by_far, after):
+        y_a, x_b = arrange(cross, grad, base, n, (by_far,), after=after)
+        return (swap(y_a, 2), swap(x_b, 1)), y_a
+
+    by_far, by_near, sent = start_sum(*chunks[0], ())
+    roots = list(pack_roots(js, as_rows(root_left), as_rows(root_right), (sent,)))
+    by_cross, sent = end_sum(*chunks[0], by_far, (roots[0],))
+    by_far_1, by_near_1, sent = start_sum(*chunks[1], (sent,))
+    terms = ((by_near[0], by_cross[1]), (by_cross[0], by_near[1]))
+    (owned,) = arrange(own, grad, *chunks[0], terms, halves=False, after=(sent,))
+    by_cross_1, sent = end_sum(*chunks[1], by_far_1, (owned,))
+    blocks = [exchange(owned)]
+    terms = ((by_near_1[0], by_cross_1[1]), (by_cross_1[0], by_near_1[1]))
+    owned, *roots[1:] = arrange(
+        own, grad, *chunks[1], terms, halves=False, through=tuple(roots[1:])
+    )
+    blocks.append(exchange(owned))
+    roots = [roots[0]] + [swap(roots[k], k) for k in (3, 1, 2)]
+    roots = [roots[0], roots[2], roots[3], roots[1]]
+
+    grad_rows, grams = gram(js, blocks, rd)
+    grad_rows = [grad_rows[0]] + [swap(grad_rows[k], k) for k in (1, 2, 3)]
+    grams = [grams[0]] + [swap(grams[k], k) for k in (1, 2, 3)]
+    *directions, direction_square = direct(js, blocks, roots, rd)
+
+    gathered = []
+    for direction in directions:
+        mine = exchange(direction)
+        x, y = swap(mine, 1), swap(mine, 2)
+        gathered.append((mine, x, y, swap(x[:half], 2), swap(y[half:], 1)))
+
+    moment, adam_square = by_rows(moment_body, js, grad_rows, [as_rows(second_moment)], True)
+    left_new, right_new = by_rows(
+        statistics_body, js, grams, [as_rows(stats_left), as_rows(stats_right)], False
+    )
+
+    adam_square = adam_square[:, :, :2, 0].reshape(replicas, row_blocks)
+    slot_ids = jnp.arange(replicas, dtype=jnp.int32)
+    adam_square = jnp.sum(
+        jnp.where((js[:, None] == slot_ids)[:, :, None], adam_square[:, None, :], 0.0), axis=0
+    )
+    squares = jnp.concatenate([adam_square, direction_square[:, :2, 0].reshape(1, row_blocks)])
+    squares = lax.all_gather(squares, ("fsdp", "replica")).reshape(
+        owners, replicas, replicas + 1, row_blocks
+    )
+    ratio = jnp.sqrt(jnp.sum(squares[:, :, :replicas], axis=1)) / jnp.sqrt(
+        squares[:, :, replicas] + 1e-06
+    )
+    row_ratio = lax.dynamic_index_in_dim(
+        ratio.reshape(columns, row_blocks), f // sub_count, 1, keepdims=False
+    )
+    scale = jnp.sum(jnp.where(row_slots[:, None] == column_ids, row_ratio, 0.0), axis=1)
+
+    owner = row_slots // replicas
+    step = lax.rem(row_slots, replicas) ^ r
+    src = step + jnp.where(step == 3, owner // half, 0)
+    item = jnp.where(step == 3, lax.rem(owner, half), owner)
+    update = ()
+    for (base, _), sources in zip(chunks, gathered):
+        update = (restore(src, item, scale, sources, base, rows, update),)
+    return (
+        update[0],
+        left_new.reshape(stats_left.shape),
+        right_new.reshape(stats_right.shape),
+        moment.reshape(second_moment.shape),
+    )
 
 
 def slot_columns(row_slots, row_count):
@@ -12,7 +475,7 @@
     return jnp.sum(jnp.where(matches, column_ids[None, :], 0), axis=1)
 
 
-def local(grads, slots, stats_left, stats_right, root_left, root_right, second_moment):
+def row_local(grads, slots, stats_left, stats_right, root_left, root_right, second_moment):
     fsdp_count = lax.axis_size("fsdp")
     replica_count = lax.axis_size("replica")
     local_grad = grads[0]
@@ -103,6 +566,15 @@
     )
 
 
+def local(*arrays):
+    replicas = lax.axis_size("replica")
+    rows, full_width = arrays[0].shape[1:]
+    per_owner = full_width // B // lax.axis_size("fsdp")
+    if replicas == 4 and per_owner == replicas and 2 * rows == B:
+        return owner_local(*arrays)
+    return row_local(*arrays)
+
+
 def solution(mesh):
     placed = (
         P("replica", "fsdp", None),

time: 713 us -> 507 us (0.71)
  waiting for transfers between devices: 382 us -> 184 us
  local copies, waits for them, and re-layouts: 161 us -> 21 us
  Pallas kernels: 0 us -> 103 us
  blocking collectives: 74.4 us -> 147 us
  starting transfers between devices: 5.16 us -> 44.8 us
  matrix products: 37.6 us -> 0 us
  other arithmetic: 36.1 us -> 4.08 us
  between operations: 13.9 us -> 1.19 us
    all_gather x3 -> x0, waiting for transfers between devices: 210 us -> none  [the longest x1 106 us: local(): lax.all_gather(root_right, 'replica', axis=3, tiled=True)]
    ppermute x0 -> x29, waiting for transfers between devices: none -> 184 us  [swap(): return lax.ppermute(x, 'replica', [(i, i ^ k) for i in range(replicas)])]
    unnamed x5 -> x0, waiting for transfers between devices: 111 us -> none
    all_gather x0 -> x1, blocking collectives: none -> 107 us  [owner_local(): lax.all_gather(squares, ('fsdp', 'replica'))]
    pallas_call x0 -> x15, Pallas kernels: none -> 103 us  [the longest x8 33.9 us: arrange(): pl.pallas_call(functools.partial(arrange_body, len(adds), len(after), len...]
    all_to_all x1 -> x3, waiting for transfers between devices: 60.7 us -> 0.01 us  [exchange(): return lax.all_to_all(x, 'fsdp', split_axis=0, concat_axis=0, tiled=True)]
    all_gather x2 -> x0, local copies, waits for them, and re-layouts: 52.5 us -> none  [local(): lax.all_gather(own_split[:, :, :, None], 'replica', axis=3, tiled=True)]
    reshape x9 -> x0, local copies, waits for them, and re-layouts: 45.1 us -> none  [the longest x2 10.8 us: local(): ordered = jnp.take(summed.reshape(row_count, columns, B), slot_cols, axis=1)]
  transfers between devices with their start and end apart: 5 -> 32, of which waited for: 4 -> 15; matrix products, arithmetic and copies ran while one was open for 21% -> 3% of each run, Pallas kernels for 0% -> 15%
where the time goes in v2:
time: 507 us; the launch traced here: 505 us
  waiting for transfers between devices  184 us (36%)
  blocking collectives  147 us (29%)
  Pallas kernels  103 us (20%)
  starting transfers between devices  44.8 us (9%)
  local copies, waits for them, and re-layouts  21 us (4%)
    ppermute x29, waiting for transfers between devices, swap(): return lax.ppermute(x, 'replica', [(i, i ^ k) for i in range(replicas)])  184 us
    all_gather x1, blocking collectives, owner_local(): lax.all_gather(squares, ('fsdp', 'replica'))  107 us
    all_to_all x1, blocking collectives, exchange(): return lax.all_to_all(x, 'fsdp', split_axis=0, concat_axis=0, tiled=True)  40.5 us
    pallas_call x8, Pallas kernels, arrange(): pl.pallas_call(functools.partial(arrange_body, len(adds), len(after), len...  33.9 us
    ppermute x29, starting transfers between devices, swap(): return lax.ppermute(x, 'replica', [(i, i ^ k) for i in range(replicas)])  31.2 us
    pallas_call x2, Pallas kernels, by_rows(): pl.pallas_call(functools.partial(body, n), grid_spec=pltpu.PrefetchScalar...  25.6 us
    all_to_all x3, starting transfers between devices, exchange(): return lax.all_to_all(x, 'fsdp', split_axis=0, concat_axis=0, tiled=True)  13.6 us
    pallas_call x2, Pallas kernels, restore(): pl.pallas_call(functools.partial(restore_body, len(sources), len(old), ba...  12.7 us
  transfers between devices with their start and end apart: 32, of which 15 were waited for; matrix products, arithmetic and copies ran while one was open for 3% of the time, Pallas kernels for 15%

profile of v2, /device:TPU:0, one launch (start us, length us, event | category | flops | bytes accessed | tf_op | source)
XLA Modules:
  0.0 505.3 jit_solution(2793852471986562646)
XLA Ops:
  2.7 3.7 shard_map.102
  6.4 3.0 collective-permute-start.2
  10.9 3.7 shard_map.103
  15.9 8.9 %shard_map.104 = (bf16[2,2,144,1152]{3,2,1,0:T(8,128)(2,1)}, bf16[2,2,144,1152]{3,2,1,0:T(8,128)(2,1)}, bf16[2,2,144,1152]{3,2,1,0:T(8,128)(2,1)}, bf16[2,2,144,1152]{3,2,1,0:T(8,128)(2,1)}) custom-call(s32[4]{0:T(128)} %iota_xor_fusion.js, bf16[4,4,144,576]{3,2,1,0:T(8,128)(2,1)} %bitcast.40, bf16[4,4,144,576]{3,2,1,0:T(8,128)(2,1)} %bitcast.41, ...), custom_call_target="tpu_custom_call" | custom-call | bytes 10616832 | tf_op jit(solution)/shard_map/pallas_call | solution.py:105
  24.8 2.2 collective-permute-done.2.refs_1_
  27.0 2.1 collective-permute-done.1.refs_0_
  29.9 4.7 shard_map.105
  36.7 3.5 shard_map.106
  40.3 3.5 shard_map.107
  44.9 14.3 %collective-permute-done.3.refs_1_ = bf16[4,80,1152]{2,1,0:T(8,128)(2,1)S(1)} collective-permute-done((bf16[4,80,1152]{2,1,0:T(8,128)(2,1)}, bf16[4,80,1152]{2,1,0:T(8,128)(2,1)S(1)}, u32[]{:S(2)}, u32[]{:S(2)}) %collective-permute-start.3) | collective-permute-done | bytes 737312 | tf_op jit(solution)/shard_map/ppermute | solution.py:387
  60.4 5.4 %shard_map.108.refs_2_ = bf16[8,80,1152]{2,1,0:T(8,128)(2,1)} custom-call(s32[8]{0:T(128)} %get-tuple-element.95.cols, bf16[288,18432]{1,0:T(8,128)(2,1)} %bitcast.34, bf16[4,80,1152]{2,1,0:T(8,128)(2,1)} %copy-done.8, bf16[4,80,1152]{2,1,0:T(8,128)(2,1)} %copy-done.9, bf16[4,80,1152]{2,1,0:T(8,128)(2,1)} %copy-done.10, bf16[4,80,1152]{2,1,0:T(8,128)(2,1)} %copy-done.7, ...), custom_call_target="tpu_custom_call" | custom-call | bytes 5898240 | tf_op jit(solution)/shard_map/pallas_call | solution.py:68
  65.8 5.0 all-to-all-start
  74.8 12.3 %collective-permute-done.8.refs_1_ = bf16[4,64,1152]{2,1,0:T(8,128)(2,1)S(1)} collective-permute-done((bf16[4,64,1152]{2,1,0:T(8,128)(2,1)}, bf16[4,64,1152]{2,1,0:T(8,128)(2,1)S(1)}, u32[]{:S(2)}, u32[]{:S(2)}) %collective-permute-start.8) | collective-permute-done | bytes 589856 | tf_op jit(solution)/shard_map/ppermute | solution.py:387
  88.8 4.4 shard_map.109
  95.8 4.0 collective-permute-done.11.refs_3_
  100.1 11.9 %collective-permute-done.9.refs_1_ = bf16[4,64,1152]{2,1,0:T(8,128)(2,1)S(1)} collective-permute-done((bf16[4,64,1152]{2,1,0:T(8,128)(2,1)}, bf16[4,64,1152]{2,1,0:T(8,128)(2,1)S(1)}, u32[]{:S(2)}, u32[]{:S(2)}) %collective-permute-start.9) | collective-permute-done | bytes 589856 | tf_op jit(solution)/shard_map/ppermute | solution.py:387
  113.0 5.0 shard_map.110
  118.1 5.0 all-to-all-start.1
  126.6 28.4 %collective-permute-done.15.refs_3_ = bf16[2,2,144,1152]{3,2,1,0:T(8,128)(2,1)S(1)} collective-permute-done((bf16[2,2,144,1152]{3,2,1,0:T(8,128)(2,1)S(1)}, bf16[2,2,144,1152]{3,2,1,0:T(8,128)(2,1)S(1)}, u32[]{:S(2)}, u32[]{:S(2)}) %collective-permute-start.15) | collective-permute-done | bytes 1327136 | tf_op jit(solution)/shard_map/ppermute | solution.py:387
  156.2 28.3 %collective-permute-done.16.refs_4_ = bf16[2,2,144,1152]{3,2,1,0:T(8,128)(2,1)S(1)} collective-permute-done((bf16[2,2,144,1152]{3,2,1,0:T(8,128)(2,1)}, bf16[2,2,144,1152]{3,2,1,0:T(8,128)(2,1)S(1)}, u32[]{:S(2)}, u32[]{:S(2)}) %collective-permute-start.16) | collective-permute-done | bytes 1327136 | tf_op jit(solution)/shard_map/ppermute | solution.py:387
  185.6 10.9 %shard_map.113 = (bf16[8,80,1152]{2,1,0:T(8,128)(2,1)}, bf16[8,64,1152]{2,1,0:T(8,128)(2,1)}, f32[2,8,128]{2,1,0:T(8,128)}) custom-call(s32[4]{0:T(128)} %iota_xor_fusion.js, bf16[8,80,1152]{2,1,0:T(8,128)(2,1)} %copy-done.2, bf16[8,64,1152]{2,1,0:T(8,128)(2,1)} %all-to-all-done.1.refs_1_, bf16[2,2,144,1152]{3,2,1,0:T(8,128)(2,1)} %get-tuple-element.42.refs_2_, ...), custom_call_target="tpu_custom_call" | custom-call | flops 3057647616 | bytes 10616832 | tf_op jit(solution)/shard_map/pallas_call | solution.py:221
  196.4 40.5 %all_to_all.20.refs_0_ = bf16[8,80,1152]{2,1,0:T(8,128)(2,1)S(1)} all-to-all(bf16[8,80,1152]{2,1,0:T(8,128)(2,1)} %get-tuple-element.66), channel_id=1, replica_groups=mesh['fsdp'=8,'replica'=4] {'fsdp'}, dimensions={0} | all-to-all | bytes 2949120 | tf_op jit(solution)/shard_map/all_to_all | solution.py:393
  236.9 3.6 all-to-all-start.2
  242.6 10.7 %shard_map.111 = (bf16[1,2,144,1152]{3,2,1,0:T(8,128)(2,1)}, bf16[1,2,144,1152]{3,2,1,0:T(8,128)(2,1)}, bf16[1,2,144,1152]{3,2,1,0:T(8,128)(2,1)}, bf16[1,2,144,...) custom-call(s32[4]{0:T(128)} %iota_xor_fusion.js, ...), custom_call_target="tpu_custom_call" | custom-call | flops 3057647616 | bytes 10616832 | tf_op jit(solution)/shard_map/pallas_call | solution.py:173
  256.9 34.6 %collective-permute-done.12.refs_1_ = bf16[1,2,144,1152]{3,2,1,0:T(8,128)(2,1)S(1)} collective-permute-done((bf16[1,2,144,1152]{3,2,1,0:T(8,128)(2,1)}, bf16[1,2,144,1152]{3,2,1,0:T(8,128)(2,1)S(1)}, u32[]{:S(2)}, u32[]{:S(2)}) %collective-permute-start.12) | collective-permute-done | bytes 663584 | tf_op jit(solution)/shard_map/ppermute | solution.py:387
  292.9 12.9 %collective-permute-done.14.refs_3_ = bf16[1,2,144,1152]{3,2,1,0:T(8,128)(2,1)} collective-permute-done((bf16[1,2,144,1152]{3,2,1,0:T(8,128)(2,1)}, bf16[1,2,144,1152]{3,2,1,0:T(8,128)(2,1)}, u32[]{:S(2)}, u32[]{:S(2)}) %collective-permute-start.14) | collective-permute-done | bytes 663584 | tf_op jit(solution)/shard_map/ppermute | solution.py:387
  310.8 12.0 %shard_map.112 = (f32[4,4,144,576]{3,2,1,0:T(8,128)}, f32[4,2,8,128]{3,2,1,0:T(8,128)}) custom-call(s32[4]{0:T(128)} %iota_xor_fusion.js, bf16[1,2,144,1152]{3,2,1,0:T(8,128)(2,1)} %get-tuple-element.56.refs_0_, bf16[1,2,144,1152]{3,2,1,0:T(8,128)(2,1)} %copy-done.13, bf16[1,2,144,1152]{3,2,1,0:T(8,128)(2,1)} %copy-done.14, ...), custom_call_target="tpu_custom_call" | custom-call | bytes 13271040 | tf_op jit(solution)/shard_map/pallas_call | solution.py:276
  327.9 31.5 %collective-permute-done.19.refs_2_ = bf16[8,64,1152]{2,1,0:T(8,128)(2,1)} collective-permute-done((bf16[8,64,1152]{2,1,0:T(8,128)(2,1)S(1)}, bf16[8,64,1152]{2,1,0:T(8,128)(2,1)}, u32[]{:S(2)}, u32[]{:S(2)}) %collective-permute-start.19) | collective-permute-done | bytes 1179680 | tf_op jit(solution)/shard_map/ppermute | solution.py:387
  367.5 106.6 %all-gather.1 = f32[32,5,4]{1,2,0:T(4,128)S(1)} all-gather(f32[1,5,4]{1,2,0:T(4,128)S(1)} %bitcast.44), channel_id=2, replica_groups=mesh['fsdp'=8,'replica'=4] {'fsdp','replica'}, dimensions={0}, use_global_device_ids=true | all-gather | bytes 2640 | tf_op jit(solution)/shard_map/all_gather | solution.py:446
  476.8 13.6 %shard_map.116 = (f32[4,4,144,576]{3,2,1,0:T(8,128)}, f32[4,4,144,576]{3,2,1,0:T(8,128)}) custom-call(s32[4]{0:T(128)} %iota_xor_fusion.js, bf16[2,2,144,1152]{3,2,1,0:T(8,128)(2,1)} %get-tuple-element.67.refs_0_, bf16[2,2,144,1152]{3,2,1,0:T(8,128)(2,1)} %collective-permute-done.26.refs_1_, bf16[2,2,144,1152]{3,2,1,0:T(8,128)(2,1)} %collective-permute-done.27.refs_2_, ...), custom_call_target="tpu_custom_call" | custom-call | bytes 26542080 | tf_op jit(solution)/shard_map/pallas_call | solution.py:276
  491.6 6.4 %shard_map.114.refs_5_ = bf16[288,18432]{1,0:T(8,128)(2,1)} custom-call(s32[32]{0:T(128)} %fusion.src, s32[32]{0:T(128)} %get-tuple-element.98.item, f32[32]{0:T(128)} %select_reduce_fusion.scale, bf16[8,80,1152]{2,1,0:T(8,128)(2,1)} %copy-done, bf16[8,80,1152]{2,1,0:T(8,128)(2,1)} %collective-permute-done.22.refs_1_, ...), custom_call_target="tpu_custom_call" | custom-call | bytes 11796480 | tf_op jit(solution)/shard_map/pallas_call | solution.py:345
  498.9 6.2 %shard_map.115 = bf16[288,18432]{1,0:T(8,128)(2,1)} custom-call(s32[32]{0:T(128)} %fusion.src, s32[32]{0:T(128)} %get-tuple-element.98.item, f32[32]{0:T(128)} %select_reduce_fusion.scale, bf16[8,64,1152]{2,1,0:T(8,128)(2,1)} %copy-done.1, bf16[8,64,1152]{2,1,0:T(8,128)(2,1)} %collective-permute-done.18.refs_1_, ...), custom_call_target="tpu_custom_call", output_to_operand_aliasing={{}: (8, {})} | custom-call | bytes 9437184 | tf_op jit(solution)/shard_map/pallas_call | solution.py:345
  (136 shorter events, 55.0 us)
Async XLA Ops:
  6.4 20.6 %collective-permute-start.2 = (bf16[4,80,1152]{2,1,0:T(8,128)(2,1)}, bf16[4,80,1152]{2,1,0:T(8,128)(2,1)S(1)}, u32[]{:S(2)}, u32[]{:S(2)}) collective-permute-start(bf16[4,80,1152]{2,1,0:T(8,128)(2,1)} %get-tuple-element.41), channel_id=1, source_target_pairs={{0,2},{1,3},{2,0},{3,1},{4,6},{5,7},{6,4},{7,5},{8,10},{9,11},{10,... | collective-permute-start | bytes 2211848 | tf_op jit(solution)/shard_map/ppermute | solution.py:387
  9.5 19.6 %collective-permute-start.1 = (bf16[4,80,1152]{2,1,0:T(8,128)(2,1)}, bf16[4,80,1152]{2,1,0:T(8,128)(2,1)S(1)}, u32[]{:S(2)}, u32[]{:S(2)}) collective-permute-start(bf16[4,80,1152]{2,1,0:T(8,128)(2,1)} %get-tuple-element.39.refs_0_), channel_id=1, source_target_pairs={{0,1},{1,0},{2,3},{3,2},{4,5},{5,4},{6,7},{7,6},{8,9},{9,8},{10,11... | collective-permute-start | bytes 2211848 | tf_op jit(solution)/shard_map/ppermute | solution.py:387
  14.6 29.2 %collective-permute-start.5 = (bf16[4,80,1152]{2,1,0:T(8,128)(2,1)}, bf16[4,80,1152]{2,1,0:T(8,128)(2,1)S(1)}, u32[]{:S(2)}, u32[]{:S(2)}) collective-permute-start(bf16[4,80,1152]{2,1,0:T(8,128)(2,1)} %get-tuple-element.45), channel_id=1, source_target_pairs={{0,2},{1,3},{2,0},{3,1},{4,6},{5,7},{6,4},{7,5},{8,10},{9,11},{10,... | collective-permute-start | bytes 2211848 | tf_op jit(solution)/shard_map/ppermute | solution.py:387
  15.2 29.7 %collective-permute-start = (bf16[4,80,1152]{2,1,0:T(8,128)(2,1)}, bf16[4,80,1152]{2,1,0:T(8,128)(2,1)S(1)}, u32[]{:S(2)}, u32[]{:S(2)}) collective-permute-start(bf16[4,80,1152]{2,1,0:T(8,128)(2,1)} %get-tuple-element.40.refs_0_), channel_id=1, source_target_pairs={{0,1},{1,0},{2,3},{3,2},{4,5},{5,4},{6,7},{7,6},{8,9},{9,8},{10,11... | collective-permute-start | bytes 2211848 | tf_op jit(solution)/shard_map/ppermute | solution.py:387
  34.7 24.5 %collective-permute-start.3 = (bf16[4,80,1152]{2,1,0:T(8,128)(2,1)}, bf16[4,80,1152]{2,1,0:T(8,128)(2,1)S(1)}, u32[]{:S(2)}, u32[]{:S(2)}) collective-permute-start(bf16[4,80,1152]{2,1,0:T(8,128)(2,1)} %get-tuple-element.43), channel_id=1, source_target_pairs={{0,1},{1,0},{2,3},{3,2},{4,5},{5,4},{6,7},{7,6},{8,9},{9,8},{10,11... | collective-permute-start | bytes 2211848 | tf_op jit(solution)/shard_map/ppermute | solution.py:387
  36.2 23.0 %collective-permute-start.4 = (bf16[4,80,1152]{2,1,0:T(8,128)(2,1)}, bf16[4,80,1152]{2,1,0:T(8,128)(2,1)S(1)}, u32[]{:S(2)}, u32[]{:S(2)}) collective-permute-start(bf16[4,80,1152]{2,1,0:T(8,128)(2,1)} %get-tuple-element.44.refs_0_), channel_id=1, source_target_pairs={{0,2},{1,3},{2,0},{3,1},{4,6},{5,7},{6,4},{7,5},{8,10},{9,11},{10,... | collective-permute-start | bytes 2211848 | tf_op jit(solution)/shard_map/ppermute | solution.py:387
  65.8 52.3 %all-to-all-start = ((bf16[8,80,1152]{2,1,0:T(8,128)(2,1)}), bf16[8,80,1152]{2,1,0:T(8,128)(2,1)S(1)}, u32[]{:S(2)}, u32[]{:S(2)}) async-start(bf16[8,80,1152]{2,1,0:T(8,128)(2,1)} %shard_map.108.refs_2_), calls=%async_computation | async-start | bytes 2949120 | tf_op jit(solution)/shard_map/all_to_all | solution.py:393
  70.8 16.3 %collective-permute-start.8 = (bf16[4,64,1152]{2,1,0:T(8,128)(2,1)}, bf16[4,64,1152]{2,1,0:T(8,128)(2,1)S(1)}, u32[]{:S(2)}, u32[]{:S(2)}) collective-permute-start(bf16[4,64,1152]{2,1,0:T(8,128)(2,1)} %get-tuple-element.48), channel_id=1, source_target_pairs={{0,2},{1,3},{2,0},{3,1},{4,6},{5,7},{6,4},{7,5},{8,10},{9,11},{10,... | collective-permute-start | bytes 1769480 | tf_op jit(solution)/shard_map/ppermute | solution.py:387
  71.3 16.2 %collective-permute-start.7 = (bf16[4,64,1152]{2,1,0:T(8,128)(2,1)S(1)}, bf16[4,64,1152]{2,1,0:T(8,128)(2,1)S(1)}, u32[]{:S(2)}, u32[]{:S(2)}) collective-permute-start(bf16[4,64,1152]{2,1,0:T(8,128)(2,1)S(1)} %copy-done.17), channel_id=1, source_target_pairs={{0,1},{1,0},{2,3},{3,2},{4,5},{5,4},{6,7},{7,6},{8,9},{9,8},{10,11... | collective-permute-start | bytes 1769480 | tf_op jit(solution)/shard_map/ppermute | solution.py:387
  72.8 27.3 %collective-permute-start.6 = (bf16[4,64,1152]{2,1,0:T(8,128)(2,1)S(1)}, bf16[4,64,1152]{2,1,0:T(8,128)(2,1)S(1)}, u32[]{:S(2)}, u32[]{:S(2)}) collective-permute-start(bf16[4,64,1152]{2,1,0:T(8,128)(2,1)S(1)} %copy-done.16), channel_id=1, source_target_pairs={{0,1},{1,0},{2,3},{3,2},{4,5},{5,4},{6,7},{7,6},{8,9},{9,8},{10,11... | collective-permute-start | bytes 1769480 | tf_op jit(solution)/shard_map/ppermute | solution.py:387
  73.3 26.4 %collective-permute-start.11 = (bf16[4,64,1152]{2,1,0:T(8,128)(2,1)S(1)}, bf16[4,64,1152]{2,1,0:T(8,128)(2,1)S(1)}, u32[]{:S(2)}, u32[]{:S(2)}) collective-permute-start(bf16[4,64,1152]{2,1,0:T(8,128)(2,1)S(1)} %copy-done.27), channel_id=1, source_target_pairs={{0,2},{1,3},{2,0},{3,1},{4,6},{5,7},{6,4},{7,5},{8,10},{9,11},{10,... | collective-permute-start | bytes 1769480 | tf_op jit(solution)/shard_map/ppermute | solution.py:387
  93.2 18.8 %collective-permute-start.9 = (bf16[4,64,1152]{2,1,0:T(8,128)(2,1)}, bf16[4,64,1152]{2,1,0:T(8,128)(2,1)S(1)}, u32[]{:S(2)}, u32[]{:S(2)}) collective-permute-start(bf16[4,64,1152]{2,1,0:T(8,128)(2,1)} %get-tuple-element.49), channel_id=1, source_target_pairs={{0,1},{1,0},{2,3},{3,2},{4,5},{5,4},{6,7},{7,6},{8,9},{9,8},{10,11... | collective-permute-start | bytes 1769480 | tf_op jit(solution)/shard_map/ppermute | solution.py:387
  94.7 17.3 %collective-permute-start.10 = (bf16[4,64,1152]{2,1,0:T(8,128)(2,1)}, bf16[4,64,1152]{2,1,0:T(8,128)(2,1)S(1)}, u32[]{:S(2)}, u32[]{:S(2)}) collective-permute-start(bf16[4,64,1152]{2,1,0:T(8,128)(2,1)} %get-tuple-element.50), channel_id=1, source_target_pairs={{0,2},{1,3},{2,0},{3,1},{4,6},{5,7},{6,4},{7,5},{8,10},{9,11},{10,... | collective-permute-start | bytes 1769480 | tf_op jit(solution)/shard_map/ppermute | solution.py:387
  118.1 67.5 %all-to-all-start.1 = ((bf16[8,64,1152]{2,1,0:T(8,128)(2,1)}), bf16[8,64,1152]{2,1,0:T(8,128)(2,1)}, u32[]{:S(2)}, u32[]{:S(2)}) async-start(bf16[8,64,1152]{2,1,0:T(8,128)(2,1)} %get-tuple-element.55), calls=%async_computation.1 | async-start | bytes 2359296 | tf_op jit(solution)/shard_map/all_to_all | solution.py:393
  123.1 32.0 %collective-permute-start.15 = (bf16[2,2,144,1152]{3,2,1,0:T(8,128)(2,1)S(1)}, bf16[2,2,144,1152]{3,2,1,0:T(8,128)(2,1)S(1)}, u32[]{:S(2)}, u32[]{:S(2)}) collective-permute-start(bf16[2,2,144,1152]{3,2,1,0:T(8,128)(2,1)S(1)} %copy-done.4), channel_id=1, source_target_pairs={{0,1},{1,0},{2,3},{3,2},{4,5},{5,4},{6,7},{7,6},{8,9},{9,8},{10,11... | collective-permute-start | bytes 3981320 | tf_op jit(solution)/shard_map/ppermute | solution.py:387
  124.6 59.8 %collective-permute-start.16 = (bf16[2,2,144,1152]{3,2,1,0:T(8,128)(2,1)}, bf16[2,2,144,1152]{3,2,1,0:T(8,128)(2,1)S(1)}, u32[]{:S(2)}, u32[]{:S(2)}) collective-permute-start(bf16[2,2,144,1152]{3,2,1,0:T(8,128)(2,1)} %get-tuple-element.62), channel_id=1, source_target_pairs={{0,2},{1,3},{2,0},{3,1},{4,6},{5,7},{6,4},{7,5},{8,10},{9,11},{10,... | collective-permute-start | bytes 3981320 | tf_op jit(solution)/shard_map/ppermute | solution.py:387
  126.2 59.4 %collective-permute-start.17 = (bf16[2,2,144,1152]{3,2,1,0:T(8,128)(2,1)}, bf16[2,2,144,1152]{3,2,1,0:T(8,128)(2,1)}, u32[]{:S(2)}, u32[]{:S(2)}) collective-permute-start(bf16[2,2,144,1152]{3,2,1,0:T(8,128)(2,1)} %get-tuple-element.63), channel_id=1, source_target_pairs={{0,3},{1,2},{2,1},{3,0},{4,7},{5,6},{6,5},{7,4},{8,11},{9,10},{10,... | collective-permute-start | bytes 3981320 | tf_op jit(solution)/shard_map/ppermute | solution.py:387
  236.9 68.9 %all-to-all-start.2 = ((bf16[8,64,1152]{2,1,0:T(8,128)(2,1)}), bf16[8,64,1152]{2,1,0:T(8,128)(2,1)S(1)}, u32[]{:S(2)}, u32[]{:S(2)}) async-start(bf16[8,64,1152]{2,1,0:T(8,128)(2,1)} %get-tuple-element.65), calls=%async_computation.2 | async-start | bytes 2359296 | tf_op jit(solution)/shard_map/all_to_all | solution.py:393
  240.5 66.8 %collective-permute-start.23 = (bf16[8,80,1152]{2,1,0:T(8,128)(2,1)S(1)}, bf16[8,80,1152]{2,1,0:T(8,128)(2,1)}, u32[]{:S(2)}, u32[]{:S(2)}) collective-permute-start(bf16[8,80,1152]{2,1,0:T(8,128)(2,1)S(1)} %all_to_all.20.refs_0_), channel_id=1, source_target_pairs={{0,2},{1,3},{2,0},{3,1},{4,6},{5,7},{6,4},{7,5},{8,10},{9,11},{10,... | collective-permute-start | bytes 4423688 | tf_op jit(solution)/shard_map/ppermute | solution.py:387
  242.1 65.8 %collective-permute-start.22 = (bf16[8,80,1152]{2,1,0:T(8,128)(2,1)S(1)}, bf16[8,80,1152]{2,1,0:T(8,128)(2,1)}, u32[]{:S(2)}, u32[]{:S(2)}) collective-permute-start(bf16[8,80,1152]{2,1,0:T(8,128)(2,1)S(1)} %all_to_all.20.refs_0_), channel_id=1, source_target_pairs={{0,1},{1,0},{2,3},{3,2},{4,5},{5,4},{6,7},{7,6},{8,9},{9,8},{10,11... | collective-permute-start | bytes 4423688 | tf_op jit(solution)/shard_map/ppermute | solution.py:387
  253.3 38.1 %collective-permute-start.12 = (bf16[1,2,144,1152]{3,2,1,0:T(8,128)(2,1)}, bf16[1,2,144,1152]{3,2,1,0:T(8,128)(2,1)S(1)}, u32[]{:S(2)}, u32[]{:S(2)}) collective-permute-start(bf16[1,2,144,1152]{3,2,1,0:T(8,128)(2,1)} %get-tuple-element.57), channel_id=1, source_target_pairs={{0,1},{1,0},{2,3},{3,2},{4,5},{5,4},{6,7},{7,6},{8,9},{9,8},{10,11... | collective-permute-start | bytes 1990664 | tf_op jit(solution)/shard_map/ppermute | solution.py:387
  254.9 37.1 %collective-permute-start.13 = (bf16[1,2,144,1152]{3,2,1,0:T(8,128)(2,1)}, bf16[1,2,144,1152]{3,2,1,0:T(8,128)(2,1)S(1)}, u32[]{:S(2)}, u32[]{:S(2)}) collective-permute-start(bf16[1,2,144,1152]{3,2,1,0:T(8,128)(2,1)} %get-tuple-element.58), channel_id=1, source_target_pairs={{0,2},{1,3},{2,0},{3,1},{4,6},{5,7},{6,4},{7,5},{8,10},{9,11},{10,... | collective-permute-start | bytes 1990664 | tf_op jit(solution)/shard_map/ppermute | solution.py:387
  255.4 50.4 %collective-permute-start.14 = (bf16[1,2,144,1152]{3,2,1,0:T(8,128)(2,1)}, bf16[1,2,144,1152]{3,2,1,0:T(8,128)(2,1)}, u32[]{:S(2)}, u32[]{:S(2)}) collective-permute-start(bf16[1,2,144,1152]{3,2,1,0:T(8,128)(2,1)} %get-tuple-element.59), channel_id=1, source_target_pairs={{0,3},{1,2},{2,1},{3,0},{4,7},{5,6},{6,5},{7,4},{8,11},{9,10},{10,... | collective-permute-start | bytes 1990664 | tf_op jit(solution)/shard_map/ppermute | solution.py:387
  291.5 74.0 %collective-permute-start.26 = (bf16[2,2,144,1152]{3,2,1,0:T(8,128)(2,1)}, bf16[2,2,144,1152]{3,2,1,0:T(8,128)(2,1)}, u32[]{:S(2)}, u32[]{:S(2)}) collective-permute-start(bf16[2,2,144,1152]{3,2,1,0:T(8,128)(2,1)} %get-tuple-element.68), channel_id=1, source_target_pairs={{0,1},{1,0},{2,3},{3,2},{4,5},{5,4},{6,7},{7,6},{8,9},{9,8},{10,11... | collective-permute-start | bytes 3981320 | tf_op jit(solution)/shard_map/ppermute | solution.py:387
  292.0 74.9 %collective-permute-start.27 = (bf16[2,2,144,1152]{3,2,1,0:T(8,128)(2,1)}, bf16[2,2,144,1152]{3,2,1,0:T(8,128)(2,1)}, u32[]{:S(2)}, u32[]{:S(2)}) collective-permute-start(bf16[2,2,144,1152]{3,2,1,0:T(8,128)(2,1)} %get-tuple-element.69), channel_id=1, source_target_pairs={{0,2},{1,3},{2,0},{3,1},{4,6},{5,7},{6,4},{7,5},{8,10},{9,11},{10,... | collective-permute-start | bytes 3981320 | tf_op jit(solution)/shard_map/ppermute | solution.py:387
  305.8 53.6 %collective-permute-start.19 = (bf16[8,64,1152]{2,1,0:T(8,128)(2,1)S(1)}, bf16[8,64,1152]{2,1,0:T(8,128)(2,1)}, u32[]{:S(2)}, u32[]{:S(2)}) collective-permute-start(bf16[8,64,1152]{2,1,0:T(8,128)(2,1)S(1)} %all-to-all-done.2.refs_0_), channel_id=1, source_target_pairs={{0,2},{1,3},{2,0},{3,1},{4,6},{5,7},{6,4},{7,5},{8,10},{9,11},{10,... | collective-permute-start | bytes 3538952 | tf_op jit(solution)/shard_map/ppermute | solution.py:387
  307.3 52.2 %collective-permute-start.18 = (bf16[8,64,1152]{2,1,0:T(8,128)(2,1)S(1)}, bf16[8,64,1152]{2,1,0:T(8,128)(2,1)}, u32[]{:S(2)}, u32[]{:S(2)}) collective-permute-start(bf16[8,64,1152]{2,1,0:T(8,128)(2,1)S(1)} %all-to-all-done.2.refs_0_), channel_id=1, source_target_pairs={{0,1},{1,0},{2,3},{3,2},{4,5},{5,4},{6,7},{7,6},{8,9},{9,8},{10,11... | collective-permute-start | bytes 3538952 | tf_op jit(solution)/shard_map/ppermute | solution.py:387
  307.8 167.9 %collective-permute-start.28 = (bf16[2,2,144,1152]{3,2,1,0:T(8,128)(2,1)}, bf16[2,2,144,1152]{3,2,1,0:T(8,128)(2,1)S(1)}, u32[]{:S(2)}, u32[]{:S(2)}) collective-permute-start(bf16[2,2,144,1152]{3,2,1,0:T(8,128)(2,1)} %get-tuple-element.70), channel_id=1, source_target_pairs={{0,3},{1,2},{2,1},{3,0},{4,7},{5,6},{6,5},{7,4},{8,11},{9,10},{10,... | collective-permute-start | bytes 3981320 | tf_op jit(solution)/shard_map/ppermute | solution.py:387
  359.4 131.0 %collective-permute-start.25 = (bf16[4,80,1152]{2,1,0:T(8,128)(2,1)}, bf16[4,80,1152]{2,1,0:T(8,128)(2,1)S(1)}, u32[]{:S(2)}, u32[]{:S(2)}) collective-permute-start(bf16[4,80,1152]{2,1,0:T(8,128)(2,1)} %slice.37), channel_id=1, source_target_pairs={{0,1},{1,0},{2,3},{3,2},{4,5},{5,4},{6,7},{7,6},{8,9},{9,8},{10,11... | collective-permute-start | bytes 2211848 | tf_op jit(solution)/shard_map/ppermute | solution.py:387
  359.5 130.9 %collective-permute-start.24 = (bf16[4,80,1152]{2,1,0:T(8,128)(2,1)}, bf16[4,80,1152]{2,1,0:T(8,128)(2,1)S(1)}, u32[]{:S(2)}, u32[]{:S(2)}) collective-permute-start(bf16[4,80,1152]{2,1,0:T(8,128)(2,1)} %slice.36), channel_id=1, source_target_pairs={{0,2},{1,3},{2,0},{3,1},{4,6},{5,7},{6,4},{7,5},{8,10},{9,11},{10,... | collective-permute-start | bytes 2211848 | tf_op jit(solution)/shard_map/ppermute | solution.py:387
  365.4 132.7 %collective-permute-start.21 = (bf16[4,64,1152]{2,1,0:T(8,128)(2,1)}, bf16[4,64,1152]{2,1,0:T(8,128)(2,1)S(1)}, u32[]{:S(2)}, u32[]{:S(2)}) collective-permute-start(bf16[4,64,1152]{2,1,0:T(8,128)(2,1)} %slice.35), channel_id=1, source_target_pairs={{0,1},{1,0},{2,3},{3,2},{4,5},{5,4},{6,7},{7,6},{8,9},{9,8},{10,11... | collective-permute-start | bytes 1769480 | tf_op jit(solution)/shard_map/ppermute | solution.py:387
  366.9 131.2 %collective-permute-start.20 = (bf16[4,64,1152]{2,1,0:T(8,128)(2,1)}, bf16[4,64,1152]{2,1,0:T(8,128)(2,1)}, u32[]{:S(2)}, u32[]{:S(2)}) collective-permute-start(bf16[4,64,1152]{2,1,0:T(8,128)(2,1)} %slice.34), channel_id=1, source_target_pairs={{0,2},{1,3},{2,0},{3,1},{4,6},{5,7},{6,4},{7,5},{8,10},{9,11},{10,... | collective-permute-start | bytes 1769480 | tf_op jit(solution)/shard_map/ppermute | solution.py:387
  (28 other events, 283.7 us)

commit v3 on v2

--- a/solution.py
+++ b/solution.py
@@ -10,7 +10,7 @@
 B = 576
 LANES = 128
 WINDOW = -(-B // LANES) * LANES
-VMEM = 56 * 1024 * 1024
+VMEM = 64 * 1024 * 1024 - 4096
 ANY = pl.BlockSpec(memory_space=pl.ANY)
 WHOLE = pl.BlockSpec(memory_space=pltpu.VMEM)
 SCALARS = pl.BlockSpec(memory_space=pltpu.SMEM)
@@ -143,8 +143,7 @@
 
 def gram_body(n, rd, n_chunks, js, *refs):
     chunks, refs = refs[:n_chunks], refs[n_chunks:]
-    rows_out, grams_out = refs[:n], refs[n : 2 * n]
-    g16, g32, l32, r32 = refs[2 * n :]
+    outs, (g16, g32, l32, r32) = refs[:n], refs[n:]
     for q in range(2):
         assemble(chunks, q, g16)
         g = g16[...]
@@ -153,9 +152,9 @@
         r32[...] = dot(g, g, ((0,), (0,)))
         lanes = slice(q * B, q * B + B)
         for k in range(n):
-            for full, out, kind in ((g32, rows_out, 0), (l32, grams_out, 0), (r32, grams_out, 1)):
+            for kind, full in enumerate((g32, l32, r32)):
                 parts = [full[own_rows(js[k], h, rd), :] for h in range(2)]
-                out[k][kind, 0, :, lanes] = jnp.concatenate(parts, axis=0).astype(jnp.bfloat16)
+                outs[k][kind, 0, :, lanes] = jnp.concatenate(parts, axis=0).astype(jnp.bfloat16)
 
 
 def gram(js, chunks, rd):
@@ -163,14 +162,7 @@
     count, _, w = chunks[0].shape
     pairs, rows = count // 4, 2 * rd
 
-    def outs(kinds):
-        return (
-            [pl.BlockSpec((kinds, 1, rows, w), lambda p, j: (0, p, 0, 0))] * n,
-            [jax.ShapeDtypeStruct((kinds, pairs, rows, w), jnp.bfloat16)] * n,
-        )
-
-    (rows_specs, rows_shapes), (gram_specs, gram_shapes) = outs(1), outs(2)
-    out = pl.pallas_call(
+    return pl.pallas_call(
         functools.partial(gram_body, n, rd, len(chunks)),
         grid_spec=pltpu.PrefetchScalarGridSpec(
             num_scalar_prefetch=1,
@@ -178,18 +170,18 @@
             in_specs=[
                 pl.BlockSpec((4,) + chunk.shape[1:], lambda p, j: (p, 0, 0)) for chunk in chunks
             ],
-            out_specs=rows_specs + gram_specs,
+            out_specs=[pl.BlockSpec((3, 1, rows, w), lambda p, j: (0, p, 0, 0))] * n,
             scratch_shapes=[pltpu.VMEM((B, B), jnp.bfloat16)] + [pltpu.VMEM((B, B), jnp.float32)] * 3,
         ),
-        out_shape=rows_shapes + gram_shapes,
+        out_shape=[jax.ShapeDtypeStruct((3, pairs, rows, w), jnp.bfloat16)] * n,
         compiler_params=params(),
         cost_estimate=cost(pairs * 8 * B**3, pairs * B * B * 2 * 8),
     )(js, *chunks)
-    return out[:n], out[n:]
-
-
-def direct_body(n, rd, n_chunks, js, *refs):
-    chunks, roots, refs = refs[:n_chunks], refs[n_chunks : n_chunks + n], refs[n_chunks + n :]
+
+
+def direct_body(n, rd, n_chunks, n_after, js, *refs):
+    chunks, roots = refs[:n_chunks], refs[n_chunks : n_chunks + n]
+    refs = refs[n_chunks + n + n_after :]
     outs, square_out = refs[:n_chunks], refs[n_chunks]
     g16, l32, r32 = refs[n_chunks + 1 :]
     for q in range(2):
@@ -213,18 +205,19 @@
             base += 2 * size
 
 
-def direct(js, chunks, roots, rd):
+def direct(js, chunks, roots, rd, after):
     n = js.shape[0]
     count, _, w = chunks[0].shape
     pairs, rows = roots[0].shape[1], roots[0].shape[2]
     chunk_specs = [pl.BlockSpec((4,) + chunk.shape[1:], lambda p, j: (p, 0, 0)) for chunk in chunks]
     return pl.pallas_call(
-        functools.partial(direct_body, n, rd, len(chunks)),
+        functools.partial(direct_body, n, rd, len(chunks), len(after)),
         grid_spec=pltpu.PrefetchScalarGridSpec(
             num_scalar_prefetch=1,
             grid=(pairs,),
             in_specs=chunk_specs
-            + [pl.BlockSpec((2, 1, rows, w), lambda p, j: (0, p, 0, 0))] * n,
+            + [pl.BlockSpec((2, 1, rows, w), lambda p, j: (0, p, 0, 0))] * n
+            + [ANY] * len(after),
             out_specs=chunk_specs + [pl.BlockSpec((1, 8, LANES), lambda p, j: (p, 0, 0))],
             scratch_shapes=[pltpu.VMEM((B, B), jnp.bfloat16)] + [pltpu.VMEM((B, B), jnp.float32)] * 2,
         ),
@@ -232,49 +225,37 @@
         + [jax.ShapeDtypeStruct((pairs, 8, LANES), jnp.float32)],
         compiler_params=params(),
         cost_estimate=cost(pairs * 8 * B**3, pairs * B * B * 2 * 8),
-    )(js, *chunks, *roots)
-
-
-def moment_body(n, js, *refs):
-    received, (moment, moment_out, square_out) = refs[:n], refs[n:]
+    )(js, *chunks, *roots, *after)
+
+
+def statistics_body(n, js, *refs):
+    received = refs[:n]
+    left, right, moment, left_out, right_out, moment_out, square_out = refs[n:]
     m = pl.program_id(0)
     for k in range(n):
 
         @pl.when(m == k)
         def _():
             for q in range(2):
-                g = received[k][0, 0, :, q * B : q * B + B].astype(jnp.float32)
+                lanes = slice(q * B, q * B + B)
+                g, left_gram, right_gram = (
+                    received[k][kind, 0, :, lanes].astype(jnp.float32) for kind in range(3)
+                )
+                left_out[q, 0] = 0.95 * left[q, 0] + 0.05 * left_gram
+                right_out[q, 0] = 0.95 * right[q, 0] + 0.05 * right_gram
                 second = 0.95 * moment[q, 0] + 0.05 * g * g
                 moment_out[q, 0] = second
                 adam = g / (jnp.sqrt(second) + 1e-08)
                 square_out[0, 0, q : q + 1, :] = jnp.full((1, LANES), jnp.sum(adam * adam))
 
 
-def statistics_body(n, js, *refs):
-    received, (left, right, left_out, right_out) = refs[:n], refs[n:]
-    m = pl.program_id(0)
-    for k in range(n):
-
-        @pl.when(m == k)
-        def _():
-            for q in range(2):
-                for kind, old, new in ((0, left, left_out), (1, right, right_out)):
-                    product = received[k][kind, 0, :, q * B : q * B + B].astype(jnp.float32)
-                    new[q, 0] = 0.95 * old[q, 0] + 0.05 * product
-
-
-def by_rows(body, js, received, olds, squares):
+def statistics(js, received, olds):
     n = js.shape[0]
     blocks, _, rows, _ = olds[0].shape
     kinds, pairs, _, w = received[0].shape
     own = pl.BlockSpec((2, 1, rows, B), lambda m, p, j: (p, j[m], 0, 0))
-    out_specs = [own] * len(olds)
-    out_shape = [jax.ShapeDtypeStruct(old.shape, jnp.float32) for old in olds]
-    if squares:
-        out_specs.append(pl.BlockSpec((1, 1, 8, LANES), lambda m, p, j: (m, p, 0, 0)))
-        out_shape.append(jax.ShapeDtypeStruct((n, pairs, 8, LANES), jnp.float32))
-    return pl.pallas_call(
-        functools.partial(body, n),
+    return pl.pallas_call(
+        functools.partial(statistics_body, n),
         grid_spec=pltpu.PrefetchScalarGridSpec(
             num_scalar_prefetch=1,
             grid=(n, pairs),
@@ -286,33 +267,28 @@
                 for k in range(n)
             ]
             + [own] * len(olds),
-            out_specs=out_specs,
+            out_specs=[own] * len(olds)
+            + [pl.BlockSpec((1, 1, 8, LANES), lambda m, p, j: (m, p, 0, 0))],
         ),
-        out_shape=out_shape,
+        out_shape=[jax.ShapeDtypeStruct(old.shape, jnp.float32) for old in olds]
+        + [jax.ShapeDtypeStruct((n, pairs, 8, LANES), jnp.float32)],
         compiler_params=params(),
         cost_estimate=cost(0, olds[0].size * 10 * len(olds)),
     )(js, *received, *olds)
 
 
-def restore_body(n_src, n_old, base, src, item, scale, *refs):
-    sources = refs[:n_src]
-    out, buffer, result, in_sems, out_sems = refs[n_src + n_old :]
+def restore_body(item, scale, source, out, buffer, result, in_sems, out_sems):
     columns, n, w = buffer.shape
     slots = result.shape[0]
 
     def fetch(c, _):
-        for k in range(n_src):
-
-            @pl.when(src[c] == k)
-            def _():
-                pltpu.make_async_copy(sources[k].at[item[c]], buffer.at[c], in_sems.at[c]).start()
-
+        pltpu.make_async_copy(source.at[item[c]], buffer.at[c], in_sems.at[c]).start()
         return 0
 
     def store(p, slot):
         start = pl.multiple_of(p * w, LANES)
         return pltpu.make_async_copy(
-            result.at[slot], out.at[pl.ds(base, 2 * n), pl.ds(start, w)], out_sems.at[slot]
+            result.at[slot], out.at[:, pl.ds(start, w)], out_sems.at[slot]
         )
 
     def step(p, _):
@@ -324,7 +300,7 @@
 
         for e in range(2):
             c = 2 * p + e
-            pltpu.make_async_copy(sources[0].at[0], buffer.at[c], in_sems.at[c]).wait()
+            pltpu.make_async_copy(source.at[item[c]], buffer.at[c], in_sems.at[c]).wait()
             scaled = (buffer[c].astype(jnp.float32) * scale[c]).astype(result.dtype)
             result[slot, :n, e * B : e * B + B] = scaled[:, :B]
             result[slot, n:, e * B : e * B + B] = scaled[:, B:]
@@ -338,25 +314,35 @@
         store(p, p % slots).wait()
 
 
-def restore(src, item, scale, sources, base, rows, old):
-    _, n, w = sources[0].shape
-    columns = src.shape[0]
+def restore(item, scale, source):
+    columns, n, w = source.shape
     slots = 4
     return pl.pallas_call(
-        functools.partial(restore_body, len(sources), len(old), base),
-        in_specs=[SCALARS] * 3 + [ANY] * (len(sources) + len(old)),
+        restore_body,
+        in_specs=[SCALARS, SCALARS, ANY],
         out_specs=ANY,
-        out_shape=jax.ShapeDtypeStruct((rows, columns * B), jnp.bfloat16),
+        out_shape=jax.ShapeDtypeStruct((2 * n, columns * B), jnp.bfloat16),
         scratch_shapes=[
             pltpu.VMEM((columns, n, w), jnp.bfloat16),
             pltpu.VMEM((slots, 2 * n, w), jnp.bfloat16),
             pltpu.SemaphoreType.DMA((columns,)),
             pltpu.SemaphoreType.DMA((slots,)),
         ],
-        input_output_aliases={3 + len(sources): 0} if old else {},
         compiler_params=params(),
         cost_estimate=cost(0, columns * n * w * 4),
-    )(src, item, scale, *sources, *old)
+    )(item, scale, source)
+
+
+def hold(arrays):
+    return pl.pallas_call(
+        lambda *refs: None,
+        in_specs=[ANY] * len(arrays),
+        out_specs=[ANY] * len(arrays),
+        out_shape=[jax.ShapeDtypeStruct(x.shape, x.dtype) for x in arrays],
+        input_output_aliases={k: k for k in range(len(arrays))},
+        compiler_params=params(),
+        cost_estimate=cost(0, 0),
+    )(*arrays)
 
 
 def owner_local(grads, slots, stats_left, stats_right, root_left, root_right, second_moment):
@@ -392,49 +378,26 @@
     def exchange(x):
         return lax.all_to_all(x, "fsdp", split_axis=0, concat_axis=0, tiled=True)
 
-    first = -(-rows // 64) * 16
-    chunks = ((0, first), (2 * first, rows // 2 - first))
-
-    def start_sum(base, n, after):
-        far_a, far_b = arrange(far, grad, base, n, after=after)
-        by_far = (swap(far_a, 1), swap(far_b, 2))
-        x_a, y_b = arrange(near, grad, base, n, after=(far_a,))
-        return by_far, (swap(x_a, 1), swap(y_b, 2)), x_a
-
-    def end_sum(base, n, by_far, after):
-        y_a, x_b = arrange(cross, grad, base, n, (by_far,), after=after)
-        return (swap(y_a, 2), swap(x_b, 1)), y_a
-
-    by_far, by_near, sent = start_sum(*chunks[0], ())
-    roots = list(pack_roots(js, as_rows(root_left), as_rows(root_right), (sent,)))
-    by_cross, sent = end_sum(*chunks[0], by_far, (roots[0],))
-    by_far_1, by_near_1, sent = start_sum(*chunks[1], (sent,))
-    terms = ((by_near[0], by_cross[1]), (by_cross[0], by_near[1]))
-    (owned,) = arrange(own, grad, *chunks[0], terms, halves=False, after=(sent,))
-    by_cross_1, sent = end_sum(*chunks[1], by_far_1, (owned,))
-    blocks = [exchange(owned)]
-    terms = ((by_near_1[0], by_cross_1[1]), (by_cross_1[0], by_near_1[1]))
-    owned, *roots[1:] = arrange(
-        own, grad, *chunks[1], terms, halves=False, through=tuple(roots[1:])
-    )
-    blocks.append(exchange(owned))
-    roots = [roots[0]] + [swap(roots[k], k) for k in (3, 1, 2)]
-    roots = [roots[0], roots[2], roots[3], roots[1]]
-
-    grad_rows, grams = gram(js, blocks, rd)
-    grad_rows = [grad_rows[0]] + [swap(grad_rows[k], k) for k in (1, 2, 3)]
-    grams = [grams[0]] + [swap(grams[k], k) for k in (1, 2, 3)]
-    *directions, direction_square = direct(js, blocks, roots, rd)
-
-    gathered = []
-    for direction in directions:
-        mine = exchange(direction)
-        x, y = swap(mine, 1), swap(mine, 2)
-        gathered.append((mine, x, y, swap(x[:half], 2), swap(y[half:], 1)))
-
-    moment, adam_square = by_rows(moment_body, js, grad_rows, [as_rows(second_moment)], True)
-    left_new, right_new = by_rows(
-        statistics_body, js, grams, [as_rows(stats_left), as_rows(stats_right)], False
+    n = rows // 2
+    far_a, far_b = arrange(far, grad, 0, n)
+    by_far = (swap(far_a, 1), swap(far_b, 2))
+    x_a, y_b = arrange(near, grad, 0, n, after=(far_a,))
+    from_x_a, from_y_b = swap(x_a, 1), swap(y_b, 2)
+    roots = pack_roots(js, as_rows(root_left), as_rows(root_right), (x_a,))
+    y_a, x_b = arrange(cross, grad, 0, n, (by_far,), after=(roots[0],))
+    terms = ((from_x_a, swap(x_b, 1)), (swap(y_a, 2), from_y_b))
+    owned, *sent = arrange(own, grad, 0, n, terms, halves=False, through=tuple(roots[1:]))
+    blocks = exchange(owned)
+    roots = [roots[0]] + [swap(x, k) for k, x in zip((1, 2, 3), sent)]
+
+    products = gram(js, [blocks], rd)
+    received = [products[0]] + [swap(products[k], k) for k in (1, 2, 3)]
+    direction, direction_square = direct(js, [blocks], roots, rd, (products[0],))
+    returned, *received[1:] = hold((exchange(direction), *received[1:]))
+    gathered = lax.all_gather(returned, "replica").reshape(columns, n, 2 * B)
+
+    left_new, right_new, moment, adam_square = statistics(
+        js, received, [as_rows(x) for x in (stats_left, stats_right, second_moment)]
     )
 
     adam_square = adam_square[:, :, :2, 0].reshape(replicas, row_blocks)
@@ -442,27 +405,21 @@
     adam_square = jnp.sum(
         jnp.where((js[:, None] == slot_ids)[:, :, None], adam_square[:, None, :], 0.0), axis=0
     )
-    squares = jnp.concatenate([adam_square, direction_square[:, :2, 0].reshape(1, row_blocks)])
-    squares = lax.all_gather(squares, ("fsdp", "replica")).reshape(
-        owners, replicas, replicas + 1, row_blocks
-    )
-    ratio = jnp.sqrt(jnp.sum(squares[:, :, :replicas], axis=1)) / jnp.sqrt(
-        squares[:, :, replicas] + 1e-06
-    )
+    direction_square = direction_square[:, :2, 0].reshape(row_blocks)
+    owner_place = jnp.arange(owners, dtype=jnp.int32)[:, None, None, None] == f
+    slot_place = (slot_ids == r)[:, None]
+    squares = jnp.stack([adam_square, jnp.where(slot_place, direction_square, 0.0)])
+    squares = lax.psum(jnp.where(owner_place, squares, 0.0), ("fsdp", "replica"))
+    ratio = jnp.sqrt(squares[:, 0]) / jnp.sqrt(squares[:, 1] + 1e-06)
     row_ratio = lax.dynamic_index_in_dim(
         ratio.reshape(columns, row_blocks), f // sub_count, 1, keepdims=False
     )
     scale = jnp.sum(jnp.where(row_slots[:, None] == column_ids, row_ratio, 0.0), axis=1)
 
-    owner = row_slots // replicas
-    step = lax.rem(row_slots, replicas) ^ r
-    src = step + jnp.where(step == 3, owner // half, 0)
-    item = jnp.where(step == 3, lax.rem(owner, half), owner)
-    update = ()
-    for (base, _), sources in zip(chunks, gathered):
-        update = (restore(src, item, scale, sources, base, rows, update),)
+    item = lax.rem(row_slots, replicas) * owners + row_slots // replicas
+    update = restore(item, scale, gathered)
     return (
-        update[0],
+        update,
         left_new.reshape(stats_left.shape),
         right_new.reshape(stats_right.shape),
         moment.reshape(second_moment.shape),

time: 507 us -> 419 us (0.83)
  blocking collectives: 147 us -> 39.8 us
  waiting for transfers between devices: 184 us -> 248 us
  Pallas kernels: 103 us -> 81.9 us
  starting transfers between devices: 44.8 us -> 23.8 us
  local copies, waits for them, and re-layouts: 21 us -> 2.61 us
  between operations: 1.19 us -> 14.2 us
    all_gather x1 -> x0, blocking collectives: 107 us -> none  [owner_local(): lax.all_gather(squares, ('fsdp', 'replica'))]
    all_to_all x3 -> x2, waiting for transfers between devices: 0.01 us -> 57.6 us  [exchange(): return lax.all_to_all(x, 'fsdp', split_axis=0, concat_axis=0, tiled=True)]
    all_to_all x1 -> x0, blocking collectives: 40.5 us -> none  [exchange(): return lax.all_to_all(x, 'fsdp', split_axis=0, concat_axis=0, tiled=True)]
    all_gather x0 -> x1, waiting for transfers between devices: none -> 40 us  [owner_local(): gathered = lax.all_gather(returned, 'replica').reshape(columns, n, 2 * B)]
    psum x0 -> x1, blocking collectives: none -> 39.8 us  [owner_local(): lax.psum(jnp.where(owner_place, squares, 0.0), ('fsdp', 'replica'))]
    ppermute x29 -> x12, waiting for transfers between devices: 184 us -> 150 us  [swap(): return lax.ppermute(x, 'replica', [(i, i ^ k) for i in range(replicas)])]
    ppermute x29 -> x12, starting transfers between devices: 31.2 us -> 14.3 us  [swap(): return lax.ppermute(x, 'replica', [(i, i ^ k) for i in range(replicas)])]
    pallas_call x8 -> x4, Pallas kernels: 33.9 us -> 21.8 us  [arrange(): pl.pallas_call(functools.partial(arrange_body, len(adds), len(after), len...]
  transfers between devices with their start and end apart: 32 -> 15, of which waited for: 15 -> 9; matrix products, arithmetic and copies ran while one was open for 3% -> 2% of each run, Pallas kernels for 15% -> 12%
where the time goes in v3:
time: 419 us; the launch traced here: 418 us
  waiting for transfers between devices  248 us (59%)
  Pallas kernels  81.9 us (20%)
  blocking collectives  39.8 us (9%)
  starting transfers between devices  23.8 us (6%)
  between operations  14.2 us (3%)
  other arithmetic  7.93 us (2%)
    ppermute x12, waiting for transfers between devices, swap(): return lax.ppermute(x, 'replica', [(i, i ^ k) for i in range(replicas)])  150 us
    all_to_all x2, waiting for transfers between devices, exchange(): return lax.all_to_all(x, 'fsdp', split_axis=0, concat_axis=0, tiled=True)  57.6 us
    all_gather x1, waiting for transfers between devices, owner_local(): gathered = lax.all_gather(returned, 'replica').reshape(columns, n, 2 * B)  40 us
    psum x1, blocking collectives, owner_local(): lax.psum(jnp.where(owner_place, squares, 0.0), ('fsdp', 'replica'))  39.8 us
    pallas_call x4, Pallas kernels, arrange(): pl.pallas_call(functools.partial(arrange_body, len(adds), len(after), len...  21.8 us
    pallas_call x1, Pallas kernels, statistics(): pl.pallas_call(functools.partial(statistics_body, n), grid_spec=pltpu.Pre...  20.4 us
    ppermute x12, starting transfers between devices, swap(): return lax.ppermute(x, 'replica', [(i, i ^ k) for i in range(replicas)])  14.3 us
    pallas_call x1, Pallas kernels, direct(): pl.pallas_call(functools.partial(direct_body, n, rd, len(chunks), len(aft...  11 us
  transfers between devices with their start and end apart: 15, of which 9 were waited for; matrix products, arithmetic and copies ran while one was open for 2% of the time, Pallas kernels for 12%

profile of v3, /device:TPU:0, one launch (start us, length us, event | category | flops | bytes accessed | tf_op | source)
XLA Modules:
  0.0 417.7 jit_solution(15782942058510433117)
XLA Ops:
  7.2 1.3 multiply_add_fusion
  9.0 0.8 select_reduce_fusion.2
  9.8 4.3 %shard_map.102 = (bf16[4,144,1152]{2,1,0:T(8,128)(2,1)}, bf16[4,144,1152]{2,1,0:T(8,128)(2,1)}) custom-call(s32[8]{0:T(128)} %get-tuple-element.79.cols, bf16[288,18432]{1,0:T(8,128)(2,1)} %bitcast.26), custom_call_target="tpu_custom_call" | custom-call | bytes 5308416 | tf_op jit(solution)/shard_map/pallas_call | solution.py:68
  14.1 3.0 collective-permute-start.2
  17.1 1.5 collective-permute-start.1
  18.6 4.3 %shard_map.103 = (bf16[4,144,1152]{2,1,0:T(8,128)(2,1)}, bf16[4,144,1152]{2,1,0:T(8,128)(2,1)}) custom-call(s32[8]{0:T(128)} %get-tuple-element.78.cols, bf16[288,18432]{1,0:T(8,128)(2,1)} %bitcast.27, bf16[4,144,1152]{2,1,0:T(8,128)(2,1)} %get-tuple-element.32.refs_0_), custom_call_target="tpu_custom_call" | custom-call | bytes 5308416 | tf_op jit(solution)/shard_map/pallas_call | solution.py:68
  24.2 9.0 %shard_map.104 = (bf16[2,2,144,1152]{3,2,1,0:T(8,128)(2,1)}, bf16[2,2,144,1152]{3,2,1,0:T(8,128)(2,1)}, bf16[2,2,144,1152]{3,2,1,0:T(8,128)(2,1)}, bf16[2,2,144,1152]{3,2,1,0:T(8,128)(2,1)}) custom-call(s32[4]{0:T(128)} %iota_xor_fusion.js, bf16[4,4,144,576]{3,2,1,0:T(8,128)(2,1)} %bitcast.33, bf16[4,4,144,576]{3,2,1,0:T(8,128)(2,1)} %bitcast.34, ...), custom_call_target="tpu_custom_call" | custom-call | bytes 10616832 | tf_op jit(solution)/shard_map/pallas_call | solution.py:105
  33.2 14.2 %collective-permute-done.2.refs_1_ = bf16[4,144,1152]{2,1,0:T(8,128)(2,1)} collective-permute-done((bf16[4,144,1152]{2,1,0:T(8,128)(2,1)}, bf16[4,144,1152]{2,1,0:T(8,128)(2,1)}, u32[]{:S(2)}, u32[]{:S(2)}) %collective-permute-start.2) | collective-permute-done | bytes 1327136 | tf_op jit(solution)/shard_map/ppermute | solution.py:373
  47.4 2.1 collective-permute-done.1.refs_0_
  49.5 6.0 %shard_map.105 = (bf16[4,144,1152]{2,1,0:T(8,128)(2,1)}, bf16[4,144,1152]{2,1,0:T(8,128)(2,1)}) custom-call(s32[8]{0:T(128)} %get-tuple-element.76.cols, bf16[288,18432]{1,0:T(8,128)(2,1)} %bitcast.28, bf16[4,144,1152]{2,1,0:T(8,128)(2,1)} %collective-permute-done.1.refs_0_, bf16[4,144,1152]{2,1,0:T(8,128)(2,1)} %collective-permute-done.2.refs_1_, ...), custom_call_target="tpu_custom_call" | custom-call | bytes 7962624 | tf_op jit(solution)/shard_map/pallas_call | solution.py:68
  55.5 1.5 collective-permute-start.3
  57.5 18.3 %collective-permute-done.5.refs_3_ = bf16[4,144,1152]{2,1,0:T(8,128)(2,1)} collective-permute-done((bf16[4,144,1152]{2,1,0:T(8,128)(2,1)}, bf16[4,144,1152]{2,1,0:T(8,128)(2,1)}, u32[]{:S(2)}, u32[]{:S(2)}) %collective-permute-start.5) | collective-permute-done | bytes 1327136 | tf_op jit(solution)/shard_map/ppermute | solution.py:373
  75.9 2.1 collective-permute-done.refs_0_
  77.9 27.0 %collective-permute-done.3.refs_1_ = bf16[4,144,1152]{2,1,0:T(8,128)(2,1)} collective-permute-done((bf16[4,144,1152]{2,1,0:T(8,128)(2,1)}, bf16[4,144,1152]{2,1,0:T(8,128)(2,1)}, u32[]{:S(2)}, u32[]{:S(2)}) %collective-permute-start.3) | collective-permute-done | bytes 1327136 | tf_op jit(solution)/shard_map/ppermute | solution.py:373
  104.9 7.2 %shard_map.106 = (bf16[8,144,1152]{2,1,0:T(8,128)(2,1)}, bf16[2,2,144,1152]{3,2,1,0:T(8,128)(2,1)}, bf16[2,2,144,1152]{3,2,1,0:T(8,128)(2,1)}, bf16[2,2,144,1152]{3,2,1,0:T(8,128)(2,1)}) custom-call(s32[8]{0:T(128)} %get-tuple-element.77.cols, bf16[288,18432]{1,0:T(8,128)(2,1)} %bitcast.29, ...), custom_call_target="tpu_custom_call", output_to_operand_aliasing={{1}: (6, {}), {2}: (7, {}), {3}: (8, {})} | custom-call | bytes 10616832 | tf_op jit(solution)/shard_map/pallas_call | solution.py:68
  112.1 4.9 %all-to-all-start = ((bf16[8,144,1152]{2,1,0:T(8,128)(2,1)}), bf16[8,144,1152]{2,1,0:T(8,128)(2,1)}, u32[]{:S(2)}, u32[]{:S(2)}) async-start(bf16[8,144,1152]{2,1,0:T(8,128)(2,1)} %get-tuple-element.42), calls=%async_computation | async-start | bytes 5308416 | tf_op jit(solution)/shard_map/all_to_all | solution.py:379
  117.0 1.5 collective-permute-start.6
  119.0 1.5 collective-permute-start.8
  120.5 57.6 %all-to-all-done.refs_0_ = bf16[8,144,1152]{2,1,0:T(8,128)(2,1)} async-done(((bf16[8,144,1152]{2,1,0:T(8,128)(2,1)}), bf16[8,144,1152]{2,1,0:T(8,128)(2,1)}, u32[]{:S(2)}, u32[]{:S(2)}) %all-to-all-start) | async-done | bytes 2654240 | tf_op jit(solution)/shard_map/all_to_all | solution.py:379
  178.1 10.8 %shard_map.107 = (bf16[3,2,144,1152]{3,2,1,0:T(8,128)(2,1)}, bf16[3,2,144,1152]{3,2,1,0:T(8,128)(2,1)}, bf16[3,2,144,1152]{3,2,1,0:T(8,128)(2,1)}, bf16[3,2,144,1152]{3,2,1,0:T(8,128)(2,1)}) custom-call(s32[4]{0:T(128)} %iota_xor_fusion.js, bf16[8,144,1152]{2,1,0:T(8,128)(2,1)} %all-to-all-done.refs_0_), custom_call_target="tpu_custom_call" | custom-call | flops 3057647616 | bytes 10616832 | tf_op jit(solution)/shard_map/pallas_call | solution.py:165
  188.9 11.0 %shard_map.108 = (bf16[8,144,1152]{2,1,0:T(8,128)(2,1)}, f32[2,8,128]{2,1,0:T(8,128)}) custom-call(s32[4]{0:T(128)} %iota_xor_fusion.js, bf16[8,144,1152]{2,1,0:T(8,128)(2,1)} %all-to-all-done.refs_0_, bf16[2,2,144,1152]{3,2,1,0:T(8,128)(2,1)} %get-tuple-element.35.refs_2_.refs_1_, bf16[2,2,144,1152]{3,2,1,0:T(8,128)(2,1)} %collective-permute-done.6.refs_2_, ...), custom_call_target="tpu_custom_call" | custom-call | flops 3057647616 | bytes 10616832 | tf_op jit(solution)/shard_map/pallas_call | solution.py:213
  200.0 4.5 %all-to-all-start.1 = ((bf16[8,144,1152]{2,1,0:T(8,128)(2,1)}), bf16[8,144,1152]{2,1,0:T(8,128)(2,1)}, u32[]{:S(2)}, u32[]{:S(2)}) async-start(bf16[8,144,1152]{2,1,0:T(8,128)(2,1)} %get-tuple-element.47), calls=%async_computation.1 | async-start | bytes 5308416 | tf_op jit(solution)/shard_map/all_to_all | solution.py:379
  204.6 1.6 collective-permute-start.9
  206.6 1.5 collective-permute-start.11
  208.1 43.0 %collective-permute-done.9.refs_1_ = bf16[3,2,144,1152]{3,2,1,0:T(8,128)(2,1)} collective-permute-done((bf16[3,2,144,1152]{3,2,1,0:T(8,128)(2,1)}, bf16[3,2,144,1152]{3,2,1,0:T(8,128)(2,1)}, u32[]{:S(2)}, u32[]{:S(2)}) %collective-permute-start.9) | collective-permute-done | bytes 1990688 | tf_op jit(solution)/shard_map/ppermute | solution.py:373
  251.2 43.2 %collective-permute-done.10.refs_2_ = bf16[3,2,144,1152]{3,2,1,0:T(8,128)(2,1)} collective-permute-done((bf16[3,2,144,1152]{3,2,1,0:T(8,128)(2,1)}, bf16[3,2,144,1152]{3,2,1,0:T(8,128)(2,1)}, u32[]{:S(2)}, u32[]{:S(2)}) %collective-permute-start.10) | collective-permute-done | bytes 1990688 | tf_op jit(solution)/shard_map/ppermute | solution.py:373
  295.7 0.8 slice_reduce_fusion
  297.2 20.4 %shard_map.110 = (f32[4,4,144,576]{3,2,1,0:T(8,128)}, f32[4,4,144,576]{3,2,1,0:T(8,128)}, f32[4,4,144,576]{3,2,1,0:T(8,128)}, f32[4,2,8,128]{3,2,1,0:T(8,128)}) custom-call(s32[4]{0:T(128)} %iota_xor_fusion.js, bf16[3,2,144,1152]{3,2,1,0:T(8,128)(2,1)} %get-tuple-element.43.refs_5_.refs_0_, bf16[3,2,144,1152]{3,2,1,0:T(8,128)(2,1)} %get-tuple-element.51.refs_1_, ...), custom_call_target="tpu_custom_call" | custom-call | bytes 39813120 | tf_op jit(solution)/shard_map/pallas_call | solution.py:257
  320.8 39.8 %psum.7 = f32[8,2,4,4]{2,0,3,1:T(8,128)S(1)} all-reduce(f32[8,2,4,4]{2,0,3,1:T(8,128)S(1)} %broadcast_select_fusion), channel_id=1, replica_groups=mesh['fsdp'=8,'replica'=4] {'fsdp','replica'}, use_global_device_ids=true, to_apply=%region_5.6 | all-reduce | flops 256 | bytes 2048 | tf_op jit(solution)/shard_map/psum | solution.py:412
  360.7 1.3 select_reduce_fusion.scale
  362.0 40.0 %all-gather.3.cloned.1.call-done.source = bf16[32,144,1152]{2,1,0:T(8,128)(2,1)} async-done(((bf16[8,144,1152]{2,1,0:T(8,128)(2,1)}), bf16[32,144,1152]{2,1,0:T(8,128)(2,1)}) %all-gather.3.cloned.1.call-update) | async-done | bytes 10616848 | tf_op jit(solution)/shard_map/all_gather | solution.py:397
  402.0 8.9 %shard_map.111 = bf16[288,18432]{1,0:T(8,128)(2,1)} custom-call(s32[32]{0:T(128)} %get-tuple-element.80.item, f32[32]{0:T(128)} %select_reduce_fusion.scale, bf16[32,144,1152]{2,1,0:T(8,128)(2,1)} %all-gather.3.cloned.1.call-done.source), custom_call_target="tpu_custom_call" | custom-call | bytes 21233664 | tf_op jit(solution)/shard_map/pallas_call | solution.py:320
  (38 shorter events, 8.6 us)
Async XLA Ops:
  8.5 0.5 copy-start.1
  14.1 33.3 %collective-permute-start.2 = (bf16[4,144,1152]{2,1,0:T(8,128)(2,1)}, bf16[4,144,1152]{2,1,0:T(8,128)(2,1)}, u32[]{:S(2)}, u32[]{:S(2)}) collective-permute-start(bf16[4,144,1152]{2,1,0:T(8,128)(2,1)} %get-tuple-element.34), channel_id=1, source_target_pairs={{0,2},{1,3},{2,0},{3,1},{4,6},{5,7},{6,4},{7,5},{8,10},{9,11},{10,... | collective-permute-start | bytes 3981320 | tf_op jit(solution)/shard_map/ppermute | solution.py:373
  17.1 32.4 %collective-permute-start.1 = (bf16[4,144,1152]{2,1,0:T(8,128)(2,1)}, bf16[4,144,1152]{2,1,0:T(8,128)(2,1)}, u32[]{:S(2)}, u32[]{:S(2)}) collective-permute-start(bf16[4,144,1152]{2,1,0:T(8,128)(2,1)} %get-tuple-element.32.refs_0_), channel_id=1, source_target_pairs={{0,1},{1,0},{2,3},{3,2},{4,5},{5,4},{6,7},{7,6},{8,9},{9,8},{10,11... | collective-permute-start | bytes 3981320 | tf_op jit(solution)/shard_map/ppermute | solution.py:373
  23.0 52.9 %collective-permute-start.5 = (bf16[4,144,1152]{2,1,0:T(8,128)(2,1)}, bf16[4,144,1152]{2,1,0:T(8,128)(2,1)}, u32[]{:S(2)}, u32[]{:S(2)}) collective-permute-start(bf16[4,144,1152]{2,1,0:T(8,128)(2,1)} %get-tuple-element.38), channel_id=1, source_target_pairs={{0,2},{1,3},{2,0},{3,1},{4,6},{5,7},{6,4},{7,5},{8,10},{9,11},{10,... | collective-permute-start | bytes 3981320 | tf_op jit(solution)/shard_map/ppermute | solution.py:373
  23.5 54.4 %collective-permute-start = (bf16[4,144,1152]{2,1,0:T(8,128)(2,1)}, bf16[4,144,1152]{2,1,0:T(8,128)(2,1)}, u32[]{:S(2)}, u32[]{:S(2)}) collective-permute-start(bf16[4,144,1152]{2,1,0:T(8,128)(2,1)} %get-tuple-element.33.refs_0_), channel_id=1, source_target_pairs={{0,1},{1,0},{2,3},{3,2},{4,5},{5,4},{6,7},{7,6},{8,9},{9,8},{10,11... | collective-permute-start | bytes 3981320 | tf_op jit(solution)/shard_map/ppermute | solution.py:373
  55.5 49.4 %collective-permute-start.3 = (bf16[4,144,1152]{2,1,0:T(8,128)(2,1)}, bf16[4,144,1152]{2,1,0:T(8,128)(2,1)}, u32[]{:S(2)}, u32[]{:S(2)}) collective-permute-start(bf16[4,144,1152]{2,1,0:T(8,128)(2,1)} %get-tuple-element.36), channel_id=1, source_target_pairs={{0,1},{1,0},{2,3},{3,2},{4,5},{5,4},{6,7},{7,6},{8,9},{9,8},{10,11... | collective-permute-start | bytes 3981320 | tf_op jit(solution)/shard_map/ppermute | solution.py:373
  57.0 47.9 %collective-permute-start.4 = (bf16[4,144,1152]{2,1,0:T(8,128)(2,1)}, bf16[4,144,1152]{2,1,0:T(8,128)(2,1)}, u32[]{:S(2)}, u32[]{:S(2)}) collective-permute-start(bf16[4,144,1152]{2,1,0:T(8,128)(2,1)} %get-tuple-element.37), channel_id=1, source_target_pairs={{0,2},{1,3},{2,0},{3,1},{4,6},{5,7},{6,4},{7,5},{8,10},{9,11},{10,... | collective-permute-start | bytes 3981320 | tf_op jit(solution)/shard_map/ppermute | solution.py:373
  112.1 66.0 %all-to-all-start = ((bf16[8,144,1152]{2,1,0:T(8,128)(2,1)}), bf16[8,144,1152]{2,1,0:T(8,128)(2,1)}, u32[]{:S(2)}, u32[]{:S(2)}) async-start(bf16[8,144,1152]{2,1,0:T(8,128)(2,1)} %get-tuple-element.42), calls=%async_computation | async-start | bytes 5308416 | tf_op jit(solution)/shard_map/all_to_all | solution.py:379
  117.0 71.9 %collective-permute-start.6 = (bf16[2,2,144,1152]{3,2,1,0:T(8,128)(2,1)}, bf16[2,2,144,1152]{3,2,1,0:T(8,128)(2,1)}, u32[]{:S(2)}, u32[]{:S(2)}) collective-permute-start(bf16[2,2,144,1152]{3,2,1,0:T(8,128)(2,1)} %get-tuple-element.44), channel_id=1, source_target_pairs={{0,1},{1,0},{2,3},{3,2},{4,5},{5,4},{6,7},{7,6},{8,9},{9,8},{10,11... | collective-permute-start | bytes 3981320 | tf_op jit(solution)/shard_map/ppermute | solution.py:373
  118.5 70.4 %collective-permute-start.7 = (bf16[2,2,144,1152]{3,2,1,0:T(8,128)(2,1)}, bf16[2,2,144,1152]{3,2,1,0:T(8,128)(2,1)}, u32[]{:S(2)}, u32[]{:S(2)}) collective-permute-start(bf16[2,2,144,1152]{3,2,1,0:T(8,128)(2,1)} %get-tuple-element.45), channel_id=1, source_target_pairs={{0,2},{1,3},{2,0},{3,1},{4,6},{5,7},{6,4},{7,5},{8,10},{9,11},{10,... | collective-permute-start | bytes 3981320 | tf_op jit(solution)/shard_map/ppermute | solution.py:373
  119.0 69.9 %collective-permute-start.8 = (bf16[2,2,144,1152]{3,2,1,0:T(8,128)(2,1)}, bf16[2,2,144,1152]{3,2,1,0:T(8,128)(2,1)}, u32[]{:S(2)}, u32[]{:S(2)}) collective-permute-start(bf16[2,2,144,1152]{3,2,1,0:T(8,128)(2,1)} %get-tuple-element.46), channel_id=1, source_target_pairs={{0,3},{1,2},{2,1},{3,0},{4,7},{5,6},{6,5},{7,4},{8,11},{9,10},{10,... | collective-permute-start | bytes 3981320 | tf_op jit(solution)/shard_map/ppermute | solution.py:373
  200.0 6.7 %copy-start.2 = (bf16[3,2,144,1152]{3,2,1,0:T(8,128)(2,1)S(1)}, bf16[3,2,144,1152]{3,2,1,0:T(8,128)(2,1)}, u32[]{:S(2)}) copy-start(bf16[3,2,144,1152]{3,2,1,0:T(8,128)(2,1)} %get-tuple-element.50) | copy-start | bytes 5971972
  200.0 94.4 %all-to-all-start.1 = ((bf16[8,144,1152]{2,1,0:T(8,128)(2,1)}), bf16[8,144,1152]{2,1,0:T(8,128)(2,1)}, u32[]{:S(2)}, u32[]{:S(2)}) async-start(bf16[8,144,1152]{2,1,0:T(8,128)(2,1)} %get-tuple-element.47), calls=%async_computation.1 | async-start | bytes 5308416 | tf_op jit(solution)/shard_map/all_to_all | solution.py:379
  204.5 197.5 %all-gather.3.cloned.1.call-start = ((), (), s32[]{:S(2)}) async-start(), calls=%async_computation.2 | async-start | bytes 13271040 | tf_op jit(solution)/shard_map/all_gather | solution.py:397
  204.6 46.6 %collective-permute-start.9 = (bf16[3,2,144,1152]{3,2,1,0:T(8,128)(2,1)}, bf16[3,2,144,1152]{3,2,1,0:T(8,128)(2,1)}, u32[]{:S(2)}, u32[]{:S(2)}) collective-permute-start(bf16[3,2,144,1152]{3,2,1,0:T(8,128)(2,1)} %get-tuple-element.48), channel_id=1, source_target_pairs={{0,1},{1,0},{2,3},{3,2},{4,5},{5,4},{6,7},{7,6},{8,9},{9,8},{10,11... | collective-permute-start | bytes 5971976 | tf_op jit(solution)/shard_map/ppermute | solution.py:373
  206.2 88.2 %collective-permute-start.10 = (bf16[3,2,144,1152]{3,2,1,0:T(8,128)(2,1)}, bf16[3,2,144,1152]{3,2,1,0:T(8,128)(2,1)}, u32[]{:S(2)}, u32[]{:S(2)}) collective-permute-start(bf16[3,2,144,1152]{3,2,1,0:T(8,128)(2,1)} %get-tuple-element.49), channel_id=1, source_target_pairs={{0,2},{1,3},{2,0},{3,1},{4,6},{5,7},{6,4},{7,5},{8,10},{9,11},{10,... | collective-permute-start | bytes 5971976 | tf_op jit(solution)/shard_map/ppermute | solution.py:373
  206.6 87.7 %collective-permute-start.11 = (bf16[3,2,144,1152]{3,2,1,0:T(8,128)(2,1)S(1)}, bf16[3,2,144,1152]{3,2,1,0:T(8,128)(2,1)}, u32[]{:S(2)}, u32[]{:S(2)}) collective-permute-start(bf16[3,2,144,1152]{3,2,1,0:T(8,128)(2,1)S(1)} %copy-done.2), channel_id=1, source_target_pairs={{0,3},{1,2},{2,1},{3,0},{4,7},{5,6},{6,5},{7,4},{8,11},{9,10},{10,... | collective-permute-start | bytes 5971976 | tf_op jit(solution)/shard_map/ppermute | solution.py:373
  294.4 0.7 copy-start
Sparse Core Ops, SparseCore 0:
  294.5 107.4 all-gather.2

commit v4 on v3

--- a/solution.py
+++ b/solution.py
@@ -24,12 +24,9 @@
     return pl.CostEstimate(flops=flops, bytes_accessed=moved, transcendentals=0)
 
 
-def arrange_body(n_add, n_after, n_pass, base, halves, cols, grad, *refs):
-    adds = refs[: 2 * n_add]
-    n_out = 2 if halves else 1
-    first = 2 * n_add + n_after + n_pass
-    outs = refs[first : first + n_out]
-    buffer, sems = refs[-2:]
+def arrange_body(n_add, offsets, n_after, base, halves, cols, grad, *refs):
+    adds, refs = refs[: 2 * n_add], refs[2 * n_add + n_after :]
+    outs, (buffer, sems) = refs[:-2], refs[-2:]
     n = outs[0].shape[1]
     count = buffer.shape[0]
     half = count // 2
@@ -55,32 +52,30 @@
 
         if n_add:
             total = out[at].astype(jnp.float32)
-            for k in range(n_add):
-                total = total + adds[2 * k + i // half][i % half].astype(jnp.float32)
+            for k in range(i // half, 2 * n_add, 2):
+                total = total + adds[k][offsets[k] + i % half].astype(jnp.float32)
             out[at] = total.astype(out.dtype)
 
 
-def arrange(cols, grad, base, n, adds=(), halves=True, after=(), through=()):
+def arrange(cols, grad, base, n, adds=(), halves=True, after=()):
     count = cols.shape[0]
     w = 2 * B
+    adds = [part for pair in adds for part in pair]
     shapes = [(count // 2, n, w)] * 2 if halves else [(count, n, w)]
-    before = 2 + 2 * len(adds) + len(after)
-    return pl.pallas_call(
-        functools.partial(arrange_body, len(adds), len(after), len(through), base, halves),
-        in_specs=[SCALARS, ANY]
-        + [WHOLE] * (2 * len(adds))
-        + [ANY] * (len(after) + len(through)),
-        out_specs=[WHOLE] * len(shapes) + [ANY] * len(through),
-        out_shape=[jax.ShapeDtypeStruct(s, grad.dtype) for s in shapes]
-        + [jax.ShapeDtypeStruct(x.shape, x.dtype) for x in through],
+    return pl.pallas_call(
+        functools.partial(
+            arrange_body, len(adds) // 2, [part[1] for part in adds], len(after), base, halves
+        ),
+        in_specs=[SCALARS, ANY] + [WHOLE] * len(adds) + [ANY] * len(after),
+        out_specs=[WHOLE] * len(shapes),
+        out_shape=[jax.ShapeDtypeStruct(s, grad.dtype) for s in shapes],
         scratch_shapes=[
             pltpu.VMEM((count, 2 * n, WINDOW), grad.dtype),
             pltpu.SemaphoreType.DMA((count,)),
         ],
-        input_output_aliases={before + k: len(shapes) + k for k in range(len(through))},
-        compiler_params=params(),
-        cost_estimate=cost(0, count * n * w * 2 * (2 + len(adds))),
-    )(cols, grad, *[term for pair in adds for term in pair], *after, *through)
+        compiler_params=params(),
+        cost_estimate=cost(0, count * n * w * (4 + len(adds))),
+    )(cols, grad, *[part[0] for part in adds], *after)
 
 
 def visit(k, m, p, last):
@@ -179,11 +174,16 @@
     )(js, *chunks)
 
 
-def direct_body(n, rd, n_chunks, n_after, js, *refs):
-    chunks, roots = refs[:n_chunks], refs[n_chunks : n_chunks + n]
-    refs = refs[n_chunks + n + n_after :]
-    outs, square_out = refs[:n_chunks], refs[n_chunks]
-    g16, l32, r32 = refs[n_chunks + 1 :]
+def direct_body(n, rd, n_chunks, n_after, js, place, *refs):
+    chunks, roots, refs = refs[:n_chunks], refs[n_chunks : n_chunks + n], refs[n_chunks + n :]
+    outs, (square_out, g16, l32, r32, result, sems) = refs[n_after:-6], refs[-6:]
+    p = pl.program_id(0)
+    f = place[0]
+    hr = result.shape[1]
+
+    def send(k):
+        return pltpu.make_async_copy(result.at[f ^ k], outs[k], sems.at[k])
+
     for q in range(2):
         assemble(chunks, q, g16)
         for k in range(n):
@@ -195,37 +195,85 @@
         direction = dot(inner, r32[...].astype(jnp.bfloat16), ((1,), (0,)))
         square_out[0, q : q + 1, :] = jnp.full((1, LANES), jnp.sum(direction * direction))
         direction = direction.astype(jnp.bfloat16)
-        base = 0
-        for out in outs:
-            size = out.shape[1]
-            for h in range(2):
-                for side in range(2):
-                    start = h * (B // 2) + base + side * size
-                    out[2 * q + h, :, side * B : side * B + B] = direction[start : start + size]
-            base += 2 * size
-
-
-def direct(js, chunks, roots, rd, after):
+        for h in range(2):
+            for side in range(2):
+                start = h * (B // 2) + side * hr
+                result[4 * p + 2 * q + h, :, side * B : side * B + B] = direction[start : start + hr]
+    for k in range(len(outs)):
+
+        @pl.when((f ^ k) // 4 == p)
+        def _():
+            send(k).start()
+
+    @pl.when(p == pl.num_programs(0) - 1)
+    def _():
+        for k in range(len(outs)):
+            send(k).wait()
+
+
+def direct(js, place, chunks, roots, rd, after):
     n = js.shape[0]
-    count, _, w = chunks[0].shape
+    owners, _, w = chunks[0].shape
+    hr = sum(chunk.shape[1] for chunk in chunks)
     pairs, rows = roots[0].shape[1], roots[0].shape[2]
-    chunk_specs = [pl.BlockSpec((4,) + chunk.shape[1:], lambda p, j: (p, 0, 0)) for chunk in chunks]
     return pl.pallas_call(
         functools.partial(direct_body, n, rd, len(chunks), len(after)),
         grid_spec=pltpu.PrefetchScalarGridSpec(
-            num_scalar_prefetch=1,
+            num_scalar_prefetch=2,
             grid=(pairs,),
-            in_specs=chunk_specs
-            + [pl.BlockSpec((2, 1, rows, w), lambda p, j: (0, p, 0, 0))] * n
+            in_specs=[pl.BlockSpec((4,) + chunk.shape[1:], lambda p, j, f: (p, 0, 0)) for chunk in chunks]
+            + [pl.BlockSpec((2, 1, rows, w), lambda p, j, f: (0, p, 0, 0))] * n
             + [ANY] * len(after),
-            out_specs=chunk_specs + [pl.BlockSpec((1, 8, LANES), lambda p, j: (p, 0, 0))],
-            scratch_shapes=[pltpu.VMEM((B, B), jnp.bfloat16)] + [pltpu.VMEM((B, B), jnp.float32)] * 2,
+            out_specs=[ANY] * owners + [pl.BlockSpec((1, 8, LANES), lambda p, j, f: (p, 0, 0))],
+            scratch_shapes=[pltpu.VMEM((B, B), jnp.bfloat16)]
+            + [pltpu.VMEM((B, B), jnp.float32)] * 2
+            + [pltpu.VMEM((owners, hr, w), jnp.bfloat16), pltpu.SemaphoreType.DMA((owners,))],
         ),
-        out_shape=[jax.ShapeDtypeStruct(chunk.shape, jnp.bfloat16) for chunk in chunks]
+        out_shape=[jax.ShapeDtypeStruct((hr, w), jnp.bfloat16)] * owners
         + [jax.ShapeDtypeStruct((pairs, 8, LANES), jnp.float32)],
         compiler_params=params(),
         cost_estimate=cost(pairs * 8 * B**3, pairs * B * B * 2 * 8),
-    )(js, *chunks, *roots, *after)
+    )(js, place, *chunks, *roots, *after)
+
+
+def follow(arrays, after):
+    return pl.pallas_call(
+        lambda *refs: None,
+        in_specs=[ANY] * (len(arrays) + len(after)),
+        out_specs=[ANY] * len(arrays),
+        out_shape=[jax.ShapeDtypeStruct(x.shape, x.dtype) for x in arrays],
+        input_output_aliases={k: k for k in range(len(arrays))},
+        compiler_params=params(),
+        cost_estimate=cost(0, 0),
+    )(*arrays, *after)
+
+
+def collect_body(count, n_through, *refs):
+    half = count // 2
+    parts, low, high, sems = refs[:count], *refs[count + n_through : count + n_through + 2], refs[-1]
+    copies = [
+        pltpu.make_async_copy(part, (low, high)[k // half].at[k % half], sems.at[k])
+        for k, part in enumerate(parts)
+    ]
+    for copy in copies:
+        copy.start()
+    for copy in copies:
+        copy.wait()
+
+
+def collect(parts, through):
+    count = len(parts)
+    halves = jax.ShapeDtypeStruct((count // 2,) + parts[0].shape, parts[0].dtype)
+    return pl.pallas_call(
+        functools.partial(collect_body, count, len(through)),
+        in_specs=[ANY] * (count + len(through)),
+        out_specs=[ANY] * (2 + len(through)),
+        out_shape=[halves] * 2 + [jax.ShapeDtypeStruct(x.shape, x.dtype) for x in through],
+        scratch_shapes=[pltpu.SemaphoreType.DMA((count,))],
+        input_output_aliases={count + k: 2 + k for k in range(len(through))},
+        compiler_params=params(),
+        cost_estimate=cost(0, 2 * count * parts[0].size * 2),
+    )(*parts, *through)
 
 
 def statistics_body(n, js, *refs):
@@ -277,12 +325,18 @@
     )(js, *received, *olds)
 
 
-def restore_body(item, scale, source, out, buffer, result, in_sems, out_sems):
+def restore_body(src, item, scale, *refs):
+    sources, (out, buffer, result, in_sems, out_sems) = refs[:-5], refs[-5:]
     columns, n, w = buffer.shape
     slots = result.shape[0]
 
     def fetch(c, _):
-        pltpu.make_async_copy(source.at[item[c]], buffer.at[c], in_sems.at[c]).start()
+        for k, source in enumerate(sources):
+
+            @pl.when(src[c] == k)
+            def _():
+                pltpu.make_async_copy(source.at[item[c]], buffer.at[c], in_sems.at[c]).start()
+
         return 0
 
     def store(p, slot):
@@ -300,7 +354,7 @@
 
         for e in range(2):
             c = 2 * p + e
-            pltpu.make_async_copy(source.at[item[c]], buffer.at[c], in_sems.at[c]).wait()
+            pltpu.make_async_copy(sources[0].at[0], buffer.at[c], in_sems.at[c]).wait()
             scaled = (buffer[c].astype(jnp.float32) * scale[c]).astype(result.dtype)
             result[slot, :n, e * B : e * B + B] = scaled[:, :B]
             result[slot, n:, e * B : e * B + B] = scaled[:, B:]
@@ -314,12 +368,13 @@
         store(p, p % slots).wait()
 
 
-def restore(item, scale, source):
-    columns, n, w = source.shape
+def restore(src, item, scale, sources):
+    columns = src.shape[0]
+    _, n, w = sources[0].shape
     slots = 4
     return pl.pallas_call(
         restore_body,
-        in_specs=[SCALARS, SCALARS, ANY],
+        in_specs=[SCALARS] * 3 + [ANY] * len(sources),
         out_specs=ANY,
         out_shape=jax.ShapeDtypeStruct((2 * n, columns * B), jnp.bfloat16),
         scratch_shapes=[
@@ -330,19 +385,7 @@
         ],
         compiler_params=params(),
         cost_estimate=cost(0, columns * n * w * 4),
-    )(item, scale, source)
-
-
-def hold(arrays):
-    return pl.pallas_call(
-        lambda *refs: None,
-        in_specs=[ANY] * len(arrays),
-        out_specs=[ANY] * len(arrays),
-        out_shape=[jax.ShapeDtypeStruct(x.shape, x.dtype) for x in arrays],
-        input_output_aliases={k: k for k in range(len(arrays))},
-        compiler_params=params(),
-        cost_estimate=cost(0, 0),
-    )(*arrays)
+    )(src, item, scale, *sources)
 
 
 def owner_local(grads, slots, stats_left, stats_right, root_left, root_right, second_moment):
@@ -360,14 +403,16 @@
     js = r ^ jnp.arange(replicas, dtype=jnp.int32)
     row_slots = lax.dynamic_index_in_dim(slots, f // sub_count, 0, keepdims=False)
     column_ids = jnp.arange(columns, dtype=jnp.int32)
-    owner_ids = replicas * jnp.arange(owners, dtype=jnp.int32)
-
-    def columns_of(low, high):
-        ids = jnp.arange(owners, dtype=jnp.int32)
-        wanted = owner_ids + (r ^ jnp.where(ids < half, low, high))
-        return jnp.sum(jnp.where(row_slots == wanted[:, None], column_ids, 0), axis=1)
-
-    far, near, cross, own = (columns_of(*k) for k in ((3, 3), (1, 2), (2, 1), (0, 0)))
+    owner_ids = jnp.arange(owners, dtype=jnp.int32)
+    halves = (owner_ids[:half], owner_ids[half:])
+    wanted = jnp.stack(
+        [
+            replicas * jnp.concatenate([halves[low], halves[high]])
+            + (r ^ jnp.where(owner_ids < half, low_step, high_step))
+            for low, low_step, high, high_step in ((0, 3, 0, 1), (1, 3, 1, 2), (0, 2, 1, 1), (0, 0, 1, 0))
+        ]
+    )
+    cols = jnp.sum(jnp.where(row_slots == wanted[:, :, None], column_ids, 0), axis=2)
 
     def swap(x, k):
         return lax.ppermute(x, "replica", [(i, i ^ k) for i in range(replicas)])
@@ -375,26 +420,36 @@
     def as_rows(x):
         return x.reshape(row_blocks, -1, sub_count * rd, B)
 
-    def exchange(x):
-        return lax.all_to_all(x, "fsdp", split_axis=0, concat_axis=0, tiled=True)
-
-    n = rows // 2
-    far_a, far_b = arrange(far, grad, 0, n)
-    by_far = (swap(far_a, 1), swap(far_b, 2))
-    x_a, y_b = arrange(near, grad, 0, n, after=(far_a,))
-    from_x_a, from_y_b = swap(x_a, 1), swap(y_b, 2)
-    roots = pack_roots(js, as_rows(root_left), as_rows(root_right), (x_a,))
-    y_a, x_b = arrange(cross, grad, 0, n, (by_far,), after=(roots[0],))
-    terms = ((from_x_a, swap(x_b, 1)), (swap(y_a, 2), from_y_b))
-    owned, *sent = arrange(own, grad, 0, n, terms, halves=False, through=tuple(roots[1:]))
-    blocks = exchange(owned)
+    first = rows // 64 * 16
+    chunks = ((0, first), (2 * first, rows // 2 - first))
+    after, early, blocks = (), [], []
+    for chunk in chunks:
+        x, y = arrange(cols[:2].reshape(-1), grad, *chunk, after=after)
+        early.append((swap(x, 1), swap(y, 2)))
+        after = (x,)
+    roots = pack_roots(js, as_rows(root_left), as_rows(root_right), after)
+    after = (roots[0],)
+    for (x, y), chunk in zip(early, chunks):
+        y_a, x_b = arrange(cols[2], grad, *chunk, [((x, 0), (y, 0))], after=after)
+        terms = [((x, half), (y, half)), ((swap(y_a, 2), 0), (swap(x_b, 1), 0))]
+        (owned,) = arrange(cols[3], grad, *chunk, terms, halves=False)
+        blocks.append(lax.all_to_all(owned, "fsdp", split_axis=0, concat_axis=0, tiled=True))
+        after = (owned,)
+    sent = follow(roots[1:], after)
     roots = [roots[0]] + [swap(x, k) for k, x in zip((1, 2, 3), sent)]
 
-    products = gram(js, [blocks], rd)
+    place = f.reshape(1)
+    products = gram(js, blocks, rd)
     received = [products[0]] + [swap(products[k], k) for k in (1, 2, 3)]
-    direction, direction_square = direct(js, [blocks], roots, rd, (products[0],))
-    returned, *received[1:] = hold((exchange(direction), *received[1:]))
-    gathered = lax.all_gather(returned, "replica").reshape(columns, n, 2 * B)
+    *direction, direction_square = direct(js, place, blocks, roots, rd, (products[0],))
+    direction[1:] = [
+        lax.ppermute(direction[k], "fsdp", [(i, i ^ k) for i in range(owners)])
+        for k in range(1, owners)
+    ]
+    a, b, *received[1:] = collect(direction, received[1:])
+
+    x_a, y_b, x_b, y_a = swap(a, 1), swap(b, 2), swap(b, 1), swap(a, 2)
+    gathered = (a, b, x_a, x_b, y_a, y_b, swap(x_a, 2), swap(y_b, 1))
 
     left_new, right_new, moment, adam_square = statistics(
         js, received, [as_rows(x) for x in (stats_left, stats_right, second_moment)]
@@ -416,8 +471,9 @@
     )
     scale = jnp.sum(jnp.where(row_slots[:, None] == column_ids, row_ratio, 0.0), axis=1)
 
-    item = lax.rem(row_slots, replicas) * owners + row_slots // replicas
-    update = restore(item, scale, gathered)
+    part = (row_slots // replicas) ^ f
+    src = 2 * (lax.rem(row_slots, replicas) ^ r) + part // half
+    update = restore(src, lax.rem(part, half), scale, gathered)
     return (
         update,
         left_new.reshape(stats_left.shape),
@@ -526,8 +582,9 @@
 def local(*arrays):
     replicas = lax.axis_size("replica")
     rows, full_width = arrays[0].shape[1:]
-    per_owner = full_width // B // lax.axis_size("fsdp")
-    if replicas == 4 and per_owner == replicas and 2 * rows == B:
+    owners = lax.axis_size("fsdp")
+    per_owner = full_width // B // owners
+    if replicas == 4 and per_owner == replicas and 2 * rows == B and owners == 8:
         return owner_local(*arrays)
     return row_local(*arrays)
 

time: 419 us -> 486 us (1.16)
  Pallas kernels: 81.9 us -> 173 us
  waiting for transfers between devices: 248 us -> 182 us
  starting transfers between devices: 23.8 us -> 51.1 us
  blocking collectives: 39.8 us -> 62.9 us
  between operations: 14.2 us -> 1 us
    pallas_call x6 -> x9, Pallas kernels: 30.6 us -> 121 us  [the longest x1 81.6 us: collect(): pl.pallas_call(functools.partial(collect_body, count, len(through)), in_s...]
    ppermute x0 -> x7, waiting for transfers between devices: none -> 46.9 us  [owner_local(): lax.ppermute(direction[k], 'fsdp', [(i, i ^ k) for i in range(owners)])]
    ppermute x12 -> x20, waiting for transfers between devices: 150 us -> 103 us  [swap(): return lax.ppermute(x, 'replica', [(i, i ^ k) for i in range(replicas)])]
    all_gather x1 -> x0, waiting for transfers between devices: 40 us -> none  [owner_local(): gathered = lax.all_gather(returned, 'replica').reshape(columns, n, 2 * B)]
    all_to_all x2, waiting for transfers between devices: 57.6 us -> 32.3 us  [owner_local(): lax.all_to_all(owned, 'fsdp', split_axis=0, concat_axis=0, tiled=True)]
    psum x1, blocking collectives: 39.8 us -> 62.9 us  [owner_local(): lax.psum(jnp.where(owner_place, squares, 0.0), ('fsdp', 'replica'))]
    ppermute x0 -> x7, starting transfers between devices: none -> 16.4 us  [owner_local(): lax.ppermute(direction[k], 'fsdp', [(i, i ^ k) for i in range(owners)])]
    ppermute x12 -> x20, starting transfers between devices: 14.3 us -> 24.7 us  [swap(): return lax.ppermute(x, 'replica', [(i, i ^ k) for i in range(replicas)])]
  transfers between devices with their start and end apart: 15 -> 29, of which waited for: 9 -> 18; matrix products, arithmetic and copies ran while one was open for 2% -> 2% of each run, Pallas kernels for 12% -> 15%
where the time goes in v4:
time: 486 us; the launch traced here: 485 us
  waiting for transfers between devices  182 us (37%)
  Pallas kernels  173 us (36%)
  blocking collectives  62.9 us (13%)
  starting transfers between devices  51.1 us (11%)
  other arithmetic  9.46 us (2%)
  local copies, waits for them, and re-layouts  5.02 us (1%)
    ppermute x20, waiting for transfers between devices, swap(): return lax.ppermute(x, 'replica', [(i, i ^ k) for i in range(replicas)])  103 us
    pallas_call x1, Pallas kernels, collect(): pl.pallas_call(functools.partial(collect_body, count, len(through)), in_s...  81.6 us
    psum x1, blocking collectives, owner_local(): lax.psum(jnp.where(owner_place, squares, 0.0), ('fsdp', 'replica'))  62.9 us
    ppermute x7, waiting for transfers between devices, owner_local(): lax.ppermute(direction[k], 'fsdp', [(i, i ^ k) for i in range(owners)])  46.9 us
    all_to_all x2, waiting for transfers between devices, owner_local(): lax.all_to_all(owned, 'fsdp', split_axis=0, concat_axis=0, tiled=True)  32.3 us
    pallas_call x6, Pallas kernels, arrange(): pl.pallas_call(functools.partial(arrange_body, len(adds) // 2, [part[1] f...  31 us
    ppermute x20, starting transfers between devices, swap(): return lax.ppermute(x, 'replica', [(i, i ^ k) for i in range(replicas)])  24.7 us
    pallas_call x1, Pallas kernels, statistics(): pl.pallas_call(functools.partial(statistics_body, n), grid_spec=pltpu.Pre...  20 us
  transfers between devices with their start and end apart: 29, of which 18 were waited for; matrix products, arithmetic and copies ran while one was open for 2% of the time, Pallas kernels for 15%

profile of v4, /device:TPU:0, one launch (start us, length us, event | category | flops | bytes accessed | tf_op | source)
XLA Modules:
  0.0 484.6 jit_solution(9395215300604483637)
XLA Ops:
  3.9 4.8 shard_map.102
  8.7 3.0 collective-permute-start.1
  13.2 5.2 %shard_map.103 = (bf16[8,80,1152]{2,1,0:T(8,128)(2,1)}, bf16[8,80,1152]{2,1,0:T(8,128)(2,1)}) custom-call(s32[16]{0:T(128)} %reshape.230.cols, bf16[288,18432]{1,0:T(8,128)(2,1)} %bitcast.36, bf16[8,64,1152]{2,1,0:T(8,128)(2,1)} %get-tuple-element.41.refs_0_), custom_call_target="tpu_custom_call" | custom-call | bytes 5898240 | tf_op jit(solution)/shard_map/pallas_call | solution.py:65
  19.0 9.0 %shard_map.104 = (bf16[2,2,144,1152]{3,2,1,0:T(8,128)(2,1)}, bf16[2,2,144,1152]{3,2,1,0:T(8,128)(2,1)}, bf16[2,2,144,1152]{3,2,1,0:T(8,128)(2,1)}, bf16[2,2,144,1152]{3,2,1,0:T(8,128)(2,1)}) custom-call(s32[4]{0:T(128)} %iota_xor_fusion.js, bf16[4,4,144,576]{3,2,1,0:T(8,128)(2,1)} %bitcast.44, bf16[4,4,144,576]{3,2,1,0:T(8,128)(2,1)} %bitcast.45, ...), custom_call_target="tpu_custom_call" | custom-call | bytes 10616832 | tf_op jit(solution)/shard_map/pallas_call | solution.py:100
  29.3 8.7 %collective-permute-done.1.refs_1_ = bf16[8,64,1152]{2,1,0:T(8,128)(2,1)} collective-permute-done((bf16[8,64,1152]{2,1,0:T(8,128)(2,1)}, bf16[8,64,1152]{2,1,0:T(8,128)(2,1)}, u32[]{:S(2)}, u32[]{:S(2)}) %collective-permute-start.1) | collective-permute-done | bytes 1179680 | tf_op jit(solution)/shard_map/ppermute | solution.py:418
  39.5 4.8 shard_map.105
  48.4 12.5 %collective-permute-done.2.refs_2_ = bf16[4,64,1152]{2,1,0:T(8,128)(2,1)} collective-permute-done((bf16[4,64,1152]{2,1,0:T(8,128)(2,1)}, bf16[4,64,1152]{2,1,0:T(8,128)(2,1)}, u32[]{:S(2)}, u32[]{:S(2)}) %collective-permute-start.2) | collective-permute-done | bytes 589856 | tf_op jit(solution)/shard_map/ppermute | solution.py:418
  61.3 5.3 %shard_map.106.refs_2_ = bf16[8,64,1152]{2,1,0:T(8,128)(2,1)} custom-call(s32[8]{0:T(128)} %get-tuple-element.94.cols, bf16[288,18432]{1,0:T(8,128)(2,1)} %bitcast.38, bf16[8,64,1152]{2,1,0:T(8,128)(2,1)} %collective-permute-done.refs_0_, bf16[8,64,1152]{2,1,0:T(8,128)(2,1)} %collective-permute-done.1.refs_1_, ...), custom_call_target="tpu_custom_call" | custom-call | bytes 4718592 | tf_op jit(solution)/shard_map/pallas_call | solution.py:65
  66.5 5.1 %all-to-all-start = ((bf16[8,64,1152]{2,1,0:T(8,128)(2,1)}), bf16[8,64,1152]{2,1,0:T(8,128)(2,1)}, u32[]{:S(2)}, u32[]{:S(2)}) async-start(bf16[8,64,1152]{2,1,0:T(8,128)(2,1)} %shard_map.106.refs_2_), calls=%async_computation | async-start | bytes 2359296 | tf_op jit(solution)/shard_map/all_to_all | solution.py:436
  71.6 18.6 %collective-permute-done.5.refs_1_ = bf16[8,80,1152]{2,1,0:T(8,128)(2,1)} collective-permute-done((bf16[8,80,1152]{2,1,0:T(8,128)(2,1)}, bf16[8,80,1152]{2,1,0:T(8,128)(2,1)}, u32[]{:S(2)}, u32[]{:S(2)}) %collective-permute-start.5) | collective-permute-done | bytes 1474592 | tf_op jit(solution)/shard_map/ppermute | solution.py:418
  90.5 5.2 %shard_map.107 = (bf16[4,80,1152]{2,1,0:T(8,128)(2,1)}, bf16[4,80,1152]{2,1,0:T(8,128)(2,1)}) custom-call(s32[8]{0:T(128)} %get-tuple-element.93.cols, bf16[288,18432]{1,0:T(8,128)(2,1)} %bitcast.39, bf16[8,80,1152]{2,1,0:T(8,128)(2,1)} %collective-permute-done.4.refs_0_, bf16[8,80,1152]{2,1,0:T(8,128)(2,1)} %collective-permute-done.5.refs_1_, ...), custom_call_target="tpu_custom_call" | custom-call | bytes 4423680 | tf_op jit(solution)/shard_map/pallas_call | solution.py:65
  98.6 13.6 %collective-permute-done.6.refs_2_ = bf16[4,80,1152]{2,1,0:T(8,128)(2,1)} collective-permute-done((bf16[4,80,1152]{2,1,0:T(8,128)(2,1)}, bf16[4,80,1152]{2,1,0:T(8,128)(2,1)}, u32[]{:S(2)}, u32[]{:S(2)}) %collective-permute-start.6) | collective-permute-done | bytes 737312 | tf_op jit(solution)/shard_map/ppermute | solution.py:418
  113.0 5.8 %shard_map.108.refs_3_ = bf16[8,80,1152]{2,1,0:T(8,128)(2,1)} custom-call(s32[8]{0:T(128)} %get-tuple-element.94.cols, bf16[288,18432]{1,0:T(8,128)(2,1)} %bitcast.40, bf16[8,80,1152]{2,1,0:T(8,128)(2,1)} %collective-permute-done.4.refs_0_, bf16[8,80,1152]{2,1,0:T(8,128)(2,1)} %collective-permute-done.5.refs_1_, ...), custom_call_target="tpu_custom_call" | custom-call | bytes 5898240 | tf_op jit(solution)/shard_map/pallas_call | solution.py:65
  118.8 4.9 %all-to-all-start.1 = ((bf16[8,80,1152]{2,1,0:T(8,128)(2,1)}), bf16[8,80,1152]{2,1,0:T(8,128)(2,1)}, u32[]{:S(2)}, u32[]{:S(2)}) async-start(bf16[8,80,1152]{2,1,0:T(8,128)(2,1)} %shard_map.108.refs_3_), calls=%async_computation.1 | async-start | bytes 2949120 | tf_op jit(solution)/shard_map/all_to_all | solution.py:436
  127.2 32.3 %all-to-all-done.1.refs_1_ = bf16[8,80,1152]{2,1,0:T(8,128)(2,1)} async-done(((bf16[8,80,1152]{2,1,0:T(8,128)(2,1)}), bf16[8,80,1152]{2,1,0:T(8,128)(2,1)}, u32[]{:S(2)}, u32[]{:S(2)}) %all-to-all-start.1) | async-done | bytes 1474592 | tf_op jit(solution)/shard_map/all_to_all | solution.py:436
  159.5 10.7 %shard_map.109 = (bf16[3,2,144,1152]{3,2,1,0:T(8,128)(2,1)}, bf16[3,2,144,1152]{3,2,1,0:T(8,128)(2,1)}, bf16[3,2,144,1152]{3,2,1,0:T(8,128)(2,1)}, bf16[3,2,144,1152]{3,2,1,0:T(8,128)(2,1)}) custom-call(s32[4]{0:T(128)} %iota_xor_fusion.js, bf16[8,64,1152]{2,1,0:T(8,128)(2,1)} %all-to-all-done.refs_0_, bf16[8,80,1152]{2,1,0:T(8,128)(2,1)} %all-to-all-done.1.refs_1_), custom_call_target="tpu_custom_call" | custom-call | flops 3057647616 | bytes 10616832 | tf_op jit(solution)/shard_map/pallas_call | solution.py:160
  173.7 12.2 %collective-permute-done.9.refs_4_ = bf16[2,2,144,1152]{3,2,1,0:T(8,128)(2,1)} collective-permute-done((bf16[2,2,144,1152]{3,2,1,0:T(8,128)(2,1)}, bf16[2,2,144,1152]{3,2,1,0:T(8,128)(2,1)}, u32[]{:S(2)}, u32[]{:S(2)}) %collective-permute-start.9) | collective-permute-done | bytes 1327136 | tf_op jit(solution)/shard_map/ppermute | solution.py:418
  186.0 11.8 %shard_map.111 = (bf16[144,1152]{1,0:T(8,128)(2,1)}, bf16[144,1152]{1,0:T(8,128)(2,1)}, bf16[144,1152]{1,0:T(8,128)(2,1)}, bf16[144,1152]{1,0:T(8,128)(2,1)}, bf...) custom-call(s32[4]{0:T(128)} %iota_xor_fusion.js, ...), custom_call_target="tpu_custom_call" | custom-call | flops 3057647616 | bytes 10616832 | tf_op jit(solution)/shard_map/pallas_call | solution.py:219
  201.4 7.5 %collective-permute-done.12.refs_2_ = bf16[144,1152]{1,0:T(8,128)(2,1)} collective-permute-done((bf16[144,1152]{1,0:T(8,128)(2,1)}, bf16[144,1152]{1,0:T(8,128)(2,1)}, u32[]{:S(2)}, u32[]{:S(2)}) %collective-permute-start.12) | collective-permute-done | bytes 331808 | tf_op jit(solution)/shard_map/ppermute | solution.py:446
  208.9 2.7 collective-permute-start.14
  211.5 9.3 %collective-permute-done.13.refs_3_ = bf16[144,1152]{1,0:T(8,128)(2,1)} collective-permute-done((bf16[144,1152]{1,0:T(8,128)(2,1)}, bf16[144,1152]{1,0:T(8,128)(2,1)}, u32[]{:S(2)}, u32[]{:S(2)}) %collective-permute-start.13) | collective-permute-done | bytes 331808 | tf_op jit(solution)/shard_map/ppermute | solution.py:446
  220.9 13.7 %collective-permute-done.14.refs_4_ = bf16[144,1152]{1,0:T(8,128)(2,1)} collective-permute-done((bf16[144,1152]{1,0:T(8,128)(2,1)}, bf16[144,1152]{1,0:T(8,128)(2,1)}, u32[]{:S(2)}, u32[]{:S(2)}) %collective-permute-start.14) | collective-permute-done | bytes 331808 | tf_op jit(solution)/shard_map/ppermute | solution.py:446
  234.6 4.0 collective-permute-start.16
  238.6 7.6 %collective-permute-done.15.refs_5_ = bf16[144,1152]{1,0:T(8,128)(2,1)} collective-permute-done((bf16[144,1152]{1,0:T(8,128)(2,1)}, bf16[144,1152]{1,0:T(8,128)(2,1)}, u32[]{:S(2)}, u32[]{:S(2)}) %collective-permute-start.15) | collective-permute-done | bytes 331808 | tf_op jit(solution)/shard_map/ppermute | solution.py:446
  246.2 6.3 %collective-permute-start.17 = (bf16[144,1152]{1,0:T(8,128)(2,1)}, bf16[144,1152]{1,0:T(8,128)(2,1)}, u32[]{:S(2)}, u32[]{:S(2)}) collective-permute-start(bf16[144,1152]{1,0:T(8,128)(2,1)} %get-tuple-element.64), channel_id=1, source_target_pairs={{0,28},{4,24},{8,20},{12,16},{16,12},{20,8},{24,4},{28,0},{1,29},{... | collective-permute-start | bytes 995336 | tf_op jit(solution)/shard_map/ppermute | solution.py:446
  252.5 8.6 %collective-permute-done.17.refs_7_ = bf16[144,1152]{1,0:T(8,128)(2,1)} collective-permute-done((bf16[144,1152]{1,0:T(8,128)(2,1)}, bf16[144,1152]{1,0:T(8,128)(2,1)}, u32[]{:S(2)}, u32[]{:S(2)}) %collective-permute-start.17) | collective-permute-done | bytes 331808 | tf_op jit(solution)/shard_map/ppermute | solution.py:446
  261.2 9.3 %collective-permute-done.19.refs_9_ = bf16[3,2,144,1152]{3,2,1,0:T(8,128)(2,1)} collective-permute-done((bf16[3,2,144,1152]{3,2,1,0:T(8,128)(2,1)}, bf16[3,2,144,1152]{3,2,1,0:T(8,128)(2,1)}, u32[]{:S(2)}, u32[]{:S(2)}) %collective-permute-start.19) | collective-permute-done | bytes 1990688 | tf_op jit(solution)/shard_map/ppermute | solution.py:418
  270.5 81.6 %shard_map.112 = (bf16[4,144,1152]{2,1,0:T(8,128)(2,1)}, bf16[4,144,1152]{2,1,0:T(8,128)(2,1)}, bf16[3,2,144,1152]{3,2,1,0:T(8,128)(2,1)}, bf16[3,2,144,1152]{3,2,1,0:T(8,128)(2,1)}, bf16[3,2,144,1152]{3,2,1,0:T(8,128)(2,1)}) custom-call(bf16[144,1152]{1,0:T(8,128)(2,1)} %get-tuple-element.57.refs_0_, ...), custom_call_target="tpu_custom_call", output_to_operand_aliasing={{2}: (8, {}), {3}: (9, {}), {4}: (10, {})} | custom-call | bytes 5308416 | tf_op jit(solution)/shard_map/pallas_call | solution.py:267
  359.3 25.2 %collective-permute-done.21.refs_2_ = bf16[4,144,1152]{2,1,0:T(8,128)(2,1)} collective-permute-done((bf16[4,144,1152]{2,1,0:T(8,128)(2,1)}, bf16[4,144,1152]{2,1,0:T(8,128)(2,1)}, u32[]{:S(2)}, u32[]{:S(2)}) %collective-permute-start.21) | collective-permute-done | bytes 1327136 | tf_op jit(solution)/shard_map/ppermute | solution.py:418
  388.1 20.0 %shard_map.113 = (f32[4,4,144,576]{3,2,1,0:T(8,128)}, f32[4,4,144,576]{3,2,1,0:T(8,128)}, f32[4,4,144,576]{3,2,1,0:T(8,128)}, f32[4,2,8,128]{3,2,1,0:T(8,128)}) custom-call(s32[4]{0:T(128)} %iota_xor_fusion.js, bf16[3,2,144,1152]{3,2,1,0:T(8,128)(2,1)} %get-tuple-element.50.refs_6_.refs_0_, bf16[3,2,144,1152]{3,2,1,0:T(8,128)(2,1)} %get-tuple-element.68.refs_1_, ...), custom_call_target="tpu_custom_call" | custom-call | bytes 39813120 | tf_op jit(solution)/shard_map/pallas_call | solution.py:305
  411.3 62.9 %psum.7 = f32[8,2,4,4]{2,0,3,1:T(8,128)S(1)} all-reduce(f32[8,2,4,4]{2,0,3,1:T(8,128)S(1)} %broadcast_select_fusion), channel_id=1, replica_groups=mesh['fsdp'=8,'replica'=4] {'fsdp','replica'}, use_global_device_ids=true, to_apply=%region_2.3 | all-reduce | flops 256 | bytes 2048 | tf_op jit(solution)/shard_map/psum | solution.py:467
  475.7 8.7 %shard_map.114 = bf16[288,18432]{1,0:T(8,128)(2,1)} custom-call(s32[32]{0:T(128)} %multiply_add_fusion.src, s32[32]{0:T(128)} %get-tuple-element.90.item, f32[32]{0:T(128)} %select_reduce_fusion.scale, bf16[4,144,1152]{2,1,0:T(8,128)(2,1)} %get-tuple-element.73.refs_0_, bf16[4,144,1152]{2,1,0:T(8,128)(2,1)} %get-tuple-element.74.refs_1_, ...), custom_call_target="tpu_custom_call" | custom-call | bytes 21233664 | tf_op jit(solution)/shard_map/pallas_call | solution.py:375
  (75 shorter events, 42.7 us)
Async XLA Ops:
  2.1 0.6 copy-start.1
  2.6 0.6 copy-start
  8.7 29.3 %collective-permute-start.1 = (bf16[8,64,1152]{2,1,0:T(8,128)(2,1)}, bf16[8,64,1152]{2,1,0:T(8,128)(2,1)}, u32[]{:S(2)}, u32[]{:S(2)}) collective-permute-start(bf16[8,64,1152]{2,1,0:T(8,128)(2,1)} %get-tuple-element.42), channel_id=1, source_target_pairs={{0,2},{1,3},{2,0},{3,1},{4,6},{5,7},{6,4},{7,5},{8,10},{9,11},{10,... | collective-permute-start | bytes 3538952 | tf_op jit(solution)/shard_map/ppermute | solution.py:418
  11.8 27.7 %collective-permute-start = (bf16[8,64,1152]{2,1,0:T(8,128)(2,1)}, bf16[8,64,1152]{2,1,0:T(8,128)(2,1)}, u32[]{:S(2)}, u32[]{:S(2)}) collective-permute-start(bf16[8,64,1152]{2,1,0:T(8,128)(2,1)} %get-tuple-element.41.refs_0_), channel_id=1, source_target_pairs={{0,1},{1,0},{2,3},{3,2},{4,5},{5,4},{6,7},{7,6},{8,9},{9,8},{10,11... | collective-permute-start | bytes 3538952 | tf_op jit(solution)/shard_map/ppermute | solution.py:418
  44.3 16.6 %collective-permute-start.2 = (bf16[4,64,1152]{2,1,0:T(8,128)(2,1)}, bf16[4,64,1152]{2,1,0:T(8,128)(2,1)}, u32[]{:S(2)}, u32[]{:S(2)}) collective-permute-start(bf16[4,64,1152]{2,1,0:T(8,128)(2,1)} %get-tuple-element.45), channel_id=1, source_target_pairs={{0,2},{1,3},{2,0},{3,1},{4,6},{5,7},{6,4},{7,5},{8,10},{9,11},{10,... | collective-permute-start | bytes 1769480 | tf_op jit(solution)/shard_map/ppermute | solution.py:418
  44.7 16.6 %collective-permute-start.3 = (bf16[4,64,1152]{2,1,0:T(8,128)(2,1)}, bf16[4,64,1152]{2,1,0:T(8,128)(2,1)}, u32[]{:S(2)}, u32[]{:S(2)}) collective-permute-start(bf16[4,64,1152]{2,1,0:T(8,128)(2,1)} %get-tuple-element.46), channel_id=1, source_target_pairs={{0,1},{1,0},{2,3},{3,2},{4,5},{5,4},{6,7},{7,6},{8,9},{9,8},{10,11... | collective-permute-start | bytes 1769480 | tf_op jit(solution)/shard_map/ppermute | solution.py:418
  46.3 43.8 %collective-permute-start.5 = (bf16[8,80,1152]{2,1,0:T(8,128)(2,1)}, bf16[8,80,1152]{2,1,0:T(8,128)(2,1)}, u32[]{:S(2)}, u32[]{:S(2)}) collective-permute-start(bf16[8,80,1152]{2,1,0:T(8,128)(2,1)} %get-tuple-element.47), channel_id=1, source_target_pairs={{0,2},{1,3},{2,0},{3,1},{4,6},{5,7},{6,4},{7,5},{8,10},{9,11},{10,... | collective-permute-start | bytes 4423688 | tf_op jit(solution)/shard_map/ppermute | solution.py:418
  47.8 42.7 %collective-permute-start.4 = (bf16[8,80,1152]{2,1,0:T(8,128)(2,1)}, bf16[8,80,1152]{2,1,0:T(8,128)(2,1)}, u32[]{:S(2)}, u32[]{:S(2)}) collective-permute-start(bf16[8,80,1152]{2,1,0:T(8,128)(2,1)} %get-tuple-element.43.refs_0_), channel_id=1, source_target_pairs={{0,1},{1,0},{2,3},{3,2},{4,5},{5,4},{6,7},{7,6},{8,9},{9,8},{10,11... | collective-permute-start | bytes 4423688 | tf_op jit(solution)/shard_map/ppermute | solution.py:418
  66.5 52.3 %all-to-all-start = ((bf16[8,64,1152]{2,1,0:T(8,128)(2,1)}), bf16[8,64,1152]{2,1,0:T(8,128)(2,1)}, u32[]{:S(2)}, u32[]{:S(2)}) async-start(bf16[8,64,1152]{2,1,0:T(8,128)(2,1)} %shard_map.106.refs_2_), calls=%async_computation | async-start | bytes 2359296 | tf_op jit(solution)/shard_map/all_to_all | solution.py:436
  95.7 16.5 %collective-permute-start.6 = (bf16[4,80,1152]{2,1,0:T(8,128)(2,1)}, bf16[4,80,1152]{2,1,0:T(8,128)(2,1)}, u32[]{:S(2)}, u32[]{:S(2)}) collective-permute-start(bf16[4,80,1152]{2,1,0:T(8,128)(2,1)} %get-tuple-element.48), channel_id=1, source_target_pairs={{0,2},{1,3},{2,0},{3,1},{4,6},{5,7},{6,4},{7,5},{8,10},{9,11},{10,... | collective-permute-start | bytes 2211848 | tf_op jit(solution)/shard_map/ppermute | solution.py:418
  97.1 15.9 %collective-permute-start.7 = (bf16[4,80,1152]{2,1,0:T(8,128)(2,1)}, bf16[4,80,1152]{2,1,0:T(8,128)(2,1)}, u32[]{:S(2)}, u32[]{:S(2)}) collective-permute-start(bf16[4,80,1152]{2,1,0:T(8,128)(2,1)} %get-tuple-element.49), channel_id=1, source_target_pairs={{0,1},{1,0},{2,3},{3,2},{4,5},{5,4},{6,7},{7,6},{8,9},{9,8},{10,11... | collective-permute-start | bytes 2211848 | tf_op jit(solution)/shard_map/ppermute | solution.py:418
  118.8 40.7 %all-to-all-start.1 = ((bf16[8,80,1152]{2,1,0:T(8,128)(2,1)}), bf16[8,80,1152]{2,1,0:T(8,128)(2,1)}, u32[]{:S(2)}, u32[]{:S(2)}) async-start(bf16[8,80,1152]{2,1,0:T(8,128)(2,1)} %shard_map.108.refs_3_), calls=%async_computation.1 | async-start | bytes 2949120 | tf_op jit(solution)/shard_map/all_to_all | solution.py:436
  123.7 48.8 %collective-permute-start.8 = (bf16[2,2,144,1152]{3,2,1,0:T(8,128)(2,1)}, bf16[2,2,144,1152]{3,2,1,0:T(8,128)(2,1)}, u32[]{:S(2)}, u32[]{:S(2)}) collective-permute-start(bf16[2,2,144,1152]{3,2,1,0:T(8,128)(2,1)} %get-tuple-element.54), channel_id=1, source_target_pairs={{0,1},{1,0},{2,3},{3,2},{4,5},{5,4},{6,7},{7,6},{8,9},{9,8},{10,11... | collective-permute-start | bytes 3981320 | tf_op jit(solution)/shard_map/ppermute | solution.py:418
  125.2 60.7 %collective-permute-start.9 = (bf16[2,2,144,1152]{3,2,1,0:T(8,128)(2,1)}, bf16[2,2,144,1152]{3,2,1,0:T(8,128)(2,1)}, u32[]{:S(2)}, u32[]{:S(2)}) collective-permute-start(bf16[2,2,144,1152]{3,2,1,0:T(8,128)(2,1)} %get-tuple-element.55), channel_id=1, source_target_pairs={{0,2},{1,3},{2,0},{3,1},{4,6},{5,7},{6,4},{7,5},{8,10},{9,11},{10,... | collective-permute-start | bytes 3981320 | tf_op jit(solution)/shard_map/ppermute | solution.py:418
  125.9 60.0 %collective-permute-start.10 = (bf16[2,2,144,1152]{3,2,1,0:T(8,128)(2,1)}, bf16[2,2,144,1152]{3,2,1,0:T(8,128)(2,1)}, u32[]{:S(2)}, u32[]{:S(2)}) collective-permute-start(bf16[2,2,144,1152]{3,2,1,0:T(8,128)(2,1)} %get-tuple-element.56), channel_id=1, source_target_pairs={{0,3},{1,2},{2,1},{3,0},{4,7},{5,6},{6,5},{7,4},{8,11},{9,10},{10,... | collective-permute-start | bytes 3981320 | tf_op jit(solution)/shard_map/ppermute | solution.py:418
  170.2 91.0 %collective-permute-start.18 = (bf16[3,2,144,1152]{3,2,1,0:T(8,128)(2,1)}, bf16[3,2,144,1152]{3,2,1,0:T(8,128)(2,1)}, u32[]{:S(2)}, u32[]{:S(2)}) collective-permute-start(bf16[3,2,144,1152]{3,2,1,0:T(8,128)(2,1)} %get-tuple-element.65), channel_id=1, source_target_pairs={{0,1},{1,0},{2,3},{3,2},{4,5},{5,4},{6,7},{7,6},{8,9},{9,8},{10,11... | collective-permute-start | bytes 5971976 | tf_op jit(solution)/shard_map/ppermute | solution.py:418
  171.7 98.8 %collective-permute-start.19 = (bf16[3,2,144,1152]{3,2,1,0:T(8,128)(2,1)}, bf16[3,2,144,1152]{3,2,1,0:T(8,128)(2,1)}, u32[]{:S(2)}, u32[]{:S(2)}) collective-permute-start(bf16[3,2,144,1152]{3,2,1,0:T(8,128)(2,1)} %get-tuple-element.66), channel_id=1, source_target_pairs={{0,2},{1,3},{2,0},{3,1},{4,6},{5,7},{6,4},{7,5},{8,10},{9,11},{10,... | collective-permute-start | bytes 5971976 | tf_op jit(solution)/shard_map/ppermute | solution.py:418
  172.4 98.1 %collective-permute-start.20 = (bf16[3,2,144,1152]{3,2,1,0:T(8,128)(2,1)}, bf16[3,2,144,1152]{3,2,1,0:T(8,128)(2,1)}, u32[]{:S(2)}, u32[]{:S(2)}) collective-permute-start(bf16[3,2,144,1152]{3,2,1,0:T(8,128)(2,1)} %get-tuple-element.67), channel_id=1, source_target_pairs={{0,3},{1,2},{2,1},{3,0},{4,7},{5,6},{6,5},{7,4},{8,11},{9,10},{10,... | collective-permute-start | bytes 5971976 | tf_op jit(solution)/shard_map/ppermute | solution.py:418
  197.8 2.0 collective-permute-start.11
  197.9 11.0 %collective-permute-start.12 = (bf16[144,1152]{1,0:T(8,128)(2,1)}, bf16[144,1152]{1,0:T(8,128)(2,1)}, u32[]{:S(2)}, u32[]{:S(2)}) collective-permute-start(bf16[144,1152]{1,0:T(8,128)(2,1)} %get-tuple-element.59), channel_id=1, source_target_pairs={{0,8},{4,12},{8,0},{12,4},{16,24},{20,28},{24,16},{28,20},{1,9},{5... | collective-permute-start | bytes 995336 | tf_op jit(solution)/shard_map/ppermute | solution.py:446
  199.8 21.0 %collective-permute-start.13 = (bf16[144,1152]{1,0:T(8,128)(2,1)}, bf16[144,1152]{1,0:T(8,128)(2,1)}, u32[]{:S(2)}, u32[]{:S(2)}) collective-permute-start(bf16[144,1152]{1,0:T(8,128)(2,1)} %get-tuple-element.60), channel_id=1, source_target_pairs={{0,12},{4,8},{8,4},{12,0},{16,28},{20,24},{24,20},{28,16},{1,13},{... | collective-permute-start | bytes 995336 | tf_op jit(solution)/shard_map/ppermute | solution.py:446
  208.9 25.7 %collective-permute-start.14 = (bf16[144,1152]{1,0:T(8,128)(2,1)}, bf16[144,1152]{1,0:T(8,128)(2,1)}, u32[]{:S(2)}, u32[]{:S(2)}) collective-permute-start(bf16[144,1152]{1,0:T(8,128)(2,1)} %get-tuple-element.61), channel_id=1, source_target_pairs={{0,16},{4,20},{8,24},{12,28},{16,0},{20,4},{24,8},{28,12},{1,17},{... | collective-permute-start | bytes 995336 | tf_op jit(solution)/shard_map/ppermute | solution.py:446
  220.9 25.4 %collective-permute-start.15 = (bf16[144,1152]{1,0:T(8,128)(2,1)}, bf16[144,1152]{1,0:T(8,128)(2,1)}, u32[]{:S(2)}, u32[]{:S(2)}) collective-permute-start(bf16[144,1152]{1,0:T(8,128)(2,1)} %get-tuple-element.62), channel_id=1, source_target_pairs={{0,20},{4,16},{8,28},{12,24},{16,4},{20,0},{24,12},{28,8},{1,21},{... | collective-permute-start | bytes 995336 | tf_op jit(solution)/shard_map/ppermute | solution.py:446
  234.6 17.9 %collective-permute-start.16 = (bf16[144,1152]{1,0:T(8,128)(2,1)}, bf16[144,1152]{1,0:T(8,128)(2,1)}, u32[]{:S(2)}, u32[]{:S(2)}) collective-permute-start(bf16[144,1152]{1,0:T(8,128)(2,1)} %get-tuple-element.63), channel_id=1, source_target_pairs={{0,24},{4,28},{8,16},{12,20},{16,8},{20,12},{24,0},{28,4},{1,25},{... | collective-permute-start | bytes 995336 | tf_op jit(solution)/shard_map/ppermute | solution.py:446
  246.2 15.0 %collective-permute-start.17 = (bf16[144,1152]{1,0:T(8,128)(2,1)}, bf16[144,1152]{1,0:T(8,128)(2,1)}, u32[]{:S(2)}, u32[]{:S(2)}) collective-permute-start(bf16[144,1152]{1,0:T(8,128)(2,1)} %get-tuple-element.64), channel_id=1, source_target_pairs={{0,28},{4,24},{8,20},{12,16},{16,12},{20,8},{24,4},{28,0},{1,29},{... | collective-permute-start | bytes 995336 | tf_op jit(solution)/shard_map/ppermute | solution.py:446
  352.1 32.4 %collective-permute-start.21 = (bf16[4,144,1152]{2,1,0:T(8,128)(2,1)}, bf16[4,144,1152]{2,1,0:T(8,128)(2,1)}, u32[]{:S(2)}, u32[]{:S(2)}) collective-permute-start(bf16[4,144,1152]{2,1,0:T(8,128)(2,1)} %get-tuple-element.73.refs_0_), channel_id=1, source_target_pairs={{0,1},{1,0},{2,3},{3,2},{4,5},{5,4},{6,7},{7,6},{8,9},{9,8},{10,11... | collective-permute-start | bytes 3981320 | tf_op jit(solution)/shard_map/ppermute | solution.py:418
  352.7 32.5 %collective-permute-start.24 = (bf16[4,144,1152]{2,1,0:T(8,128)(2,1)}, bf16[4,144,1152]{2,1,0:T(8,128)(2,1)}, u32[]{:S(2)}, u32[]{:S(2)}) collective-permute-start(bf16[4,144,1152]{2,1,0:T(8,128)(2,1)} %get-tuple-element.74.refs_1_), channel_id=1, source_target_pairs={{0,2},{1,3},{2,0},{3,1},{4,6},{5,7},{6,4},{7,5},{8,10},{9,11},{10,... | collective-permute-start | bytes 3981320 | tf_op jit(solution)/shard_map/ppermute | solution.py:418
  357.0 118.6 %collective-permute-start.23 = (bf16[4,144,1152]{2,1,0:T(8,128)(2,1)}, bf16[4,144,1152]{2,1,0:T(8,128)(2,1)}, u32[]{:S(2)}, u32[]{:S(2)}) collective-permute-start(bf16[4,144,1152]{2,1,0:T(8,128)(2,1)} %get-tuple-element.73.refs_0_), channel_id=1, source_target_pairs={{0,2},{1,3},{2,0},{3,1},{4,6},{5,7},{6,4},{7,5},{8,10},{9,11},{10,... | collective-permute-start | bytes 3981320 | tf_op jit(solution)/shard_map/ppermute | solution.py:418
  357.8 117.9 %collective-permute-start.22 = (bf16[4,144,1152]{2,1,0:T(8,128)(2,1)}, bf16[4,144,1152]{2,1,0:T(8,128)(2,1)}, u32[]{:S(2)}, u32[]{:S(2)}) collective-permute-start(bf16[4,144,1152]{2,1,0:T(8,128)(2,1)} %get-tuple-element.74.refs_1_), channel_id=1, source_target_pairs={{0,1},{1,0},{2,3},{3,2},{4,5},{5,4},{6,7},{7,6},{8,9},{9,8},{10,11... | collective-permute-start | bytes 3981320 | tf_op jit(solution)/shard_map/ppermute | solution.py:418
  384.5 91.2 %collective-permute-start.25 = (bf16[4,144,1152]{2,1,0:T(8,128)(2,1)}, bf16[4,144,1152]{2,1,0:T(8,128)(2,1)}, u32[]{:S(2)}, u32[]{:S(2)}) collective-permute-start(bf16[4,144,1152]{2,1,0:T(8,128)(2,1)} %collective-permute-done.21.refs_2_), channel_id=1, source_target_pairs={{0,2},{1,3},{2,0},{3,1},{4,6},{5,7},{6,4},{7,5},{8,10},{9,11},{10,... | collective-permute-start | bytes 3981320 | tf_op jit(solution)/shard_map/ppermute | solution.py:418
  385.2 90.5 %collective-permute-start.26 = (bf16[4,144,1152]{2,1,0:T(8,128)(2,1)}, bf16[4,144,1152]{2,1,0:T(8,128)(2,1)}, u32[]{:S(2)}, u32[]{:S(2)}) collective-permute-start(bf16[4,144,1152]{2,1,0:T(8,128)(2,1)} %collective-permute-done.24.refs_5_), channel_id=1, source_target_pairs={{0,1},{1,0},{2,3},{3,2},{4,5},{5,4},{6,7},{7,6},{8,9},{9,8},{10,11... | collective-permute-start | bytes 3981320 | tf_op jit(solution)/shard_map/ppermute | solution.py:418

commit v5 on v4

--- a/solution.py
+++ b/solution.py
@@ -248,62 +248,78 @@
     )(*arrays, *after)
 
 
-def collect_body(count, n_through, *refs):
-    half = count // 2
-    parts, low, high, sems = refs[:count], *refs[count + n_through : count + n_through + 2], refs[-1]
-    copies = [
-        pltpu.make_async_copy(part, (low, high)[k // half].at[k % half], sems.at[k])
-        for k, part in enumerate(parts)
-    ]
-    for copy in copies:
-        copy.start()
-    for copy in copies:
-        copy.wait()
-
-
-def collect(parts, through):
+def collect_body(*refs):
+    *parts, low, high, buffer, in_sems, out_sems = refs
+    half = len(parts) // 2
+
+    def arrive(k):
+        return pltpu.make_async_copy(parts[k], buffer.at[k], in_sems.at[k])
+
+    def leave(k):
+        return pltpu.make_async_copy(
+            buffer.at[k], (low, high)[k // half].at[k % half], out_sems.at[k]
+        )
+
+    for k in range(len(parts)):
+        arrive(k).start()
+    for k in range(len(parts)):
+        arrive(k).wait()
+        leave(k).start()
+    for k in range(len(parts)):
+        leave(k).wait()
+
+
+def collect(parts):
     count = len(parts)
     halves = jax.ShapeDtypeStruct((count // 2,) + parts[0].shape, parts[0].dtype)
     return pl.pallas_call(
-        functools.partial(collect_body, count, len(through)),
-        in_specs=[ANY] * (count + len(through)),
-        out_specs=[ANY] * (2 + len(through)),
-        out_shape=[halves] * 2 + [jax.ShapeDtypeStruct(x.shape, x.dtype) for x in through],
-        scratch_shapes=[pltpu.SemaphoreType.DMA((count,))],
-        input_output_aliases={count + k: 2 + k for k in range(len(through))},
+        collect_body,
+        in_specs=[ANY] * count,
+        out_specs=[ANY] * 2,
+        out_shape=[halves] * 2,
+        scratch_shapes=[pltpu.VMEM((count,) + parts[0].shape, parts[0].dtype)]
+        + [pltpu.SemaphoreType.DMA((count,))] * 2,
         compiler_params=params(),
         cost_estimate=cost(0, 2 * count * parts[0].size * 2),
-    )(*parts, *through)
-
-
-def statistics_body(n, js, *refs):
-    received = refs[:n]
-    left, right, moment, left_out, right_out, moment_out, square_out = refs[n:]
+    )(*parts)
+
+
+def moment_body(q, received, moment, moment_out, square_out):
+    g = received[0, 0, :, q * B : q * B + B].astype(jnp.float32)
+    second = 0.95 * moment[q, 0] + 0.05 * g * g
+    moment_out[q, 0] = second
+    adam = g / (jnp.sqrt(second) + 1e-08)
+    square_out[0, 0, q : q + 1, :] = jnp.full((1, LANES), jnp.sum(adam * adam))
+
+
+def gram_update_body(q, received, left, right, left_out, right_out):
+    for kind, old, new in ((1, left, left_out), (2, right, right_out)):
+        product = received[kind, 0, :, q * B : q * B + B].astype(jnp.float32)
+        new[q, 0] = 0.95 * old[q, 0] + 0.05 * product
+
+
+def by_rows_body(body, n, js, *refs):
     m = pl.program_id(0)
     for k in range(n):
 
         @pl.when(m == k)
         def _():
             for q in range(2):
-                lanes = slice(q * B, q * B + B)
-                g, left_gram, right_gram = (
-                    received[k][kind, 0, :, lanes].astype(jnp.float32) for kind in range(3)
-                )
-                left_out[q, 0] = 0.95 * left[q, 0] + 0.05 * left_gram
-                right_out[q, 0] = 0.95 * right[q, 0] + 0.05 * right_gram
-                second = 0.95 * moment[q, 0] + 0.05 * g * g
-                moment_out[q, 0] = second
-                adam = g / (jnp.sqrt(second) + 1e-08)
-                square_out[0, 0, q : q + 1, :] = jnp.full((1, LANES), jnp.sum(adam * adam))
-
-
-def statistics(js, received, olds):
+                body(q, refs[k], *refs[n:])
+
+
+def by_rows(body, kinds, js, received, olds, squares):
     n = js.shape[0]
     blocks, _, rows, _ = olds[0].shape
-    kinds, pairs, _, w = received[0].shape
+    pairs, w = received[0].shape[1], received[0].shape[3]
     own = pl.BlockSpec((2, 1, rows, B), lambda m, p, j: (p, j[m], 0, 0))
-    return pl.pallas_call(
-        functools.partial(statistics_body, n),
+    out_specs = [own] * len(olds)
+    out_shape = [jax.ShapeDtypeStruct(old.shape, jnp.float32) for old in olds]
+    if squares:
+        out_specs.append(pl.BlockSpec((1, 1, 8, LANES), lambda m, p, j: (m, p, 0, 0)))
+        out_shape.append(jax.ShapeDtypeStruct((n, pairs, 8, LANES), jnp.float32))
+    return pl.pallas_call(
+        functools.partial(by_rows_body, body, n),
         grid_spec=pltpu.PrefetchScalarGridSpec(
             num_scalar_prefetch=1,
             grid=(n, pairs),
@@ -315,11 +331,9 @@
                 for k in range(n)
             ]
             + [own] * len(olds),
-            out_specs=[own] * len(olds)
-            + [pl.BlockSpec((1, 1, 8, LANES), lambda m, p, j: (m, p, 0, 0))],
+            out_specs=out_specs,
         ),
-        out_shape=[jax.ShapeDtypeStruct(old.shape, jnp.float32) for old in olds]
-        + [jax.ShapeDtypeStruct((n, pairs, 8, LANES), jnp.float32)],
+        out_shape=out_shape,
         compiler_params=params(),
         cost_estimate=cost(0, olds[0].size * 10 * len(olds)),
     )(js, *received, *olds)
@@ -421,20 +435,29 @@
         return x.reshape(row_blocks, -1, sub_count * rd, B)
 
     first = rows // 64 * 16
-    chunks = ((0, first), (2 * first, rows // 2 - first))
-    after, early, blocks = (), [], []
-    for chunk in chunks:
-        x, y = arrange(cols[:2].reshape(-1), grad, *chunk, after=after)
-        early.append((swap(x, 1), swap(y, 2)))
-        after = (x,)
-    roots = pack_roots(js, as_rows(root_left), as_rows(root_right), after)
-    after = (roots[0],)
-    for (x, y), chunk in zip(early, chunks):
-        y_a, x_b = arrange(cols[2], grad, *chunk, [((x, 0), (y, 0))], after=after)
-        terms = [((x, half), (y, half)), ((swap(y_a, 2), 0), (swap(x_b, 1), 0))]
-        (owned,) = arrange(cols[3], grad, *chunk, terms, halves=False)
-        blocks.append(lax.all_to_all(owned, "fsdp", split_axis=0, concat_axis=0, tiled=True))
-        after = (owned,)
+    lower, upper = (0, first), (2 * first, rows // 2 - first)
+
+    def exchange(x):
+        return lax.all_to_all(x, "fsdp", split_axis=0, concat_axis=0, tiled=True)
+
+    x, y = arrange(cols[:2].reshape(-1), grad, *lower)
+    early = (swap(x, 1), swap(y, 2))
+    far_a, far_b = arrange(cols[:2, :half].reshape(-1), grad, *upper, after=(x,))
+    far = (swap(far_a, 1), swap(far_b, 2))
+    x_a, y_b = arrange(cols[:2, half:].reshape(-1), grad, *upper, after=(far_a,))
+    near = (swap(x_a, 1), swap(y_b, 2))
+    roots = pack_roots(js, as_rows(root_left), as_rows(root_right), (x_a,))
+    y_a, x_b = arrange(cols[2], grad, *lower, [[(x, 0) for x in early]], after=(roots[0],))
+    cross = (swap(y_a, 2), swap(x_b, 1))
+    y_a, x_b = arrange(cols[2], grad, *upper, [[(x, 0) for x in far]], after=(y_a,))
+    late = (swap(y_a, 2), swap(x_b, 1))
+    terms = [[(x, half) for x in early], [(x, 0) for x in cross]]
+    (owned,) = arrange(cols[3], grad, *lower, terms, halves=False, after=(y_a,))
+    blocks = [exchange(owned)]
+    terms = [[(x, 0) for x in near], [(x, 0) for x in late]]
+    (owned,) = arrange(cols[3], grad, *upper, terms, halves=False, after=(owned,))
+    blocks.append(exchange(owned))
+    after = (owned,)
     sent = follow(roots[1:], after)
     roots = [roots[0]] + [swap(x, k) for k, x in zip((1, 2, 3), sent)]
 
@@ -446,15 +469,15 @@
         lax.ppermute(direction[k], "fsdp", [(i, i ^ k) for i in range(owners)])
         for k in range(1, owners)
     ]
-    a, b, *received[1:] = collect(direction, received[1:])
-
-    x_a, y_b, x_b, y_a = swap(a, 1), swap(b, 2), swap(b, 1), swap(a, 2)
-    gathered = (a, b, x_a, x_b, y_a, y_b, swap(x_a, 2), swap(y_b, 1))
-
-    left_new, right_new, moment, adam_square = statistics(
-        js, received, [as_rows(x) for x in (stats_left, stats_right, second_moment)]
-    )
-
+    a, b = collect(direction)
+
+    x_a, y_b = swap(a, 1), swap(b, 2)
+    late_a, late_b = follow((a, b), received[1:])
+    x_b, y_a = swap(late_b, 1), swap(late_a, 2)
+
+    moment, adam_square = by_rows(
+        moment_body, 1, js, received, [as_rows(second_moment)], True
+    )
     adam_square = adam_square[:, :, :2, 0].reshape(replicas, row_blocks)
     slot_ids = jnp.arange(replicas, dtype=jnp.int32)
     adam_square = jnp.sum(
@@ -471,8 +494,13 @@
     )
     scale = jnp.sum(jnp.where(row_slots[:, None] == column_ids, row_ratio, 0.0), axis=1)
 
+    x_a, y_b = follow((x_a, y_b), (scale, x_b, y_a))
+    left_new, right_new = by_rows(
+        gram_update_body, 3, js, received, [as_rows(stats_left), as_rows(stats_right)], False
+    )
     part = (row_slots // replicas) ^ f
     src = 2 * (lax.rem(row_slots, replicas) ^ r) + part // half
+    gathered = (late_a, late_b, x_a, x_b, y_a, y_b, swap(x_a, 2), swap(y_b, 1))
     update = restore(src, lax.rem(part, half), scale, gathered)
     return (
         update,

time: 486 us -> 444 us (0.914)
  Pallas kernels: 173 us -> 101 us
  waiting for transfers between devices: 182 us -> 232 us
  blocking collectives: 62.9 us -> 43.5 us
    pallas_call x2 -> x3, Pallas kernels: 102 us -> 28.8 us  [the longest x2 26.2 us: by_rows(): pl.pallas_call(functools.partial(by_rows_body, body, n), grid_spec=pltpu....]
    ppermute x20 -> x22, waiting for transfers between devices: 103 us -> 163 us  [swap(): return lax.ppermute(x, 'replica', [(i, i ^ k) for i in range(replicas)])]
    psum x1, blocking collectives: 62.9 us -> 43.5 us  [owner_local(): lax.psum(jnp.where(owner_place, squares, 0.0), ('fsdp', 'replica'))]
    ppermute x7, waiting for transfers between devices: 46.9 us -> 36.7 us  [owner_local(): lax.ppermute(direction[k], 'fsdp', [(i, i ^ k) for i in range(owners)])]
    ppermute x7, starting transfers between devices: 16.4 us -> 10.2 us  [owner_local(): lax.ppermute(direction[k], 'fsdp', [(i, i ^ k) for i in range(owners)])]
    ppermute x20 -> x22, starting transfers between devices: 24.7 us -> 26.8 us  [swap(): return lax.ppermute(x, 'replica', [(i, i ^ k) for i in range(replicas)])]
    pallas_call x6 -> x7, Pallas kernels: 31 us -> 32.4 us  [arrange(): pl.pallas_call(functools.partial(arrange_body, len(adds) // 2, [part[1] f...]
  transfers between devices with their start and end apart: 29 -> 31, of which waited for: 18 -> 18; matrix products, arithmetic and copies ran while one was open for 2% -> 3% of each run, Pallas kernels for 15% -> 16%
where the time goes in v5:
time: 444 us; the launch traced here: 442 us
  waiting for transfers between devices  232 us (52%)
  Pallas kernels  101 us (23%)
  starting transfers between devices  46.8 us (11%)
  blocking collectives  43.5 us (10%)
  other arithmetic  9.48 us (2%)
  local copies, waits for them, and re-layouts  8.26 us (2%)
    ppermute x22, waiting for transfers between devices, swap(): return lax.ppermute(x, 'replica', [(i, i ^ k) for i in range(replicas)])  163 us
    psum x1, blocking collectives, owner_local(): lax.psum(jnp.where(owner_place, squares, 0.0), ('fsdp', 'replica'))  43.5 us
    ppermute x7, waiting for transfers between devices, owner_local(): lax.ppermute(direction[k], 'fsdp', [(i, i ^ k) for i in range(owners)])  36.7 us
    pallas_call x7, Pallas kernels, arrange(): pl.pallas_call(functools.partial(arrange_body, len(adds) // 2, [part[1] f...  32.4 us
    all_to_all x2, waiting for transfers between devices, exchange(): return lax.all_to_all(x, 'fsdp', split_axis=0, concat_axis=0, tiled=True)  32.3 us
    ppermute x22, starting transfers between devices, swap(): return lax.ppermute(x, 'replica', [(i, i ^ k) for i in range(replicas)])  26.8 us
    pallas_call x2, Pallas kernels, by_rows(): pl.pallas_call(functools.partial(by_rows_body, body, n), grid_spec=pltpu....  26.2 us
    pallas_call x1, Pallas kernels, direct(): pl.pallas_call(functools.partial(direct_body, n, rd, len(chunks), len(aft...  11.8 us
  transfers between devices with their start and end apart: 31, of which 18 were waited for; matrix products, arithmetic and copies ran while one was open for 3% of the time, Pallas kernels for 16%

profile of v5, /device:TPU:0, one launch (start us, length us, event | category | flops | bytes accessed | tf_op | source)
XLA Modules:
  0.0 442.4 jit_solution(260472657064913697)
XLA Ops:
  3.9 4.8 %shard_map.102 = (bf16[8,64,1152]{2,1,0:T(8,128)(2,1)}, bf16[8,64,1152]{2,1,0:T(8,128)(2,1)}) custom-call(s32[16]{0:T(128)} %reshape.235.cols, bf16[288,18432]{1,0:T(8,128)(2,1)} %bitcast.35), custom_call_target="tpu_custom_call" | custom-call | bytes 4718592 | tf_op jit(solution)/shard_map/pallas_call | solution.py:65
  8.7 3.0 collective-permute-start.1
  15.2 3.7 shard_map.103
  20.9 3.7 shard_map.104
  25.2 9.0 %shard_map.105 = (bf16[2,2,144,1152]{3,2,1,0:T(8,128)(2,1)}, bf16[2,2,144,1152]{3,2,1,0:T(8,128)(2,1)}, bf16[2,2,144,1152]{3,2,1,0:T(8,128)(2,1)}, bf16[2,2,144,1152]{3,2,1,0:T(8,128)(2,1)}) custom-call(s32[4]{0:T(128)} %iota_xor_fusion.js, bf16[4,4,144,576]{3,2,1,0:T(8,128)(2,1)} %bitcast.45, bf16[4,4,144,576]{3,2,1,0:T(8,128)(2,1)} %bitcast.46, ...), custom_call_target="tpu_custom_call" | custom-call | bytes 10616832 | tf_op jit(solution)/shard_map/pallas_call | solution.py:100
  35.6 3.3 collective-permute-done.1.refs_1_
  40.9 4.8 %shard_map.106 = (bf16[4,64,1152]{2,1,0:T(8,128)(2,1)}, bf16[4,64,1152]{2,1,0:T(8,128)(2,1)}) custom-call(s32[8]{0:T(128)} %get-tuple-element.101.cols, bf16[288,18432]{1,0:T(8,128)(2,1)} %bitcast.38, bf16[8,64,1152]{2,1,0:T(8,128)(2,1)} %collective-permute-done.refs_0_, bf16[8,64,1152]{2,1,0:T(8,128)(2,1)} %collective-permute-done.1.refs_1_, ...), custom_call_target="tpu_custom_call" | custom-call | bytes 3538944 | tf_op jit(solution)/shard_map/pallas_call | solution.py:65
  47.8 6.8 %collective-permute-done.5.refs_1_ = bf16[4,80,1152]{2,1,0:T(8,128)(2,1)} collective-permute-done((bf16[4,80,1152]{2,1,0:T(8,128)(2,1)}, bf16[4,80,1152]{2,1,0:T(8,128)(2,1)}, u32[]{:S(2)}, u32[]{:S(2)}) %collective-permute-start.5) | collective-permute-done | bytes 737312 | tf_op jit(solution)/shard_map/ppermute | solution.py:432
  56.7 4.7 %shard_map.107 = (bf16[4,80,1152]{2,1,0:T(8,128)(2,1)}, bf16[4,80,1152]{2,1,0:T(8,128)(2,1)}) custom-call(s32[8]{0:T(128)} %get-tuple-element.101.cols, bf16[288,18432]{1,0:T(8,128)(2,1)} %bitcast.39, bf16[4,80,1152]{2,1,0:T(8,128)(2,1)} %collective-permute-done.4.refs_0_, bf16[4,80,1152]{2,1,0:T(8,128)(2,1)} %collective-permute-done.5.refs_1_, ...), custom_call_target="tpu_custom_call" | custom-call | bytes 4423680 | tf_op jit(solution)/shard_map/pallas_call | solution.py:65
  61.4 6.5 %collective-permute-done.3.refs_3_ = bf16[4,64,1152]{2,1,0:T(8,128)(2,1)} collective-permute-done((bf16[4,64,1152]{2,1,0:T(8,128)(2,1)}, bf16[4,64,1152]{2,1,0:T(8,128)(2,1)}, u32[]{:S(2)}, u32[]{:S(2)}) %collective-permute-start.3) | collective-permute-done | bytes 589856 | tf_op jit(solution)/shard_map/ppermute | solution.py:432
  67.9 5.3 %shard_map.108.refs_4_ = bf16[8,64,1152]{2,1,0:T(8,128)(2,1)} custom-call(s32[8]{0:T(128)} %get-tuple-element.102.cols, bf16[288,18432]{1,0:T(8,128)(2,1)} %bitcast.40, bf16[8,64,1152]{2,1,0:T(8,128)(2,1)} %collective-permute-done.refs_0_, bf16[8,64,1152]{2,1,0:T(8,128)(2,1)} %collective-permute-done.1.refs_1_, ...), custom_call_target="tpu_custom_call" | custom-call | bytes 4718592 | tf_op jit(solution)/shard_map/pallas_call | solution.py:65
  73.2 5.0 %all-to-all-start = ((bf16[8,64,1152]{2,1,0:T(8,128)(2,1)}), bf16[8,64,1152]{2,1,0:T(8,128)(2,1)}, u32[]{:S(2)}, u32[]{:S(2)}) async-start(bf16[8,64,1152]{2,1,0:T(8,128)(2,1)} %shard_map.108.refs_4_), calls=%async_computation | async-start | bytes 2359296 | tf_op jit(solution)/shard_map/all_to_all | solution.py:441
  82.4 16.9 %collective-permute-done.7.refs_1_ = bf16[4,80,1152]{2,1,0:T(8,128)(2,1)} collective-permute-done((bf16[4,80,1152]{2,1,0:T(8,128)(2,1)S(1)}, bf16[4,80,1152]{2,1,0:T(8,128)(2,1)}, u32[]{:S(2)}, u32[]{:S(2)}) %collective-permute-start.7) | collective-permute-done | bytes 737312 | tf_op jit(solution)/shard_map/ppermute | solution.py:432
  99.3 13.8 %collective-permute-done.9.refs_3_ = bf16[4,80,1152]{2,1,0:T(8,128)(2,1)} collective-permute-done((bf16[4,80,1152]{2,1,0:T(8,128)(2,1)}, bf16[4,80,1152]{2,1,0:T(8,128)(2,1)}, u32[]{:S(2)}, u32[]{:S(2)}) %collective-permute-start.9) | collective-permute-done | bytes 737312 | tf_op jit(solution)/shard_map/ppermute | solution.py:432
  114.3 5.4 %shard_map.109.refs_3_ = bf16[8,80,1152]{2,1,0:T(8,128)(2,1)} custom-call(s32[8]{0:T(128)} %get-tuple-element.102.cols, bf16[288,18432]{1,0:T(8,128)(2,1)} %bitcast.41, bf16[4,80,1152]{2,1,0:T(8,128)(2,1)} %collective-permute-done.6.refs_0_, bf16[4,80,1152]{2,1,0:T(8,128)(2,1)} %collective-permute-done.7.refs_1_, ...), custom_call_target="tpu_custom_call" | custom-call | bytes 5898240 | tf_op jit(solution)/shard_map/pallas_call | solution.py:65
  119.6 4.8 %all-to-all-start.1 = ((bf16[8,80,1152]{2,1,0:T(8,128)(2,1)}), bf16[8,80,1152]{2,1,0:T(8,128)(2,1)}, u32[]{:S(2)}, u32[]{:S(2)}) async-start(bf16[8,80,1152]{2,1,0:T(8,128)(2,1)} %shard_map.109.refs_3_), calls=%async_computation.1 | async-start | bytes 2949120 | tf_op jit(solution)/shard_map/all_to_all | solution.py:441
  128.0 32.3 %all-to-all-done.1.refs_1_ = bf16[8,80,1152]{2,1,0:T(8,128)(2,1)} async-done(((bf16[8,80,1152]{2,1,0:T(8,128)(2,1)}), bf16[8,80,1152]{2,1,0:T(8,128)(2,1)}, u32[]{:S(2)}, u32[]{:S(2)}) %all-to-all-start.1) | async-done | bytes 1474592 | tf_op jit(solution)/shard_map/all_to_all | solution.py:441
  160.2 10.7 %shard_map.110 = (bf16[3,2,144,1152]{3,2,1,0:T(8,128)(2,1)}, bf16[3,2,144,1152]{3,2,1,0:T(8,128)(2,1)}, bf16[3,2,144,1152]{3,2,1,0:T(8,128)(2,1)}, bf16[3,2,144,1152]{3,2,1,0:T(8,128)(2,1)}) custom-call(s32[4]{0:T(128)} %iota_xor_fusion.js, bf16[8,64,1152]{2,1,0:T(8,128)(2,1)} %all-to-all-done.refs_0_, bf16[8,80,1152]{2,1,0:T(8,128)(2,1)} %all-to-all-done.1.refs_1_), custom_call_target="tpu_custom_call" | custom-call | flops 3057647616 | bytes 10616832 | tf_op jit(solution)/shard_map/pallas_call | solution.py:160
  171.0 14.0 %collective-permute-done.14.refs_4_ = bf16[2,2,144,1152]{3,2,1,0:T(8,128)(2,1)} collective-permute-done((bf16[2,2,144,1152]{3,2,1,0:T(8,128)(2,1)}, bf16[2,2,144,1152]{3,2,1,0:T(8,128)(2,1)}, u32[]{:S(2)}, u32[]{:S(2)}) %collective-permute-start.14) | collective-permute-done | bytes 1327136 | tf_op jit(solution)/shard_map/ppermute | solution.py:432
  185.0 11.8 %shard_map.113 = (bf16[144,1152]{1,0:T(8,128)(2,1)}, bf16[144,1152]{1,0:T(8,128)(2,1)}, bf16[144,1152]{1,0:T(8,128)(2,1)}, bf16[144,1152]{1,0:T(8,128)(2,1)}, bf...) custom-call(s32[4]{0:T(128)} %iota_xor_fusion.js, ...), custom_call_target="tpu_custom_call" | custom-call | flops 3057647616 | bytes 10616832 | tf_op jit(solution)/shard_map/pallas_call | solution.py:219
  202.9 18.7 %collective-permute-done.17.refs_2_ = bf16[144,1152]{1,0:T(8,128)(2,1)} collective-permute-done((bf16[144,1152]{1,0:T(8,128)(2,1)}, bf16[144,1152]{1,0:T(8,128)(2,1)}, u32[]{:S(2)}, u32[]{:S(2)}) %collective-permute-start.17) | collective-permute-done | bytes 331808 | tf_op jit(solution)/shard_map/ppermute | solution.py:469
  222.7 5.0 %collective-permute-done.18.refs_3_ = bf16[144,1152]{1,0:T(8,128)(2,1)} collective-permute-done((bf16[144,1152]{1,0:T(8,128)(2,1)}, bf16[144,1152]{1,0:T(8,128)(2,1)}, u32[]{:S(2)}, u32[]{:S(2)}) %collective-permute-start.18) | collective-permute-done | bytes 331808 | tf_op jit(solution)/shard_map/ppermute | solution.py:469
  230.7 4.2 collective-permute-start.22
  234.8 7.2 %collective-permute-done.21.refs_6_ = bf16[144,1152]{1,0:T(8,128)(2,1)} collective-permute-done((bf16[144,1152]{1,0:T(8,128)(2,1)}, bf16[144,1152]{1,0:T(8,128)(2,1)}, u32[]{:S(2)}, u32[]{:S(2)}) %collective-permute-start.21) | collective-permute-done | bytes 331808 | tf_op jit(solution)/shard_map/ppermute | solution.py:469
  242.0 5.9 %collective-permute-done.22.refs_7_ = bf16[144,1152]{1,0:T(8,128)(2,1)} collective-permute-done((bf16[144,1152]{1,0:T(8,128)(2,1)}, bf16[144,1152]{1,0:T(8,128)(2,1)}, u32[]{:S(2)}, u32[]{:S(2)}) %collective-permute-start.22) | collective-permute-done | bytes 331808 | tf_op jit(solution)/shard_map/ppermute | solution.py:469
  254.5 64.0 %collective-permute-done.23.refs_0_ = bf16[4,144,1152]{2,1,0:T(8,128)(2,1)} collective-permute-done((bf16[4,144,1152]{2,1,0:T(8,128)(2,1)}, bf16[4,144,1152]{2,1,0:T(8,128)(2,1)}, u32[]{:S(2)}, u32[]{:S(2)}) %collective-permute-start.23) | collective-permute-done | bytes 1327136 | tf_op jit(solution)/shard_map/ppermute | solution.py:432
  318.5 18.9 %collective-permute-done.24.refs_1_ = bf16[4,144,1152]{2,1,0:T(8,128)(2,1)} collective-permute-done((bf16[4,144,1152]{2,1,0:T(8,128)(2,1)}, bf16[4,144,1152]{2,1,0:T(8,128)(2,1)}, u32[]{:S(2)}, u32[]{:S(2)}) %collective-permute-start.24) | collective-permute-done | bytes 1327136 | tf_op jit(solution)/shard_map/ppermute | solution.py:432
  341.0 12.0 %shard_map.111 = (f32[4,4,144,576]{3,2,1,0:T(8,128)}, f32[4,2,8,128]{3,2,1,0:T(8,128)}) custom-call(s32[4]{0:T(128)} %iota_xor_fusion.js, bf16[3,2,144,1152]{3,2,1,0:T(8,128)(2,1)} %get-tuple-element.55.refs_0_.refs_6_, bf16[3,2,144,1152]{3,2,1,0:T(8,128)(2,1)} %collective-permute-done.10.refs_1_.refs_2_, ...), custom_call_target="tpu_custom_call" | custom-call | bytes 13271040 | tf_op jit(solution)/shard_map/pallas_call | solution.py:321
  356.3 43.5 %psum.7 = f32[8,2,4,4]{2,0,3,1:T(8,128)S(1)} all-reduce(f32[8,2,4,4]{2,0,3,1:T(8,128)S(1)} %broadcast_select_fusion), channel_id=1, replica_groups=mesh['fsdp'=8,'replica'=4] {'fsdp','replica'}, use_global_device_ids=true, to_apply=%region_2.3 | all-reduce | flops 256 | bytes 2048 | tf_op jit(solution)/shard_map/psum | solution.py:490
  406.0 14.2 %shard_map.118 = (f32[4,4,144,576]{3,2,1,0:T(8,128)}, f32[4,4,144,576]{3,2,1,0:T(8,128)}) custom-call(s32[4]{0:T(128)} %iota_xor_fusion.js, bf16[3,2,144,1152]{3,2,1,0:T(8,128)(2,1)} %get-tuple-element.55.refs_0_.refs_6_, bf16[3,2,144,1152]{3,2,1,0:T(8,128)(2,1)} %collective-permute-done.10.refs_1_.refs_2_, ...), custom_call_target="tpu_custom_call" | custom-call | bytes 26542080 | tf_op jit(solution)/shard_map/pallas_call | solution.py:321
  420.2 11.9 %collective-permute-done.27.refs_6_ = bf16[4,144,1152]{2,1,0:T(8,128)(2,1)} collective-permute-done((bf16[4,144,1152]{2,1,0:T(8,128)(2,1)}, bf16[4,144,1152]{2,1,0:T(8,128)(2,1)}, u32[]{:S(2)}, u32[]{:S(2)}) %collective-permute-start.27) | collective-permute-done | bytes 1327136 | tf_op jit(solution)/shard_map/ppermute | solution.py:432
  433.5 8.7 %shard_map.117 = bf16[288,18432]{1,0:T(8,128)(2,1)} custom-call(s32[32]{0:T(128)} %multiply_add_fusion.src, s32[32]{0:T(128)} %get-tuple-element.96.item, f32[32]{0:T(128)} %select_reduce_fusion.refs_2_.scale, bf16[4,144,1152]{2,1,0:T(8,128)(2,1)} %get-tuple-element.77.refs_0_, bf16[4,144,1152]{2,1,0:T(8,128)(2,1)} %get-tuple-element.78.refs_1_, ...), custom_call_target="tpu_custom_call" | custom-call | bytes 21233664 | tf_op jit(solution)/shard_map/pallas_call | solution.py:389
  (92 shorter events, 57.0 us)
Async XLA Ops:
  8.7 30.1 %collective-permute-start.1 = (bf16[8,64,1152]{2,1,0:T(8,128)(2,1)}, bf16[8,64,1152]{2,1,0:T(8,128)(2,1)}, u32[]{:S(2)}, u32[]{:S(2)}) collective-permute-start(bf16[8,64,1152]{2,1,0:T(8,128)(2,1)} %get-tuple-element.45), channel_id=1, source_target_pairs={{0,2},{1,3},{2,0},{3,1},{4,6},{5,7},{6,4},{7,5},{8,10},{9,11},{10,... | collective-permute-start | bytes 3538952 | tf_op jit(solution)/shard_map/ppermute | solution.py:432
  11.7 29.2 %collective-permute-start = (bf16[8,64,1152]{2,1,0:T(8,128)(2,1)}, bf16[8,64,1152]{2,1,0:T(8,128)(2,1)}, u32[]{:S(2)}, u32[]{:S(2)}) collective-permute-start(bf16[8,64,1152]{2,1,0:T(8,128)(2,1)} %get-tuple-element.44.refs_0_), channel_id=1, source_target_pairs={{0,1},{1,0},{2,3},{3,2},{4,5},{5,4},{6,7},{7,6},{8,9},{9,8},{10,11... | collective-permute-start | bytes 3538952 | tf_op jit(solution)/shard_map/ppermute | solution.py:432
  18.9 35.7 %collective-permute-start.5 = (bf16[4,80,1152]{2,1,0:T(8,128)(2,1)}, bf16[4,80,1152]{2,1,0:T(8,128)(2,1)}, u32[]{:S(2)}, u32[]{:S(2)}) collective-permute-start(bf16[4,80,1152]{2,1,0:T(8,128)(2,1)} %get-tuple-element.51), channel_id=1, source_target_pairs={{0,2},{1,3},{2,0},{3,1},{4,6},{5,7},{6,4},{7,5},{8,10},{9,11},{10,... | collective-permute-start | bytes 2211848 | tf_op jit(solution)/shard_map/ppermute | solution.py:432
  19.5 37.2 %collective-permute-start.4 = (bf16[4,80,1152]{2,1,0:T(8,128)(2,1)}, bf16[4,80,1152]{2,1,0:T(8,128)(2,1)}, u32[]{:S(2)}, u32[]{:S(2)}) collective-permute-start(bf16[4,80,1152]{2,1,0:T(8,128)(2,1)} %get-tuple-element.46.refs_0_), channel_id=1, source_target_pairs={{0,1},{1,0},{2,3},{3,2},{4,5},{5,4},{6,7},{7,6},{8,9},{9,8},{10,11... | collective-permute-start | bytes 2211848 | tf_op jit(solution)/shard_map/ppermute | solution.py:432
  45.7 22.2 %collective-permute-start.3 = (bf16[4,64,1152]{2,1,0:T(8,128)(2,1)}, bf16[4,64,1152]{2,1,0:T(8,128)(2,1)}, u32[]{:S(2)}, u32[]{:S(2)}) collective-permute-start(bf16[4,64,1152]{2,1,0:T(8,128)(2,1)} %get-tuple-element.50), channel_id=1, source_target_pairs={{0,1},{1,0},{2,3},{3,2},{4,5},{5,4},{6,7},{7,6},{8,9},{9,8},{10,11... | collective-permute-start | bytes 1769480 | tf_op jit(solution)/shard_map/ppermute | solution.py:432
  47.3 20.6 %collective-permute-start.2 = (bf16[4,64,1152]{2,1,0:T(8,128)(2,1)}, bf16[4,64,1152]{2,1,0:T(8,128)(2,1)}, u32[]{:S(2)}, u32[]{:S(2)}) collective-permute-start(bf16[4,64,1152]{2,1,0:T(8,128)(2,1)} %get-tuple-element.49.refs_2_), channel_id=1, source_target_pairs={{0,2},{1,3},{2,0},{3,1},{4,6},{5,7},{6,4},{7,5},{8,10},{9,11},{10,... | collective-permute-start | bytes 1769480 | tf_op jit(solution)/shard_map/ppermute | solution.py:432
  73.2 7.6 %copy-start.1 = (bf16[4,80,1152]{2,1,0:T(8,128)(2,1)S(1)}, bf16[4,80,1152]{2,1,0:T(8,128)(2,1)}, u32[]{:S(2)}) copy-start(bf16[4,80,1152]{2,1,0:T(8,128)(2,1)} %get-tuple-element.52.refs_4_) | copy-start | bytes 2211844
  73.2 46.4 %all-to-all-start = ((bf16[8,64,1152]{2,1,0:T(8,128)(2,1)}), bf16[8,64,1152]{2,1,0:T(8,128)(2,1)}, u32[]{:S(2)}, u32[]{:S(2)}) async-start(bf16[8,64,1152]{2,1,0:T(8,128)(2,1)} %shard_map.108.refs_4_), calls=%async_computation | async-start | bytes 2359296 | tf_op jit(solution)/shard_map/all_to_all | solution.py:441
  78.3 21.0 %collective-permute-start.6 = (bf16[4,80,1152]{2,1,0:T(8,128)(2,1)S(1)}, bf16[4,80,1152]{2,1,0:T(8,128)(2,1)}, u32[]{:S(2)}, u32[]{:S(2)}) collective-permute-start(bf16[4,80,1152]{2,1,0:T(8,128)(2,1)S(1)} %copy-done), channel_id=1, source_target_pairs={{0,1},{1,0},{2,3},{3,2},{4,5},{5,4},{6,7},{7,6},{8,9},{9,8},{10,11... | collective-permute-start | bytes 2211848 | tf_op jit(solution)/shard_map/ppermute | solution.py:432
  79.8 19.4 %collective-permute-start.7 = (bf16[4,80,1152]{2,1,0:T(8,128)(2,1)S(1)}, bf16[4,80,1152]{2,1,0:T(8,128)(2,1)}, u32[]{:S(2)}, u32[]{:S(2)}) collective-permute-start(bf16[4,80,1152]{2,1,0:T(8,128)(2,1)S(1)} %copy-done.4), channel_id=1, source_target_pairs={{0,2},{1,3},{2,0},{3,1},{4,6},{5,7},{6,4},{7,5},{8,10},{9,11},{10,... | collective-permute-start | bytes 2211848 | tf_op jit(solution)/shard_map/ppermute | solution.py:432
  80.3 32.7 %collective-permute-start.9 = (bf16[4,80,1152]{2,1,0:T(8,128)(2,1)}, bf16[4,80,1152]{2,1,0:T(8,128)(2,1)}, u32[]{:S(2)}, u32[]{:S(2)}) collective-permute-start(bf16[4,80,1152]{2,1,0:T(8,128)(2,1)} %get-tuple-element.54), channel_id=1, source_target_pairs={{0,1},{1,0},{2,3},{3,2},{4,5},{5,4},{6,7},{7,6},{8,9},{9,8},{10,11... | collective-permute-start | bytes 2211848 | tf_op jit(solution)/shard_map/ppermute | solution.py:432
  80.9 33.4 %collective-permute-start.8 = (bf16[4,80,1152]{2,1,0:T(8,128)(2,1)S(1)}, bf16[4,80,1152]{2,1,0:T(8,128)(2,1)}, u32[]{:S(2)}, u32[]{:S(2)}) collective-permute-start(bf16[4,80,1152]{2,1,0:T(8,128)(2,1)S(1)} %copy-done.1), channel_id=1, source_target_pairs={{0,2},{1,3},{2,0},{3,1},{4,6},{5,7},{6,4},{7,5},{8,10},{9,11},{10,... | collective-permute-start | bytes 2211848 | tf_op jit(solution)/shard_map/ppermute | solution.py:432
  119.6 40.6 %all-to-all-start.1 = ((bf16[8,80,1152]{2,1,0:T(8,128)(2,1)}), bf16[8,80,1152]{2,1,0:T(8,128)(2,1)}, u32[]{:S(2)}, u32[]{:S(2)}) async-start(bf16[8,80,1152]{2,1,0:T(8,128)(2,1)} %shard_map.109.refs_3_), calls=%async_computation.1 | async-start | bytes 2949120 | tf_op jit(solution)/shard_map/all_to_all | solution.py:441
  124.4 46.6 %collective-permute-start.13 = (bf16[2,2,144,1152]{3,2,1,0:T(8,128)(2,1)}, bf16[2,2,144,1152]{3,2,1,0:T(8,128)(2,1)}, u32[]{:S(2)}, u32[]{:S(2)}) collective-permute-start(bf16[2,2,144,1152]{3,2,1,0:T(8,128)(2,1)} %get-tuple-element.63), channel_id=1, source_target_pairs={{0,1},{1,0},{2,3},{3,2},{4,5},{5,4},{6,7},{7,6},{8,9},{9,8},{10,11... | collective-permute-start | bytes 3981320 | tf_op jit(solution)/shard_map/ppermute | solution.py:432
  125.0 59.9 %collective-permute-start.14 = (bf16[2,2,144,1152]{3,2,1,0:T(8,128)(2,1)}, bf16[2,2,144,1152]{3,2,1,0:T(8,128)(2,1)}, u32[]{:S(2)}, u32[]{:S(2)}) collective-permute-start(bf16[2,2,144,1152]{3,2,1,0:T(8,128)(2,1)} %get-tuple-element.64), channel_id=1, source_target_pairs={{0,2},{1,3},{2,0},{3,1},{4,6},{5,7},{6,4},{7,5},{8,10},{9,11},{10,... | collective-permute-start | bytes 3981320 | tf_op jit(solution)/shard_map/ppermute | solution.py:432
  125.5 59.4 %collective-permute-start.15 = (bf16[2,2,144,1152]{3,2,1,0:T(8,128)(2,1)}, bf16[2,2,144,1152]{3,2,1,0:T(8,128)(2,1)}, u32[]{:S(2)}, u32[]{:S(2)}) collective-permute-start(bf16[2,2,144,1152]{3,2,1,0:T(8,128)(2,1)} %get-tuple-element.65), channel_id=1, source_target_pairs={{0,3},{1,2},{2,1},{3,0},{4,7},{5,6},{6,5},{7,4},{8,11},{9,10},{10,... | collective-permute-start | bytes 3981320 | tf_op jit(solution)/shard_map/ppermute | solution.py:432
  196.8 4.5 %collective-permute-start.16 = (bf16[144,1152]{1,0:T(8,128)(2,1)}, bf16[144,1152]{1,0:T(8,128)(2,1)}, u32[]{:S(2)}, u32[]{:S(2)}) collective-permute-start(bf16[144,1152]{1,0:T(8,128)(2,1)} %get-tuple-element.68), channel_id=1, source_target_pairs={{0,4},{4,0},{8,12},{12,8},{16,20},{20,16},{24,28},{28,24},{1,5},{5... | collective-permute-start | bytes 995336 | tf_op jit(solution)/shard_map/ppermute | solution.py:469
  196.9 24.6 %collective-permute-start.17 = (bf16[144,1152]{1,0:T(8,128)(2,1)}, bf16[144,1152]{1,0:T(8,128)(2,1)}, u32[]{:S(2)}, u32[]{:S(2)}) collective-permute-start(bf16[144,1152]{1,0:T(8,128)(2,1)} %get-tuple-element.69), channel_id=1, source_target_pairs={{0,8},{4,12},{8,0},{12,4},{16,24},{20,28},{24,16},{28,20},{1,9},{5... | collective-permute-start | bytes 995336 | tf_op jit(solution)/shard_map/ppermute | solution.py:469
  198.6 29.1 %collective-permute-start.18 = (bf16[144,1152]{1,0:T(8,128)(2,1)}, bf16[144,1152]{1,0:T(8,128)(2,1)}, u32[]{:S(2)}, u32[]{:S(2)}) collective-permute-start(bf16[144,1152]{1,0:T(8,128)(2,1)} %get-tuple-element.70), channel_id=1, source_target_pairs={{0,12},{4,8},{8,4},{12,0},{16,28},{20,24},{24,20},{28,16},{1,13},{... | collective-permute-start | bytes 995336 | tf_op jit(solution)/shard_map/ppermute | solution.py:469
  198.8 30.4 %collective-permute-start.19 = (bf16[144,1152]{1,0:T(8,128)(2,1)}, bf16[144,1152]{1,0:T(8,128)(2,1)}, u32[]{:S(2)}, u32[]{:S(2)}) collective-permute-start(bf16[144,1152]{1,0:T(8,128)(2,1)} %get-tuple-element.71), channel_id=1, source_target_pairs={{0,16},{4,20},{8,24},{12,28},{16,0},{20,4},{24,8},{28,12},{1,17},{... | collective-permute-start | bytes 995336 | tf_op jit(solution)/shard_map/ppermute | solution.py:469
  201.3 29.4 %collective-permute-start.20 = (bf16[144,1152]{1,0:T(8,128)(2,1)}, bf16[144,1152]{1,0:T(8,128)(2,1)}, u32[]{:S(2)}, u32[]{:S(2)}) collective-permute-start(bf16[144,1152]{1,0:T(8,128)(2,1)} %get-tuple-element.72), channel_id=1, source_target_pairs={{0,20},{4,16},{8,28},{12,24},{16,4},{20,0},{24,12},{28,8},{1,21},{... | collective-permute-start | bytes 995336 | tf_op jit(solution)/shard_map/ppermute | solution.py:469
  201.4 136.1 %collective-permute-start.10 = (bf16[3,2,144,1152]{3,2,1,0:T(8,128)(2,1)}, bf16[3,2,144,1152]{3,2,1,0:T(8,128)(2,1)}, u32[]{:S(2)}, u32[]{:S(2)}) collective-permute-start(bf16[3,2,144,1152]{3,2,1,0:T(8,128)(2,1)} %get-tuple-element.56), channel_id=1, source_target_pairs={{0,1},{1,0},{2,3},{3,2},{4,5},{5,4},{6,7},{7,6},{8,9},{9,8},{10,11... | collective-permute-start | bytes 5971976 | tf_op jit(solution)/shard_map/ppermute | solution.py:432
  221.5 115.9 %collective-permute-start.11 = (bf16[3,2,144,1152]{3,2,1,0:T(8,128)(2,1)}, bf16[3,2,144,1152]{3,2,1,0:T(8,128)(2,1)}, u32[]{:S(2)}, u32[]{:S(2)}) collective-permute-start(bf16[3,2,144,1152]{3,2,1,0:T(8,128)(2,1)} %get-tuple-element.57), channel_id=1, source_target_pairs={{0,2},{1,3},{2,0},{3,1},{4,6},{5,7},{6,4},{7,5},{8,10},{9,11},{10,... | collective-permute-start | bytes 5971976 | tf_op jit(solution)/shard_map/ppermute | solution.py:432
  227.7 109.7 %collective-permute-start.12 = (bf16[3,2,144,1152]{3,2,1,0:T(8,128)(2,1)}, bf16[3,2,144,1152]{3,2,1,0:T(8,128)(2,1)}, u32[]{:S(2)}, u32[]{:S(2)}) collective-permute-start(bf16[3,2,144,1152]{3,2,1,0:T(8,128)(2,1)} %get-tuple-element.58), channel_id=1, source_target_pairs={{0,3},{1,2},{2,1},{3,0},{4,7},{5,6},{6,5},{7,4},{8,11},{9,10},{10,... | collective-permute-start | bytes 5971976 | tf_op jit(solution)/shard_map/ppermute | solution.py:432
  229.2 12.8 %collective-permute-start.21 = (bf16[144,1152]{1,0:T(8,128)(2,1)}, bf16[144,1152]{1,0:T(8,128)(2,1)}, u32[]{:S(2)}, u32[]{:S(2)}) collective-permute-start(bf16[144,1152]{1,0:T(8,128)(2,1)} %get-tuple-element.73), channel_id=1, source_target_pairs={{0,24},{4,28},{8,16},{12,20},{16,8},{20,12},{24,0},{28,4},{1,25},{... | collective-permute-start | bytes 995336 | tf_op jit(solution)/shard_map/ppermute | solution.py:469
  230.7 17.2 %collective-permute-start.22 = (bf16[144,1152]{1,0:T(8,128)(2,1)}, bf16[144,1152]{1,0:T(8,128)(2,1)}, u32[]{:S(2)}, u32[]{:S(2)}) collective-permute-start(bf16[144,1152]{1,0:T(8,128)(2,1)} %get-tuple-element.74), channel_id=1, source_target_pairs={{0,28},{4,24},{8,20},{12,16},{16,12},{20,8},{24,4},{28,0},{1,29},{... | collective-permute-start | bytes 995336 | tf_op jit(solution)/shard_map/ppermute | solution.py:469
  250.5 68.0 %collective-permute-start.23 = (bf16[4,144,1152]{2,1,0:T(8,128)(2,1)}, bf16[4,144,1152]{2,1,0:T(8,128)(2,1)}, u32[]{:S(2)}, u32[]{:S(2)}) collective-permute-start(bf16[4,144,1152]{2,1,0:T(8,128)(2,1)} %get-tuple-element.75.refs_0_), channel_id=1, source_target_pairs={{0,1},{1,0},{2,3},{3,2},{4,5},{5,4},{6,7},{7,6},{8,9},{9,8},{10,11... | collective-permute-start | bytes 3981320 | tf_op jit(solution)/shard_map/ppermute | solution.py:432
  251.8 85.6 %collective-permute-start.24 = (bf16[4,144,1152]{2,1,0:T(8,128)(2,1)}, bf16[4,144,1152]{2,1,0:T(8,128)(2,1)}, u32[]{:S(2)}, u32[]{:S(2)}) collective-permute-start(bf16[4,144,1152]{2,1,0:T(8,128)(2,1)} %get-tuple-element.76.refs_1_), channel_id=1, source_target_pairs={{0,2},{1,3},{2,0},{3,1},{4,6},{5,7},{6,4},{7,5},{8,10},{9,11},{10,... | collective-permute-start | bytes 3981320 | tf_op jit(solution)/shard_map/ppermute | solution.py:432
  337.4 63.9 %collective-permute-start.26 = (bf16[4,144,1152]{2,1,0:T(8,128)(2,1)}, bf16[4,144,1152]{2,1,0:T(8,128)(2,1)}, u32[]{:S(2)}, u32[]{:S(2)}) collective-permute-start(bf16[4,144,1152]{2,1,0:T(8,128)(2,1)} %get-tuple-element.77.refs_0_), channel_id=1, source_target_pairs={{0,2},{1,3},{2,0},{3,1},{4,6},{5,7},{6,4},{7,5},{8,10},{9,11},{10,... | collective-permute-start | bytes 3981320 | tf_op jit(solution)/shard_map/ppermute | solution.py:432
  338.7 62.6 %collective-permute-start.25 = (bf16[4,144,1152]{2,1,0:T(8,128)(2,1)}, bf16[4,144,1152]{2,1,0:T(8,128)(2,1)}, u32[]{:S(2)}, u32[]{:S(2)}) collective-permute-start(bf16[4,144,1152]{2,1,0:T(8,128)(2,1)} %get-tuple-element.78.refs_1_), channel_id=1, source_target_pairs={{0,1},{1,0},{2,3},{3,2},{4,5},{5,4},{6,7},{7,6},{8,9},{9,8},{10,11... | collective-permute-start | bytes 3981320 | tf_op jit(solution)/shard_map/ppermute | solution.py:432
  401.3 30.7 %collective-permute-start.27 = (bf16[4,144,1152]{2,1,0:T(8,128)(2,1)}, bf16[4,144,1152]{2,1,0:T(8,128)(2,1)}, u32[]{:S(2)}, u32[]{:S(2)}) collective-permute-start(bf16[4,144,1152]{2,1,0:T(8,128)(2,1)} %get-tuple-element.79.refs_2_), channel_id=1, source_target_pairs={{0,2},{1,3},{2,0},{3,1},{4,6},{5,7},{6,4},{7,5},{8,10},{9,11},{10,... | collective-permute-start | bytes 3981320 | tf_op jit(solution)/shard_map/ppermute | solution.py:432
  403.6 29.9 %collective-permute-start.28 = (bf16[4,144,1152]{2,1,0:T(8,128)(2,1)}, bf16[4,144,1152]{2,1,0:T(8,128)(2,1)}, u32[]{:S(2)}, u32[]{:S(2)}) collective-permute-start(bf16[4,144,1152]{2,1,0:T(8,128)(2,1)} %get-tuple-element.80.refs_5_), channel_id=1, source_target_pairs={{0,1},{1,0},{2,3},{3,2},{4,5},{5,4},{6,7},{7,6},{8,9},{9,8},{10,11... | collective-permute-start | bytes 3981320 | tf_op jit(solution)/shard_map/ppermute | solution.py:432
  (4 other events, 12.8 us)

commit v6 on v5

--- a/solution.py
+++ b/solution.py
@@ -248,9 +248,10 @@
     )(*arrays, *after)
 
 
-def collect_body(*refs):
-    *parts, low, high, buffer, in_sems, out_sems = refs
-    half = len(parts) // 2
+def collect_body(count, n_through, *refs):
+    parts, half = refs[:count], count // 2
+    low, high = refs[count + n_through : count + n_through + 2]
+    buffer, in_sems, out_sems = refs[-3:]
 
     def arrive(k):
         return pltpu.make_async_copy(parts[k], buffer.at[k], in_sems.at[k])
@@ -269,19 +270,20 @@
         leave(k).wait()
 
 
-def collect(parts):
+def collect(parts, through):
     count = len(parts)
     halves = jax.ShapeDtypeStruct((count // 2,) + parts[0].shape, parts[0].dtype)
     return pl.pallas_call(
-        collect_body,
-        in_specs=[ANY] * count,
-        out_specs=[ANY] * 2,
-        out_shape=[halves] * 2,
+        functools.partial(collect_body, count, len(through)),
+        in_specs=[ANY] * (count + len(through)),
+        out_specs=[ANY] * (2 + len(through)),
+        out_shape=[halves] * 2 + [jax.ShapeDtypeStruct(x.shape, x.dtype) for x in through],
         scratch_shapes=[pltpu.VMEM((count,) + parts[0].shape, parts[0].dtype)]
         + [pltpu.SemaphoreType.DMA((count,))] * 2,
+        input_output_aliases={count + k: 2 + k for k in range(len(through))},
         compiler_params=params(),
         cost_estimate=cost(0, 2 * count * parts[0].size * 2),
-    )(*parts)
+    )(*parts, *through)
 
 
 def moment_body(q, received, moment, moment_out, square_out):
@@ -435,29 +437,20 @@
         return x.reshape(row_blocks, -1, sub_count * rd, B)
 
     first = rows // 64 * 16
-    lower, upper = (0, first), (2 * first, rows // 2 - first)
-
-    def exchange(x):
-        return lax.all_to_all(x, "fsdp", split_axis=0, concat_axis=0, tiled=True)
-
-    x, y = arrange(cols[:2].reshape(-1), grad, *lower)
-    early = (swap(x, 1), swap(y, 2))
-    far_a, far_b = arrange(cols[:2, :half].reshape(-1), grad, *upper, after=(x,))
-    far = (swap(far_a, 1), swap(far_b, 2))
-    x_a, y_b = arrange(cols[:2, half:].reshape(-1), grad, *upper, after=(far_a,))
-    near = (swap(x_a, 1), swap(y_b, 2))
-    roots = pack_roots(js, as_rows(root_left), as_rows(root_right), (x_a,))
-    y_a, x_b = arrange(cols[2], grad, *lower, [[(x, 0) for x in early]], after=(roots[0],))
-    cross = (swap(y_a, 2), swap(x_b, 1))
-    y_a, x_b = arrange(cols[2], grad, *upper, [[(x, 0) for x in far]], after=(y_a,))
-    late = (swap(y_a, 2), swap(x_b, 1))
-    terms = [[(x, half) for x in early], [(x, 0) for x in cross]]
-    (owned,) = arrange(cols[3], grad, *lower, terms, halves=False, after=(y_a,))
-    blocks = [exchange(owned)]
-    terms = [[(x, 0) for x in near], [(x, 0) for x in late]]
-    (owned,) = arrange(cols[3], grad, *upper, terms, halves=False, after=(owned,))
-    blocks.append(exchange(owned))
-    after = (owned,)
+    chunks = ((0, first), (2 * first, rows // 2 - first))
+    after, early, blocks = (), [], []
+    for chunk in chunks:
+        x, y = arrange(cols[:2].reshape(-1), grad, *chunk, after=after)
+        early.append((swap(x, 1), swap(y, 2)))
+        after = (x,)
+    roots = pack_roots(js, as_rows(root_left), as_rows(root_right), after)
+    after = (roots[0],)
+    for (x, y), chunk in zip(early, chunks):
+        y_a, x_b = arrange(cols[2], grad, *chunk, [((x, 0), (y, 0))], after=after)
+        terms = [((x, half), (y, half)), ((swap(y_a, 2), 0), (swap(x_b, 1), 0))]
+        (owned,) = arrange(cols[3], grad, *chunk, terms, halves=False)
+        blocks.append(lax.all_to_all(owned, "fsdp", split_axis=0, concat_axis=0, tiled=True))
+        after = (owned,)
     sent = follow(roots[1:], after)
     roots = [roots[0]] + [swap(x, k) for k, x in zip((1, 2, 3), sent)]
 
@@ -469,11 +462,9 @@
         lax.ppermute(direction[k], "fsdp", [(i, i ^ k) for i in range(owners)])
         for k in range(1, owners)
     ]
-    a, b = collect(direction)
-
-    x_a, y_b = swap(a, 1), swap(b, 2)
-    late_a, late_b = follow((a, b), received[1:])
-    x_b, y_a = swap(late_b, 1), swap(late_a, 2)
+    a, b, *received[1:] = collect(direction, received[1:])
+
+    x_a, y_b, x_b, y_a = swap(a, 1), swap(b, 2), swap(b, 1), swap(a, 2)
 
     moment, adam_square = by_rows(
         moment_body, 1, js, received, [as_rows(second_moment)], True
@@ -484,10 +475,10 @@
         jnp.where((js[:, None] == slot_ids)[:, :, None], adam_square[:, None, :], 0.0), axis=0
     )
     direction_square = direction_square[:, :2, 0].reshape(row_blocks)
-    owner_place = jnp.arange(owners, dtype=jnp.int32)[:, None, None, None] == f
     slot_place = (slot_ids == r)[:, None]
     squares = jnp.stack([adam_square, jnp.where(slot_place, direction_square, 0.0)])
-    squares = lax.psum(jnp.where(owner_place, squares, 0.0), ("fsdp", "replica"))
+    squares = lax.psum(squares, "replica")
+    squares = lax.psum(jnp.where(owner_ids[:, None, None, None] == f, squares, 0.0), "fsdp")
     ratio = jnp.sqrt(squares[:, 0]) / jnp.sqrt(squares[:, 1] + 1e-06)
     row_ratio = lax.dynamic_index_in_dim(
         ratio.reshape(columns, row_blocks), f // sub_count, 1, keepdims=False
@@ -500,7 +491,7 @@
     )
     part = (row_slots // replicas) ^ f
     src = 2 * (lax.rem(row_slots, replicas) ^ r) + part // half
-    gathered = (late_a, late_b, x_a, x_b, y_a, y_b, swap(x_a, 2), swap(y_b, 1))
+    gathered = (a, b, x_a, x_b, y_a, y_b, swap(x_a, 2), swap(y_b, 1))
     update = restore(src, lax.rem(part, half), scale, gathered)
     return (
         update,

time: 444 us -> 404 us (0.910)
  waiting for transfers between devices: 232 us -> 166 us
  blocking collectives: 43.5 us -> 69.7 us
    ppermute x22 -> x20, waiting for transfers between devices: 163 us -> 89 us  [swap(): return lax.ppermute(x, 'replica', [(i, i ^ k) for i in range(replicas)])]
    psum x1 -> x2, blocking collectives: 43.5 us -> 69.7 us  [the longest x1 43.6 us: owner_local(): squares = lax.psum(squares, 'replica')]
    ppermute x7, waiting for transfers between devices: 36.7 us -> 45.1 us  [owner_local(): lax.ppermute(direction[k], 'fsdp', [(i, i ^ k) for i in range(owners)])]
    ppermute x7, starting transfers between devices: 10.2 us -> 16.5 us  [owner_local(): lax.ppermute(direction[k], 'fsdp', [(i, i ^ k) for i in range(owners)])]
    ppermute x22 -> x20, starting transfers between devices: 26.8 us -> 24.6 us  [swap(): return lax.ppermute(x, 'replica', [(i, i ^ k) for i in range(replicas)])]
    pallas_call x7 -> x6, Pallas kernels: 32.4 us -> 31 us  [arrange(): pl.pallas_call(functools.partial(arrange_body, len(adds) // 2, [part[1] f...]
  transfers between devices with their start and end apart: 31 -> 29, of which waited for: 18 -> 19; matrix products, arithmetic and copies ran while one was open for 3% -> 3% of each run, Pallas kernels for 16% -> 20%
where the time goes in v6:
time: 404 us; the launch traced here: 403 us
  waiting for transfers between devices  166 us (41%)
  Pallas kernels  100 us (25%)
  blocking collectives  69.7 us (17%)
  starting transfers between devices  51 us (13%)
  other arithmetic  9.32 us (2%)
  local copies, waits for them, and re-layouts  4.98 us (1%)
    ppermute x20, waiting for transfers between devices, swap(): return lax.ppermute(x, 'replica', [(i, i ^ k) for i in range(replicas)])  89 us
    ppermute x7, waiting for transfers between devices, owner_local(): lax.ppermute(direction[k], 'fsdp', [(i, i ^ k) for i in range(owners)])  45.1 us
    psum x1, blocking collectives, owner_local(): squares = lax.psum(squares, 'replica')  43.6 us
    all_to_all x2, waiting for transfers between devices, owner_local(): lax.all_to_all(owned, 'fsdp', split_axis=0, concat_axis=0, tiled=True)  32.3 us
    pallas_call x6, Pallas kernels, arrange(): pl.pallas_call(functools.partial(arrange_body, len(adds) // 2, [part[1] f...  31 us
    pallas_call x2, Pallas kernels, by_rows(): pl.pallas_call(functools.partial(by_rows_body, body, n), grid_spec=pltpu....  26.2 us
    psum x1, blocking collectives, owner_local(): lax.psum(jnp.where(owner_ids[:, None, None, None] == f, squares, 0.0), 'f...  26.2 us
    ppermute x20, starting transfers between devices, swap(): return lax.ppermute(x, 'replica', [(i, i ^ k) for i in range(replicas)])  24.6 us
  transfers between devices with their start and end apart: 29, of which 19 were waited for; matrix products, arithmetic and copies ran while one was open for 3% of the time, Pallas kernels for 20%

profile of v6, /device:TPU:0, one launch (start us, length us, event | category | flops | bytes accessed | tf_op | source)
XLA Modules:
  0.0 402.6 jit_solution(3332589022468225084)
XLA Ops:
  3.9 4.8 %shard_map.102 = (bf16[8,64,1152]{2,1,0:T(8,128)(2,1)}, bf16[8,64,1152]{2,1,0:T(8,128)(2,1)}) custom-call(s32[16]{0:T(128)} %reshape.230.cols, bf16[288,18432]{1,0:T(8,128)(2,1)} %bitcast.35), custom_call_target="tpu_custom_call" | custom-call | bytes 4718592 | tf_op jit(solution)/shard_map/pallas_call | solution.py:65
  8.7 3.0 collective-permute-start.1
  13.3 5.2 %shard_map.103 = (bf16[8,80,1152]{2,1,0:T(8,128)(2,1)}, bf16[8,80,1152]{2,1,0:T(8,128)(2,1)}) custom-call(s32[16]{0:T(128)} %reshape.230.cols, bf16[288,18432]{1,0:T(8,128)(2,1)} %bitcast.36, bf16[8,64,1152]{2,1,0:T(8,128)(2,1)} %get-tuple-element.43.refs_0_), custom_call_target="tpu_custom_call" | custom-call | bytes 5898240 | tf_op jit(solution)/shard_map/pallas_call | solution.py:65
  19.0 9.0 %shard_map.104 = (bf16[2,2,144,1152]{3,2,1,0:T(8,128)(2,1)}, bf16[2,2,144,1152]{3,2,1,0:T(8,128)(2,1)}, bf16[2,2,144,1152]{3,2,1,0:T(8,128)(2,1)}, bf16[2,2,144,1152]{3,2,1,0:T(8,128)(2,1)}) custom-call(s32[4]{0:T(128)} %iota_xor_fusion.js, bf16[4,4,144,576]{3,2,1,0:T(8,128)(2,1)} %bitcast.44, bf16[4,4,144,576]{3,2,1,0:T(8,128)(2,1)} %bitcast.45, ...), custom_call_target="tpu_custom_call" | custom-call | bytes 10616832 | tf_op jit(solution)/shard_map/pallas_call | solution.py:100
  29.2 8.8 %collective-permute-done.1.refs_1_ = bf16[8,64,1152]{2,1,0:T(8,128)(2,1)} collective-permute-done((bf16[8,64,1152]{2,1,0:T(8,128)(2,1)}, bf16[8,64,1152]{2,1,0:T(8,128)(2,1)}, u32[]{:S(2)}, u32[]{:S(2)}) %collective-permute-start.1) | collective-permute-done | bytes 1179680 | tf_op jit(solution)/shard_map/ppermute | solution.py:434
  39.5 4.7 %shard_map.105 = (bf16[4,64,1152]{2,1,0:T(8,128)(2,1)}, bf16[4,64,1152]{2,1,0:T(8,128)(2,1)}) custom-call(s32[8]{0:T(128)} %get-tuple-element.97.cols, bf16[288,18432]{1,0:T(8,128)(2,1)} %bitcast.37, bf16[8,64,1152]{2,1,0:T(8,128)(2,1)} %collective-permute-done.refs_0_, bf16[8,64,1152]{2,1,0:T(8,128)(2,1)} %collective-permute-done.1.refs_1_, ...), custom_call_target="tpu_custom_call" | custom-call | bytes 3538944 | tf_op jit(solution)/shard_map/pallas_call | solution.py:65
  48.4 12.5 %collective-permute-done.2.refs_2_ = bf16[4,64,1152]{2,1,0:T(8,128)(2,1)} collective-permute-done((bf16[4,64,1152]{2,1,0:T(8,128)(2,1)}, bf16[4,64,1152]{2,1,0:T(8,128)(2,1)}, u32[]{:S(2)}, u32[]{:S(2)}) %collective-permute-start.2) | collective-permute-done | bytes 589856 | tf_op jit(solution)/shard_map/ppermute | solution.py:434
  61.3 5.3 %shard_map.106.refs_2_ = bf16[8,64,1152]{2,1,0:T(8,128)(2,1)} custom-call(s32[8]{0:T(128)} %get-tuple-element.98.cols, bf16[288,18432]{1,0:T(8,128)(2,1)} %bitcast.38, bf16[8,64,1152]{2,1,0:T(8,128)(2,1)} %collective-permute-done.refs_0_, bf16[8,64,1152]{2,1,0:T(8,128)(2,1)} %collective-permute-done.1.refs_1_, ...), custom_call_target="tpu_custom_call" | custom-call | bytes 4718592 | tf_op jit(solution)/shard_map/pallas_call | solution.py:65
  66.5 5.1 %all-to-all-start = ((bf16[8,64,1152]{2,1,0:T(8,128)(2,1)}), bf16[8,64,1152]{2,1,0:T(8,128)(2,1)}, u32[]{:S(2)}, u32[]{:S(2)}) async-start(bf16[8,64,1152]{2,1,0:T(8,128)(2,1)} %shard_map.106.refs_2_), calls=%async_computation | async-start | bytes 2359296 | tf_op jit(solution)/shard_map/all_to_all | solution.py:452
  71.6 18.5 %collective-permute-done.5.refs_1_ = bf16[8,80,1152]{2,1,0:T(8,128)(2,1)} collective-permute-done((bf16[8,80,1152]{2,1,0:T(8,128)(2,1)}, bf16[8,80,1152]{2,1,0:T(8,128)(2,1)}, u32[]{:S(2)}, u32[]{:S(2)}) %collective-permute-start.5) | collective-permute-done | bytes 1474592 | tf_op jit(solution)/shard_map/ppermute | solution.py:434
  90.5 5.2 %shard_map.107 = (bf16[4,80,1152]{2,1,0:T(8,128)(2,1)}, bf16[4,80,1152]{2,1,0:T(8,128)(2,1)}) custom-call(s32[8]{0:T(128)} %get-tuple-element.97.cols, bf16[288,18432]{1,0:T(8,128)(2,1)} %bitcast.39, bf16[8,80,1152]{2,1,0:T(8,128)(2,1)} %collective-permute-done.4.refs_0_, bf16[8,80,1152]{2,1,0:T(8,128)(2,1)} %collective-permute-done.5.refs_1_, ...), custom_call_target="tpu_custom_call" | custom-call | bytes 4423680 | tf_op jit(solution)/shard_map/pallas_call | solution.py:65
  98.6 13.6 %collective-permute-done.6.refs_2_ = bf16[4,80,1152]{2,1,0:T(8,128)(2,1)} collective-permute-done((bf16[4,80,1152]{2,1,0:T(8,128)(2,1)}, bf16[4,80,1152]{2,1,0:T(8,128)(2,1)}, u32[]{:S(2)}, u32[]{:S(2)}) %collective-permute-start.6) | collective-permute-done | bytes 737312 | tf_op jit(solution)/shard_map/ppermute | solution.py:434
  113.0 5.8 %shard_map.108.refs_3_ = bf16[8,80,1152]{2,1,0:T(8,128)(2,1)} custom-call(s32[8]{0:T(128)} %get-tuple-element.98.cols, bf16[288,18432]{1,0:T(8,128)(2,1)} %bitcast.40, bf16[8,80,1152]{2,1,0:T(8,128)(2,1)} %collective-permute-done.4.refs_0_, bf16[8,80,1152]{2,1,0:T(8,128)(2,1)} %collective-permute-done.5.refs_1_, ...), custom_call_target="tpu_custom_call" | custom-call | bytes 5898240 | tf_op jit(solution)/shard_map/pallas_call | solution.py:65
  118.8 4.9 %all-to-all-start.1 = ((bf16[8,80,1152]{2,1,0:T(8,128)(2,1)}), bf16[8,80,1152]{2,1,0:T(8,128)(2,1)}, u32[]{:S(2)}, u32[]{:S(2)}) async-start(bf16[8,80,1152]{2,1,0:T(8,128)(2,1)} %shard_map.108.refs_3_), calls=%async_computation.1 | async-start | bytes 2949120 | tf_op jit(solution)/shard_map/all_to_all | solution.py:452
  127.2 32.3 %all-to-all-done.1.refs_1_ = bf16[8,80,1152]{2,1,0:T(8,128)(2,1)} async-done(((bf16[8,80,1152]{2,1,0:T(8,128)(2,1)}), bf16[8,80,1152]{2,1,0:T(8,128)(2,1)}, u32[]{:S(2)}, u32[]{:S(2)}) %all-to-all-start.1) | async-done | bytes 1474592 | tf_op jit(solution)/shard_map/all_to_all | solution.py:452
  159.5 10.7 %shard_map.109 = (bf16[3,2,144,1152]{3,2,1,0:T(8,128)(2,1)}, bf16[3,2,144,1152]{3,2,1,0:T(8,128)(2,1)}, bf16[3,2,144,1152]{3,2,1,0:T(8,128)(2,1)}, bf16[3,2,144,1152]{3,2,1,0:T(8,128)(2,1)}) custom-call(s32[4]{0:T(128)} %iota_xor_fusion.js, bf16[8,64,1152]{2,1,0:T(8,128)(2,1)} %all-to-all-done.refs_0_, bf16[8,80,1152]{2,1,0:T(8,128)(2,1)} %all-to-all-done.1.refs_1_), custom_call_target="tpu_custom_call" | custom-call | flops 3057647616 | bytes 10616832 | tf_op jit(solution)/shard_map/pallas_call | solution.py:160
  173.7 12.2 %collective-permute-done.9.refs_4_ = bf16[2,2,144,1152]{3,2,1,0:T(8,128)(2,1)} collective-permute-done((bf16[2,2,144,1152]{3,2,1,0:T(8,128)(2,1)}, bf16[2,2,144,1152]{3,2,1,0:T(8,128)(2,1)}, u32[]{:S(2)}, u32[]{:S(2)}) %collective-permute-start.9) | collective-permute-done | bytes 1327136 | tf_op jit(solution)/shard_map/ppermute | solution.py:434
  186.0 11.8 %shard_map.111 = (bf16[144,1152]{1,0:T(8,128)(2,1)}, bf16[144,1152]{1,0:T(8,128)(2,1)}, bf16[144,1152]{1,0:T(8,128)(2,1)}, bf16[144,1152]{1,0:T(8,128)(2,1)}, bf...) custom-call(s32[4]{0:T(128)} %iota_xor_fusion.js, ...), custom_call_target="tpu_custom_call" | custom-call | flops 3057647616 | bytes 10616832 | tf_op jit(solution)/shard_map/pallas_call | solution.py:219
  201.4 7.5 %collective-permute-done.12.refs_2_ = bf16[144,1152]{1,0:T(8,128)(2,1)} collective-permute-done((bf16[144,1152]{1,0:T(8,128)(2,1)}, bf16[144,1152]{1,0:T(8,128)(2,1)}, u32[]{:S(2)}, u32[]{:S(2)}) %collective-permute-start.12) | collective-permute-done | bytes 331808 | tf_op jit(solution)/shard_map/ppermute | solution.py:462
  211.6 9.3 %collective-permute-done.13.refs_3_ = bf16[144,1152]{1,0:T(8,128)(2,1)} collective-permute-done((bf16[144,1152]{1,0:T(8,128)(2,1)}, bf16[144,1152]{1,0:T(8,128)(2,1)}, u32[]{:S(2)}, u32[]{:S(2)}) %collective-permute-start.13) | collective-permute-done | bytes 331808 | tf_op jit(solution)/shard_map/ppermute | solution.py:462
  220.9 13.7 %collective-permute-done.14.refs_4_ = bf16[144,1152]{1,0:T(8,128)(2,1)} collective-permute-done((bf16[144,1152]{1,0:T(8,128)(2,1)}, bf16[144,1152]{1,0:T(8,128)(2,1)}, u32[]{:S(2)}, u32[]{:S(2)}) %collective-permute-start.14) | collective-permute-done | bytes 331808 | tf_op jit(solution)/shard_map/ppermute | solution.py:462
  234.7 4.0 collective-permute-start.16
  238.7 7.6 %collective-permute-done.15.refs_5_ = bf16[144,1152]{1,0:T(8,128)(2,1)} collective-permute-done((bf16[144,1152]{1,0:T(8,128)(2,1)}, bf16[144,1152]{1,0:T(8,128)(2,1)}, u32[]{:S(2)}, u32[]{:S(2)}) %collective-permute-start.15) | collective-permute-done | bytes 331808 | tf_op jit(solution)/shard_map/ppermute | solution.py:462
  246.3 6.3 %collective-permute-start.17 = (bf16[144,1152]{1,0:T(8,128)(2,1)}, bf16[144,1152]{1,0:T(8,128)(2,1)}, u32[]{:S(2)}, u32[]{:S(2)}) collective-permute-start(bf16[144,1152]{1,0:T(8,128)(2,1)} %get-tuple-element.66), channel_id=1, source_target_pairs={{0,28},{4,24},{8,20},{12,16},{16,12},{20,8},{24,4},{28,0},{1,29},{... | collective-permute-start | bytes 995336 | tf_op jit(solution)/shard_map/ppermute | solution.py:462
  254.4 6.9 %collective-permute-done.17.refs_7_ = bf16[144,1152]{1,0:T(8,128)(2,1)} collective-permute-done((bf16[144,1152]{1,0:T(8,128)(2,1)}, bf16[144,1152]{1,0:T(8,128)(2,1)}, u32[]{:S(2)}, u32[]{:S(2)}) %collective-permute-start.17) | collective-permute-done | bytes 331808 | tf_op jit(solution)/shard_map/ppermute | solution.py:462
  261.3 9.2 %collective-permute-done.19.refs_9_ = bf16[3,2,144,1152]{3,2,1,0:T(8,128)(2,1)} collective-permute-done((bf16[3,2,144,1152]{3,2,1,0:T(8,128)(2,1)}, bf16[3,2,144,1152]{3,2,1,0:T(8,128)(2,1)}, u32[]{:S(2)}, u32[]{:S(2)}) %collective-permute-start.19) | collective-permute-done | bytes 1990688 | tf_op jit(solution)/shard_map/ppermute | solution.py:434
  278.9 12.0 %shard_map.113 = (f32[4,4,144,576]{3,2,1,0:T(8,128)}, f32[4,2,8,128]{3,2,1,0:T(8,128)}) custom-call(s32[4]{0:T(128)} %iota_xor_fusion.js, bf16[3,2,144,1152]{3,2,1,0:T(8,128)(2,1)} %get-tuple-element.52.refs_6_.refs_0_, bf16[3,2,144,1152]{3,2,1,0:T(8,128)(2,1)} %get-tuple-element.70.refs_1_, bf16[3,2,144,1152]{3,2,1,0:T(8,128)(2,1)} %get-tuple-element.71.refs_2_, ...), custom_call_target="tpu_custom_call" | custom-call | bytes 13271040 | tf_op jit(solution)/shard_map/pallas_call | solution.py:323
  293.2 43.6 %psum.14 = f32[2,4,4]{2,1,0:T(4,128)S(1)} all-reduce(f32[2,4,4]{2,1,0:T(4,128)S(1)} %pad_maximum_fusion), channel_id=1, replica_groups=mesh['fsdp'=8,'replica'=4] {'replica'}, use_global_device_ids=true, to_apply=%region_2.3 | all-reduce | flops 32 | bytes 256 | tf_op jit(solution)/shard_map/psum | solution.py:480
  337.6 26.2 %psum.15 = f32[8,2,4,4]{2,0,3,1:T(8,128)S(1)} all-reduce(f32[8,2,4,4]{2,0,3,1:T(8,128)S(1)} %broadcast_select_fusion), channel_id=1, replica_groups=mesh['fsdp'=8,'replica'=4] {'fsdp'}, use_global_device_ids=true, to_apply=%region_3.4 | all-reduce | flops 256 | bytes 2048 | tf_op jit(solution)/shard_map/psum | solution.py:481
  368.4 14.2 %shard_map.116 = (f32[4,4,144,576]{3,2,1,0:T(8,128)}, f32[4,4,144,576]{3,2,1,0:T(8,128)}) custom-call(s32[4]{0:T(128)} %iota_xor_fusion.js, bf16[3,2,144,1152]{3,2,1,0:T(8,128)(2,1)} %get-tuple-element.52.refs_6_.refs_0_, bf16[3,2,144,1152]{3,2,1,0:T(8,128)(2,1)} %get-tuple-element.70.refs_1_, bf16[3,2,144,1152]{3,2,1,0:T(8,128)(2,1)} %get-tuple-element.71.refs_2_, ...), custom_call_target="tpu_custom_call" | custom-call | bytes 26542080 | tf_op jit(solution)/shard_map/pallas_call | solution.py:323
  382.6 10.6 %collective-permute-done.25.refs_6_ = bf16[4,144,1152]{2,1,0:T(8,128)(2,1)} collective-permute-done((bf16[4,144,1152]{2,1,0:T(8,128)(2,1)}, bf16[4,144,1152]{2,1,0:T(8,128)(2,1)}, u32[]{:S(2)}, u32[]{:S(2)}) %collective-permute-start.25) | collective-permute-done | bytes 1327136 | tf_op jit(solution)/shard_map/ppermute | solution.py:434
  393.6 8.8 %shard_map.115 = bf16[288,18432]{1,0:T(8,128)(2,1)} custom-call(s32[32]{0:T(128)} %multiply_add_fusion.src, s32[32]{0:T(128)} %get-tuple-element.94.item, f32[32]{0:T(128)} %select_reduce_fusion.refs_2_.scale, bf16[4,144,1152]{2,1,0:T(8,128)(2,1)} %get-tuple-element.75.refs_0_, bf16[4,144,1152]{2,1,0:T(8,128)(2,1)} %get-tuple-element.76.refs_1_, ...), custom_call_target="tpu_custom_call" | custom-call | bytes 21233664 | tf_op jit(solution)/shard_map/pallas_call | solution.py:391
  (78 shorter events, 48.3 us)
Async XLA Ops:
  2.1 0.6 copy-start.1
  2.7 0.6 copy-start
  8.7 29.3 %collective-permute-start.1 = (bf16[8,64,1152]{2,1,0:T(8,128)(2,1)}, bf16[8,64,1152]{2,1,0:T(8,128)(2,1)}, u32[]{:S(2)}, u32[]{:S(2)}) collective-permute-start(bf16[8,64,1152]{2,1,0:T(8,128)(2,1)} %get-tuple-element.44), channel_id=1, source_target_pairs={{0,2},{1,3},{2,0},{3,1},{4,6},{5,7},{6,4},{7,5},{8,10},{9,11},{10,... | collective-permute-start | bytes 3538952 | tf_op jit(solution)/shard_map/ppermute | solution.py:434
  11.7 27.7 %collective-permute-start = (bf16[8,64,1152]{2,1,0:T(8,128)(2,1)}, bf16[8,64,1152]{2,1,0:T(8,128)(2,1)}, u32[]{:S(2)}, u32[]{:S(2)}) collective-permute-start(bf16[8,64,1152]{2,1,0:T(8,128)(2,1)} %get-tuple-element.43.refs_0_), channel_id=1, source_target_pairs={{0,1},{1,0},{2,3},{3,2},{4,5},{5,4},{6,7},{7,6},{8,9},{9,8},{10,11... | collective-permute-start | bytes 3538952 | tf_op jit(solution)/shard_map/ppermute | solution.py:434
  44.2 16.6 %collective-permute-start.2 = (bf16[4,64,1152]{2,1,0:T(8,128)(2,1)}, bf16[4,64,1152]{2,1,0:T(8,128)(2,1)}, u32[]{:S(2)}, u32[]{:S(2)}) collective-permute-start(bf16[4,64,1152]{2,1,0:T(8,128)(2,1)} %get-tuple-element.47), channel_id=1, source_target_pairs={{0,2},{1,3},{2,0},{3,1},{4,6},{5,7},{6,4},{7,5},{8,10},{9,11},{10,... | collective-permute-start | bytes 1769480 | tf_op jit(solution)/shard_map/ppermute | solution.py:434
  44.7 16.6 %collective-permute-start.3 = (bf16[4,64,1152]{2,1,0:T(8,128)(2,1)}, bf16[4,64,1152]{2,1,0:T(8,128)(2,1)}, u32[]{:S(2)}, u32[]{:S(2)}) collective-permute-start(bf16[4,64,1152]{2,1,0:T(8,128)(2,1)} %get-tuple-element.48), channel_id=1, source_target_pairs={{0,1},{1,0},{2,3},{3,2},{4,5},{5,4},{6,7},{7,6},{8,9},{9,8},{10,11... | collective-permute-start | bytes 1769480 | tf_op jit(solution)/shard_map/ppermute | solution.py:434
  46.3 43.8 %collective-permute-start.5 = (bf16[8,80,1152]{2,1,0:T(8,128)(2,1)}, bf16[8,80,1152]{2,1,0:T(8,128)(2,1)}, u32[]{:S(2)}, u32[]{:S(2)}) collective-permute-start(bf16[8,80,1152]{2,1,0:T(8,128)(2,1)} %get-tuple-element.49), channel_id=1, source_target_pairs={{0,2},{1,3},{2,0},{3,1},{4,6},{5,7},{6,4},{7,5},{8,10},{9,11},{10,... | collective-permute-start | bytes 4423688 | tf_op jit(solution)/shard_map/ppermute | solution.py:434
  47.8 42.7 %collective-permute-start.4 = (bf16[8,80,1152]{2,1,0:T(8,128)(2,1)}, bf16[8,80,1152]{2,1,0:T(8,128)(2,1)}, u32[]{:S(2)}, u32[]{:S(2)}) collective-permute-start(bf16[8,80,1152]{2,1,0:T(8,128)(2,1)} %get-tuple-element.45.refs_0_), channel_id=1, source_target_pairs={{0,1},{1,0},{2,3},{3,2},{4,5},{5,4},{6,7},{7,6},{8,9},{9,8},{10,11... | collective-permute-start | bytes 4423688 | tf_op jit(solution)/shard_map/ppermute | solution.py:434
  66.5 52.2 %all-to-all-start = ((bf16[8,64,1152]{2,1,0:T(8,128)(2,1)}), bf16[8,64,1152]{2,1,0:T(8,128)(2,1)}, u32[]{:S(2)}, u32[]{:S(2)}) async-start(bf16[8,64,1152]{2,1,0:T(8,128)(2,1)} %shard_map.106.refs_2_), calls=%async_computation | async-start | bytes 2359296 | tf_op jit(solution)/shard_map/all_to_all | solution.py:452
  95.7 16.5 %collective-permute-start.6 = (bf16[4,80,1152]{2,1,0:T(8,128)(2,1)}, bf16[4,80,1152]{2,1,0:T(8,128)(2,1)}, u32[]{:S(2)}, u32[]{:S(2)}) collective-permute-start(bf16[4,80,1152]{2,1,0:T(8,128)(2,1)} %get-tuple-element.50), channel_id=1, source_target_pairs={{0,2},{1,3},{2,0},{3,1},{4,6},{5,7},{6,4},{7,5},{8,10},{9,11},{10,... | collective-permute-start | bytes 2211848 | tf_op jit(solution)/shard_map/ppermute | solution.py:434
  97.1 15.9 %collective-permute-start.7 = (bf16[4,80,1152]{2,1,0:T(8,128)(2,1)}, bf16[4,80,1152]{2,1,0:T(8,128)(2,1)}, u32[]{:S(2)}, u32[]{:S(2)}) collective-permute-start(bf16[4,80,1152]{2,1,0:T(8,128)(2,1)} %get-tuple-element.51), channel_id=1, source_target_pairs={{0,1},{1,0},{2,3},{3,2},{4,5},{5,4},{6,7},{7,6},{8,9},{9,8},{10,11... | collective-permute-start | bytes 2211848 | tf_op jit(solution)/shard_map/ppermute | solution.py:434
  118.8 40.7 %all-to-all-start.1 = ((bf16[8,80,1152]{2,1,0:T(8,128)(2,1)}), bf16[8,80,1152]{2,1,0:T(8,128)(2,1)}, u32[]{:S(2)}, u32[]{:S(2)}) async-start(bf16[8,80,1152]{2,1,0:T(8,128)(2,1)} %shard_map.108.refs_3_), calls=%async_computation.1 | async-start | bytes 2949120 | tf_op jit(solution)/shard_map/all_to_all | solution.py:452
  123.7 48.8 %collective-permute-start.8 = (bf16[2,2,144,1152]{3,2,1,0:T(8,128)(2,1)}, bf16[2,2,144,1152]{3,2,1,0:T(8,128)(2,1)}, u32[]{:S(2)}, u32[]{:S(2)}) collective-permute-start(bf16[2,2,144,1152]{3,2,1,0:T(8,128)(2,1)} %get-tuple-element.56), channel_id=1, source_target_pairs={{0,1},{1,0},{2,3},{3,2},{4,5},{5,4},{6,7},{7,6},{8,9},{9,8},{10,11... | collective-permute-start | bytes 3981320 | tf_op jit(solution)/shard_map/ppermute | solution.py:434
  125.3 60.7 %collective-permute-start.9 = (bf16[2,2,144,1152]{3,2,1,0:T(8,128)(2,1)}, bf16[2,2,144,1152]{3,2,1,0:T(8,128)(2,1)}, u32[]{:S(2)}, u32[]{:S(2)}) collective-permute-start(bf16[2,2,144,1152]{3,2,1,0:T(8,128)(2,1)} %get-tuple-element.57), channel_id=1, source_target_pairs={{0,2},{1,3},{2,0},{3,1},{4,6},{5,7},{6,4},{7,5},{8,10},{9,11},{10,... | collective-permute-start | bytes 3981320 | tf_op jit(solution)/shard_map/ppermute | solution.py:434
  126.0 60.0 %collective-permute-start.10 = (bf16[2,2,144,1152]{3,2,1,0:T(8,128)(2,1)}, bf16[2,2,144,1152]{3,2,1,0:T(8,128)(2,1)}, u32[]{:S(2)}, u32[]{:S(2)}) collective-permute-start(bf16[2,2,144,1152]{3,2,1,0:T(8,128)(2,1)} %get-tuple-element.58), channel_id=1, source_target_pairs={{0,3},{1,2},{2,1},{3,0},{4,7},{5,6},{6,5},{7,4},{8,11},{9,10},{10,... | collective-permute-start | bytes 3981320 | tf_op jit(solution)/shard_map/ppermute | solution.py:434
  170.2 91.0 %collective-permute-start.18 = (bf16[3,2,144,1152]{3,2,1,0:T(8,128)(2,1)}, bf16[3,2,144,1152]{3,2,1,0:T(8,128)(2,1)}, u32[]{:S(2)}, u32[]{:S(2)}) collective-permute-start(bf16[3,2,144,1152]{3,2,1,0:T(8,128)(2,1)} %get-tuple-element.67), channel_id=1, source_target_pairs={{0,1},{1,0},{2,3},{3,2},{4,5},{5,4},{6,7},{7,6},{8,9},{9,8},{10,11... | collective-permute-start | bytes 5971976 | tf_op jit(solution)/shard_map/ppermute | solution.py:434
  171.7 98.8 %collective-permute-start.19 = (bf16[3,2,144,1152]{3,2,1,0:T(8,128)(2,1)}, bf16[3,2,144,1152]{3,2,1,0:T(8,128)(2,1)}, u32[]{:S(2)}, u32[]{:S(2)}) collective-permute-start(bf16[3,2,144,1152]{3,2,1,0:T(8,128)(2,1)} %get-tuple-element.68), channel_id=1, source_target_pairs={{0,2},{1,3},{2,0},{3,1},{4,6},{5,7},{6,4},{7,5},{8,10},{9,11},{10,... | collective-permute-start | bytes 5971976 | tf_op jit(solution)/shard_map/ppermute | solution.py:434
  172.5 98.1 %collective-permute-start.20 = (bf16[3,2,144,1152]{3,2,1,0:T(8,128)(2,1)}, bf16[3,2,144,1152]{3,2,1,0:T(8,128)(2,1)}, u32[]{:S(2)}, u32[]{:S(2)}) collective-permute-start(bf16[3,2,144,1152]{3,2,1,0:T(8,128)(2,1)} %get-tuple-element.69), channel_id=1, source_target_pairs={{0,3},{1,2},{2,1},{3,0},{4,7},{5,6},{6,5},{7,4},{8,11},{9,10},{10,... | collective-permute-start | bytes 5971976 | tf_op jit(solution)/shard_map/ppermute | solution.py:434
  197.8 2.0 collective-permute-start.11
  197.9 11.0 %collective-permute-start.12 = (bf16[144,1152]{1,0:T(8,128)(2,1)}, bf16[144,1152]{1,0:T(8,128)(2,1)}, u32[]{:S(2)}, u32[]{:S(2)}) collective-permute-start(bf16[144,1152]{1,0:T(8,128)(2,1)} %get-tuple-element.61), channel_id=1, source_target_pairs={{0,8},{4,12},{8,0},{12,4},{16,24},{20,28},{24,16},{28,20},{1,9},{5... | collective-permute-start | bytes 995336 | tf_op jit(solution)/shard_map/ppermute | solution.py:462
  199.9 21.1 %collective-permute-start.13 = (bf16[144,1152]{1,0:T(8,128)(2,1)}, bf16[144,1152]{1,0:T(8,128)(2,1)}, u32[]{:S(2)}, u32[]{:S(2)}) collective-permute-start(bf16[144,1152]{1,0:T(8,128)(2,1)} %get-tuple-element.62), channel_id=1, source_target_pairs={{0,12},{4,8},{8,4},{12,0},{16,28},{20,24},{24,20},{28,16},{1,13},{... | collective-permute-start | bytes 995336 | tf_op jit(solution)/shard_map/ppermute | solution.py:462
  208.9 25.8 %collective-permute-start.14 = (bf16[144,1152]{1,0:T(8,128)(2,1)}, bf16[144,1152]{1,0:T(8,128)(2,1)}, u32[]{:S(2)}, u32[]{:S(2)}) collective-permute-start(bf16[144,1152]{1,0:T(8,128)(2,1)} %get-tuple-element.63), channel_id=1, source_target_pairs={{0,16},{4,20},{8,24},{12,28},{16,0},{20,4},{24,8},{28,12},{1,17},{... | collective-permute-start | bytes 995336 | tf_op jit(solution)/shard_map/ppermute | solution.py:462
  220.9 25.4 %collective-permute-start.15 = (bf16[144,1152]{1,0:T(8,128)(2,1)}, bf16[144,1152]{1,0:T(8,128)(2,1)}, u32[]{:S(2)}, u32[]{:S(2)}) collective-permute-start(bf16[144,1152]{1,0:T(8,128)(2,1)} %get-tuple-element.64), channel_id=1, source_target_pairs={{0,20},{4,16},{8,28},{12,24},{16,4},{20,0},{24,12},{28,8},{1,21},{... | collective-permute-start | bytes 995336 | tf_op jit(solution)/shard_map/ppermute | solution.py:462
  234.7 19.7 %collective-permute-start.16 = (bf16[144,1152]{1,0:T(8,128)(2,1)}, bf16[144,1152]{1,0:T(8,128)(2,1)}, u32[]{:S(2)}, u32[]{:S(2)}) collective-permute-start(bf16[144,1152]{1,0:T(8,128)(2,1)} %get-tuple-element.65), channel_id=1, source_target_pairs={{0,24},{4,28},{8,16},{12,20},{16,8},{20,12},{24,0},{28,4},{1,25},{... | collective-permute-start | bytes 995336 | tf_op jit(solution)/shard_map/ppermute | solution.py:462
  246.3 15.0 %collective-permute-start.17 = (bf16[144,1152]{1,0:T(8,128)(2,1)}, bf16[144,1152]{1,0:T(8,128)(2,1)}, u32[]{:S(2)}, u32[]{:S(2)}) collective-permute-start(bf16[144,1152]{1,0:T(8,128)(2,1)} %get-tuple-element.66), channel_id=1, source_target_pairs={{0,28},{4,24},{8,20},{12,16},{16,12},{20,8},{24,4},{28,0},{1,29},{... | collective-permute-start | bytes 995336 | tf_op jit(solution)/shard_map/ppermute | solution.py:462
  273.2 92.1 %collective-permute-start.24 = (bf16[4,144,1152]{2,1,0:T(8,128)(2,1)}, bf16[4,144,1152]{2,1,0:T(8,128)(2,1)}, u32[]{:S(2)}, u32[]{:S(2)}) collective-permute-start(bf16[4,144,1152]{2,1,0:T(8,128)(2,1)} %get-tuple-element.75.refs_0_), channel_id=1, source_target_pairs={{0,2},{1,3},{2,0},{3,1},{4,6},{5,7},{6,4},{7,5},{8,10},{9,11},{10,... | collective-permute-start | bytes 3981320 | tf_op jit(solution)/shard_map/ppermute | solution.py:434
  274.0 91.3 %collective-permute-start.21 = (bf16[4,144,1152]{2,1,0:T(8,128)(2,1)}, bf16[4,144,1152]{2,1,0:T(8,128)(2,1)}, u32[]{:S(2)}, u32[]{:S(2)}) collective-permute-start(bf16[4,144,1152]{2,1,0:T(8,128)(2,1)} %get-tuple-element.75.refs_0_), channel_id=1, source_target_pairs={{0,1},{1,0},{2,3},{3,2},{4,5},{5,4},{6,7},{7,6},{8,9},{9,8},{10,11... | collective-permute-start | bytes 3981320 | tf_op jit(solution)/shard_map/ppermute | solution.py:434
  275.1 90.2 %collective-permute-start.23 = (bf16[4,144,1152]{2,1,0:T(8,128)(2,1)}, bf16[4,144,1152]{2,1,0:T(8,128)(2,1)}, u32[]{:S(2)}, u32[]{:S(2)}) collective-permute-start(bf16[4,144,1152]{2,1,0:T(8,128)(2,1)} %get-tuple-element.76.refs_1_), channel_id=1, source_target_pairs={{0,1},{1,0},{2,3},{3,2},{4,5},{5,4},{6,7},{7,6},{8,9},{9,8},{10,11... | collective-permute-start | bytes 3981320 | tf_op jit(solution)/shard_map/ppermute | solution.py:434
  276.0 89.3 %collective-permute-start.22 = (bf16[4,144,1152]{2,1,0:T(8,128)(2,1)}, bf16[4,144,1152]{2,1,0:T(8,128)(2,1)}, u32[]{:S(2)}, u32[]{:S(2)}) collective-permute-start(bf16[4,144,1152]{2,1,0:T(8,128)(2,1)} %get-tuple-element.76.refs_1_), channel_id=1, source_target_pairs={{0,2},{1,3},{2,0},{3,1},{4,6},{5,7},{6,4},{7,5},{8,10},{9,11},{10,... | collective-permute-start | bytes 3981320 | tf_op jit(solution)/shard_map/ppermute | solution.py:434
  365.3 27.8 %collective-permute-start.25 = (bf16[4,144,1152]{2,1,0:T(8,128)(2,1)}, bf16[4,144,1152]{2,1,0:T(8,128)(2,1)}, u32[]{:S(2)}, u32[]{:S(2)}) collective-permute-start(bf16[4,144,1152]{2,1,0:T(8,128)(2,1)} %get-tuple-element.77.refs_2_), channel_id=1, source_target_pairs={{0,2},{1,3},{2,0},{3,1},{4,6},{5,7},{6,4},{7,5},{8,10},{9,11},{10,... | collective-permute-start | bytes 3981320 | tf_op jit(solution)/shard_map/ppermute | solution.py:434
  366.1 27.5 %collective-permute-start.26 = (bf16[4,144,1152]{2,1,0:T(8,128)(2,1)}, bf16[4,144,1152]{2,1,0:T(8,128)(2,1)}, u32[]{:S(2)}, u32[]{:S(2)}) collective-permute-start(bf16[4,144,1152]{2,1,0:T(8,128)(2,1)} %get-tuple-element.78.refs_5_), channel_id=1, source_target_pairs={{0,1},{1,0},{2,3},{3,2},{4,5},{5,4},{6,7},{7,6},{8,9},{9,8},{10,11... | collective-permute-start | bytes 3981320 | tf_op jit(solution)/shard_map/ppermute | solution.py:434

commit v7 on v6

--- a/solution.py
+++ b/solution.py
@@ -436,7 +436,7 @@
     def as_rows(x):
         return x.reshape(row_blocks, -1, sub_count * rd, B)
 
-    first = rows // 64 * 16
+    first = -(-rows // 64) * 16
     chunks = ((0, first), (2 * first, rows // 2 - first))
     after, early, blocks = (), [], []
     for chunk in chunks:
@@ -451,7 +451,7 @@
         (owned,) = arrange(cols[3], grad, *chunk, terms, halves=False)
         blocks.append(lax.all_to_all(owned, "fsdp", split_axis=0, concat_axis=0, tiled=True))
         after = (owned,)
-    sent = follow(roots[1:], after)
+    sent = follow(roots[1:], (y_a,))
     roots = [roots[0]] + [swap(x, k) for k, x in zip((1, 2, 3), sent)]
 
     place = f.reshape(1)
@@ -477,8 +477,8 @@
     direction_square = direction_square[:, :2, 0].reshape(row_blocks)
     slot_place = (slot_ids == r)[:, None]
     squares = jnp.stack([adam_square, jnp.where(slot_place, direction_square, 0.0)])
+    squares = lax.psum(jnp.where(owner_ids[:, None, None, None] == f, squares, 0.0), "fsdp")
     squares = lax.psum(squares, "replica")
-    squares = lax.psum(jnp.where(owner_ids[:, None, None, None] == f, squares, 0.0), "fsdp")
     ratio = jnp.sqrt(squares[:, 0]) / jnp.sqrt(squares[:, 1] + 1e-06)
     row_ratio = lax.dynamic_index_in_dim(
         ratio.reshape(columns, row_blocks), f // sub_count, 1, keepdims=False

time: 404 us -> 399 us (0.988)
  blocking collectives: 69.7 us -> 49.8 us
  waiting for transfers between devices: 166 us -> 183 us
    ppermute x20, waiting for transfers between devices: 89 us -> 112 us  [swap(): return lax.ppermute(x, 'replica', [(i, i ^ k) for i in range(replicas)])]
    psum x1, blocking collectives: 43.6 us -> 22 us  [owner_local(): squares = lax.psum(squares, 'replica')]
    all_to_all x2, waiting for transfers between devices: 32.3 us -> 25.9 us  [owner_local(): lax.all_to_all(owned, 'fsdp', split_axis=0, concat_axis=0, tiled=True)]
  transfers between devices with their start and end apart: 29 -> 29, of which waited for: 19 -> 19; matrix products, arithmetic and copies ran while one was open for 3% -> 3% of each run, Pallas kernels for 20% -> 18%
where the time goes in v7:
time: 399 us; the launch traced here: 398 us
  waiting for transfers between devices  183 us (46%)
  Pallas kernels  100 us (25%)
  starting transfers between devices  50.2 us (13%)
  blocking collectives  49.8 us (12%)
  other arithmetic  9.26 us (2%)
  local copies, waits for them, and re-layouts  4.9 us (1%)
    ppermute x20, waiting for transfers between devices, swap(): return lax.ppermute(x, 'replica', [(i, i ^ k) for i in range(replicas)])  112 us
    ppermute x7, waiting for transfers between devices, owner_local(): lax.ppermute(direction[k], 'fsdp', [(i, i ^ k) for i in range(owners)])  45 us
    pallas_call x6, Pallas kernels, arrange(): pl.pallas_call(functools.partial(arrange_body, len(adds) // 2, [part[1] f...  31 us
    psum x1, blocking collectives, owner_local(): lax.psum(jnp.where(owner_ids[:, None, None, None] == f, squares, 0.0), 'f...  27.8 us
    pallas_call x2, Pallas kernels, by_rows(): pl.pallas_call(functools.partial(by_rows_body, body, n), grid_spec=pltpu....  26.2 us
    all_to_all x2, waiting for transfers between devices, owner_local(): lax.all_to_all(owned, 'fsdp', split_axis=0, concat_axis=0, tiled=True)  25.9 us
    ppermute x20, starting transfers between devices, swap(): return lax.ppermute(x, 'replica', [(i, i ^ k) for i in range(replicas)])  24.3 us
    psum x1, blocking collectives, owner_local(): squares = lax.psum(squares, 'replica')  22 us
  transfers between devices with their start and end apart: 29, of which 19 were waited for; matrix products, arithmetic and copies ran while one was open for 3% of the time, Pallas kernels for 18%

profile of v7, /device:TPU:0, one launch (start us, length us, event | category | flops | bytes accessed | tf_op | source)
XLA Modules:
  0.0 397.8 jit_solution(15918446061985918981)
XLA Ops:
  3.9 5.2 %shard_map.102 = (bf16[8,80,1152]{2,1,0:T(8,128)(2,1)}, bf16[8,80,1152]{2,1,0:T(8,128)(2,1)}) custom-call(s32[16]{0:T(128)} %reshape.230.cols, bf16[288,18432]{1,0:T(8,128)(2,1)} %bitcast.35), custom_call_target="tpu_custom_call" | custom-call | bytes 5898240 | tf_op jit(solution)/shard_map/pallas_call | solution.py:65
  9.0 3.0 collective-permute-start.1
  13.5 4.8 %shard_map.103 = (bf16[8,64,1152]{2,1,0:T(8,128)(2,1)}, bf16[8,64,1152]{2,1,0:T(8,128)(2,1)}) custom-call(s32[16]{0:T(128)} %reshape.230.cols, bf16[288,18432]{1,0:T(8,128)(2,1)} %bitcast.36, bf16[8,80,1152]{2,1,0:T(8,128)(2,1)} %get-tuple-element.43.refs_0_), custom_call_target="tpu_custom_call" | custom-call | bytes 4718592 | tf_op jit(solution)/shard_map/pallas_call | solution.py:65
  18.9 9.0 %shard_map.104 = (bf16[2,2,144,1152]{3,2,1,0:T(8,128)(2,1)}, bf16[2,2,144,1152]{3,2,1,0:T(8,128)(2,1)}, bf16[2,2,144,1152]{3,2,1,0:T(8,128)(2,1)}, bf16[2,2,144,1152]{3,2,1,0:T(8,128)(2,1)}) custom-call(s32[4]{0:T(128)} %iota_xor_fusion.js, bf16[4,4,144,576]{3,2,1,0:T(8,128)(2,1)} %bitcast.44, bf16[4,4,144,576]{3,2,1,0:T(8,128)(2,1)} %bitcast.45, ...), custom_call_target="tpu_custom_call" | custom-call | bytes 10616832 | tf_op jit(solution)/shard_map/pallas_call | solution.py:100
  29.2 15.5 %collective-permute-done.1.refs_1_ = bf16[8,80,1152]{2,1,0:T(8,128)(2,1)} collective-permute-done((bf16[8,80,1152]{2,1,0:T(8,128)(2,1)}, bf16[8,80,1152]{2,1,0:T(8,128)(2,1)}, u32[]{:S(2)}, u32[]{:S(2)}) %collective-permute-start.1) | collective-permute-done | bytes 1474592 | tf_op jit(solution)/shard_map/ppermute | solution.py:434
  46.1 5.2 %shard_map.105 = (bf16[4,80,1152]{2,1,0:T(8,128)(2,1)}, bf16[4,80,1152]{2,1,0:T(8,128)(2,1)}) custom-call(s32[8]{0:T(128)} %get-tuple-element.97.cols, bf16[288,18432]{1,0:T(8,128)(2,1)} %bitcast.37, bf16[8,80,1152]{2,1,0:T(8,128)(2,1)} %collective-permute-done.refs_0_, bf16[8,80,1152]{2,1,0:T(8,128)(2,1)} %collective-permute-done.1.refs_1_, ...), custom_call_target="tpu_custom_call" | custom-call | bytes 4423680 | tf_op jit(solution)/shard_map/pallas_call | solution.py:65
  53.4 15.3 %collective-permute-done.2.refs_2_ = bf16[4,80,1152]{2,1,0:T(8,128)(2,1)} collective-permute-done((bf16[4,80,1152]{2,1,0:T(8,128)(2,1)}, bf16[4,80,1152]{2,1,0:T(8,128)(2,1)}, u32[]{:S(2)}, u32[]{:S(2)}) %collective-permute-start.2) | collective-permute-done | bytes 737312 | tf_op jit(solution)/shard_map/ppermute | solution.py:434
  69.1 5.8 %shard_map.106.refs_2_ = bf16[8,80,1152]{2,1,0:T(8,128)(2,1)} custom-call(s32[8]{0:T(128)} %get-tuple-element.98.cols, bf16[288,18432]{1,0:T(8,128)(2,1)} %bitcast.38, bf16[8,80,1152]{2,1,0:T(8,128)(2,1)} %collective-permute-done.refs_0_, bf16[8,80,1152]{2,1,0:T(8,128)(2,1)} %collective-permute-done.1.refs_1_, ...), custom_call_target="tpu_custom_call" | custom-call | bytes 5898240 | tf_op jit(solution)/shard_map/pallas_call | solution.py:65
  74.9 4.9 %all-to-all-start = ((bf16[8,80,1152]{2,1,0:T(8,128)(2,1)}), bf16[8,80,1152]{2,1,0:T(8,128)(2,1)}, u32[]{:S(2)}, u32[]{:S(2)}) async-start(bf16[8,80,1152]{2,1,0:T(8,128)(2,1)} %shard_map.106.refs_2_), calls=%async_computation | async-start | bytes 2949120 | tf_op jit(solution)/shard_map/all_to_all | solution.py:452
  82.9 25.5 %collective-permute-done.5.refs_1_ = bf16[8,64,1152]{2,1,0:T(8,128)(2,1)} collective-permute-done((bf16[8,64,1152]{2,1,0:T(8,128)(2,1)S(1)}, bf16[8,64,1152]{2,1,0:T(8,128)(2,1)}, u32[]{:S(2)}, u32[]{:S(2)}) %collective-permute-start.5) | collective-permute-done | bytes 1179680 | tf_op jit(solution)/shard_map/ppermute | solution.py:434
  109.5 4.8 %shard_map.107 = (bf16[4,64,1152]{2,1,0:T(8,128)(2,1)}, bf16[4,64,1152]{2,1,0:T(8,128)(2,1)}) custom-call(s32[8]{0:T(128)} %get-tuple-element.97.cols, bf16[288,18432]{1,0:T(8,128)(2,1)} %bitcast.39, bf16[8,64,1152]{2,1,0:T(8,128)(2,1)} %collective-permute-done.4.refs_0_, bf16[8,64,1152]{2,1,0:T(8,128)(2,1)} %collective-permute-done.5.refs_1_, ...), custom_call_target="tpu_custom_call" | custom-call | bytes 3538944 | tf_op jit(solution)/shard_map/pallas_call | solution.py:65
  116.5 12.7 %collective-permute-done.7.refs_3_ = bf16[4,64,1152]{2,1,0:T(8,128)(2,1)} collective-permute-done((bf16[4,64,1152]{2,1,0:T(8,128)(2,1)}, bf16[4,64,1152]{2,1,0:T(8,128)(2,1)}, u32[]{:S(2)}, u32[]{:S(2)}) %collective-permute-start.7) | collective-permute-done | bytes 589856 | tf_op jit(solution)/shard_map/ppermute | solution.py:434
  130.4 5.3 %shard_map.108 = bf16[8,64,1152]{2,1,0:T(8,128)(2,1)} custom-call(s32[8]{0:T(128)} %get-tuple-element.98.cols, bf16[288,18432]{1,0:T(8,128)(2,1)} %bitcast.40, bf16[8,64,1152]{2,1,0:T(8,128)(2,1)} %collective-permute-done.4.refs_0_, bf16[8,64,1152]{2,1,0:T(8,128)(2,1)} %collective-permute-done.5.refs_1_, ...), custom_call_target="tpu_custom_call" | custom-call | bytes 4718592 | tf_op jit(solution)/shard_map/pallas_call | solution.py:65
  135.7 4.5 %all-to-all-start.1 = ((bf16[8,64,1152]{2,1,0:T(8,128)(2,1)}), bf16[8,64,1152]{2,1,0:T(8,128)(2,1)}, u32[]{:S(2)}, u32[]{:S(2)}) async-start(bf16[8,64,1152]{2,1,0:T(8,128)(2,1)} %shard_map.108), calls=%async_computation.1 | async-start | bytes 2359296 | tf_op jit(solution)/shard_map/all_to_all | solution.py:452
  143.8 25.9 %all-to-all-done.1.refs_1_ = bf16[8,64,1152]{2,1,0:T(8,128)(2,1)} async-done(((bf16[8,64,1152]{2,1,0:T(8,128)(2,1)}), bf16[8,64,1152]{2,1,0:T(8,128)(2,1)}, u32[]{:S(2)}, u32[]{:S(2)}) %all-to-all-start.1) | async-done | bytes 1179680 | tf_op jit(solution)/shard_map/all_to_all | solution.py:452
  169.7 10.7 %shard_map.109 = (bf16[3,2,144,1152]{3,2,1,0:T(8,128)(2,1)}, bf16[3,2,144,1152]{3,2,1,0:T(8,128)(2,1)}, bf16[3,2,144,1152]{3,2,1,0:T(8,128)(2,1)}, bf16[3,2,144,1152]{3,2,1,0:T(8,128)(2,1)}) custom-call(s32[4]{0:T(128)} %iota_xor_fusion.js, bf16[8,80,1152]{2,1,0:T(8,128)(2,1)} %all-to-all-done.refs_0_, bf16[8,64,1152]{2,1,0:T(8,128)(2,1)} %all-to-all-done.1.refs_1_), custom_call_target="tpu_custom_call" | custom-call | flops 3057647616 | bytes 10616832 | tf_op jit(solution)/shard_map/pallas_call | solution.py:160
  183.8 16.6 %collective-permute-done.9.refs_4_ = bf16[2,2,144,1152]{3,2,1,0:T(8,128)(2,1)} collective-permute-done((bf16[2,2,144,1152]{3,2,1,0:T(8,128)(2,1)}, bf16[2,2,144,1152]{3,2,1,0:T(8,128)(2,1)}, u32[]{:S(2)}, u32[]{:S(2)}) %collective-permute-start.9) | collective-permute-done | bytes 1327136 | tf_op jit(solution)/shard_map/ppermute | solution.py:434
  201.1 11.8 %shard_map.111 = (bf16[144,1152]{1,0:T(8,128)(2,1)}, bf16[144,1152]{1,0:T(8,128)(2,1)}, bf16[144,1152]{1,0:T(8,128)(2,1)}, bf16[144,1152]{1,0:T(8,128)(2,1)}, bf...) custom-call(s32[4]{0:T(128)} %iota_xor_fusion.js, ...), custom_call_target="tpu_custom_call" | custom-call | flops 3057647616 | bytes 10616832 | tf_op jit(solution)/shard_map/pallas_call | solution.py:219
  216.6 7.3 %collective-permute-done.12.refs_2_ = bf16[144,1152]{1,0:T(8,128)(2,1)} collective-permute-done((bf16[144,1152]{1,0:T(8,128)(2,1)}, bf16[144,1152]{1,0:T(8,128)(2,1)}, u32[]{:S(2)}, u32[]{:S(2)}) %collective-permute-start.12) | collective-permute-done | bytes 331808 | tf_op jit(solution)/shard_map/ppermute | solution.py:462
  226.8 9.3 %collective-permute-done.13.refs_3_ = bf16[144,1152]{1,0:T(8,128)(2,1)} collective-permute-done((bf16[144,1152]{1,0:T(8,128)(2,1)}, bf16[144,1152]{1,0:T(8,128)(2,1)}, u32[]{:S(2)}, u32[]{:S(2)}) %collective-permute-start.13) | collective-permute-done | bytes 331808 | tf_op jit(solution)/shard_map/ppermute | solution.py:462
  236.1 14.0 %collective-permute-done.14.refs_4_ = bf16[144,1152]{1,0:T(8,128)(2,1)} collective-permute-done((bf16[144,1152]{1,0:T(8,128)(2,1)}, bf16[144,1152]{1,0:T(8,128)(2,1)}, u32[]{:S(2)}, u32[]{:S(2)}) %collective-permute-start.14) | collective-permute-done | bytes 331808 | tf_op jit(solution)/shard_map/ppermute | solution.py:462
  250.1 3.7 collective-permute-start.16
  253.8 7.6 %collective-permute-done.15.refs_5_ = bf16[144,1152]{1,0:T(8,128)(2,1)} collective-permute-done((bf16[144,1152]{1,0:T(8,128)(2,1)}, bf16[144,1152]{1,0:T(8,128)(2,1)}, u32[]{:S(2)}, u32[]{:S(2)}) %collective-permute-start.15) | collective-permute-done | bytes 331808 | tf_op jit(solution)/shard_map/ppermute | solution.py:462
  261.5 6.3 %collective-permute-start.17 = (bf16[144,1152]{1,0:T(8,128)(2,1)}, bf16[144,1152]{1,0:T(8,128)(2,1)}, u32[]{:S(2)}, u32[]{:S(2)}) collective-permute-start(bf16[144,1152]{1,0:T(8,128)(2,1)} %get-tuple-element.66), channel_id=1, source_target_pairs={{0,28},{4,24},{8,20},{12,16},{16,12},{20,8},{24,4},{28,0},{1,29},{... | collective-permute-start | bytes 995336 | tf_op jit(solution)/shard_map/ppermute | solution.py:462
  269.5 6.7 %collective-permute-done.17.refs_7_ = bf16[144,1152]{1,0:T(8,128)(2,1)} collective-permute-done((bf16[144,1152]{1,0:T(8,128)(2,1)}, bf16[144,1152]{1,0:T(8,128)(2,1)}, u32[]{:S(2)}, u32[]{:S(2)}) %collective-permute-start.17) | collective-permute-done | bytes 331808 | tf_op jit(solution)/shard_map/ppermute | solution.py:462
  276.3 9.8 %collective-permute-done.19.refs_9_ = bf16[3,2,144,1152]{3,2,1,0:T(8,128)(2,1)} collective-permute-done((bf16[3,2,144,1152]{3,2,1,0:T(8,128)(2,1)}, bf16[3,2,144,1152]{3,2,1,0:T(8,128)(2,1)}, u32[]{:S(2)}, u32[]{:S(2)}) %collective-permute-start.19) | collective-permute-done | bytes 1990688 | tf_op jit(solution)/shard_map/ppermute | solution.py:434
  294.4 12.0 %shard_map.113 = (f32[4,4,144,576]{3,2,1,0:T(8,128)}, f32[4,2,8,128]{3,2,1,0:T(8,128)}) custom-call(s32[4]{0:T(128)} %iota_xor_fusion.js, bf16[3,2,144,1152]{3,2,1,0:T(8,128)(2,1)} %get-tuple-element.52.refs_6_.refs_0_, bf16[3,2,144,1152]{3,2,1,0:T(8,128)(2,1)} %get-tuple-element.70.refs_1_, bf16[3,2,144,1152]{3,2,1,0:T(8,128)(2,1)} %get-tuple-element.71.refs_2_, ...), custom_call_target="tpu_custom_call" | custom-call | bytes 13271040 | tf_op jit(solution)/shard_map/pallas_call | solution.py:323
  309.6 27.8 %psum.14 = f32[8,2,4,4]{2,0,3,1:T(8,128)S(1)} all-reduce(f32[8,2,4,4]{2,0,3,1:T(8,128)S(1)} %broadcast_select_fusion), channel_id=1, replica_groups=mesh['fsdp'=8,'replica'=4] {'fsdp'}, use_global_device_ids=true, to_apply=%region_2.3 | all-reduce | flops 256 | bytes 2048 | tf_op jit(solution)/shard_map/psum | solution.py:480
  337.4 22.0 %psum.15 = f32[8,2,4,4]{2,0,3,1:T(8,128)S(1)} all-reduce(f32[8,2,4,4]{2,0,3,1:T(8,128)S(1)} %psum.14), channel_id=1, replica_groups=mesh['fsdp'=8,'replica'=4] {'replica'}, use_global_device_ids=true, to_apply=%region_3.4 | all-reduce | flops 256 | bytes 2048 | tf_op jit(solution)/shard_map/psum | solution.py:481
  363.4 14.2 %shard_map.116 = (f32[4,4,144,576]{3,2,1,0:T(8,128)}, f32[4,4,144,576]{3,2,1,0:T(8,128)}) custom-call(s32[4]{0:T(128)} %iota_xor_fusion.js, bf16[3,2,144,1152]{3,2,1,0:T(8,128)(2,1)} %get-tuple-element.52.refs_6_.refs_0_, bf16[3,2,144,1152]{3,2,1,0:T(8,128)(2,1)} %get-tuple-element.70.refs_1_, bf16[3,2,144,1152]{3,2,1,0:T(8,128)(2,1)} %get-tuple-element.71.refs_2_, ...), custom_call_target="tpu_custom_call" | custom-call | bytes 26542080 | tf_op jit(solution)/shard_map/pallas_call | solution.py:323
  377.6 11.0 %collective-permute-done.25.refs_6_ = bf16[4,144,1152]{2,1,0:T(8,128)(2,1)} collective-permute-done((bf16[4,144,1152]{2,1,0:T(8,128)(2,1)}, bf16[4,144,1152]{2,1,0:T(8,128)(2,1)}, u32[]{:S(2)}, u32[]{:S(2)}) %collective-permute-start.25) | collective-permute-done | bytes 1327136 | tf_op jit(solution)/shard_map/ppermute | solution.py:434
  388.9 8.7 %shard_map.115 = bf16[288,18432]{1,0:T(8,128)(2,1)} custom-call(s32[32]{0:T(128)} %multiply_add_fusion.src, s32[32]{0:T(128)} %get-tuple-element.94.item, f32[32]{0:T(128)} %select_reduce_fusion.refs_2_.scale, bf16[4,144,1152]{2,1,0:T(8,128)(2,1)} %get-tuple-element.75.refs_0_, bf16[4,144,1152]{2,1,0:T(8,128)(2,1)} %get-tuple-element.76.refs_1_, ...), custom_call_target="tpu_custom_call" | custom-call | bytes 21233664 | tf_op jit(solution)/shard_map/pallas_call | solution.py:391
  (82 shorter events, 49.8 us)
Async XLA Ops:
  2.7 0.6 copy-start.1
  9.0 35.6 %collective-permute-start.1 = (bf16[8,80,1152]{2,1,0:T(8,128)(2,1)}, bf16[8,80,1152]{2,1,0:T(8,128)(2,1)}, u32[]{:S(2)}, u32[]{:S(2)}) collective-permute-start(bf16[8,80,1152]{2,1,0:T(8,128)(2,1)} %get-tuple-element.44), channel_id=1, source_target_pairs={{0,2},{1,3},{2,0},{3,1},{4,6},{5,7},{6,4},{7,5},{8,10},{9,11},{10,... | collective-permute-start | bytes 4423688 | tf_op jit(solution)/shard_map/ppermute | solution.py:434
  12.1 34.1 %collective-permute-start = (bf16[8,80,1152]{2,1,0:T(8,128)(2,1)}, bf16[8,80,1152]{2,1,0:T(8,128)(2,1)}, u32[]{:S(2)}, u32[]{:S(2)}) collective-permute-start(bf16[8,80,1152]{2,1,0:T(8,128)(2,1)} %get-tuple-element.43.refs_0_), channel_id=1, source_target_pairs={{0,1},{1,0},{2,3},{3,2},{4,5},{5,4},{6,7},{7,6},{8,9},{9,8},{10,11... | collective-permute-start | bytes 4423688 | tf_op jit(solution)/shard_map/ppermute | solution.py:434
  51.3 17.4 %collective-permute-start.2 = (bf16[4,80,1152]{2,1,0:T(8,128)(2,1)}, bf16[4,80,1152]{2,1,0:T(8,128)(2,1)}, u32[]{:S(2)}, u32[]{:S(2)}) collective-permute-start(bf16[4,80,1152]{2,1,0:T(8,128)(2,1)} %get-tuple-element.47), channel_id=1, source_target_pairs={{0,2},{1,3},{2,0},{3,1},{4,6},{5,7},{6,4},{7,5},{8,10},{9,11},{10,... | collective-permute-start | bytes 2211848 | tf_op jit(solution)/shard_map/ppermute | solution.py:434
  51.7 17.4 %collective-permute-start.3 = (bf16[4,80,1152]{2,1,0:T(8,128)(2,1)}, bf16[4,80,1152]{2,1,0:T(8,128)(2,1)}, u32[]{:S(2)}, u32[]{:S(2)}) collective-permute-start(bf16[4,80,1152]{2,1,0:T(8,128)(2,1)} %get-tuple-element.48), channel_id=1, source_target_pairs={{0,1},{1,0},{2,3},{3,2},{4,5},{5,4},{6,7},{7,6},{8,9},{9,8},{10,11... | collective-permute-start | bytes 2211848 | tf_op jit(solution)/shard_map/ppermute | solution.py:434
  74.9 5.0 %copy-start.3 = (bf16[8,64,1152]{2,1,0:T(8,128)(2,1)S(1)}, bf16[8,64,1152]{2,1,0:T(8,128)(2,1)}, u32[]{:S(2)}) copy-start(bf16[8,64,1152]{2,1,0:T(8,128)(2,1)} %get-tuple-element.49) | copy-start | bytes 3538948
  74.9 6.4 %copy-start = (bf16[8,64,1152]{2,1,0:T(8,128)(2,1)S(1)}, bf16[8,64,1152]{2,1,0:T(8,128)(2,1)}, u32[]{:S(2)}) copy-start(bf16[8,64,1152]{2,1,0:T(8,128)(2,1)} %get-tuple-element.45.refs_0_) | copy-start | bytes 3538948
  74.9 60.8 %all-to-all-start = ((bf16[8,80,1152]{2,1,0:T(8,128)(2,1)}), bf16[8,80,1152]{2,1,0:T(8,128)(2,1)}, u32[]{:S(2)}, u32[]{:S(2)}) async-start(bf16[8,80,1152]{2,1,0:T(8,128)(2,1)} %shard_map.106.refs_2_), calls=%async_computation | async-start | bytes 2949120 | tf_op jit(solution)/shard_map/all_to_all | solution.py:452
  79.9 28.5 %collective-permute-start.5 = (bf16[8,64,1152]{2,1,0:T(8,128)(2,1)S(1)}, bf16[8,64,1152]{2,1,0:T(8,128)(2,1)}, u32[]{:S(2)}, u32[]{:S(2)}) collective-permute-start(bf16[8,64,1152]{2,1,0:T(8,128)(2,1)S(1)} %copy-done.3), channel_id=1, source_target_pairs={{0,2},{1,3},{2,0},{3,1},{4,6},{5,7},{6,4},{7,5},{8,10},{9,11},{10,... | collective-permute-start | bytes 3538952 | tf_op jit(solution)/shard_map/ppermute | solution.py:434
  81.4 28.1 %collective-permute-start.4 = (bf16[8,64,1152]{2,1,0:T(8,128)(2,1)S(1)}, bf16[8,64,1152]{2,1,0:T(8,128)(2,1)}, u32[]{:S(2)}, u32[]{:S(2)}) collective-permute-start(bf16[8,64,1152]{2,1,0:T(8,128)(2,1)S(1)} %copy-done), channel_id=1, source_target_pairs={{0,1},{1,0},{2,3},{3,2},{4,5},{5,4},{6,7},{7,6},{8,9},{9,8},{10,11... | collective-permute-start | bytes 3538952 | tf_op jit(solution)/shard_map/ppermute | solution.py:434
  114.3 14.9 %collective-permute-start.7 = (bf16[4,64,1152]{2,1,0:T(8,128)(2,1)}, bf16[4,64,1152]{2,1,0:T(8,128)(2,1)}, u32[]{:S(2)}, u32[]{:S(2)}) collective-permute-start(bf16[4,64,1152]{2,1,0:T(8,128)(2,1)} %get-tuple-element.51), channel_id=1, source_target_pairs={{0,1},{1,0},{2,3},{3,2},{4,5},{5,4},{6,7},{7,6},{8,9},{9,8},{10,11... | collective-permute-start | bytes 1769480 | tf_op jit(solution)/shard_map/ppermute | solution.py:434
  115.8 14.6 %collective-permute-start.6 = (bf16[4,64,1152]{2,1,0:T(8,128)(2,1)}, bf16[4,64,1152]{2,1,0:T(8,128)(2,1)}, u32[]{:S(2)}, u32[]{:S(2)}) collective-permute-start(bf16[4,64,1152]{2,1,0:T(8,128)(2,1)} %get-tuple-element.50.refs_3_), channel_id=1, source_target_pairs={{0,2},{1,3},{2,0},{3,1},{4,6},{5,7},{6,4},{7,5},{8,10},{9,11},{10,... | collective-permute-start | bytes 1769480 | tf_op jit(solution)/shard_map/ppermute | solution.py:434
  135.7 33.9 %all-to-all-start.1 = ((bf16[8,64,1152]{2,1,0:T(8,128)(2,1)}), bf16[8,64,1152]{2,1,0:T(8,128)(2,1)}, u32[]{:S(2)}, u32[]{:S(2)}) async-start(bf16[8,64,1152]{2,1,0:T(8,128)(2,1)} %shard_map.108), calls=%async_computation.1 | async-start | bytes 2359296 | tf_op jit(solution)/shard_map/all_to_all | solution.py:452
  140.2 41.3 %collective-permute-start.8 = (bf16[2,2,144,1152]{3,2,1,0:T(8,128)(2,1)}, bf16[2,2,144,1152]{3,2,1,0:T(8,128)(2,1)}, u32[]{:S(2)}, u32[]{:S(2)}) collective-permute-start(bf16[2,2,144,1152]{3,2,1,0:T(8,128)(2,1)} %get-tuple-element.56), channel_id=1, source_target_pairs={{0,1},{1,0},{2,3},{3,2},{4,5},{5,4},{6,7},{7,6},{8,9},{9,8},{10,11... | collective-permute-start | bytes 3981320 | tf_op jit(solution)/shard_map/ppermute | solution.py:434
  140.8 59.7 %collective-permute-start.9 = (bf16[2,2,144,1152]{3,2,1,0:T(8,128)(2,1)}, bf16[2,2,144,1152]{3,2,1,0:T(8,128)(2,1)}, u32[]{:S(2)}, u32[]{:S(2)}) collective-permute-start(bf16[2,2,144,1152]{3,2,1,0:T(8,128)(2,1)} %get-tuple-element.57), channel_id=1, source_target_pairs={{0,2},{1,3},{2,0},{3,1},{4,6},{5,7},{6,4},{7,5},{8,10},{9,11},{10,... | collective-permute-start | bytes 3981320 | tf_op jit(solution)/shard_map/ppermute | solution.py:434
  141.4 59.7 %collective-permute-start.10 = (bf16[2,2,144,1152]{3,2,1,0:T(8,128)(2,1)}, bf16[2,2,144,1152]{3,2,1,0:T(8,128)(2,1)}, u32[]{:S(2)}, u32[]{:S(2)}) collective-permute-start(bf16[2,2,144,1152]{3,2,1,0:T(8,128)(2,1)} %get-tuple-element.58), channel_id=1, source_target_pairs={{0,3},{1,2},{2,1},{3,0},{4,7},{5,6},{6,5},{7,4},{8,11},{9,10},{10,... | collective-permute-start | bytes 3981320 | tf_op jit(solution)/shard_map/ppermute | solution.py:434
  180.3 95.9 %collective-permute-start.18 = (bf16[3,2,144,1152]{3,2,1,0:T(8,128)(2,1)}, bf16[3,2,144,1152]{3,2,1,0:T(8,128)(2,1)}, u32[]{:S(2)}, u32[]{:S(2)}) collective-permute-start(bf16[3,2,144,1152]{3,2,1,0:T(8,128)(2,1)} %get-tuple-element.67), channel_id=1, source_target_pairs={{0,1},{1,0},{2,3},{3,2},{4,5},{5,4},{6,7},{7,6},{8,9},{9,8},{10,11... | collective-permute-start | bytes 5971976 | tf_op jit(solution)/shard_map/ppermute | solution.py:434
  180.9 105.2 %collective-permute-start.19 = (bf16[3,2,144,1152]{3,2,1,0:T(8,128)(2,1)}, bf16[3,2,144,1152]{3,2,1,0:T(8,128)(2,1)}, u32[]{:S(2)}, u32[]{:S(2)}) collective-permute-start(bf16[3,2,144,1152]{3,2,1,0:T(8,128)(2,1)} %get-tuple-element.68), channel_id=1, source_target_pairs={{0,2},{1,3},{2,0},{3,1},{4,6},{5,7},{6,4},{7,5},{8,10},{9,11},{10,... | collective-permute-start | bytes 5971976 | tf_op jit(solution)/shard_map/ppermute | solution.py:434
  181.5 104.6 %collective-permute-start.20 = (bf16[3,2,144,1152]{3,2,1,0:T(8,128)(2,1)}, bf16[3,2,144,1152]{3,2,1,0:T(8,128)(2,1)}, u32[]{:S(2)}, u32[]{:S(2)}) collective-permute-start(bf16[3,2,144,1152]{3,2,1,0:T(8,128)(2,1)} %get-tuple-element.69), channel_id=1, source_target_pairs={{0,3},{1,2},{2,1},{3,0},{4,7},{5,6},{6,5},{7,4},{8,11},{9,10},{10,... | collective-permute-start | bytes 5971976 | tf_op jit(solution)/shard_map/ppermute | solution.py:434
  212.9 2.1 collective-permute-start.11
  213.0 11.0 %collective-permute-start.12 = (bf16[144,1152]{1,0:T(8,128)(2,1)}, bf16[144,1152]{1,0:T(8,128)(2,1)}, u32[]{:S(2)}, u32[]{:S(2)}) collective-permute-start(bf16[144,1152]{1,0:T(8,128)(2,1)} %get-tuple-element.61), channel_id=1, source_target_pairs={{0,8},{4,12},{8,0},{12,4},{16,24},{20,28},{24,16},{28,20},{1,9},{5... | collective-permute-start | bytes 995336 | tf_op jit(solution)/shard_map/ppermute | solution.py:462
  214.9 21.1 %collective-permute-start.13 = (bf16[144,1152]{1,0:T(8,128)(2,1)}, bf16[144,1152]{1,0:T(8,128)(2,1)}, u32[]{:S(2)}, u32[]{:S(2)}) collective-permute-start(bf16[144,1152]{1,0:T(8,128)(2,1)} %get-tuple-element.62), channel_id=1, source_target_pairs={{0,12},{4,8},{8,4},{12,0},{16,28},{20,24},{24,20},{28,16},{1,13},{... | collective-permute-start | bytes 995336 | tf_op jit(solution)/shard_map/ppermute | solution.py:462
  223.9 26.2 %collective-permute-start.14 = (bf16[144,1152]{1,0:T(8,128)(2,1)}, bf16[144,1152]{1,0:T(8,128)(2,1)}, u32[]{:S(2)}, u32[]{:S(2)}) collective-permute-start(bf16[144,1152]{1,0:T(8,128)(2,1)} %get-tuple-element.63), channel_id=1, source_target_pairs={{0,16},{4,20},{8,24},{12,28},{16,0},{20,4},{24,8},{28,12},{1,17},{... | collective-permute-start | bytes 995336 | tf_op jit(solution)/shard_map/ppermute | solution.py:462
  236.1 25.4 %collective-permute-start.15 = (bf16[144,1152]{1,0:T(8,128)(2,1)}, bf16[144,1152]{1,0:T(8,128)(2,1)}, u32[]{:S(2)}, u32[]{:S(2)}) collective-permute-start(bf16[144,1152]{1,0:T(8,128)(2,1)} %get-tuple-element.64), channel_id=1, source_target_pairs={{0,20},{4,16},{8,28},{12,24},{16,4},{20,0},{24,12},{28,8},{1,21},{... | collective-permute-start | bytes 995336 | tf_op jit(solution)/shard_map/ppermute | solution.py:462
  250.1 19.5 %collective-permute-start.16 = (bf16[144,1152]{1,0:T(8,128)(2,1)}, bf16[144,1152]{1,0:T(8,128)(2,1)}, u32[]{:S(2)}, u32[]{:S(2)}) collective-permute-start(bf16[144,1152]{1,0:T(8,128)(2,1)} %get-tuple-element.65), channel_id=1, source_target_pairs={{0,24},{4,28},{8,16},{12,20},{16,8},{20,12},{24,0},{28,4},{1,25},{... | collective-permute-start | bytes 995336 | tf_op jit(solution)/shard_map/ppermute | solution.py:462
  261.5 14.8 %collective-permute-start.17 = (bf16[144,1152]{1,0:T(8,128)(2,1)}, bf16[144,1152]{1,0:T(8,128)(2,1)}, u32[]{:S(2)}, u32[]{:S(2)}) collective-permute-start(bf16[144,1152]{1,0:T(8,128)(2,1)} %get-tuple-element.66), channel_id=1, source_target_pairs={{0,28},{4,24},{8,20},{12,16},{16,12},{20,8},{24,4},{28,0},{1,29},{... | collective-permute-start | bytes 995336 | tf_op jit(solution)/shard_map/ppermute | solution.py:462
  288.7 72.1 %collective-permute-start.24 = (bf16[4,144,1152]{2,1,0:T(8,128)(2,1)}, bf16[4,144,1152]{2,1,0:T(8,128)(2,1)}, u32[]{:S(2)}, u32[]{:S(2)}) collective-permute-start(bf16[4,144,1152]{2,1,0:T(8,128)(2,1)} %get-tuple-element.75.refs_0_), channel_id=1, source_target_pairs={{0,2},{1,3},{2,0},{3,1},{4,6},{5,7},{6,4},{7,5},{8,10},{9,11},{10,... | collective-permute-start | bytes 3981320 | tf_op jit(solution)/shard_map/ppermute | solution.py:434
  290.0 70.8 %collective-permute-start.21 = (bf16[4,144,1152]{2,1,0:T(8,128)(2,1)}, bf16[4,144,1152]{2,1,0:T(8,128)(2,1)}, u32[]{:S(2)}, u32[]{:S(2)}) collective-permute-start(bf16[4,144,1152]{2,1,0:T(8,128)(2,1)} %get-tuple-element.75.refs_0_), channel_id=1, source_target_pairs={{0,1},{1,0},{2,3},{3,2},{4,5},{5,4},{6,7},{7,6},{8,9},{9,8},{10,11... | collective-permute-start | bytes 3981320 | tf_op jit(solution)/shard_map/ppermute | solution.py:434
  290.9 70.0 %collective-permute-start.23 = (bf16[4,144,1152]{2,1,0:T(8,128)(2,1)}, bf16[4,144,1152]{2,1,0:T(8,128)(2,1)}, u32[]{:S(2)}, u32[]{:S(2)}) collective-permute-start(bf16[4,144,1152]{2,1,0:T(8,128)(2,1)} %get-tuple-element.76.refs_1_), channel_id=1, source_target_pairs={{0,1},{1,0},{2,3},{3,2},{4,5},{5,4},{6,7},{7,6},{8,9},{9,8},{10,11... | collective-permute-start | bytes 3981320 | tf_op jit(solution)/shard_map/ppermute | solution.py:434
  292.0 68.8 %collective-permute-start.22 = (bf16[4,144,1152]{2,1,0:T(8,128)(2,1)}, bf16[4,144,1152]{2,1,0:T(8,128)(2,1)}, u32[]{:S(2)}, u32[]{:S(2)}) collective-permute-start(bf16[4,144,1152]{2,1,0:T(8,128)(2,1)} %get-tuple-element.76.refs_1_), channel_id=1, source_target_pairs={{0,2},{1,3},{2,0},{3,1},{4,6},{5,7},{6,4},{7,5},{8,10},{9,11},{10,... | collective-permute-start | bytes 3981320 | tf_op jit(solution)/shard_map/ppermute | solution.py:434
  360.9 27.7 %collective-permute-start.25 = (bf16[4,144,1152]{2,1,0:T(8,128)(2,1)}, bf16[4,144,1152]{2,1,0:T(8,128)(2,1)}, u32[]{:S(2)}, u32[]{:S(2)}) collective-permute-start(bf16[4,144,1152]{2,1,0:T(8,128)(2,1)} %get-tuple-element.77.refs_2_), channel_id=1, source_target_pairs={{0,2},{1,3},{2,0},{3,1},{4,6},{5,7},{6,4},{7,5},{8,10},{9,11},{10,... | collective-permute-start | bytes 3981320 | tf_op jit(solution)/shard_map/ppermute | solution.py:434
  361.7 27.2 %collective-permute-start.26 = (bf16[4,144,1152]{2,1,0:T(8,128)(2,1)}, bf16[4,144,1152]{2,1,0:T(8,128)(2,1)}, u32[]{:S(2)}, u32[]{:S(2)}) collective-permute-start(bf16[4,144,1152]{2,1,0:T(8,128)(2,1)} %get-tuple-element.78.refs_5_), channel_id=1, source_target_pairs={{0,1},{1,0},{2,3},{3,2},{4,5},{5,4},{6,7},{7,6},{8,9},{9,8},{10,11... | collective-permute-start | bytes 3981320 | tf_op jit(solution)/shard_map/ppermute | solution.py:434
  (1 other events, 0.6 us)

commit v8 on v6

--- a/solution.py
+++ b/solution.py
@@ -286,52 +286,48 @@
     )(*parts, *through)
 
 
-def moment_body(q, received, moment, moment_out, square_out):
-    g = received[0, 0, :, q * B : q * B + B].astype(jnp.float32)
-    second = 0.95 * moment[q, 0] + 0.05 * g * g
-    moment_out[q, 0] = second
+def moment_body(p, q, received, moment, moment_out, square_out):
+    a = 2 * p + q
+    g = received[0, p, :, q * B : q * B + B].astype(jnp.float32)
+    second = 0.95 * moment[a, 0] + 0.05 * g * g
+    moment_out[a, 0] = second
     adam = g / (jnp.sqrt(second) + 1e-08)
-    square_out[0, 0, q : q + 1, :] = jnp.full((1, LANES), jnp.sum(adam * adam))
-
-
-def gram_update_body(q, received, left, right, left_out, right_out):
+    square_out[0, a : a + 1, :] = jnp.full((1, LANES), jnp.sum(adam * adam))
+
+
+def gram_update_body(p, q, received, left, right, left_out, right_out):
     for kind, old, new in ((1, left, left_out), (2, right, right_out)):
-        product = received[kind, 0, :, q * B : q * B + B].astype(jnp.float32)
-        new[q, 0] = 0.95 * old[q, 0] + 0.05 * product
-
-
-def by_rows_body(body, n, js, *refs):
+        product = received[kind, p, :, q * B : q * B + B].astype(jnp.float32)
+        new[2 * p + q, 0] = 0.95 * old[2 * p + q, 0] + 0.05 * product
+
+
+def by_rows_body(body, n, pairs, js, *refs):
     m = pl.program_id(0)
     for k in range(n):
 
         @pl.when(m == k)
         def _():
-            for q in range(2):
-                body(q, refs[k], *refs[n:])
+            for p in range(pairs):
+                for q in range(2):
+                    body(p, q, refs[k], *refs[n:])
 
 
 def by_rows(body, kinds, js, received, olds, squares):
     n = js.shape[0]
     blocks, _, rows, _ = olds[0].shape
     pairs, w = received[0].shape[1], received[0].shape[3]
-    own = pl.BlockSpec((2, 1, rows, B), lambda m, p, j: (p, j[m], 0, 0))
+    own = pl.BlockSpec((blocks, 1, rows, B), lambda m, j: (0, j[m], 0, 0))
     out_specs = [own] * len(olds)
     out_shape = [jax.ShapeDtypeStruct(old.shape, jnp.float32) for old in olds]
     if squares:
-        out_specs.append(pl.BlockSpec((1, 1, 8, LANES), lambda m, p, j: (m, p, 0, 0)))
-        out_shape.append(jax.ShapeDtypeStruct((n, pairs, 8, LANES), jnp.float32))
-    return pl.pallas_call(
-        functools.partial(by_rows_body, body, n),
+        out_specs.append(pl.BlockSpec((1, 8, LANES), lambda m, j: (m, 0, 0)))
+        out_shape.append(jax.ShapeDtypeStruct((n, 8, LANES), jnp.float32))
+    return pl.pallas_call(
+        functools.partial(by_rows_body, body, n, pairs),
         grid_spec=pltpu.PrefetchScalarGridSpec(
             num_scalar_prefetch=1,
-            grid=(n, pairs),
-            in_specs=[
-                pl.BlockSpec(
-                    (kinds, 1, rows, w),
-                    lambda m, p, j, k=k: (0, visit(k, m, p, pairs - 1), 0, 0),
-                )
-                for k in range(n)
-            ]
+            grid=(n,),
+            in_specs=[pl.BlockSpec((kinds, pairs, rows, w), lambda m, j: (0, 0, 0, 0))] * n
             + [own] * len(olds),
             out_specs=out_specs,
         ),
@@ -469,7 +465,7 @@
     moment, adam_square = by_rows(
         moment_body, 1, js, received, [as_rows(second_moment)], True
     )
-    adam_square = adam_square[:, :, :2, 0].reshape(replicas, row_blocks)
+    adam_square = adam_square[:, :row_blocks, 0]
     slot_ids = jnp.arange(replicas, dtype=jnp.int32)
     adam_square = jnp.sum(
         jnp.where((js[:, None] == slot_ids)[:, :, None], adam_square[:, None, :], 0.0), axis=0
@@ -477,8 +473,8 @@
     direction_square = direction_square[:, :2, 0].reshape(row_blocks)
     slot_place = (slot_ids == r)[:, None]
     squares = jnp.stack([adam_square, jnp.where(slot_place, direction_square, 0.0)])
+    squares = lax.psum(jnp.where(owner_ids[:, None, None, None] == f, squares, 0.0), "fsdp")
     squares = lax.psum(squares, "replica")
-    squares = lax.psum(jnp.where(owner_ids[:, None, None, None] == f, squares, 0.0), "fsdp")
     ratio = jnp.sqrt(squares[:, 0]) / jnp.sqrt(squares[:, 1] + 1e-06)
     row_ratio = lax.dynamic_index_in_dim(
         ratio.reshape(columns, row_blocks), f // sub_count, 1, keepdims=False

time: 404 us -> 382 us (0.946)
  blocking collectives: 69.7 us -> 50.5 us
    psum x1, blocking collectives: 43.6 us -> 23.6 us  [owner_local(): squares = lax.psum(squares, 'replica')]
where the time goes in v8:
time: 382 us; the launch traced here: 381 us
  waiting for transfers between devices  166 us (43%)
  Pallas kernels  97.1 us (25%)
  starting transfers between devices  50.6 us (13%)
  blocking collectives  50.5 us (13%)
  other arithmetic  10.5 us (3%)
  local copies, waits for them, and re-layouts  4.8 us (1%)
    ppermute x20, waiting for transfers between devices, swap(): return lax.ppermute(x, 'replica', [(i, i ^ k) for i in range(replicas)])  89.8 us
    ppermute x7, waiting for transfers between devices, owner_local(): lax.ppermute(direction[k], 'fsdp', [(i, i ^ k) for i in range(owners)])  44.4 us
    all_to_all x2, waiting for transfers between devices, owner_local(): lax.all_to_all(owned, 'fsdp', split_axis=0, concat_axis=0, tiled=True)  32.3 us
    pallas_call x6, Pallas kernels, arrange(): pl.pallas_call(functools.partial(arrange_body, len(adds) // 2, [part[1] f...  31 us
    psum x1, blocking collectives, owner_local(): lax.psum(jnp.where(owner_ids[:, None, None, None] == f, squares, 0.0), 'f...  26.9 us
    ppermute x20, starting transfers between devices, swap(): return lax.ppermute(x, 'replica', [(i, i ^ k) for i in range(replicas)])  24.2 us
    psum x1, blocking collectives, owner_local(): squares = lax.psum(squares, 'replica')  23.6 us
    pallas_call x2, Pallas kernels, by_rows(): pl.pallas_call(functools.partial(by_rows_body, body, n, pairs), grid_spec...  23.2 us
  transfers between devices with their start and end apart: 29, of which 19 were waited for; matrix products, arithmetic and copies ran while one was open for 3% of the time, Pallas kernels for 20%

profile of v8, /device:TPU:0, one launch (start us, length us, event | category | flops | bytes accessed | tf_op | source)
XLA Modules:
  0.0 381.1 jit_solution(8540295895558176855)
XLA Ops:
  3.9 4.8 %shard_map.102 = (bf16[8,64,1152]{2,1,0:T(8,128)(2,1)}, bf16[8,64,1152]{2,1,0:T(8,128)(2,1)}) custom-call(s32[16]{0:T(128)} %reshape.230.cols, bf16[288,18432]{1,0:T(8,128)(2,1)} %bitcast.34), custom_call_target="tpu_custom_call" | custom-call | bytes 4718592 | tf_op jit(solution)/shard_map/pallas_call | solution.py:65
  8.7 3.0 collective-permute-start.1
  13.3 5.1 %shard_map.103 = (bf16[8,80,1152]{2,1,0:T(8,128)(2,1)}, bf16[8,80,1152]{2,1,0:T(8,128)(2,1)}) custom-call(s32[16]{0:T(128)} %reshape.230.cols, bf16[288,18432]{1,0:T(8,128)(2,1)} %bitcast.35, bf16[8,64,1152]{2,1,0:T(8,128)(2,1)} %get-tuple-element.43.refs_0_), custom_call_target="tpu_custom_call" | custom-call | bytes 5898240 | tf_op jit(solution)/shard_map/pallas_call | solution.py:65
  19.0 9.0 %shard_map.104 = (bf16[2,2,144,1152]{3,2,1,0:T(8,128)(2,1)}, bf16[2,2,144,1152]{3,2,1,0:T(8,128)(2,1)}, bf16[2,2,144,1152]{3,2,1,0:T(8,128)(2,1)}, bf16[2,2,144,1152]{3,2,1,0:T(8,128)(2,1)}) custom-call(s32[4]{0:T(128)} %iota_xor_fusion.js, bf16[4,4,144,576]{3,2,1,0:T(8,128)(2,1)} %bitcast.43, bf16[4,4,144,576]{3,2,1,0:T(8,128)(2,1)} %bitcast.44, ...), custom_call_target="tpu_custom_call" | custom-call | bytes 10616832 | tf_op jit(solution)/shard_map/pallas_call | solution.py:100
  29.3 8.8 %collective-permute-done.1.refs_1_ = bf16[8,64,1152]{2,1,0:T(8,128)(2,1)} collective-permute-done((bf16[8,64,1152]{2,1,0:T(8,128)(2,1)}, bf16[8,64,1152]{2,1,0:T(8,128)(2,1)}, u32[]{:S(2)}, u32[]{:S(2)}) %collective-permute-start.1) | collective-permute-done | bytes 1179680 | tf_op jit(solution)/shard_map/ppermute | solution.py:430
  39.5 4.8 %shard_map.105 = (bf16[4,64,1152]{2,1,0:T(8,128)(2,1)}, bf16[4,64,1152]{2,1,0:T(8,128)(2,1)}) custom-call(s32[8]{0:T(128)} %get-tuple-element.97.cols, bf16[288,18432]{1,0:T(8,128)(2,1)} %bitcast.36, bf16[8,64,1152]{2,1,0:T(8,128)(2,1)} %collective-permute-done.refs_0_, bf16[8,64,1152]{2,1,0:T(8,128)(2,1)} %collective-permute-done.1.refs_1_, ...), custom_call_target="tpu_custom_call" | custom-call | bytes 3538944 | tf_op jit(solution)/shard_map/pallas_call | solution.py:65
  48.4 12.5 %collective-permute-done.2.refs_2_ = bf16[4,64,1152]{2,1,0:T(8,128)(2,1)} collective-permute-done((bf16[4,64,1152]{2,1,0:T(8,128)(2,1)}, bf16[4,64,1152]{2,1,0:T(8,128)(2,1)}, u32[]{:S(2)}, u32[]{:S(2)}) %collective-permute-start.2) | collective-permute-done | bytes 589856 | tf_op jit(solution)/shard_map/ppermute | solution.py:430
  61.3 5.3 %shard_map.106.refs_2_ = bf16[8,64,1152]{2,1,0:T(8,128)(2,1)} custom-call(s32[8]{0:T(128)} %get-tuple-element.98.cols, bf16[288,18432]{1,0:T(8,128)(2,1)} %bitcast.37, bf16[8,64,1152]{2,1,0:T(8,128)(2,1)} %collective-permute-done.refs_0_, bf16[8,64,1152]{2,1,0:T(8,128)(2,1)} %collective-permute-done.1.refs_1_, ...), custom_call_target="tpu_custom_call" | custom-call | bytes 4718592 | tf_op jit(solution)/shard_map/pallas_call | solution.py:65
  66.5 5.1 %all-to-all-start = ((bf16[8,64,1152]{2,1,0:T(8,128)(2,1)}), bf16[8,64,1152]{2,1,0:T(8,128)(2,1)}, u32[]{:S(2)}, u32[]{:S(2)}) async-start(bf16[8,64,1152]{2,1,0:T(8,128)(2,1)} %shard_map.106.refs_2_), calls=%async_computation | async-start | bytes 2359296 | tf_op jit(solution)/shard_map/all_to_all | solution.py:448
  71.6 18.5 %collective-permute-done.5.refs_1_ = bf16[8,80,1152]{2,1,0:T(8,128)(2,1)} collective-permute-done((bf16[8,80,1152]{2,1,0:T(8,128)(2,1)}, bf16[8,80,1152]{2,1,0:T(8,128)(2,1)}, u32[]{:S(2)}, u32[]{:S(2)}) %collective-permute-start.5) | collective-permute-done | bytes 1474592 | tf_op jit(solution)/shard_map/ppermute | solution.py:430
  90.5 5.2 %shard_map.107 = (bf16[4,80,1152]{2,1,0:T(8,128)(2,1)}, bf16[4,80,1152]{2,1,0:T(8,128)(2,1)}) custom-call(s32[8]{0:T(128)} %get-tuple-element.97.cols, bf16[288,18432]{1,0:T(8,128)(2,1)} %bitcast.38, bf16[8,80,1152]{2,1,0:T(8,128)(2,1)} %collective-permute-done.4.refs_0_, bf16[8,80,1152]{2,1,0:T(8,128)(2,1)} %collective-permute-done.5.refs_1_, ...), custom_call_target="tpu_custom_call" | custom-call | bytes 4423680 | tf_op jit(solution)/shard_map/pallas_call | solution.py:65
  98.6 13.6 %collective-permute-done.6.refs_2_ = bf16[4,80,1152]{2,1,0:T(8,128)(2,1)} collective-permute-done((bf16[4,80,1152]{2,1,0:T(8,128)(2,1)}, bf16[4,80,1152]{2,1,0:T(8,128)(2,1)}, u32[]{:S(2)}, u32[]{:S(2)}) %collective-permute-start.6) | collective-permute-done | bytes 737312 | tf_op jit(solution)/shard_map/ppermute | solution.py:430
  113.0 5.8 %shard_map.108.refs_3_ = bf16[8,80,1152]{2,1,0:T(8,128)(2,1)} custom-call(s32[8]{0:T(128)} %get-tuple-element.98.cols, bf16[288,18432]{1,0:T(8,128)(2,1)} %bitcast.39, bf16[8,80,1152]{2,1,0:T(8,128)(2,1)} %collective-permute-done.4.refs_0_, bf16[8,80,1152]{2,1,0:T(8,128)(2,1)} %collective-permute-done.5.refs_1_, ...), custom_call_target="tpu_custom_call" | custom-call | bytes 5898240 | tf_op jit(solution)/shard_map/pallas_call | solution.py:65
  118.8 4.9 %all-to-all-start.1 = ((bf16[8,80,1152]{2,1,0:T(8,128)(2,1)}), bf16[8,80,1152]{2,1,0:T(8,128)(2,1)}, u32[]{:S(2)}, u32[]{:S(2)}) async-start(bf16[8,80,1152]{2,1,0:T(8,128)(2,1)} %shard_map.108.refs_3_), calls=%async_computation.1 | async-start | bytes 2949120 | tf_op jit(solution)/shard_map/all_to_all | solution.py:448
  127.3 32.3 %all-to-all-done.1.refs_1_ = bf16[8,80,1152]{2,1,0:T(8,128)(2,1)} async-done(((bf16[8,80,1152]{2,1,0:T(8,128)(2,1)}), bf16[8,80,1152]{2,1,0:T(8,128)(2,1)}, u32[]{:S(2)}, u32[]{:S(2)}) %all-to-all-start.1) | async-done | bytes 1474592 | tf_op jit(solution)/shard_map/all_to_all | solution.py:448
  159.5 10.7 %shard_map.109 = (bf16[3,2,144,1152]{3,2,1,0:T(8,128)(2,1)}, bf16[3,2,144,1152]{3,2,1,0:T(8,128)(2,1)}, bf16[3,2,144,1152]{3,2,1,0:T(8,128)(2,1)}, bf16[3,2,144,1152]{3,2,1,0:T(8,128)(2,1)}) custom-call(s32[4]{0:T(128)} %iota_xor_fusion.js, bf16[8,64,1152]{2,1,0:T(8,128)(2,1)} %all-to-all-done.refs_0_, bf16[8,80,1152]{2,1,0:T(8,128)(2,1)} %all-to-all-done.1.refs_1_), custom_call_target="tpu_custom_call" | custom-call | flops 3057647616 | bytes 10616832 | tf_op jit(solution)/shard_map/pallas_call | solution.py:160
  173.7 12.3 %collective-permute-done.9.refs_4_ = bf16[2,2,144,1152]{3,2,1,0:T(8,128)(2,1)} collective-permute-done((bf16[2,2,144,1152]{3,2,1,0:T(8,128)(2,1)}, bf16[2,2,144,1152]{3,2,1,0:T(8,128)(2,1)}, u32[]{:S(2)}, u32[]{:S(2)}) %collective-permute-start.9) | collective-permute-done | bytes 1327136 | tf_op jit(solution)/shard_map/ppermute | solution.py:430
  186.0 11.8 %shard_map.111 = (bf16[144,1152]{1,0:T(8,128)(2,1)}, bf16[144,1152]{1,0:T(8,128)(2,1)}, bf16[144,1152]{1,0:T(8,128)(2,1)}, bf16[144,1152]{1,0:T(8,128)(2,1)}, bf...) custom-call(s32[4]{0:T(128)} %iota_xor_fusion.js, ...), custom_call_target="tpu_custom_call" | custom-call | flops 3057647616 | bytes 10616832 | tf_op jit(solution)/shard_map/pallas_call | solution.py:219
  201.5 7.5 %collective-permute-done.12.refs_2_ = bf16[144,1152]{1,0:T(8,128)(2,1)} collective-permute-done((bf16[144,1152]{1,0:T(8,128)(2,1)}, bf16[144,1152]{1,0:T(8,128)(2,1)}, u32[]{:S(2)}, u32[]{:S(2)}) %collective-permute-start.12) | collective-permute-done | bytes 331808 | tf_op jit(solution)/shard_map/ppermute | solution.py:458
  211.6 9.3 %collective-permute-done.13.refs_3_ = bf16[144,1152]{1,0:T(8,128)(2,1)} collective-permute-done((bf16[144,1152]{1,0:T(8,128)(2,1)}, bf16[144,1152]{1,0:T(8,128)(2,1)}, u32[]{:S(2)}, u32[]{:S(2)}) %collective-permute-start.13) | collective-permute-done | bytes 331808 | tf_op jit(solution)/shard_map/ppermute | solution.py:458
  221.6 13.2 %collective-permute-done.14.refs_4_ = bf16[144,1152]{1,0:T(8,128)(2,1)} collective-permute-done((bf16[144,1152]{1,0:T(8,128)(2,1)}, bf16[144,1152]{1,0:T(8,128)(2,1)}, u32[]{:S(2)}, u32[]{:S(2)}) %collective-permute-start.14) | collective-permute-done | bytes 331808 | tf_op jit(solution)/shard_map/ppermute | solution.py:458
  234.8 3.9 %collective-permute-start.16 = (bf16[144,1152]{1,0:T(8,128)(2,1)}, bf16[144,1152]{1,0:T(8,128)(2,1)}, u32[]{:S(2)}, u32[]{:S(2)}) collective-permute-start(bf16[144,1152]{1,0:T(8,128)(2,1)} %get-tuple-element.65), channel_id=1, source_target_pairs={{0,24},{4,28},{8,16},{12,20},{16,8},{20,12},{24,0},{28,4},{1,25},{... | collective-permute-start | bytes 995336 | tf_op jit(solution)/shard_map/ppermute | solution.py:458
  238.7 7.6 %collective-permute-done.15.refs_5_ = bf16[144,1152]{1,0:T(8,128)(2,1)} collective-permute-done((bf16[144,1152]{1,0:T(8,128)(2,1)}, bf16[144,1152]{1,0:T(8,128)(2,1)}, u32[]{:S(2)}, u32[]{:S(2)}) %collective-permute-start.15) | collective-permute-done | bytes 331808 | tf_op jit(solution)/shard_map/ppermute | solution.py:458
  246.3 6.3 %collective-permute-start.17 = (bf16[144,1152]{1,0:T(8,128)(2,1)}, bf16[144,1152]{1,0:T(8,128)(2,1)}, u32[]{:S(2)}, u32[]{:S(2)}) collective-permute-start(bf16[144,1152]{1,0:T(8,128)(2,1)} %get-tuple-element.66), channel_id=1, source_target_pairs={{0,28},{4,24},{8,20},{12,16},{16,12},{20,8},{24,4},{28,0},{1,29},{... | collective-permute-start | bytes 995336 | tf_op jit(solution)/shard_map/ppermute | solution.py:458
  254.5 6.7 %collective-permute-done.17.refs_7_ = bf16[144,1152]{1,0:T(8,128)(2,1)} collective-permute-done((bf16[144,1152]{1,0:T(8,128)(2,1)}, bf16[144,1152]{1,0:T(8,128)(2,1)}, u32[]{:S(2)}, u32[]{:S(2)}) %collective-permute-start.17) | collective-permute-done | bytes 331808 | tf_op jit(solution)/shard_map/ppermute | solution.py:458
  261.2 9.3 %collective-permute-done.19.refs_9_ = bf16[3,2,144,1152]{3,2,1,0:T(8,128)(2,1)} collective-permute-done((bf16[3,2,144,1152]{3,2,1,0:T(8,128)(2,1)}, bf16[3,2,144,1152]{3,2,1,0:T(8,128)(2,1)}, u32[]{:S(2)}, u32[]{:S(2)}) %collective-permute-start.19) | collective-permute-done | bytes 1990688 | tf_op jit(solution)/shard_map/ppermute | solution.py:430
  279.6 10.3 %shard_map.113 = (f32[4,4,144,576]{3,2,1,0:T(8,128)}, f32[4,8,128]{2,1,0:T(8,128)}) custom-call(s32[4]{0:T(128)} %iota_xor_fusion.js, bf16[3,2,144,1152]{3,2,1,0:T(8,128)(2,1)} %get-tuple-element.52.refs_6_.refs_0_, bf16[3,2,144,1152]{3,2,1,0:T(8,128)(2,1)} %get-tuple-element.70.refs_1_, bf16[3,2,144,1152]{3,2,1,0:T(8,128)(2,1)} %get-tuple-element.71.refs_2_, ...), custom_call_target="tpu_custom_call" | custom-call | bytes 13271040 | tf_op jit(solution)/shard_map/pallas_call | solution.py:325
  292.8 26.9 %psum.14 = f32[8,2,4,4]{2,0,3,1:T(8,128)S(1)} all-reduce(f32[8,2,4,4]{2,0,3,1:T(8,128)S(1)} %broadcast_select_fusion), channel_id=1, replica_groups=mesh['fsdp'=8,'replica'=4] {'fsdp'}, use_global_device_ids=true, to_apply=%region_2.3 | all-reduce | flops 256 | bytes 2048 | tf_op jit(solution)/shard_map/psum | solution.py:476
  319.7 23.6 %psum.15 = f32[8,2,4,4]{2,0,3,1:T(8,128)S(1)} all-reduce(f32[8,2,4,4]{2,0,3,1:T(8,128)S(1)} %psum.14), channel_id=1, replica_groups=mesh['fsdp'=8,'replica'=4] {'replica'}, use_global_device_ids=true, to_apply=%region_3.4 | all-reduce | flops 256 | bytes 2048 | tf_op jit(solution)/shard_map/psum | solution.py:477
  347.5 13.0 %shard_map.116 = (f32[4,4,144,576]{3,2,1,0:T(8,128)}, f32[4,4,144,576]{3,2,1,0:T(8,128)}) custom-call(s32[4]{0:T(128)} %iota_xor_fusion.js, bf16[3,2,144,1152]{3,2,1,0:T(8,128)(2,1)} %get-tuple-element.52.refs_6_.refs_0_, bf16[3,2,144,1152]{3,2,1,0:T(8,128)(2,1)} %get-tuple-element.70.refs_1_, bf16[3,2,144,1152]{3,2,1,0:T(8,128)(2,1)} %get-tuple-element.71.refs_2_, ...), custom_call_target="tpu_custom_call" | custom-call | bytes 26542080 | tf_op jit(solution)/shard_map/pallas_call | solution.py:325
  360.4 11.3 %collective-permute-done.25.refs_6_ = bf16[4,144,1152]{2,1,0:T(8,128)(2,1)} collective-permute-done((bf16[4,144,1152]{2,1,0:T(8,128)(2,1)}, bf16[4,144,1152]{2,1,0:T(8,128)(2,1)}, u32[]{:S(2)}, u32[]{:S(2)}) %collective-permute-start.25) | collective-permute-done | bytes 1327136 | tf_op jit(solution)/shard_map/ppermute | solution.py:430
  372.2 8.7 %shard_map.115 = bf16[288,18432]{1,0:T(8,128)(2,1)} custom-call(s32[32]{0:T(128)} %multiply_add_fusion.src, s32[32]{0:T(128)} %get-tuple-element.94.item, f32[32]{0:T(128)} %select_reduce_fusion.refs_2_.scale, bf16[4,144,1152]{2,1,0:T(8,128)(2,1)} %get-tuple-element.75.refs_0_, bf16[4,144,1152]{2,1,0:T(8,128)(2,1)} %get-tuple-element.76.refs_1_, ...), custom_call_target="tpu_custom_call" | custom-call | bytes 21233664 | tf_op jit(solution)/shard_map/pallas_call | solution.py:387
  (76 shorter events, 48.9 us)
Async XLA Ops:
  2.1 0.5 copy-start.1
  2.6 0.6 copy-start
  8.7 29.3 %collective-permute-start.1 = (bf16[8,64,1152]{2,1,0:T(8,128)(2,1)}, bf16[8,64,1152]{2,1,0:T(8,128)(2,1)}, u32[]{:S(2)}, u32[]{:S(2)}) collective-permute-start(bf16[8,64,1152]{2,1,0:T(8,128)(2,1)} %get-tuple-element.44), channel_id=1, source_target_pairs={{0,2},{1,3},{2,0},{3,1},{4,6},{5,7},{6,4},{7,5},{8,10},{9,11},{10,... | collective-permute-start | bytes 3538952 | tf_op jit(solution)/shard_map/ppermute | solution.py:430
  11.8 27.7 %collective-permute-start = (bf16[8,64,1152]{2,1,0:T(8,128)(2,1)}, bf16[8,64,1152]{2,1,0:T(8,128)(2,1)}, u32[]{:S(2)}, u32[]{:S(2)}) collective-permute-start(bf16[8,64,1152]{2,1,0:T(8,128)(2,1)} %get-tuple-element.43.refs_0_), channel_id=1, source_target_pairs={{0,1},{1,0},{2,3},{3,2},{4,5},{5,4},{6,7},{7,6},{8,9},{9,8},{10,11... | collective-permute-start | bytes 3538952 | tf_op jit(solution)/shard_map/ppermute | solution.py:430
  44.3 16.6 %collective-permute-start.2 = (bf16[4,64,1152]{2,1,0:T(8,128)(2,1)}, bf16[4,64,1152]{2,1,0:T(8,128)(2,1)}, u32[]{:S(2)}, u32[]{:S(2)}) collective-permute-start(bf16[4,64,1152]{2,1,0:T(8,128)(2,1)} %get-tuple-element.47), channel_id=1, source_target_pairs={{0,2},{1,3},{2,0},{3,1},{4,6},{5,7},{6,4},{7,5},{8,10},{9,11},{10,... | collective-permute-start | bytes 1769480 | tf_op jit(solution)/shard_map/ppermute | solution.py:430
  44.7 16.6 %collective-permute-start.3 = (bf16[4,64,1152]{2,1,0:T(8,128)(2,1)}, bf16[4,64,1152]{2,1,0:T(8,128)(2,1)}, u32[]{:S(2)}, u32[]{:S(2)}) collective-permute-start(bf16[4,64,1152]{2,1,0:T(8,128)(2,1)} %get-tuple-element.48), channel_id=1, source_target_pairs={{0,1},{1,0},{2,3},{3,2},{4,5},{5,4},{6,7},{7,6},{8,9},{9,8},{10,11... | collective-permute-start | bytes 1769480 | tf_op jit(solution)/shard_map/ppermute | solution.py:430
  46.3 43.8 %collective-permute-start.5 = (bf16[8,80,1152]{2,1,0:T(8,128)(2,1)}, bf16[8,80,1152]{2,1,0:T(8,128)(2,1)}, u32[]{:S(2)}, u32[]{:S(2)}) collective-permute-start(bf16[8,80,1152]{2,1,0:T(8,128)(2,1)} %get-tuple-element.49), channel_id=1, source_target_pairs={{0,2},{1,3},{2,0},{3,1},{4,6},{5,7},{6,4},{7,5},{8,10},{9,11},{10,... | collective-permute-start | bytes 4423688 | tf_op jit(solution)/shard_map/ppermute | solution.py:430
  47.8 42.7 %collective-permute-start.4 = (bf16[8,80,1152]{2,1,0:T(8,128)(2,1)}, bf16[8,80,1152]{2,1,0:T(8,128)(2,1)}, u32[]{:S(2)}, u32[]{:S(2)}) collective-permute-start(bf16[8,80,1152]{2,1,0:T(8,128)(2,1)} %get-tuple-element.45.refs_0_), channel_id=1, source_target_pairs={{0,1},{1,0},{2,3},{3,2},{4,5},{5,4},{6,7},{7,6},{8,9},{9,8},{10,11... | collective-permute-start | bytes 4423688 | tf_op jit(solution)/shard_map/ppermute | solution.py:430
  66.5 52.3 %all-to-all-start = ((bf16[8,64,1152]{2,1,0:T(8,128)(2,1)}), bf16[8,64,1152]{2,1,0:T(8,128)(2,1)}, u32[]{:S(2)}, u32[]{:S(2)}) async-start(bf16[8,64,1152]{2,1,0:T(8,128)(2,1)} %shard_map.106.refs_2_), calls=%async_computation | async-start | bytes 2359296 | tf_op jit(solution)/shard_map/all_to_all | solution.py:448
  95.7 16.5 %collective-permute-start.6 = (bf16[4,80,1152]{2,1,0:T(8,128)(2,1)}, bf16[4,80,1152]{2,1,0:T(8,128)(2,1)}, u32[]{:S(2)}, u32[]{:S(2)}) collective-permute-start(bf16[4,80,1152]{2,1,0:T(8,128)(2,1)} %get-tuple-element.50), channel_id=1, source_target_pairs={{0,2},{1,3},{2,0},{3,1},{4,6},{5,7},{6,4},{7,5},{8,10},{9,11},{10,... | collective-permute-start | bytes 2211848 | tf_op jit(solution)/shard_map/ppermute | solution.py:430
  97.1 15.9 %collective-permute-start.7 = (bf16[4,80,1152]{2,1,0:T(8,128)(2,1)}, bf16[4,80,1152]{2,1,0:T(8,128)(2,1)}, u32[]{:S(2)}, u32[]{:S(2)}) collective-permute-start(bf16[4,80,1152]{2,1,0:T(8,128)(2,1)} %get-tuple-element.51), channel_id=1, source_target_pairs={{0,1},{1,0},{2,3},{3,2},{4,5},{5,4},{6,7},{7,6},{8,9},{9,8},{10,11... | collective-permute-start | bytes 2211848 | tf_op jit(solution)/shard_map/ppermute | solution.py:430
  118.8 40.7 %all-to-all-start.1 = ((bf16[8,80,1152]{2,1,0:T(8,128)(2,1)}), bf16[8,80,1152]{2,1,0:T(8,128)(2,1)}, u32[]{:S(2)}, u32[]{:S(2)}) async-start(bf16[8,80,1152]{2,1,0:T(8,128)(2,1)} %shard_map.108.refs_3_), calls=%async_computation.1 | async-start | bytes 2949120 | tf_op jit(solution)/shard_map/all_to_all | solution.py:448
  123.7 48.8 %collective-permute-start.8 = (bf16[2,2,144,1152]{3,2,1,0:T(8,128)(2,1)}, bf16[2,2,144,1152]{3,2,1,0:T(8,128)(2,1)}, u32[]{:S(2)}, u32[]{:S(2)}) collective-permute-start(bf16[2,2,144,1152]{3,2,1,0:T(8,128)(2,1)} %get-tuple-element.56), channel_id=1, source_target_pairs={{0,1},{1,0},{2,3},{3,2},{4,5},{5,4},{6,7},{7,6},{8,9},{9,8},{10,11... | collective-permute-start | bytes 3981320 | tf_op jit(solution)/shard_map/ppermute | solution.py:430
  125.3 60.7 %collective-permute-start.9 = (bf16[2,2,144,1152]{3,2,1,0:T(8,128)(2,1)}, bf16[2,2,144,1152]{3,2,1,0:T(8,128)(2,1)}, u32[]{:S(2)}, u32[]{:S(2)}) collective-permute-start(bf16[2,2,144,1152]{3,2,1,0:T(8,128)(2,1)} %get-tuple-element.57), channel_id=1, source_target_pairs={{0,2},{1,3},{2,0},{3,1},{4,6},{5,7},{6,4},{7,5},{8,10},{9,11},{10,... | collective-permute-start | bytes 3981320 | tf_op jit(solution)/shard_map/ppermute | solution.py:430
  126.0 60.0 %collective-permute-start.10 = (bf16[2,2,144,1152]{3,2,1,0:T(8,128)(2,1)}, bf16[2,2,144,1152]{3,2,1,0:T(8,128)(2,1)}, u32[]{:S(2)}, u32[]{:S(2)}) collective-permute-start(bf16[2,2,144,1152]{3,2,1,0:T(8,128)(2,1)} %get-tuple-element.58), channel_id=1, source_target_pairs={{0,3},{1,2},{2,1},{3,0},{4,7},{5,6},{6,5},{7,4},{8,11},{9,10},{10,... | collective-permute-start | bytes 3981320 | tf_op jit(solution)/shard_map/ppermute | solution.py:430
  170.3 91.0 %collective-permute-start.18 = (bf16[3,2,144,1152]{3,2,1,0:T(8,128)(2,1)}, bf16[3,2,144,1152]{3,2,1,0:T(8,128)(2,1)}, u32[]{:S(2)}, u32[]{:S(2)}) collective-permute-start(bf16[3,2,144,1152]{3,2,1,0:T(8,128)(2,1)} %get-tuple-element.67), channel_id=1, source_target_pairs={{0,1},{1,0},{2,3},{3,2},{4,5},{5,4},{6,7},{7,6},{8,9},{9,8},{10,11... | collective-permute-start | bytes 5971976 | tf_op jit(solution)/shard_map/ppermute | solution.py:430
  171.8 98.8 %collective-permute-start.19 = (bf16[3,2,144,1152]{3,2,1,0:T(8,128)(2,1)}, bf16[3,2,144,1152]{3,2,1,0:T(8,128)(2,1)}, u32[]{:S(2)}, u32[]{:S(2)}) collective-permute-start(bf16[3,2,144,1152]{3,2,1,0:T(8,128)(2,1)} %get-tuple-element.68), channel_id=1, source_target_pairs={{0,2},{1,3},{2,0},{3,1},{4,6},{5,7},{6,4},{7,5},{8,10},{9,11},{10,... | collective-permute-start | bytes 5971976 | tf_op jit(solution)/shard_map/ppermute | solution.py:430
  172.5 98.1 %collective-permute-start.20 = (bf16[3,2,144,1152]{3,2,1,0:T(8,128)(2,1)}, bf16[3,2,144,1152]{3,2,1,0:T(8,128)(2,1)}, u32[]{:S(2)}, u32[]{:S(2)}) collective-permute-start(bf16[3,2,144,1152]{3,2,1,0:T(8,128)(2,1)} %get-tuple-element.69), channel_id=1, source_target_pairs={{0,3},{1,2},{2,1},{3,0},{4,7},{5,6},{6,5},{7,4},{8,11},{9,10},{10,... | collective-permute-start | bytes 5971976 | tf_op jit(solution)/shard_map/ppermute | solution.py:430
  197.9 2.0 collective-permute-start.11
  197.9 11.0 %collective-permute-start.12 = (bf16[144,1152]{1,0:T(8,128)(2,1)}, bf16[144,1152]{1,0:T(8,128)(2,1)}, u32[]{:S(2)}, u32[]{:S(2)}) collective-permute-start(bf16[144,1152]{1,0:T(8,128)(2,1)} %get-tuple-element.61), channel_id=1, source_target_pairs={{0,8},{4,12},{8,0},{12,4},{16,24},{20,28},{24,16},{28,20},{1,9},{5... | collective-permute-start | bytes 995336 | tf_op jit(solution)/shard_map/ppermute | solution.py:458
  199.9 21.1 %collective-permute-start.13 = (bf16[144,1152]{1,0:T(8,128)(2,1)}, bf16[144,1152]{1,0:T(8,128)(2,1)}, u32[]{:S(2)}, u32[]{:S(2)}) collective-permute-start(bf16[144,1152]{1,0:T(8,128)(2,1)} %get-tuple-element.62), channel_id=1, source_target_pairs={{0,12},{4,8},{8,4},{12,0},{16,28},{20,24},{24,20},{28,16},{1,13},{... | collective-permute-start | bytes 995336 | tf_op jit(solution)/shard_map/ppermute | solution.py:458
  208.9 25.9 %collective-permute-start.14 = (bf16[144,1152]{1,0:T(8,128)(2,1)}, bf16[144,1152]{1,0:T(8,128)(2,1)}, u32[]{:S(2)}, u32[]{:S(2)}) collective-permute-start(bf16[144,1152]{1,0:T(8,128)(2,1)} %get-tuple-element.63), channel_id=1, source_target_pairs={{0,16},{4,20},{8,24},{12,28},{16,0},{20,4},{24,8},{28,12},{1,17},{... | collective-permute-start | bytes 995336 | tf_op jit(solution)/shard_map/ppermute | solution.py:458
  221.0 25.4 %collective-permute-start.15 = (bf16[144,1152]{1,0:T(8,128)(2,1)}, bf16[144,1152]{1,0:T(8,128)(2,1)}, u32[]{:S(2)}, u32[]{:S(2)}) collective-permute-start(bf16[144,1152]{1,0:T(8,128)(2,1)} %get-tuple-element.64), channel_id=1, source_target_pairs={{0,20},{4,16},{8,28},{12,24},{16,4},{20,0},{24,12},{28,8},{1,21},{... | collective-permute-start | bytes 995336 | tf_op jit(solution)/shard_map/ppermute | solution.py:458
  234.8 19.7 %collective-permute-start.16 = (bf16[144,1152]{1,0:T(8,128)(2,1)}, bf16[144,1152]{1,0:T(8,128)(2,1)}, u32[]{:S(2)}, u32[]{:S(2)}) collective-permute-start(bf16[144,1152]{1,0:T(8,128)(2,1)} %get-tuple-element.65), channel_id=1, source_target_pairs={{0,24},{4,28},{8,16},{12,20},{16,8},{20,12},{24,0},{28,4},{1,25},{... | collective-permute-start | bytes 995336 | tf_op jit(solution)/shard_map/ppermute | solution.py:458
  246.3 14.9 %collective-permute-start.17 = (bf16[144,1152]{1,0:T(8,128)(2,1)}, bf16[144,1152]{1,0:T(8,128)(2,1)}, u32[]{:S(2)}, u32[]{:S(2)}) collective-permute-start(bf16[144,1152]{1,0:T(8,128)(2,1)} %get-tuple-element.66), channel_id=1, source_target_pairs={{0,28},{4,24},{8,20},{12,16},{16,12},{20,8},{24,4},{28,0},{1,29},{... | collective-permute-start | bytes 995336 | tf_op jit(solution)/shard_map/ppermute | solution.py:458
  273.2 71.5 %collective-permute-start.24 = (bf16[4,144,1152]{2,1,0:T(8,128)(2,1)}, bf16[4,144,1152]{2,1,0:T(8,128)(2,1)}, u32[]{:S(2)}, u32[]{:S(2)}) collective-permute-start(bf16[4,144,1152]{2,1,0:T(8,128)(2,1)} %get-tuple-element.75.refs_0_), channel_id=1, source_target_pairs={{0,2},{1,3},{2,0},{3,1},{4,6},{5,7},{6,4},{7,5},{8,10},{9,11},{10,... | collective-permute-start | bytes 3981320 | tf_op jit(solution)/shard_map/ppermute | solution.py:430
  274.0 70.8 %collective-permute-start.21 = (bf16[4,144,1152]{2,1,0:T(8,128)(2,1)}, bf16[4,144,1152]{2,1,0:T(8,128)(2,1)}, u32[]{:S(2)}, u32[]{:S(2)}) collective-permute-start(bf16[4,144,1152]{2,1,0:T(8,128)(2,1)} %get-tuple-element.75.refs_0_), channel_id=1, source_target_pairs={{0,1},{1,0},{2,3},{3,2},{4,5},{5,4},{6,7},{7,6},{8,9},{9,8},{10,11... | collective-permute-start | bytes 3981320 | tf_op jit(solution)/shard_map/ppermute | solution.py:430
  275.1 69.7 %collective-permute-start.23 = (bf16[4,144,1152]{2,1,0:T(8,128)(2,1)}, bf16[4,144,1152]{2,1,0:T(8,128)(2,1)}, u32[]{:S(2)}, u32[]{:S(2)}) collective-permute-start(bf16[4,144,1152]{2,1,0:T(8,128)(2,1)} %get-tuple-element.76.refs_1_), channel_id=1, source_target_pairs={{0,1},{1,0},{2,3},{3,2},{4,5},{5,4},{6,7},{7,6},{8,9},{9,8},{10,11... | collective-permute-start | bytes 3981320 | tf_op jit(solution)/shard_map/ppermute | solution.py:430
  276.0 68.7 %collective-permute-start.22 = (bf16[4,144,1152]{2,1,0:T(8,128)(2,1)}, bf16[4,144,1152]{2,1,0:T(8,128)(2,1)}, u32[]{:S(2)}, u32[]{:S(2)}) collective-permute-start(bf16[4,144,1152]{2,1,0:T(8,128)(2,1)} %get-tuple-element.76.refs_1_), channel_id=1, source_target_pairs={{0,2},{1,3},{2,0},{3,1},{4,6},{5,7},{6,4},{7,5},{8,10},{9,11},{10,... | collective-permute-start | bytes 3981320 | tf_op jit(solution)/shard_map/ppermute | solution.py:430
  344.8 26.9 %collective-permute-start.25 = (bf16[4,144,1152]{2,1,0:T(8,128)(2,1)}, bf16[4,144,1152]{2,1,0:T(8,128)(2,1)}, u32[]{:S(2)}, u32[]{:S(2)}) collective-permute-start(bf16[4,144,1152]{2,1,0:T(8,128)(2,1)} %get-tuple-element.77.refs_2_), channel_id=1, source_target_pairs={{0,2},{1,3},{2,0},{3,1},{4,6},{5,7},{6,4},{7,5},{8,10},{9,11},{10,... | collective-permute-start | bytes 3981320 | tf_op jit(solution)/shard_map/ppermute | solution.py:430
  345.6 26.6 %collective-permute-start.26 = (bf16[4,144,1152]{2,1,0:T(8,128)(2,1)}, bf16[4,144,1152]{2,1,0:T(8,128)(2,1)}, u32[]{:S(2)}, u32[]{:S(2)}) collective-permute-start(bf16[4,144,1152]{2,1,0:T(8,128)(2,1)} %get-tuple-element.78.refs_5_), channel_id=1, source_target_pairs={{0,1},{1,0},{2,3},{3,2},{4,5},{5,4},{6,7},{7,6},{8,9},{9,8},{10,11... | collective-permute-start | bytes 3981320 | tf_op jit(solution)/shard_map/ppermute | solution.py:430

commit v9 on v8

--- a/solution.py
+++ b/solution.py
@@ -429,6 +429,9 @@
     def swap(x, k):
         return lax.ppermute(x, "replica", [(i, i ^ k) for i in range(replicas)])
 
+    def plus(x, y):
+        return (x.astype(jnp.float32) + y.astype(jnp.float32)).astype(x.dtype)
+
     def as_rows(x):
         return x.reshape(row_blocks, -1, sub_count * rd, B)
 
@@ -442,7 +445,8 @@
     roots = pack_roots(js, as_rows(root_left), as_rows(root_right), after)
     after = (roots[0],)
     for (x, y), chunk in zip(early, chunks):
-        y_a, x_b = arrange(cols[2], grad, *chunk, [((x, 0), (y, 0))], after=after)
+        y_a, x_b = arrange(cols[2], grad, *chunk, after=after)
+        y_a, x_b = plus(y_a, x[:half]), plus(x_b, y[:half])
         terms = [((x, half), (y, half)), ((swap(y_a, 2), 0), (swap(x_b, 1), 0))]
         (owned,) = arrange(cols[3], grad, *chunk, terms, halves=False)
         blocks.append(lax.all_to_all(owned, "fsdp", split_axis=0, concat_axis=0, tiled=True))

time: 382 us -> 390 us (1.021)
  waiting for transfers between devices: 166 us -> 172 us
  other arithmetic: 10.5 us -> 16 us
    convert_element_type x0 -> x4, other arithmetic: none -> 5.49 us  [plus(): return (x.astype(jnp.float32) + y.astype(jnp.float32)).astype(x.dtype)]
    ppermute x20, waiting for transfers between devices: 89.8 us -> 95 us  [swap(): return lax.ppermute(x, 'replica', [(i, i ^ k) for i in range(replicas)])]
  transfers between devices with their start and end apart: 29 -> 29, of which waited for: 19 -> 15; matrix products, arithmetic and copies ran while one was open for 3% -> 5% of each run, Pallas kernels for 20% -> 20%
where the time goes in v9:
time: 390 us; the launch traced here: 389 us
  waiting for transfers between devices  172 us (44%)
  Pallas kernels  94.4 us (24%)
  blocking collectives  51.1 us (13%)
  starting transfers between devices  49.9 us (13%)
  other arithmetic  16 us (4%)
  local copies, waits for them, and re-layouts  4.74 us (1%)
    ppermute x20, waiting for transfers between devices, swap(): return lax.ppermute(x, 'replica', [(i, i ^ k) for i in range(replicas)])  95 us
    ppermute x7, waiting for transfers between devices, owner_local(): lax.ppermute(direction[k], 'fsdp', [(i, i ^ k) for i in range(owners)])  44.4 us
    all_to_all x2, waiting for transfers between devices, owner_local(): lax.all_to_all(owned, 'fsdp', split_axis=0, concat_axis=0, tiled=True)  32.3 us
    pallas_call x6, Pallas kernels, arrange(): pl.pallas_call(functools.partial(arrange_body, len(adds) // 2, [part[1] f...  28.3 us
    psum x1, blocking collectives, owner_local(): lax.psum(jnp.where(owner_ids[:, None, None, None] == f, squares, 0.0), 'f...  27.7 us
    ppermute x20, starting transfers between devices, swap(): return lax.ppermute(x, 'replica', [(i, i ^ k) for i in range(replicas)])  23.6 us
    psum x1, blocking collectives, owner_local(): squares = lax.psum(squares, 'replica')  23.4 us
    pallas_call x2, Pallas kernels, by_rows(): pl.pallas_call(functools.partial(by_rows_body, body, n, pairs), grid_spec...  23.2 us
  transfers between devices with their start and end apart: 29, of which 15 were waited for; matrix products, arithmetic and copies ran while one was open for 5% of the time, Pallas kernels for 20%

profile of v9, /device:TPU:0, one launch (start us, length us, event | category | flops | bytes accessed | tf_op | source)
XLA Modules:
  0.0 388.8 jit_solution(13789356706707547931)
XLA Ops:
  3.8 4.8 %shard_map.102 = (bf16[8,64,1152]{2,1,0:T(8,128)(2,1)}, bf16[8,64,1152]{2,1,0:T(8,128)(2,1)}) custom-call(s32[16]{0:T(128)} %reshape.230.cols, bf16[288,18432]{1,0:T(8,128)(2,1)} %bitcast.34), custom_call_target="tpu_custom_call" | custom-call | bytes 4718592 | tf_op jit(solution)/shard_map/pallas_call | solution.py:65
  8.7 3.0 collective-permute-start.1
  13.2 5.1 %shard_map.103 = (bf16[8,80,1152]{2,1,0:T(8,128)(2,1)}, bf16[8,80,1152]{2,1,0:T(8,128)(2,1)}) custom-call(s32[16]{0:T(128)} %reshape.230.cols, bf16[288,18432]{1,0:T(8,128)(2,1)} %bitcast.35, bf16[8,64,1152]{2,1,0:T(8,128)(2,1)} %get-tuple-element.43.refs_0_), custom_call_target="tpu_custom_call" | custom-call | bytes 5898240 | tf_op jit(solution)/shard_map/pallas_call | solution.py:65
  19.6 9.0 %shard_map.104 = (bf16[2,2,144,1152]{3,2,1,0:T(8,128)(2,1)}, bf16[2,2,144,1152]{3,2,1,0:T(8,128)(2,1)}, bf16[2,2,144,1152]{3,2,1,0:T(8,128)(2,1)}, bf16[2,2,144,1152]{3,2,1,0:T(8,128)(2,1)}) custom-call(s32[4]{0:T(128)} %iota_xor_fusion.js, bf16[4,4,144,576]{3,2,1,0:T(8,128)(2,1)} %bitcast.43, bf16[4,4,144,576]{3,2,1,0:T(8,128)(2,1)} %bitcast.44, ...), custom_call_target="tpu_custom_call" | custom-call | bytes 10616832 | tf_op jit(solution)/shard_map/pallas_call | solution.py:100
  29.9 3.5 shard_map.105
  33.4 5.4 %collective-permute-done.1.refs_1_ = bf16[8,64,1152]{2,1,0:T(8,128)(2,1)} collective-permute-done((bf16[8,64,1152]{2,1,0:T(8,128)(2,1)}, bf16[8,64,1152]{2,1,0:T(8,128)(2,1)}, u32[]{:S(2)}, u32[]{:S(2)}) %collective-permute-start.1) | collective-permute-done | bytes 1179680 | tf_op jit(solution)/shard_map/ppermute | solution.py:430
  45.1 38.6 %collective-permute-done.3.refs_3_ = bf16[4,64,1152]{2,1,0:T(8,128)(2,1)} collective-permute-done((bf16[4,64,1152]{2,1,0:T(8,128)(2,1)S(1)}, bf16[4,64,1152]{2,1,0:T(8,128)(2,1)}, u32[]{:S(2)}, u32[]{:S(2)}) %collective-permute-start.3) | collective-permute-done | bytes 589856 | tf_op jit(solution)/shard_map/ppermute | solution.py:430
  83.7 5.3 %shard_map.106.refs_0_ = bf16[8,64,1152]{2,1,0:T(8,128)(2,1)} custom-call(s32[8]{0:T(128)} %get-tuple-element.98.cols, bf16[288,18432]{1,0:T(8,128)(2,1)} %bitcast.37, bf16[8,64,1152]{2,1,0:T(8,128)(2,1)} %collective-permute-done.refs_0_, bf16[8,64,1152]{2,1,0:T(8,128)(2,1)} %collective-permute-done.1.refs_1_, ...), custom_call_target="tpu_custom_call" | custom-call | bytes 4718592 | tf_op jit(solution)/shard_map/pallas_call | solution.py:65
  89.0 4.9 %all-to-all-start = ((bf16[8,64,1152]{2,1,0:T(8,128)(2,1)}), bf16[8,64,1152]{2,1,0:T(8,128)(2,1)}, u32[]{:S(2)}, u32[]{:S(2)}) async-start(bf16[8,64,1152]{2,1,0:T(8,128)(2,1)} %shard_map.106.refs_0_), calls=%async_computation | async-start | bytes 2359296 | tf_op jit(solution)/shard_map/all_to_all | solution.py:452
  93.8 3.7 shard_map.107
  102.6 15.6 %collective-permute-done.7.refs_3_ = bf16[4,80,1152]{2,1,0:T(8,128)(2,1)} collective-permute-done((bf16[4,80,1152]{2,1,0:T(8,128)(2,1)S(1)}, bf16[4,80,1152]{2,1,0:T(8,128)(2,1)}, u32[]{:S(2)}, u32[]{:S(2)}) %collective-permute-start.7) | collective-permute-done | bytes 737312 | tf_op jit(solution)/shard_map/ppermute | solution.py:430
  120.8 5.8 %shard_map.108.refs_3_ = bf16[8,80,1152]{2,1,0:T(8,128)(2,1)} custom-call(s32[8]{0:T(128)} %get-tuple-element.98.cols, bf16[288,18432]{1,0:T(8,128)(2,1)} %bitcast.39, bf16[8,80,1152]{2,1,0:T(8,128)(2,1)} %collective-permute-done.4.refs_0_, bf16[8,80,1152]{2,1,0:T(8,128)(2,1)} %collective-permute-done.5.refs_1_, ...), custom_call_target="tpu_custom_call" | custom-call | bytes 5898240 | tf_op jit(solution)/shard_map/pallas_call | solution.py:65
  126.6 4.8 %all-to-all-start.1 = ((bf16[8,80,1152]{2,1,0:T(8,128)(2,1)}), bf16[8,80,1152]{2,1,0:T(8,128)(2,1)}, u32[]{:S(2)}, u32[]{:S(2)}) async-start(bf16[8,80,1152]{2,1,0:T(8,128)(2,1)} %shard_map.108.refs_3_), calls=%async_computation.1 | async-start | bytes 2949120 | tf_op jit(solution)/shard_map/all_to_all | solution.py:452
  134.9 32.3 %all-to-all-done.1.refs_1_ = bf16[8,80,1152]{2,1,0:T(8,128)(2,1)} async-done(((bf16[8,80,1152]{2,1,0:T(8,128)(2,1)}), bf16[8,80,1152]{2,1,0:T(8,128)(2,1)}, u32[]{:S(2)}, u32[]{:S(2)}) %all-to-all-start.1) | async-done | bytes 1474592 | tf_op jit(solution)/shard_map/all_to_all | solution.py:452
  167.2 10.7 %shard_map.109 = (bf16[3,2,144,1152]{3,2,1,0:T(8,128)(2,1)}, bf16[3,2,144,1152]{3,2,1,0:T(8,128)(2,1)}, bf16[3,2,144,1152]{3,2,1,0:T(8,128)(2,1)}, bf16[3,2,144,1152]{3,2,1,0:T(8,128)(2,1)}) custom-call(s32[4]{0:T(128)} %iota_xor_fusion.js, bf16[8,64,1152]{2,1,0:T(8,128)(2,1)} %all-to-all-done.refs_0_, bf16[8,80,1152]{2,1,0:T(8,128)(2,1)} %all-to-all-done.1.refs_1_), custom_call_target="tpu_custom_call" | custom-call | flops 3057647616 | bytes 10616832 | tf_op jit(solution)/shard_map/pallas_call | solution.py:160
  181.4 10.5 %collective-permute-done.9.refs_4_ = bf16[2,2,144,1152]{3,2,1,0:T(8,128)(2,1)} collective-permute-done((bf16[2,2,144,1152]{3,2,1,0:T(8,128)(2,1)}, bf16[2,2,144,1152]{3,2,1,0:T(8,128)(2,1)}, u32[]{:S(2)}, u32[]{:S(2)}) %collective-permute-start.9) | collective-permute-done | bytes 1327136 | tf_op jit(solution)/shard_map/ppermute | solution.py:430
  192.1 11.8 %shard_map.111 = (bf16[144,1152]{1,0:T(8,128)(2,1)}, bf16[144,1152]{1,0:T(8,128)(2,1)}, bf16[144,1152]{1,0:T(8,128)(2,1)}, bf16[144,1152]{1,0:T(8,128)(2,1)}, bf...) custom-call(s32[4]{0:T(128)} %iota_xor_fusion.js, ...), custom_call_target="tpu_custom_call" | custom-call | flops 3057647616 | bytes 10616832 | tf_op jit(solution)/shard_map/pallas_call | solution.py:219
  207.8 7.3 %collective-permute-done.12.refs_2_ = bf16[144,1152]{1,0:T(8,128)(2,1)} collective-permute-done((bf16[144,1152]{1,0:T(8,128)(2,1)}, bf16[144,1152]{1,0:T(8,128)(2,1)}, u32[]{:S(2)}, u32[]{:S(2)}) %collective-permute-start.12) | collective-permute-done | bytes 331808 | tf_op jit(solution)/shard_map/ppermute | solution.py:462
  215.1 2.8 collective-permute-start.14
  217.9 9.3 %collective-permute-done.13.refs_3_ = bf16[144,1152]{1,0:T(8,128)(2,1)} collective-permute-done((bf16[144,1152]{1,0:T(8,128)(2,1)}, bf16[144,1152]{1,0:T(8,128)(2,1)}, u32[]{:S(2)}, u32[]{:S(2)}) %collective-permute-start.13) | collective-permute-done | bytes 331808 | tf_op jit(solution)/shard_map/ppermute | solution.py:462
  227.8 13.5 %collective-permute-done.14.refs_4_ = bf16[144,1152]{1,0:T(8,128)(2,1)} collective-permute-done((bf16[144,1152]{1,0:T(8,128)(2,1)}, bf16[144,1152]{1,0:T(8,128)(2,1)}, u32[]{:S(2)}, u32[]{:S(2)}) %collective-permute-start.14) | collective-permute-done | bytes 331808 | tf_op jit(solution)/shard_map/ppermute | solution.py:462
  241.3 3.7 collective-permute-start.16
  245.0 7.6 %collective-permute-done.15.refs_5_ = bf16[144,1152]{1,0:T(8,128)(2,1)} collective-permute-done((bf16[144,1152]{1,0:T(8,128)(2,1)}, bf16[144,1152]{1,0:T(8,128)(2,1)}, u32[]{:S(2)}, u32[]{:S(2)}) %collective-permute-start.15) | collective-permute-done | bytes 331808 | tf_op jit(solution)/shard_map/ppermute | solution.py:462
  252.6 6.3 %collective-permute-start.17 = (bf16[144,1152]{1,0:T(8,128)(2,1)}, bf16[144,1152]{1,0:T(8,128)(2,1)}, u32[]{:S(2)}, u32[]{:S(2)}) collective-permute-start(bf16[144,1152]{1,0:T(8,128)(2,1)} %get-tuple-element.66), channel_id=1, source_target_pairs={{0,28},{4,24},{8,20},{12,16},{16,12},{20,8},{24,4},{28,0},{1,29},{... | collective-permute-start | bytes 995336 | tf_op jit(solution)/shard_map/ppermute | solution.py:462
  260.8 6.6 %collective-permute-done.17.refs_7_ = bf16[144,1152]{1,0:T(8,128)(2,1)} collective-permute-done((bf16[144,1152]{1,0:T(8,128)(2,1)}, bf16[144,1152]{1,0:T(8,128)(2,1)}, u32[]{:S(2)}, u32[]{:S(2)}) %collective-permute-start.17) | collective-permute-done | bytes 331808 | tf_op jit(solution)/shard_map/ppermute | solution.py:462
  267.4 9.8 %collective-permute-done.19.refs_9_ = bf16[3,2,144,1152]{3,2,1,0:T(8,128)(2,1)} collective-permute-done((bf16[3,2,144,1152]{3,2,1,0:T(8,128)(2,1)}, bf16[3,2,144,1152]{3,2,1,0:T(8,128)(2,1)}, u32[]{:S(2)}, u32[]{:S(2)}) %collective-permute-start.19) | collective-permute-done | bytes 1990688 | tf_op jit(solution)/shard_map/ppermute | solution.py:430
  286.2 10.3 %shard_map.113 = (f32[4,4,144,576]{3,2,1,0:T(8,128)}, f32[4,8,128]{2,1,0:T(8,128)}) custom-call(s32[4]{0:T(128)} %iota_xor_fusion.js, bf16[3,2,144,1152]{3,2,1,0:T(8,128)(2,1)} %get-tuple-element.52.refs_6_.refs_0_, bf16[3,2,144,1152]{3,2,1,0:T(8,128)(2,1)} %get-tuple-element.70.refs_1_, bf16[3,2,144,1152]{3,2,1,0:T(8,128)(2,1)} %get-tuple-element.71.refs_2_, ...), custom_call_target="tpu_custom_call" | custom-call | bytes 13271040 | tf_op jit(solution)/shard_map/pallas_call | solution.py:325
  299.5 27.7 %psum.14 = f32[8,2,4,4]{2,0,3,1:T(8,128)S(1)} all-reduce(f32[8,2,4,4]{2,0,3,1:T(8,128)S(1)} %broadcast_select_fusion), channel_id=1, replica_groups=mesh['fsdp'=8,'replica'=4] {'fsdp'}, use_global_device_ids=true, to_apply=%region_2.3 | all-reduce | flops 256 | bytes 2048 | tf_op jit(solution)/shard_map/psum | solution.py:480
  327.2 23.4 %psum.15 = f32[8,2,4,4]{2,0,3,1:T(8,128)S(1)} all-reduce(f32[8,2,4,4]{2,0,3,1:T(8,128)S(1)} %psum.14), channel_id=1, replica_groups=mesh['fsdp'=8,'replica'=4] {'replica'}, use_global_device_ids=true, to_apply=%region_3.4 | all-reduce | flops 256 | bytes 2048 | tf_op jit(solution)/shard_map/psum | solution.py:481
  354.7 13.0 %shard_map.116 = (f32[4,4,144,576]{3,2,1,0:T(8,128)}, f32[4,4,144,576]{3,2,1,0:T(8,128)}) custom-call(s32[4]{0:T(128)} %iota_xor_fusion.js, bf16[3,2,144,1152]{3,2,1,0:T(8,128)(2,1)} %get-tuple-element.52.refs_6_.refs_0_, bf16[3,2,144,1152]{3,2,1,0:T(8,128)(2,1)} %get-tuple-element.70.refs_1_, bf16[3,2,144,1152]{3,2,1,0:T(8,128)(2,1)} %get-tuple-element.71.refs_2_, ...), custom_call_target="tpu_custom_call" | custom-call | bytes 26542080 | tf_op jit(solution)/shard_map/pallas_call | solution.py:325
  367.6 11.7 %collective-permute-done.25.refs_6_ = bf16[4,144,1152]{2,1,0:T(8,128)(2,1)} collective-permute-done((bf16[4,144,1152]{2,1,0:T(8,128)(2,1)}, bf16[4,144,1152]{2,1,0:T(8,128)(2,1)}, u32[]{:S(2)}, u32[]{:S(2)}) %collective-permute-start.25) | collective-permute-done | bytes 1327136 | tf_op jit(solution)/shard_map/ppermute | solution.py:430
  379.9 8.7 %shard_map.115 = bf16[288,18432]{1,0:T(8,128)(2,1)} custom-call(s32[32]{0:T(128)} %multiply_add_fusion.src, s32[32]{0:T(128)} %get-tuple-element.94.item, f32[32]{0:T(128)} %select_reduce_fusion.refs_2_.scale, bf16[4,144,1152]{2,1,0:T(8,128)(2,1)} %get-tuple-element.75.refs_0_, bf16[4,144,1152]{2,1,0:T(8,128)(2,1)} %get-tuple-element.76.refs_1_, ...), custom_call_target="tpu_custom_call" | custom-call | bytes 21233664 | tf_op jit(solution)/shard_map/pallas_call | solution.py:387
  (84 shorter events, 51.1 us)
Async XLA Ops:
  2.6 0.6 copy-start.2
  8.7 30.2 %collective-permute-start.1 = (bf16[8,64,1152]{2,1,0:T(8,128)(2,1)}, bf16[8,64,1152]{2,1,0:T(8,128)(2,1)}, u32[]{:S(2)}, u32[]{:S(2)}) collective-permute-start(bf16[8,64,1152]{2,1,0:T(8,128)(2,1)} %get-tuple-element.44), channel_id=1, source_target_pairs={{0,2},{1,3},{2,0},{3,1},{4,6},{5,7},{6,4},{7,5},{8,10},{9,11},{10,... | collective-permute-start | bytes 3538952 | tf_op jit(solution)/shard_map/ppermute | solution.py:430
  11.7 30.6 %collective-permute-start = (bf16[8,64,1152]{2,1,0:T(8,128)(2,1)}, bf16[8,64,1152]{2,1,0:T(8,128)(2,1)}, u32[]{:S(2)}, u32[]{:S(2)}) collective-permute-start(bf16[8,64,1152]{2,1,0:T(8,128)(2,1)} %get-tuple-element.43.refs_0_), channel_id=1, source_target_pairs={{0,1},{1,0},{2,3},{3,2},{4,5},{5,4},{6,7},{7,6},{8,9},{9,8},{10,11... | collective-permute-start | bytes 3538952 | tf_op jit(solution)/shard_map/ppermute | solution.py:430
  18.4 79.2 %collective-permute-start.5 = (bf16[8,80,1152]{2,1,0:T(8,128)(2,1)}, bf16[8,80,1152]{2,1,0:T(8,128)(2,1)}, u32[]{:S(2)}, u32[]{:S(2)}) collective-permute-start(bf16[8,80,1152]{2,1,0:T(8,128)(2,1)} %get-tuple-element.49), channel_id=1, source_target_pairs={{0,2},{1,3},{2,0},{3,1},{4,6},{5,7},{6,4},{7,5},{8,10},{9,11},{10,... | collective-permute-start | bytes 4423688 | tf_op jit(solution)/shard_map/ppermute | solution.py:430
  18.9 81.8 %collective-permute-start.4 = (bf16[8,80,1152]{2,1,0:T(8,128)(2,1)}, bf16[8,80,1152]{2,1,0:T(8,128)(2,1)}, u32[]{:S(2)}, u32[]{:S(2)}) collective-permute-start(bf16[8,80,1152]{2,1,0:T(8,128)(2,1)} %get-tuple-element.45.refs_0_), channel_id=1, source_target_pairs={{0,1},{1,0},{2,3},{3,2},{4,5},{5,4},{6,7},{7,6},{8,9},{9,8},{10,11... | collective-permute-start | bytes 4423688 | tf_op jit(solution)/shard_map/ppermute | solution.py:430
  33.4 8.9 %copy-start.1 = (bf16[4,64,1152]{2,1,0:T(8,128)(2,1)S(1)}, bf16[4,64,1152]{2,1,0:T(8,128)(2,1)}, u32[]{:S(2)}) copy-start(bf16[4,64,1152]{2,1,0:T(8,128)(2,1)} %get-tuple-element.47) | copy-start | bytes 1769476
  40.2 43.5 %collective-permute-start.3 = (bf16[4,64,1152]{2,1,0:T(8,128)(2,1)S(1)}, bf16[4,64,1152]{2,1,0:T(8,128)(2,1)}, u32[]{:S(2)}, u32[]{:S(2)}) collective-permute-start(bf16[4,64,1152]{2,1,0:T(8,128)(2,1)S(1)} %add_convert_fusion.2), channel_id=1, source_target_pairs={{0,1},{1,0},{2,3},{3,2},{4,5},{5,4},{6,7},{7,6},{8,9},{9,8},{10,11... | collective-permute-start | bytes 1769480 | tf_op jit(solution)/shard_map/ppermute | solution.py:430
  43.5 40.2 %collective-permute-start.2 = (bf16[4,64,1152]{2,1,0:T(8,128)(2,1)S(1)}, bf16[4,64,1152]{2,1,0:T(8,128)(2,1)}, u32[]{:S(2)}, u32[]{:S(2)}) collective-permute-start(bf16[4,64,1152]{2,1,0:T(8,128)(2,1)S(1)} %add_convert_fusion.3), channel_id=1, source_target_pairs={{0,2},{1,3},{2,0},{3,1},{4,6},{5,7},{6,4},{7,5},{8,10},{9,11},{10,... | collective-permute-start | bytes 1769480 | tf_op jit(solution)/shard_map/ppermute | solution.py:430
  89.0 37.6 %all-to-all-start = ((bf16[8,64,1152]{2,1,0:T(8,128)(2,1)}), bf16[8,64,1152]{2,1,0:T(8,128)(2,1)}, u32[]{:S(2)}, u32[]{:S(2)}) async-start(bf16[8,64,1152]{2,1,0:T(8,128)(2,1)} %shard_map.106.refs_0_), calls=%async_computation | async-start | bytes 2359296 | tf_op jit(solution)/shard_map/all_to_all | solution.py:452
  97.5 3.2 copy-start
  99.2 19.1 %collective-permute-start.7 = (bf16[4,80,1152]{2,1,0:T(8,128)(2,1)S(1)}, bf16[4,80,1152]{2,1,0:T(8,128)(2,1)}, u32[]{:S(2)}, u32[]{:S(2)}) collective-permute-start(bf16[4,80,1152]{2,1,0:T(8,128)(2,1)S(1)} %add_convert_fusion), channel_id=1, source_target_pairs={{0,1},{1,0},{2,3},{3,2},{4,5},{5,4},{6,7},{7,6},{8,9},{9,8},{10,11... | collective-permute-start | bytes 2211848 | tf_op jit(solution)/shard_map/ppermute | solution.py:430
  102.0 18.8 %collective-permute-start.6 = (bf16[4,80,1152]{2,1,0:T(8,128)(2,1)S(1)}, bf16[4,80,1152]{2,1,0:T(8,128)(2,1)}, u32[]{:S(2)}, u32[]{:S(2)}) collective-permute-start(bf16[4,80,1152]{2,1,0:T(8,128)(2,1)S(1)} %add_convert_fusion.1), channel_id=1, source_target_pairs={{0,2},{1,3},{2,0},{3,1},{4,6},{5,7},{6,4},{7,5},{8,10},{9,11},{10,... | collective-permute-start | bytes 2211848 | tf_op jit(solution)/shard_map/ppermute | solution.py:430
  126.6 40.6 %all-to-all-start.1 = ((bf16[8,80,1152]{2,1,0:T(8,128)(2,1)}), bf16[8,80,1152]{2,1,0:T(8,128)(2,1)}, u32[]{:S(2)}, u32[]{:S(2)}) async-start(bf16[8,80,1152]{2,1,0:T(8,128)(2,1)} %shard_map.108.refs_3_), calls=%async_computation.1 | async-start | bytes 2949120 | tf_op jit(solution)/shard_map/all_to_all | solution.py:452
  131.4 47.6 %collective-permute-start.8 = (bf16[2,2,144,1152]{3,2,1,0:T(8,128)(2,1)}, bf16[2,2,144,1152]{3,2,1,0:T(8,128)(2,1)}, u32[]{:S(2)}, u32[]{:S(2)}) collective-permute-start(bf16[2,2,144,1152]{3,2,1,0:T(8,128)(2,1)} %get-tuple-element.56), channel_id=1, source_target_pairs={{0,1},{1,0},{2,3},{3,2},{4,5},{5,4},{6,7},{7,6},{8,9},{9,8},{10,11... | collective-permute-start | bytes 3981320 | tf_op jit(solution)/shard_map/ppermute | solution.py:430
  132.0 60.0 %collective-permute-start.9 = (bf16[2,2,144,1152]{3,2,1,0:T(8,128)(2,1)}, bf16[2,2,144,1152]{3,2,1,0:T(8,128)(2,1)}, u32[]{:S(2)}, u32[]{:S(2)}) collective-permute-start(bf16[2,2,144,1152]{3,2,1,0:T(8,128)(2,1)} %get-tuple-element.57), channel_id=1, source_target_pairs={{0,2},{1,3},{2,0},{3,1},{4,6},{5,7},{6,4},{7,5},{8,10},{9,11},{10,... | collective-permute-start | bytes 3981320 | tf_op jit(solution)/shard_map/ppermute | solution.py:430
  132.5 59.6 %collective-permute-start.10 = (bf16[2,2,144,1152]{3,2,1,0:T(8,128)(2,1)}, bf16[2,2,144,1152]{3,2,1,0:T(8,128)(2,1)}, u32[]{:S(2)}, u32[]{:S(2)}) collective-permute-start(bf16[2,2,144,1152]{3,2,1,0:T(8,128)(2,1)} %get-tuple-element.58), channel_id=1, source_target_pairs={{0,3},{1,2},{2,1},{3,0},{4,7},{5,6},{6,5},{7,4},{8,11},{9,10},{10,... | collective-permute-start | bytes 3981320 | tf_op jit(solution)/shard_map/ppermute | solution.py:430
  177.9 89.5 %collective-permute-start.18 = (bf16[3,2,144,1152]{3,2,1,0:T(8,128)(2,1)}, bf16[3,2,144,1152]{3,2,1,0:T(8,128)(2,1)}, u32[]{:S(2)}, u32[]{:S(2)}) collective-permute-start(bf16[3,2,144,1152]{3,2,1,0:T(8,128)(2,1)} %get-tuple-element.67), channel_id=1, source_target_pairs={{0,1},{1,0},{2,3},{3,2},{4,5},{5,4},{6,7},{7,6},{8,9},{9,8},{10,11... | collective-permute-start | bytes 5971976 | tf_op jit(solution)/shard_map/ppermute | solution.py:430
  178.5 98.8 %collective-permute-start.19 = (bf16[3,2,144,1152]{3,2,1,0:T(8,128)(2,1)}, bf16[3,2,144,1152]{3,2,1,0:T(8,128)(2,1)}, u32[]{:S(2)}, u32[]{:S(2)}) collective-permute-start(bf16[3,2,144,1152]{3,2,1,0:T(8,128)(2,1)} %get-tuple-element.68), channel_id=1, source_target_pairs={{0,2},{1,3},{2,0},{3,1},{4,6},{5,7},{6,4},{7,5},{8,10},{9,11},{10,... | collective-permute-start | bytes 5971976 | tf_op jit(solution)/shard_map/ppermute | solution.py:430
  179.0 98.3 %collective-permute-start.20 = (bf16[3,2,144,1152]{3,2,1,0:T(8,128)(2,1)}, bf16[3,2,144,1152]{3,2,1,0:T(8,128)(2,1)}, u32[]{:S(2)}, u32[]{:S(2)}) collective-permute-start(bf16[3,2,144,1152]{3,2,1,0:T(8,128)(2,1)} %get-tuple-element.69), channel_id=1, source_target_pairs={{0,3},{1,2},{2,1},{3,0},{4,7},{5,6},{6,5},{7,4},{8,11},{9,10},{10,... | collective-permute-start | bytes 5971976 | tf_op jit(solution)/shard_map/ppermute | solution.py:430
  204.0 2.1 collective-permute-start.11
  204.1 11.1 %collective-permute-start.12 = (bf16[144,1152]{1,0:T(8,128)(2,1)}, bf16[144,1152]{1,0:T(8,128)(2,1)}, u32[]{:S(2)}, u32[]{:S(2)}) collective-permute-start(bf16[144,1152]{1,0:T(8,128)(2,1)} %get-tuple-element.61), channel_id=1, source_target_pairs={{0,8},{4,12},{8,0},{12,4},{16,24},{20,28},{24,16},{28,20},{1,9},{5... | collective-permute-start | bytes 995336 | tf_op jit(solution)/shard_map/ppermute | solution.py:462
  206.1 21.2 %collective-permute-start.13 = (bf16[144,1152]{1,0:T(8,128)(2,1)}, bf16[144,1152]{1,0:T(8,128)(2,1)}, u32[]{:S(2)}, u32[]{:S(2)}) collective-permute-start(bf16[144,1152]{1,0:T(8,128)(2,1)} %get-tuple-element.62), channel_id=1, source_target_pairs={{0,12},{4,8},{8,4},{12,0},{16,28},{20,24},{24,20},{28,16},{1,13},{... | collective-permute-start | bytes 995336 | tf_op jit(solution)/shard_map/ppermute | solution.py:462
  215.1 26.2 %collective-permute-start.14 = (bf16[144,1152]{1,0:T(8,128)(2,1)}, bf16[144,1152]{1,0:T(8,128)(2,1)}, u32[]{:S(2)}, u32[]{:S(2)}) collective-permute-start(bf16[144,1152]{1,0:T(8,128)(2,1)} %get-tuple-element.63), channel_id=1, source_target_pairs={{0,16},{4,20},{8,24},{12,28},{16,0},{20,4},{24,8},{28,12},{1,17},{... | collective-permute-start | bytes 995336 | tf_op jit(solution)/shard_map/ppermute | solution.py:462
  227.3 25.4 %collective-permute-start.15 = (bf16[144,1152]{1,0:T(8,128)(2,1)}, bf16[144,1152]{1,0:T(8,128)(2,1)}, u32[]{:S(2)}, u32[]{:S(2)}) collective-permute-start(bf16[144,1152]{1,0:T(8,128)(2,1)} %get-tuple-element.64), channel_id=1, source_target_pairs={{0,20},{4,16},{8,28},{12,24},{16,4},{20,0},{24,12},{28,8},{1,21},{... | collective-permute-start | bytes 995336 | tf_op jit(solution)/shard_map/ppermute | solution.py:462
  241.3 19.5 %collective-permute-start.16 = (bf16[144,1152]{1,0:T(8,128)(2,1)}, bf16[144,1152]{1,0:T(8,128)(2,1)}, u32[]{:S(2)}, u32[]{:S(2)}) collective-permute-start(bf16[144,1152]{1,0:T(8,128)(2,1)} %get-tuple-element.65), channel_id=1, source_target_pairs={{0,24},{4,28},{8,16},{12,20},{16,8},{20,12},{24,0},{28,4},{1,25},{... | collective-permute-start | bytes 995336 | tf_op jit(solution)/shard_map/ppermute | solution.py:462
  252.6 14.8 %collective-permute-start.17 = (bf16[144,1152]{1,0:T(8,128)(2,1)}, bf16[144,1152]{1,0:T(8,128)(2,1)}, u32[]{:S(2)}, u32[]{:S(2)}) collective-permute-start(bf16[144,1152]{1,0:T(8,128)(2,1)} %get-tuple-element.66), channel_id=1, source_target_pairs={{0,28},{4,24},{8,20},{12,16},{16,12},{20,8},{24,4},{28,0},{1,29},{... | collective-permute-start | bytes 995336 | tf_op jit(solution)/shard_map/ppermute | solution.py:462
  279.9 72.1 %collective-permute-start.24 = (bf16[4,144,1152]{2,1,0:T(8,128)(2,1)}, bf16[4,144,1152]{2,1,0:T(8,128)(2,1)}, u32[]{:S(2)}, u32[]{:S(2)}) collective-permute-start(bf16[4,144,1152]{2,1,0:T(8,128)(2,1)} %get-tuple-element.75.refs_0_), channel_id=1, source_target_pairs={{0,2},{1,3},{2,0},{3,1},{4,6},{5,7},{6,4},{7,5},{8,10},{9,11},{10,... | collective-permute-start | bytes 3981320 | tf_op jit(solution)/shard_map/ppermute | solution.py:430
  281.2 70.8 %collective-permute-start.21 = (bf16[4,144,1152]{2,1,0:T(8,128)(2,1)}, bf16[4,144,1152]{2,1,0:T(8,128)(2,1)}, u32[]{:S(2)}, u32[]{:S(2)}) collective-permute-start(bf16[4,144,1152]{2,1,0:T(8,128)(2,1)} %get-tuple-element.75.refs_0_), channel_id=1, source_target_pairs={{0,1},{1,0},{2,3},{3,2},{4,5},{5,4},{6,7},{7,6},{8,9},{9,8},{10,11... | collective-permute-start | bytes 3981320 | tf_op jit(solution)/shard_map/ppermute | solution.py:430
  282.0 70.0 %collective-permute-start.23 = (bf16[4,144,1152]{2,1,0:T(8,128)(2,1)}, bf16[4,144,1152]{2,1,0:T(8,128)(2,1)}, u32[]{:S(2)}, u32[]{:S(2)}) collective-permute-start(bf16[4,144,1152]{2,1,0:T(8,128)(2,1)} %get-tuple-element.76.refs_1_), channel_id=1, source_target_pairs={{0,1},{1,0},{2,3},{3,2},{4,5},{5,4},{6,7},{7,6},{8,9},{9,8},{10,11... | collective-permute-start | bytes 3981320 | tf_op jit(solution)/shard_map/ppermute | solution.py:430
  283.3 68.7 %collective-permute-start.22 = (bf16[4,144,1152]{2,1,0:T(8,128)(2,1)}, bf16[4,144,1152]{2,1,0:T(8,128)(2,1)}, u32[]{:S(2)}, u32[]{:S(2)}) collective-permute-start(bf16[4,144,1152]{2,1,0:T(8,128)(2,1)} %get-tuple-element.76.refs_1_), channel_id=1, source_target_pairs={{0,2},{1,3},{2,0},{3,1},{4,6},{5,7},{6,4},{7,5},{8,10},{9,11},{10,... | collective-permute-start | bytes 3981320 | tf_op jit(solution)/shard_map/ppermute | solution.py:430
  352.0 27.4 %collective-permute-start.25 = (bf16[4,144,1152]{2,1,0:T(8,128)(2,1)}, bf16[4,144,1152]{2,1,0:T(8,128)(2,1)}, u32[]{:S(2)}, u32[]{:S(2)}) collective-permute-start(bf16[4,144,1152]{2,1,0:T(8,128)(2,1)} %get-tuple-element.77.refs_2_), channel_id=1, source_target_pairs={{0,2},{1,3},{2,0},{3,1},{4,6},{5,7},{6,4},{7,5},{8,10},{9,11},{10,... | collective-permute-start | bytes 3981320 | tf_op jit(solution)/shard_map/ppermute | solution.py:430
  352.9 27.0 %collective-permute-start.26 = (bf16[4,144,1152]{2,1,0:T(8,128)(2,1)}, bf16[4,144,1152]{2,1,0:T(8,128)(2,1)}, u32[]{:S(2)}, u32[]{:S(2)}) collective-permute-start(bf16[4,144,1152]{2,1,0:T(8,128)(2,1)} %get-tuple-element.78.refs_5_), channel_id=1, source_target_pairs={{0,1},{1,0},{2,3},{3,2},{4,5},{5,4},{6,7},{7,6},{8,9},{9,8},{10,11... | collective-permute-start | bytes 3981320 | tf_op jit(solution)/shard_map/ppermute | solution.py:430
  (1 other events, 0.5 us)
